TPU v7x, 32 devices: a whole 2x2x4 slice. The times are simulated.
32 devices in a mesh: section: 4 (over x, core), seq: 8 (over z, y).
Axes of the slice: x: 2, y: 2, z: 4, core: 2. Of those that a mesh axis runs over, the one named last changes fastest.
Arguments:
- inputs: bfloat16 [4, 2048, 1536], P('section', 'seq'), may hold values from -6 to 6
- lengths: int32 [4], replicated, may hold values from 256 to 2048, as said below
- cotangent: bfloat16 [4, 2048, 1536], P('section', 'seq'), may hold values from -6 to 6
- attn_gain: float32 [4, 1536], P('section', 'seq'), may hold values from 0.5 to 1.5
- w_query: float32 [4, 1536, 1536], P('section', 'seq'), may hold values from -0.15625 to 0.15625
- key_projection: float32 [4, 1536, 768], P('section', 'seq'), may hold values from -0.15625 to 0.15625
- value_projection: float32 [4, 1536, 768], P('section', 'seq'), may hold values from -0.15625 to 0.15625
- w_out: float32 [4, 1536, 1536], P('section', None, 'seq'), may hold values from -3.5 to 3.5
- mlp_gain: float32 [4, 1536], P('section', 'seq'), may hold values from 0.5 to 1.5
- w_gate: float32 [4, 1536, 4096], P('section', 'seq'), may hold values from -0.15625 to 0.15625
- w_up: float32 [4, 1536, 4096], P('section', 'seq'), may hold values from -0.15625 to 0.15625
- w_down: float32 [4, 4096, 1536], P('section', None, 'seq'), may hold values from -0.09375 to 0.09375
Outputs:
- output: bfloat16 [4, 2048, 1536], P('section', 'seq')
- input_grad: bfloat16 [4, 2048, 1536], P('section', 'seq')
- attn_gain_grad: float32 [4, 1536], P('section', 'seq')
- query_weight_grad: float32 [4, 1536, 1536], P('section', 'seq')
- key_weight_grad: float32 [4, 1536, 768], P('section', 'seq')
- value_weight_grad: float32 [4, 1536, 768], P('section', 'seq')
- out_weight_grad: float32 [4, 1536, 1536], P('section', None, 'seq')
- mlp_gain_grad: float32 [4, 1536], P('section', 'seq')
- gate_weight_grad: float32 [4, 1536, 4096], P('section', 'seq')
- up_weight_grad: float32 [4, 1536, 4096], P('section', 'seq')
- down_weight_grad: float32 [4, 4096, 1536], P('section', None, 'seq')
Inputs may be any that keep to these rules, and one draw needn't show every extreme that they name: Every micro-batch's sequence holds its first lengths[m] positions; one has 2048 and one 2048 // 8.
All inputs are finite; a program needn't handle non-finite values.
Results may differ from a plain program's by a relative error of at most 0.035.
Values may be sent and summed in bfloat16 or wider, within the bound.
A program may use at most 704 MiB of HBM per device.

v0:
```python
import math

import jax
import jax.numpy as jnp
from jax import lax
from jax.sharding import PartitionSpec as P

QUERY_HEADS = 16
KEY_VALUE_HEADS = 8
HEAD_SIZE = 96
FF = 4096


EPS = 1e-05
THETA = 100000.0
LOWER_LIMIT = -1e30


def from_behind(array, axis, by):
    peers = lax.axis_size(axis)
    pairs = [(i, i + by) for i in range(peers) if 0 <= i + by < peers]
    return lax.ppermute(array, axis, pairs)


def rope_tables(start_pos, count_of_rows, head_dim):
    positions = (start_pos + jnp.arange(count_of_rows)).astype(jnp.float32)
    exponents = 2.0 * jnp.arange(head_dim // 2).astype(jnp.float32) / head_dim
    angles = positions[:, None] * (THETA ** (-exponents))[None, :]
    return (jnp.cos(angles)[:, None, :], jnp.sin(angles)[:, None, :])


def rotate_halves(tensor, cosine_table, sine_values):
    half_width = tensor.shape[-1] // 2
    first_half = tensor[..., :half_width]
    second_half = tensor[..., half_width:]
    return jnp.concatenate(
        [
            first_half * cosine_table - second_half * sine_values,
            second_half * cosine_table + first_half * sine_values,
        ],
        axis=-1,
    )


def when_live(is_active, compute, operand):

    def placeholder(inner):
        return jax.tree.map(jnp.zeros_like, compute(inner))

    return lax.cond(is_active, compute, placeholder, operand)


def put(buffer, element, slot_index, is_active):
    previous = lax.dynamic_index_in_dim(buffer, slot_index, 0, keepdims=False)
    return lax.dynamic_update_index_in_dim(
        buffer, jnp.where(is_active, element, previous), slot_index, 0
    )


def norm_back(upstream, normed, inverse, gain_row):
    scaled = upstream * gain_row
    return inverse * (scaled - normed * jnp.mean(scaled * normed, axis=-1, keepdims=True))


def body(
    inputs,
    lengths,
    cotangent,
    attn_gain,
    w_query,
    key_projection,
    value_projection,
    w_out,
    mlp_gain,
    w_gate,
    w_up,
    w_down,
):
    section_count = lax.axis_size("section")
    section_index = lax.axis_index("section")
    device_rows = inputs.shape[1]
    width = inputs.shape[2]
    micro_count = lengths.shape[0]
    tick_count = micro_count + section_count - 1
    head_groups = QUERY_HEADS // KEY_VALUE_HEADS
    key_value_columns = KEY_VALUE_HEADS * HEAD_SIZE
    q_cols = QUERY_HEADS * HEAD_SIZE
    score_scale = 1.0 / math.sqrt(HEAD_SIZE)
    first_pos = lax.axis_index("seq") * device_rows
    seq_total = device_rows * lax.axis_size("seq")
    query_pos = first_pos + jnp.arange(device_rows)
    cosine_table, sine_values = rope_tables(first_pos, device_rows, HEAD_SIZE)

    def fetch():
        return (
            lax.all_gather(attn_gain[0].astype(jnp.bfloat16), "seq", axis=0, tiled=True),
            lax.all_gather(w_query[0].astype(jnp.bfloat16), "seq", axis=0, tiled=True),
            lax.all_gather(key_projection[0].astype(jnp.bfloat16), "seq", axis=0, tiled=True),
            lax.all_gather(value_projection[0].astype(jnp.bfloat16), "seq", axis=0, tiled=True),
            lax.all_gather(w_out[0].astype(jnp.bfloat16), "seq", axis=1, tiled=True),
            lax.all_gather(mlp_gain[0].astype(jnp.bfloat16), "seq", axis=0, tiled=True),
            lax.all_gather(w_gate[0].astype(jnp.bfloat16), "seq", axis=0, tiled=True),
            lax.all_gather(w_up[0].astype(jnp.bfloat16), "seq", axis=0, tiled=True),
            lax.all_gather(w_down[0].astype(jnp.bfloat16), "seq", axis=1, tiled=True),
        )

    def allowed_keys(key_total_count, length):
        key_positions = jnp.arange(key_total_count)
        allowed = (key_positions[None, :] <= query_pos[:, None]) & (key_positions[None, :] < length)
        return allowed[:, None, None, :]

    def buffer_of(columns, dtype):
        return jnp.zeros((micro_count, device_rows, columns), dtype)

    params = fetch()

    def front(block_in):
        x_full = block_in.astype(jnp.float32)
        inverse = lax.rsqrt(jnp.mean(x_full * x_full, axis=-1, keepdims=True) + EPS)
        first_input = (x_full * inverse * params[0].astype(jnp.float32)).astype(jnp.bfloat16)
        query_matrix = jnp.dot(first_input, params[1], preferred_element_type=jnp.float32).reshape(
            device_rows, QUERY_HEADS, HEAD_SIZE
        )
        key_rows = jnp.dot(first_input, params[2], preferred_element_type=jnp.float32).reshape(
            device_rows, KEY_VALUE_HEADS, HEAD_SIZE
        )
        values_low = jnp.dot(first_input, params[3], preferred_element_type=jnp.float32).astype(
            jnp.bfloat16
        )
        query_lower = (
            rotate_halves(query_matrix, cosine_table, sine_values)
            .astype(jnp.bfloat16)
            .reshape(device_rows, q_cols)
        )
        keys_low = (
            rotate_halves(key_rows, cosine_table, sine_values)
            .astype(jnp.bfloat16)
            .reshape(device_rows, key_value_columns)
        )
        return (inverse, first_input, query_lower, keys_low, values_low)

    def rear(operand):
        block_in, running_max, running_sum, summed = operand
        attended_output = (summed / running_sum[..., None]).reshape(device_rows, q_cols)
        logarithm_total = (running_max + jnp.log(running_sum)).reshape(device_rows, QUERY_HEADS)
        middle = block_in.astype(jnp.float32) + jnp.dot(
            attended_output.astype(jnp.bfloat16), params[4], preferred_element_type=jnp.float32
        )
        inverse_mid = lax.rsqrt(jnp.mean(middle * middle, axis=-1, keepdims=True) + EPS)
        second_in = (middle * inverse_mid * params[5].astype(jnp.float32)).astype(jnp.bfloat16)
        gate_pre = jnp.dot(second_in, params[6], preferred_element_type=jnp.float32)
        up_pre = jnp.dot(second_in, params[7], preferred_element_type=jnp.float32)
        hidden = (jax.nn.silu(gate_pre) * up_pre).astype(jnp.bfloat16)
        block_out = middle + jnp.dot(hidden, params[8], preferred_element_type=jnp.float32)
        return (
            block_out,
            attended_output,
            logarithm_total,
            middle,
            inverse_mid,
            second_in,
            gate_pre,
            up_pre,
            hidden,
        )

    def forward_fold(query_lower, length, is_active):
        heads_of_query = query_lower.reshape(device_rows, KEY_VALUE_HEADS, head_groups, HEAD_SIZE)

        def fold_step(fold_state, key_portion, piece_start):

            def accumulate(inner_state):
                running_max, running_sum, summed = inner_state
                key_total_count = key_portion[0].shape[0]
                heads_of_key = key_portion[0].reshape(key_total_count, KEY_VALUE_HEADS, HEAD_SIZE)
                heads_of_value = key_portion[1].reshape(key_total_count, KEY_VALUE_HEADS, HEAD_SIZE)
                scores = (
                    jnp.einsum(
                        "tkgd,nkd->tkgn",
                        heads_of_query,
                        heads_of_key,
                        preferred_element_type=jnp.float32,
                    )
                    * score_scale
                )
                allowed = allowed_keys(key_total_count, length)
                scores = jnp.where(allowed, scores, LOWER_LIMIT)
                new_max = jnp.maximum(running_max, jnp.max(scores, axis=-1))
                weights_now = jnp.where(allowed, jnp.exp(scores - new_max[..., None]), 0.0)
                running_sum = jnp.sum(weights_now, axis=-1)
                summed = jnp.einsum(
                    "tkgn,nkd->tkgd",
                    weights_now.astype(jnp.bfloat16),
                    heads_of_value,
                    preferred_element_type=jnp.float32,
                )
                return (new_max, running_sum, summed)

            return lax.cond(is_active, accumulate, lambda inner_state: inner_state, fold_state)

        start_state = (
            jnp.full((device_rows, KEY_VALUE_HEADS, head_groups), LOWER_LIMIT, jnp.float32),
            jnp.zeros((device_rows, KEY_VALUE_HEADS, head_groups), jnp.float32),
            jnp.zeros((device_rows, KEY_VALUE_HEADS, head_groups, HEAD_SIZE), jnp.float32),
        )
        return (fold_step, start_state)

    saved = (
        buffer_of(width, jnp.bfloat16),
        buffer_of(1, jnp.float32),
        buffer_of(width, jnp.bfloat16),
        buffer_of(q_cols, jnp.bfloat16),
        buffer_of(key_value_columns, jnp.bfloat16),
        buffer_of(key_value_columns, jnp.bfloat16),
        buffer_of(q_cols, jnp.float32),
        buffer_of(QUERY_HEADS, jnp.float32),
        buffer_of(width, jnp.float32),
        buffer_of(1, jnp.float32),
        buffer_of(width, jnp.bfloat16),
        buffer_of(FF, jnp.float32),
        buffer_of(FF, jnp.float32),
        buffer_of(FF, jnp.bfloat16),
    )
    lane_pair = jnp.stack([inputs[0], jnp.zeros_like(inputs[0])])
    received = jnp.zeros_like(inputs[0])
    for tick_step in range(tick_count):
        position = tick_step - section_index
        is_active = (position >= 0) & (position < micro_count)
        slot_index = jnp.clip(position, 0, micro_count - 1)
        length = lengths[slot_index]
        block_in = jnp.where(section_index == 0, lane_pair[0], received)
        inverse, first_input, query_lower, keys_low, values_low = when_live(
            is_active, front, block_in
        )
        fold_step, start_state = forward_fold(query_lower, length, is_active)
        running_max, running_sum, summed = fold_step(
            start_state,
            (
                lax.all_gather(keys_low, "seq", axis=0, tiled=True),
                lax.all_gather(values_low, "seq", axis=0, tiled=True),
            ),
            jnp.int32(0),
        )
        (
            block_out,
            attended_output,
            logarithm_total,
            middle,
            inverse_mid,
            second_in,
            gate_pre,
            up_pre,
            hidden,
        ) = when_live(is_active, rear, (block_in, running_max, running_sum, summed))
        current = (
            block_in,
            inverse,
            first_input,
            query_lower,
            keys_low,
            values_low,
            attended_output,
            logarithm_total,
            middle,
            inverse_mid,
            second_in,
            gate_pre,
            up_pre,
            hidden,
        )
        saved = tuple(
            (put(buffer, element, slot_index, is_active) for buffer, element in zip(saved, current))
        )
        block_low = block_out.astype(jnp.bfloat16)
        lane_pair = jnp.stack(
            [lane_pair[0], jnp.where(section_index == section_count - 1, block_low, lane_pair[1])]
        )
        if tick_step + 1 < tick_count:
            received = from_behind(block_low, "section", 1)
            lane_pair = from_behind(lane_pair, "section", -1)
    output = lane_pair[1][None]
    params = fetch()

    def back_first(operand):
        upstream, middle, inverse_mid, gate_pre, up_pre, attended_output = operand
        hidden_grad = jnp.einsum(
            "td,fd->tf", upstream, params[8], preferred_element_type=jnp.float32
        )
        sigmoid_gate = jax.nn.sigmoid(gate_pre)
        gate_grad = hidden_grad * up_pre * sigmoid_gate * (1.0 + gate_pre * (1.0 - sigmoid_gate))
        up_grad = hidden_grad * gate_pre * sigmoid_gate
        pair_grad = jnp.concatenate([gate_grad, up_grad], axis=-1).astype(jnp.bfloat16)
        second_grad = jnp.einsum(
            "tf,df->td", pair_grad[:, :FF], params[6], preferred_element_type=jnp.float32
        ) + jnp.einsum(
            "tf,df->td", pair_grad[:, FF:], params[7], preferred_element_type=jnp.float32
        )
        normed_mid = middle * inverse_mid
        gain_two = jnp.sum(second_grad * normed_mid, axis=0)
        middle_grad = upstream.astype(jnp.float32) + norm_back(
            second_grad, normed_mid, inverse_mid, params[5].astype(jnp.float32)
        )
        attn_grad = middle_grad.astype(jnp.bfloat16)
        output_gradient = jnp.einsum(
            "td,cd->tc", attn_grad, params[4], preferred_element_type=jnp.float32
        ).astype(jnp.bfloat16)
        delta = jnp.sum(
            (output_gradient.astype(jnp.float32) * attended_output).reshape(
                device_rows, KEY_VALUE_HEADS, head_groups, HEAD_SIZE
            ),
            axis=-1,
        )
        return (middle_grad, pair_grad, attn_grad, output_gradient, delta, gain_two)

    def back_second(operand):
        query_grad, key_value_gradient, block_in, inverse, middle_grad = operand
        q_low = (
            rotate_halves(
                query_grad.reshape(device_rows, QUERY_HEADS, HEAD_SIZE), cosine_table, -sine_values
            )
            .astype(jnp.bfloat16)
            .reshape(device_rows, q_cols)
        )
        k_low = (
            rotate_halves(
                key_value_gradient[:, :key_value_columns].reshape(
                    device_rows, KEY_VALUE_HEADS, HEAD_SIZE
                ),
                cosine_table,
                -sine_values,
            )
            .astype(jnp.bfloat16)
            .reshape(device_rows, key_value_columns)
        )
        v_low = key_value_gradient[:, key_value_columns:].astype(jnp.bfloat16)
        first_grad = (
            jnp.einsum("tc,dc->td", q_low, params[1], preferred_element_type=jnp.float32)
            + jnp.einsum("tc,dc->td", k_low, params[2], preferred_element_type=jnp.float32)
            + jnp.einsum("tc,dc->td", v_low, params[3], preferred_element_type=jnp.float32)
        )
        normed = block_in.astype(jnp.float32) * inverse
        gain_one = jnp.sum(first_grad * normed, axis=0)
        in_grad = middle_grad + norm_back(
            first_grad, normed, inverse, params[0].astype(jnp.float32)
        )
        return (in_grad, jnp.concatenate([q_low, k_low, v_low], axis=-1), gain_one)

    def backward_fold(query_lower, output_gradient, delta, logarithm_total, length, is_active):
        heads_of_query = query_lower.reshape(device_rows, KEY_VALUE_HEADS, head_groups, HEAD_SIZE)
        gradient_heads = output_gradient.reshape(
            device_rows, KEY_VALUE_HEADS, head_groups, HEAD_SIZE
        )
        logarithm_heads = logarithm_total.reshape(device_rows, KEY_VALUE_HEADS, head_groups)

        def fold_step(fold_state, key_portion, piece_start):

            def accumulate(inner_state):
                key_total_count = key_portion[0].shape[0]
                heads_of_key = key_portion[0].reshape(key_total_count, KEY_VALUE_HEADS, HEAD_SIZE)
                heads_of_value = key_portion[1].reshape(key_total_count, KEY_VALUE_HEADS, HEAD_SIZE)
                scores = (
                    jnp.einsum(
                        "tkgd,nkd->tkgn",
                        heads_of_query,
                        heads_of_key,
                        preferred_element_type=jnp.float32,
                    )
                    * score_scale
                )
                allowed = allowed_keys(key_total_count, length)
                weights_now = jnp.where(
                    allowed,
                    jnp.exp(jnp.where(allowed, scores, LOWER_LIMIT) - logarithm_heads[..., None]),
                    0.0,
                )
                weight_grad = jnp.einsum(
                    "tkgd,nkd->tkgn",
                    gradient_heads,
                    heads_of_value,
                    preferred_element_type=jnp.float32,
                )
                score_grad = (weights_now * (weight_grad - delta[..., None])).astype(jnp.bfloat16)
                query_grad = (
                    jnp.einsum(
                        "tkgn,nkd->tkgd",
                        score_grad,
                        heads_of_key,
                        preferred_element_type=jnp.float32,
                    )
                    * score_scale
                )
                weight_rows = jnp.transpose(weights_now.astype(jnp.bfloat16), (3, 0, 1, 2)).reshape(
                    key_total_count, device_rows * QUERY_HEADS
                )
                score_rows = jnp.transpose(score_grad, (3, 0, 1, 2)).reshape(
                    key_total_count, device_rows * QUERY_HEADS
                )
                return (query_grad, weight_rows, score_rows)

            return lax.cond(is_active, accumulate, lambda inner_state: inner_state, fold_state)

        query_begin = jnp.zeros((device_rows, KEY_VALUE_HEADS, head_groups, HEAD_SIZE), jnp.float32)
        start_state = (
            query_begin,
            jnp.zeros((seq_total, device_rows * QUERY_HEADS), jnp.bfloat16),
            jnp.zeros((seq_total, device_rows * QUERY_HEADS), jnp.bfloat16),
        )
        return (fold_step, start_state)

    masked_start = jnp.where(
        (query_pos < lengths[section_index])[:, None], cotangent[0], jnp.zeros_like(cotangent[0])
    )
    lane_pair = jnp.stack([masked_start, jnp.zeros_like(masked_start)])
    received = jnp.zeros_like(masked_start)
    later = (
        buffer_of(q_cols + 2 * key_value_columns, jnp.bfloat16),
        buffer_of(width, jnp.bfloat16),
        buffer_of(2 * FF, jnp.bfloat16),
        buffer_of(width, jnp.bfloat16),
    )
    gain_first = jnp.zeros((width,), jnp.float32)
    gain_second = jnp.zeros((width,), jnp.float32)
    for tick_step in range(tick_count):
        position = tick_count - 1 - tick_step - section_index
        is_active = (position >= 0) & (position < micro_count)
        slot_index = jnp.clip(position, 0, micro_count - 1)
        length = lengths[slot_index]
        upstream = jnp.where(section_index == section_count - 1, lane_pair[0], received)
        held = tuple(
            (lax.dynamic_index_in_dim(buffer, slot_index, 0, keepdims=False) for buffer in saved)
        )
        (
            block_in,
            inverse,
            first_input,
            query_lower,
            keys_low,
            values_low,
            attended_output,
            logarithm_total,
            middle,
            inverse_mid,
            second_in,
            gate_pre,
            up_pre,
            hidden,
        ) = held
        middle_grad, pair_grad, attn_grad, output_gradient, delta, gain_two = when_live(
            is_active,
            back_first,
            (upstream, middle, inverse_mid, gate_pre, up_pre, attended_output),
        )
        fold_step, start_state = backward_fold(
            query_lower, output_gradient, delta, logarithm_total, length, is_active
        )
        fold_result = fold_step(
            start_state,
            (
                lax.all_gather(keys_low, "seq", axis=0, tiled=True),
                lax.all_gather(values_low, "seq", axis=0, tiled=True),
            ),
            jnp.int32(0),
        )
        query_grad = fold_result[0]
        probability_saved = fold_result[1]
        score_saved = fold_result[2]
        heads_of_query = query_lower.reshape(device_rows, KEY_VALUE_HEADS, head_groups, HEAD_SIZE)
        gradient_heads = output_gradient.reshape(
            device_rows, KEY_VALUE_HEADS, head_groups, HEAD_SIZE
        )
        count_of_rows = device_rows * lax.axis_size("seq")
        key_weight_rows = probability_saved.reshape(
            count_of_rows, device_rows, KEY_VALUE_HEADS, head_groups
        )
        key_score_rows = score_saved.reshape(
            count_of_rows, device_rows, KEY_VALUE_HEADS, head_groups
        )
        key_part = (
            jnp.einsum(
                "ntkg,tkgd->nkd", key_score_rows, heads_of_query, preferred_element_type=jnp.float32
            )
            * score_scale
        )
        value_part = jnp.einsum(
            "ntkg,tkgd->nkd", key_weight_rows, gradient_heads, preferred_element_type=jnp.float32
        )
        key_value_gradient = lax.psum_scatter(
            jnp.concatenate(
                [
                    key_part.reshape(count_of_rows, key_value_columns),
                    value_part.reshape(count_of_rows, key_value_columns),
                ],
                axis=-1,
            ).astype(jnp.bfloat16),
            "seq",
            scatter_dimension=0,
            tiled=True,
        ).astype(jnp.float32)
        in_grad, qkv_grad, gain_one = when_live(
            is_active, back_second, (query_grad, key_value_gradient, block_in, inverse, middle_grad)
        )
        current = (qkv_grad, attn_grad, pair_grad, upstream)
        later = tuple(
            (put(buffer, element, slot_index, is_active) for buffer, element in zip(later, current))
        )
        gain_first = gain_first + gain_one
        gain_second = gain_second + gain_two
        grad_low = in_grad.astype(jnp.bfloat16)
        lane_pair = jnp.stack([lane_pair[0], jnp.where(section_index == 0, grad_low, lane_pair[1])])
        if tick_step + 1 < tick_count:
            received = from_behind(grad_low, "section", -1)
            lane_pair = from_behind(lane_pair, "section", 1)
    input_grad = lane_pair[1][None]
    token_rows = micro_count * device_rows

    def flatten(buffer):
        return buffer.reshape(token_rows, buffer.shape[2])

    first_all = flatten(saved[2])
    attended_all = flatten(saved[6]).astype(jnp.bfloat16)
    second_all = flatten(saved[10])
    hidden_all = flatten(saved[13])
    qkv_all = flatten(later[0])
    attn_all = flatten(later[1])
    pair_all = flatten(later[2])
    mlp_all = flatten(later[3])
    weight_grad = lax.psum_scatter(
        jnp.concatenate(
            [
                jnp.einsum("tr,tc->rc", first_all, qkv_all, preferred_element_type=jnp.float32),
                jnp.einsum("tr,tc->rc", second_all, pair_all, preferred_element_type=jnp.float32),
                jnp.einsum("tr,tc->rc", attn_all, attended_all, preferred_element_type=jnp.float32),
                jnp.einsum("tr,tc->rc", mlp_all, hidden_all, preferred_element_type=jnp.float32),
            ],
            axis=1,
        ).astype(jnp.bfloat16),
        "seq",
        scatter_dimension=0,
        tiled=True,
    ).astype(jnp.float32)
    gain_one_part, gain_two_part = (
        lax.psum_scatter(gain_first, "seq", scatter_dimension=0, tiled=True),
        lax.psum_scatter(gain_second, "seq", scatter_dimension=0, tiled=True),
    )
    pair_start = q_cols + 2 * key_value_columns
    out_start = pair_start + 2 * FF
    down_start = out_start + q_cols
    grad_query = weight_grad[:, :q_cols]
    grad_key = weight_grad[:, q_cols : q_cols + key_value_columns]
    grad_value = weight_grad[:, q_cols + key_value_columns : pair_start]
    grad_gate = weight_grad[:, pair_start : pair_start + FF]
    grad_up = weight_grad[:, pair_start + FF : out_start]
    grad_out = weight_grad[:, out_start:down_start].T
    grad_down = weight_grad[:, down_start : down_start + FF].T
    return (
        output,
        input_grad,
        gain_one_part[None],
        grad_query[None],
        grad_key[None],
        grad_value[None],
        grad_out[None],
        gain_two_part[None],
        grad_gate[None],
        grad_up[None],
        grad_down[None],
    )


def solution(mesh):
    in_specs = (
        P("section", "seq", None),
        P(),
        P("section", "seq", None),
        P("section", "seq"),
        P("section", "seq", None),
        P("section", "seq", None),
        P("section", "seq", None),
        P("section", None, "seq"),
        P("section", "seq"),
        P("section", "seq", None),
        P("section", "seq", None),
        P("section", None, "seq"),
    )
    out_specs = (
        P("section", "seq", None),
        P("section", "seq", None),
        P("section", "seq"),
        P("section", "seq", None),
        P("section", "seq", None),
        P("section", "seq", None),
        P("section", None, "seq"),
        P("section", "seq"),
        P("section", "seq", None),
        P("section", "seq", None),
        P("section", None, "seq"),
    )
    return jax.shard_map(body, mesh=mesh, in_specs=in_specs, out_specs=out_specs, check_vma=False)
```

profile of v0, /device:TPU:2, one launch (start us, length us, event | category | flops | bytes accessed | tf_op | source)
XLA Modules:
  0.0 5862.1 jit_solution(16989010403023444026)
XLA Ops:
  64.4 53.4 all-gather.91.cloned.1.call-done
  117.8 81.2 %all-gather.87.cloned.1.call-done = bf16[1,1536,1536]{2,1,0:T(8,128)(2,1)} async-done(((bf16[1,192,1536]{2,1,0:T(8,128)(2,1)}), bf16[1,1536,1536]{2,1,0:T(8,128)(2,1)}) %all-gather.87.cloned.1.call-update) | async-done | bytes 4718608 | tf_op jit(solution)/shard_map/all_gather | solution.py:97
  217.6 57.4 all-gather.59.cloned.1.call-done
  275.0 63.2 %all-gather.61.cloned.1.call-done = bf16[2048,768]{0,1:T(8,128)(2,1)} async-done(((bf16[256,768]{0,1:T(8,128)(2,1)}), bf16[2048,768]{0,1:T(8,128)(2,1)}) %all-gather.61.cloned.1.call-update) | async-done | bytes 3145744 | tf_op jit(solution)/shard_map/all_gather | solution.py:240
  340.3 78.6 %all-gather.93.cloned.1.call-done = bf16[1,1536,1536]{1,2,0:T(8,128)(2,1)} async-done(((bf16[1,1536,192]{1,2,0:T(8,128)(2,1)}), bf16[1,1536,1536]{1,2,0:T(8,128)(2,1)}) %all-gather.93.cloned.1.call-update) | async-done | bytes 4718608 | tf_op jit(solution)/shard_map/all_gather | solution.py:100
  418.9 177.4 %all-gather.95.cloned.1.call-done = bf16[1,1536,4096]{2,1,0:T(8,128)(2,1)} async-done(((bf16[1,192,4096]{2,1,0:T(8,128)(2,1)}), bf16[1,1536,4096]{2,1,0:T(8,128)(2,1)}) %all-gather.95.cloned.1.call-update) | async-done | bytes 12582928 | tf_op jit(solution)/shard_map/all_gather | solution.py:102
  596.3 176.8 %all-gather.97.cloned.1.call-done = bf16[1,1536,4096]{2,1,0:T(8,128)(2,1)} async-done(((bf16[1,192,4096]{2,1,0:T(8,128)(2,1)}), bf16[1,1536,4096]{2,1,0:T(8,128)(2,1)}) %all-gather.97.cloned.1.call-update) | async-done | bytes 12582928 | tf_op jit(solution)/shard_map/all_gather | solution.py:103
  773.1 176.8 %all-gather.99.cloned.1.call-done = bf16[1,4096,1536]{1,2,0:T(8,128)(2,1)} async-done(((bf16[1,4096,192]{1,2,0:T(8,128)(2,1)}), bf16[1,4096,1536]{1,2,0:T(8,128)(2,1)}) %all-gather.99.cloned.1.call-update) | async-done | bytes 12582928 | tf_op jit(solution)/shard_map/all_gather | solution.py:104
  1011.6 71.4 %all-gather.63.cloned.1.call-done = bf16[2048,768]{0,1:T(8,128)(2,1)} async-done(((bf16[256,768]{0,1:T(8,128)(2,1)}), bf16[2048,768]{0,1:T(8,128)(2,1)}) %all-gather.63.cloned.1.call-update) | async-done | bytes 3145744 | tf_op jit(solution)/shard_map/all_gather | solution.py:239
  1083.0 63.3 %all-gather.65.cloned.1.call-done = bf16[2048,768]{0,1:T(8,128)(2,1)} async-done(((bf16[256,768]{0,1:T(8,128)(2,1)}), bf16[2048,768]{0,1:T(8,128)(2,1)}) %all-gather.65.cloned.1.call-update) | async-done | bytes 3145744 | tf_op jit(solution)/shard_map/all_gather | solution.py:240
  1164.0 74.9 %collective-permute-start.2 = (bf16[2,256,1536]{2,1,0:T(8,128)(2,1)}, bf16[2,256,1536]{2,1,0:T(8,128)(2,1)}, u32[]{:S(2)}, u32[]{:S(2)}) collective-permute-start(bf16[2,256,1536]{2,1,0:T(8,128)(2,1)} %pad_maximum_fusion.44), channel_id=1, source_target_pairs={{8,0},{16,8},{24,16},{9,1},{17,9},{25,17},{10,2},{18,10},{26,18},{... | collective-permute-start | bytes 4718600 | tf_op jit(solution)/shard_map/ppermute | solution.py:22
  1276.9 61.6 %all-gather.67.cloned.1.call-done = bf16[2048,768]{0,1:T(8,128)(2,1)} async-done(((bf16[256,768]{0,1:T(8,128)(2,1)}), bf16[2048,768]{0,1:T(8,128)(2,1)}) %all-gather.67.cloned.1.call-update) | async-done | bytes 3145744 | tf_op jit(solution)/shard_map/all_gather | solution.py:239
  1338.5 63.3 %all-gather.69.cloned.1.call-done = bf16[2048,768]{0,1:T(8,128)(2,1)} async-done(((bf16[256,768]{0,1:T(8,128)(2,1)}), bf16[2048,768]{0,1:T(8,128)(2,1)}) %all-gather.69.cloned.1.call-update) | async-done | bytes 3145744 | tf_op jit(solution)/shard_map/all_gather | solution.py:240
  1401.9 48.5 conditional.49
  1450.4 38.9 conditional.50
  1543.0 52.3 all-gather.71.cloned.1.call-done
  1595.2 63.2 %all-gather.73.cloned.1.call-done = bf16[2048,768]{0,1:T(8,128)(2,1)} async-done(((bf16[256,768]{0,1:T(8,128)(2,1)}), bf16[2048,768]{0,1:T(8,128)(2,1)}) %all-gather.73.cloned.1.call-update) | async-done | bytes 3145744 | tf_op jit(solution)/shard_map/all_gather | solution.py:240
  1658.4 48.6 conditional.52
  1707.0 38.5 conditional.53
  1851.0 60.2 %all-gather.77.cloned.1.call-done = bf16[2048,768]{0,1:T(8,128)(2,1)} async-done(((bf16[256,768]{0,1:T(8,128)(2,1)}), bf16[2048,768]{0,1:T(8,128)(2,1)}) %all-gather.77.cloned.1.call-update) | async-done | bytes 3145744 | tf_op jit(solution)/shard_map/all_gather | solution.py:240
  1911.2 48.8 conditional.55
  1960.0 38.6 conditional.56
  2101.1 63.3 %all-gather.81.cloned.1.call-done = bf16[2048,768]{0,1:T(8,128)(2,1)} async-done(((bf16[256,768]{0,1:T(8,128)(2,1)}), bf16[2048,768]{0,1:T(8,128)(2,1)}) %all-gather.81.cloned.1.call-update) | async-done | bytes 3145744 | tf_op jit(solution)/shard_map/all_gather | solution.py:240
  2164.4 48.7 conditional.58
  2213.1 38.7 conditional.59
  2472.4 63.3 %all-gather.105.cloned.1.call-done = bf16[1,2048,768]{1,2,0:T(8,128)(2,1)} async-done(((bf16[1,256,768]{1,2,0:T(8,128)(2,1)}), bf16[1,2048,768]{1,2,0:T(8,128)(2,1)}) %all-gather.105.cloned.1.call-update) | async-done | bytes 3145744 | tf_op jit(solution)/shard_map/all_gather | solution.py:459
  2585.1 197.5 %reduce-scatter.9.cloned.1.call-done = bf16[256,1536]{0,1:T(8,128)(2,1)} async-done(((bf16[2048,1536]{0,1:T(8,128)(2,1)}), bf16[256,1536]{0,1:T(8,128)(2,1)}) %reduce-scatter.9.cloned.1.call-update) | async-done | bytes 786448 | tf_op jit(solution)/shard_map/reduce_scatter | solution.py:487
  2814.6 50.1 conditional.66
  2864.7 45.4 all-gather.109.cloned.1.call-done
  2910.1 82.5 %conditional.67 = (f32[256,8,2,96]{0,3,2,1:T(8,128)}, bf16[2048,256,8,2]{1,0,3,2:T(8,128)(2,1)}, bf16[2048,256,8,2]{1,0,3,2:T(8,128)(2,1)}) conditional(s32[]{:T(128)} %convert_element_type.1112, () %tuple.551, (s32[256]{0:T(256)}, s32[]{:T(128)}, bf16[2048,768]{0,1:T(8,128)(2,1)}, bf16[256,8,2,96]{0,3,2,1:T(8,128)(2,1)}, ...), branch_computations={%region_87.88_spmd, %region_88.89_spmd} | conditional | flops 4960159744 | bytes 216145952 | solution.py:400
  3026.5 115.2 %reduce-scatter.11.cloned.1.call-done = bf16[256,1536]{0,1:T(8,128)(2,1)} async-done(((bf16[2048,1536]{0,1:T(8,128)(2,1)}), bf16[256,1536]{0,1:T(8,128)(2,1)}) %reduce-scatter.11.cloned.1.call-update) | async-done | bytes 786448 | tf_op jit(solution)/shard_map/reduce_scatter | solution.py:487
  3184.3 49.9 conditional.69
  3269.3 82.6 %conditional.70 = (f32[256,8,2,96]{0,3,2,1:T(8,128)}, bf16[2048,256,8,2]{1,0,3,2:T(8,128)(2,1)}, bf16[2048,256,8,2]{1,0,3,2:T(8,128)(2,1)}) conditional(s32[]{:T(128)} %convert_element_type.1111, () %tuple.557, (s32[256]{0:T(256)}, s32[]{:T(128)}, bf16[2048,768]{0,1:T(8,128)(2,1)}, bf16[256,8,2,96]{0,3,2,1:T(8,128)(2,1)}, ...), branch_computations={%region_99.100_spmd, %region_100.101_spmd} | conditional | flops 4960159744 | bytes 216145952 | solution.py:400
  3385.8 115.2 %reduce-scatter.13.cloned.1.call-done = bf16[256,1536]{0,1:T(8,128)(2,1)} async-done(((bf16[2048,1536]{0,1:T(8,128)(2,1)}), bf16[256,1536]{0,1:T(8,128)(2,1)}) %reduce-scatter.13.cloned.1.call-update) | async-done | bytes 786448 | tf_op jit(solution)/shard_map/reduce_scatter | solution.py:487
  3543.7 49.8 conditional.72
  3593.5 35.1 all-gather.117.cloned.1.call-done
  3628.6 82.6 %conditional.73 = (f32[256,8,2,96]{0,3,2,1:T(8,128)}, bf16[2048,256,8,2]{1,0,3,2:T(8,128)(2,1)}, bf16[2048,256,8,2]{1,0,3,2:T(8,128)(2,1)}) conditional(s32[]{:T(128)} %convert_element_type.1110, () %tuple.563, (s32[256]{0:T(256)}, s32[]{:T(128)}, bf16[2048,768]{0,1:T(8,128)(2,1)}, bf16[256,8,2,96]{0,3,2,1:T(8,128)(2,1)}, ...), branch_computations={%region_111.112_spmd, %region_112.113_spmd} | conditional | flops 4960159744 | bytes 216145952 | solution.py:400
  3745.1 115.1 %reduce-scatter.15.cloned.1.call-done = bf16[256,1536]{0,1:T(8,128)(2,1)} async-done(((bf16[2048,1536]{0,1:T(8,128)(2,1)}), bf16[256,1536]{0,1:T(8,128)(2,1)}) %reduce-scatter.15.cloned.1.call-update) | async-done | bytes 786448 | tf_op jit(solution)/shard_map/reduce_scatter | solution.py:487
  3902.8 49.8 conditional.75
  3952.6 35.8 all-gather.121.cloned.1.call-done
  3988.5 82.5 %conditional.76 = (f32[256,8,2,96]{0,3,2,1:T(8,128)}, bf16[2048,256,8,2]{1,0,3,2:T(8,128)(2,1)}, bf16[2048,256,8,2]{1,0,3,2:T(8,128)(2,1)}) conditional(s32[]{:T(128)} %convert_element_type.1109, () %tuple.569, (s32[256]{0:T(256)}, s32[]{:T(128)}, bf16[2048,768]{0,1:T(8,128)(2,1)}, bf16[256,8,2,96]{0,3,2,1:T(8,128)(2,1)}, ...), branch_computations={%region_123.124_spmd, %region_124.125_spmd} | conditional | flops 4960159744 | bytes 216145952 | solution.py:400
  4104.7 115.4 %reduce-scatter.17.cloned.1.call-done = bf16[256,1536]{0,1:T(8,128)(2,1)} async-done(((bf16[2048,1536]{0,1:T(8,128)(2,1)}), bf16[256,1536]{0,1:T(8,128)(2,1)}) %reduce-scatter.17.cloned.1.call-update) | async-done | bytes 786448 | tf_op jit(solution)/shard_map/reduce_scatter | solution.py:487
  4284.2 63.9 %all-gather.125.cloned.1.call-done = bf16[1,2048,768]{1,2,0:T(8,128)(2,1)} async-done(((bf16[1,256,768]{1,2,0:T(8,128)(2,1)}), bf16[1,2048,768]{1,2,0:T(8,128)(2,1)}) %all-gather.125.cloned.1.call-update) | async-done | bytes 3145744 | tf_op jit(solution)/shard_map/all_gather | solution.py:459
  4601.2 77.8 %collective-permute-start.23 = (bf16[256,1536]{1,0:T(8,128)(2,1)}, bf16[256,1536]{1,0:T(8,128)(2,1)}, u32[]{:S(2)}, u32[]{:S(2)}) collective-permute-start(bf16[256,1536]{1,0:T(8,128)(2,1)} %get-tuple-element.2667), channel_id=1, source_target_pairs={{8,0},{16,8},{24,16},{9,1},{17,9},{25,17},{10,2},{18,10},{26,18},{... | collective-permute-start | bytes 2359304 | tf_op jit(solution)/shard_map/ppermute | solution.py:22
  4781.6 36.6 bitcast_convert_fusion
  4818.2 143.8 %reduce-scatter.21.cloned.1.call-done = bf16[256,1536]{0,1:T(8,128)(2,1)} async-done(((bf16[2048,1536]{0,1:T(8,128)(2,1)}), bf16[256,1536]{0,1:T(8,128)(2,1)}) %reduce-scatter.21.cloned.1.call-update) | async-done | bytes 786448 | tf_op jit(solution)/shard_map/reduce_scatter | solution.py:487
  5025.0 36.1 all-reduce.4
  5064.5 779.6 %reduce-scatter.23.cloned.1.call-done = bf16[192,16896]{1,0:T(8,128)(2,1)} async-done(((bf16[1536,16896]{1,0:T(8,128)(2,1)}), bf16[192,16896]{1,0:T(8,128)(2,1)}) %reduce-scatter.23.cloned.1.call-update) | async-done | bytes 6488080 | tf_op jit(solution)/shard_map/reduce_scatter | solution.py:527
  (1350 shorter events, 2644.9 us)
Async XLA Ops:
  7.2 57.2 all-gather.89.cloned.1.call-start
  9.2 108.6 %all-gather.91.cloned.1.call-start = ((), (), s32[]{:S(2)}) async-start(), calls=%async_computation.32 | async-start | bytes 2654208 | tf_op jit(solution)/shard_map/all_gather | solution.py:99
  11.1 188.0 %all-gather.87.cloned.1.call-start = ((), (), s32[]{:S(2)}) async-start(), calls=%async_computation.30 | async-start | bytes 5308416 | tf_op jit(solution)/shard_map/all_gather | solution.py:97
  12.0 263.0 %all-gather.59.cloned.1.call-start = ((), (), s32[]{:S(2)}) async-start(), calls=%async_computation.8 | async-start | bytes 3538944 | tf_op jit(solution)/shard_map/all_gather | solution.py:239
  203.4 134.8 %all-gather.61.cloned.1.call-start = ((), (), s32[]{:S(2)}) async-start(), calls=%async_computation.9 | async-start | bytes 3538944 | tf_op jit(solution)/shard_map/all_gather | solution.py:240
  204.0 214.9 %all-gather.93.cloned.1.call-start = ((), (), s32[]{:S(2)}) async-start(), calls=%async_computation.33 | async-start | bytes 5308416 | tf_op jit(solution)/shard_map/all_gather | solution.py:100
  206.3 390.0 %all-gather.95.cloned.1.call-start = ((), (), s32[]{:S(2)}) async-start(), calls=%async_computation.34 | async-start | bytes 14155776 | tf_op jit(solution)/shard_map/all_gather | solution.py:102
  209.6 563.5 %all-gather.97.cloned.1.call-start = ((), (), s32[]{:S(2)}) async-start(), calls=%async_computation.35 | async-start | bytes 14155776 | tf_op jit(solution)/shard_map/all_gather | solution.py:103
  212.9 737.1 %all-gather.99.cloned.1.call-start = ((), (), s32[]{:S(2)}) async-start(), calls=%async_computation.36 | async-start | bytes 14155776 | tf_op jit(solution)/shard_map/all_gather | solution.py:104
  216.3 866.7 %all-gather.63.cloned.1.call-start = ((), (), s32[]{:S(2)}) async-start(), calls=%async_computation.10 | async-start | bytes 3538944 | tf_op jit(solution)/shard_map/all_gather | solution.py:239
  963.9 39.4 collective-permute-start
  965.8 36.6 collective-permute-start.1
  1010.8 135.5 %all-gather.65.cloned.1.call-start = ((), (), s32[]{:S(2)}) async-start(), calls=%async_computation.11 | async-start | bytes 3538944 | tf_op jit(solution)/shard_map/all_gather | solution.py:240
  1011.5 327.0 %all-gather.67.cloned.1.call-start = ((), (), s32[]{:S(2)}) async-start(), calls=%async_computation.12 | async-start | bytes 3538944 | tf_op jit(solution)/shard_map/all_gather | solution.py:239
  1164.0 93.1 %collective-permute-start.2 = (bf16[2,256,1536]{2,1,0:T(8,128)(2,1)}, bf16[2,256,1536]{2,1,0:T(8,128)(2,1)}, u32[]{:S(2)}, u32[]{:S(2)}) collective-permute-start(bf16[2,256,1536]{2,1,0:T(8,128)(2,1)} %pad_maximum_fusion.44), channel_id=1, source_target_pairs={{8,0},{16,8},{24,16},{9,1},{17,9},{25,17},{10,2},{18,10},{26,18},{... | collective-permute-start | bytes 4718600 | tf_op jit(solution)/shard_map/ppermute | solution.py:22
  1276.1 125.8 %all-gather.69.cloned.1.call-start = ((), (), s32[]{:S(2)}) async-start(), calls=%async_computation.13 | async-start | bytes 3538944 | tf_op jit(solution)/shard_map/all_gather | solution.py:240
  1276.9 318.4 %all-gather.71.cloned.1.call-start = ((), (), s32[]{:S(2)}) async-start(), calls=%async_computation.14 | async-start | bytes 3538944 | tf_op jit(solution)/shard_map/all_gather | solution.py:239
  1533.2 125.2 %all-gather.73.cloned.1.call-start = ((), (), s32[]{:S(2)}) async-start(), calls=%async_computation.15 | async-start | bytes 3538944 | tf_op jit(solution)/shard_map/all_gather | solution.py:240
  1533.8 317.2 %all-gather.75.cloned.1.call-start = ((), (), s32[]{:S(2)}) async-start(), calls=%async_computation.16 | async-start | bytes 3538944 | tf_op jit(solution)/shard_map/all_gather | solution.py:239
  1786.0 125.2 %all-gather.77.cloned.1.call-start = ((), (), s32[]{:S(2)}) async-start(), calls=%async_computation.17 | async-start | bytes 3538944 | tf_op jit(solution)/shard_map/all_gather | solution.py:240
  1826.7 274.4 %all-gather.79.cloned.1.call-start = ((), (), s32[]{:S(2)}) async-start(), calls=%async_computation.18 | async-start | bytes 3538944 | tf_op jit(solution)/shard_map/all_gather | solution.py:239
  2039.6 124.9 %all-gather.81.cloned.1.call-start = ((), (), s32[]{:S(2)}) async-start(), calls=%async_computation.19 | async-start | bytes 3538944 | tf_op jit(solution)/shard_map/all_gather | solution.py:240
  2069.1 327.2 %all-gather.83.cloned.1.call-start = ((), (), s32[]{:S(2)}) async-start(), calls=%async_computation.20 | async-start | bytes 3538944 | tf_op jit(solution)/shard_map/all_gather | solution.py:239
  2282.3 126.8 %all-gather.85.cloned.1.call-start = ((), (), s32[]{:S(2)}) async-start(), calls=%async_computation.21 | async-start | bytes 3538944 | tf_op jit(solution)/shard_map/all_gather | solution.py:240
  2314.2 158.2 %all-gather.107.cloned.1.call-start = ((), (), s32[]{:S(2)}) async-start(), calls=%async_computation.40 | async-start | bytes 3538944 | tf_op jit(solution)/shard_map/all_gather | solution.py:460
  2349.0 186.7 %all-gather.105.cloned.1.call-start = ((), (), s32[]{:S(2)}) async-start(), calls=%async_computation.39 | async-start | bytes 3538944 | tf_op jit(solution)/shard_map/all_gather | solution.py:459
  2381.2 401.4 %reduce-scatter.9.cloned.1.call-start = ((), (), s32[]{:S(2)}) async-start(), calls=%async_computation.22 | async-start | bytes 7077888 | tf_op jit(solution)/shard_map/reduce_scatter | solution.py:487
  2578.9 285.8 %all-gather.111.cloned.1.call-start = ((), (), s32[]{:S(2)}) async-start(), calls=%async_computation.42 | async-start | bytes 3538944 | tf_op jit(solution)/shard_map/all_gather | solution.py:460
  2579.7 330.4 %all-gather.109.cloned.1.call-start = ((), (), s32[]{:S(2)}) async-start(), calls=%async_computation.41 | async-start | bytes 3538944 | tf_op jit(solution)/shard_map/all_gather | solution.py:459
  2580.3 561.4 %reduce-scatter.11.cloned.1.call-start = ((), (), s32[]{:S(2)}) async-start(), calls=%async_computation.23 | async-start | bytes 7077888 | tf_op jit(solution)/shard_map/reduce_scatter | solution.py:487
  3025.0 209.3 %all-gather.115.cloned.1.call-start = ((), (), s32[]{:S(2)}) async-start(), calls=%async_computation.44 | async-start | bytes 3538944 | tf_op jit(solution)/shard_map/all_gather | solution.py:460
  3025.7 243.6 %all-gather.113.cloned.1.call-start = ((), (), s32[]{:S(2)}) async-start(), calls=%async_computation.43 | async-start | bytes 3538944 | tf_op jit(solution)/shard_map/all_gather | solution.py:459
  3026.4 474.6 %reduce-scatter.13.cloned.1.call-start = ((), (), s32[]{:S(2)}) async-start(), calls=%async_computation.24 | async-start | bytes 7077888 | tf_op jit(solution)/shard_map/reduce_scatter | solution.py:487
  3384.3 209.2 %all-gather.119.cloned.1.call-start = ((), (), s32[]{:S(2)}) async-start(), calls=%async_computation.46 | async-start | bytes 3538944 | tf_op jit(solution)/shard_map/all_gather | solution.py:460
  3385.0 243.6 %all-gather.117.cloned.1.call-start = ((), (), s32[]{:S(2)}) async-start(), calls=%async_computation.45 | async-start | bytes 3538944 | tf_op jit(solution)/shard_map/all_gather | solution.py:459
  3385.8 474.5 %reduce-scatter.15.cloned.1.call-start = ((), (), s32[]{:S(2)}) async-start(), calls=%async_computation.25 | async-start | bytes 7077888 | tf_op jit(solution)/shard_map/reduce_scatter | solution.py:487
  3743.6 209.0 %all-gather.123.cloned.1.call-start = ((), (), s32[]{:S(2)}) async-start(), calls=%async_computation.48 | async-start | bytes 3538944 | tf_op jit(solution)/shard_map/all_gather | solution.py:460
  3744.3 244.1 %all-gather.121.cloned.1.call-start = ((), (), s32[]{:S(2)}) async-start(), calls=%async_computation.47 | async-start | bytes 3538944 | tf_op jit(solution)/shard_map/all_gather | solution.py:459
  3745.1 474.9 %reduce-scatter.17.cloned.1.call-start = ((), (), s32[]{:S(2)}) async-start(), calls=%async_computation.26 | async-start | bytes 7077888 | tf_op jit(solution)/shard_map/reduce_scatter | solution.py:487
  4103.3 180.9 %all-gather.127.cloned.1.call-start = ((), (), s32[]{:S(2)}) async-start(), calls=%async_computation.50 | async-start | bytes 3538944 | tf_op jit(solution)/shard_map/all_gather | solution.py:460
  4103.9 244.2 %all-gather.125.cloned.1.call-start = ((), (), s32[]{:S(2)}) async-start(), calls=%async_computation.49 | async-start | bytes 3538944 | tf_op jit(solution)/shard_map/all_gather | solution.py:459
  4104.6 487.6 %reduce-scatter.19.cloned.1.call-start = ((), (), s32[]{:S(2)}) async-start(), calls=%async_computation.27 | async-start | bytes 7077888 | tf_op jit(solution)/shard_map/reduce_scatter | solution.py:487
  4391.1 310.3 %all-gather.103.cloned.1.call-start = ((), (), s32[]{:S(2)}) async-start(), calls=%async_computation.38 | async-start | bytes 3538944 | tf_op jit(solution)/shard_map/all_gather | solution.py:460
  4414.6 287.1 %all-gather.101.cloned.1.call-start = ((), (), s32[]{:S(2)}) async-start(), calls=%async_computation.37 | async-start | bytes 3538944 | tf_op jit(solution)/shard_map/all_gather | solution.py:459
  4439.8 522.2 %reduce-scatter.21.cloned.1.call-start = ((), (), s32[]{:S(2)}) async-start(), calls=%async_computation.28 | async-start | bytes 7077888 | tf_op jit(solution)/shard_map/reduce_scatter | solution.py:487
  4597.2 96.2 %collective-permute-start.22 = (bf16[2,256,1536]{2,1,0:T(8,128)(2,1)}, bf16[2,256,1536]{2,1,0:T(8,128)(2,1)}, u32[]{:S(2)}, u32[]{:S(2)}) collective-permute-start(bf16[2,256,1536]{2,1,0:T(8,128)(2,1)} %pad_maximum_fusion.54), channel_id=1, source_target_pairs={{0,8},{8,16},{16,24},{1,9},{9,17},{17,25},{2,10},{10,18},{18,26},{... | collective-permute-start | bytes 4718600 | tf_op jit(solution)/shard_map/ppermute | solution.py:22
  4601.2 87.6 %collective-permute-start.23 = (bf16[256,1536]{1,0:T(8,128)(2,1)}, bf16[256,1536]{1,0:T(8,128)(2,1)}, u32[]{:S(2)}, u32[]{:S(2)}) collective-permute-start(bf16[256,1536]{1,0:T(8,128)(2,1)} %get-tuple-element.2667), channel_id=1, source_target_pairs={{8,0},{16,8},{24,16},{9,1},{17,9},{25,17},{10,2},{18,10},{26,18},{... | collective-permute-start | bytes 2359304 | tf_op jit(solution)/shard_map/ppermute | solution.py:22
  4745.1 1099.0 %reduce-scatter.23.cloned.1.call-start = ((), (), s32[]{:S(2)}) async-start(), calls=%async_computation.29 | async-start | bytes 58392576 | tf_op jit(solution)/shard_map/reduce_scatter | solution.py:527
  (249 other events, 18888.5 us)
Sparse Core Ops, SparseCore 0:
  10.8 53.5 all-gather.88
  67.2 50.5 all-gather.90
  120.6 78.4 all-gather.86
  203.6 71.4 all-gather.58
  276.9 61.2 all-gather.60
  340.8 78.0 all-gather.92
  421.7 174.5 all-gather.94
  598.5 174.6 all-gather.96
  775.3 174.6 all-gather.98
  1010.9 72.0 all-gather.62
  1085.1 61.2 all-gather.64
  1276.2 62.2 all-gather.66
  1340.6 61.2 all-gather.68
  1533.3 61.8 all-gather.70
  1597.1 61.2 all-gather.72
  1786.1 61.8 all-gather.74
  1849.9 61.2 all-gather.76
  2039.7 61.3 all-gather.78
  2103.2 61.2 all-gather.80
  2282.4 63.2 all-gather.82
  2347.8 61.2 all-gather.84
  2411.1 61.2 all-gather.106
  2474.4 61.2 all-gather.104
  2579.0 203.5 reduce-scatter.8
  2784.7 62.1 all-gather.110
  2848.8 61.2 all-gather.108
  3025.1 116.5 reduce-scatter.10
  3143.7 62.2 all-gather.114
  3208.0 61.2 all-gather.112
  3384.4 116.5 reduce-scatter.12
  3503.1 62.1 all-gather.118
  3567.4 61.2 all-gather.116
  3743.7 116.5 reduce-scatter.14
  3862.3 62.1 all-gather.122
  3927.2 61.2 all-gather.120
  4103.4 116.5 reduce-scatter.16
  4221.9 62.1 all-gather.126
  4286.8 61.2 all-gather.124
  4391.3 182.6 reduce-scatter.18
  4576.1 62.2 all-gather.102
  4640.4 61.2 all-gather.100
  4745.2 216.7 reduce-scatter.20
  5022.8 821.2 reduce-scatter.22
where the time goes:
time: 5880 us; the launch traced here: 5860 us
  waiting for transfers between devices  3460 us (59%)
  matrix products  1010 us (17%)
  other arithmetic  587 us (10%)
  local copies, waits for them, and re-layouts  492 us (8%)
  starting transfers between devices  220 us (4%)
    reduce_scatter x7, waiting for transfers between devices, body(): lax.psum_scatter(jnp.concatenate([key_part.reshape(count_of_rows, key_val...  802 us
    reduce_scatter x1, waiting for transfers between devices, body(): lax.psum_scatter(jnp.concatenate([jnp.einsum('tr,tc->rc', first_all, qkv_...  780 us
    all_gather x14, waiting for transfers between devices, body(): lax.all_gather(keys_low, 'seq', axis=0, tiled=True)  523 us
    all_gather x14, waiting for transfers between devices, body(): lax.all_gather(values_low, 'seq', axis=0, tiled=True)  433 us
    dynamic_update_slice x116, other arithmetic, put(): lax.dynamic_update_index_in_dim(buffer, jnp.where(is_active, element, pre...  242 us
    ppermute x24, starting transfers between devices, from_behind(): return lax.ppermute(array, axis, pairs)  217 us
    dynamic_slice x95, local copies, waits for them, and re-layouts, put(): previous = lax.dynamic_index_in_dim(buffer, slot_index, 0, keepdims=False)  206 us
    all_gather x1, waiting for transfers between devices, fetch(): lax.all_gather(w_gate[0].astype(jnp.bfloat16), 'seq', axis=0, tiled=True)  177 us
  transfers between devices with their start and end apart: 67, of which 55 were waited for; matrix products, arithmetic and copies ran while one was open for 16% of the time, Pallas kernels for 0%

commit v1 on v0

v1 whole, which is shorter than its diff:
```python
import math

import jax
import jax.numpy as jnp
from jax import lax
from jax.sharding import Mesh
from jax.sharding import PartitionSpec as P

QUERY_HEADS = 16
KEY_VALUE_HEADS = 8
HEAD_SIZE = 96
FF = 4096

EPS = 1e-05
THETA = 100000.0
LOWER_LIMIT = -1e30

BF = jnp.bfloat16
F32 = jnp.float32

PLANE = ("x", "c", "y")


def dot(a, b, dims):
    return lax.dot_general(a, b, (dims, ((), ())), preferred_element_type=F32)


def dot_nn(a, b):
    return dot(a, b, ((1,), (0,)))


def dot_nt(a, b):
    return dot(a, b, ((1,), (1,)))


def dot_tn(a, b):
    return dot(a, b, ((0,), (0,)))


def rotate_halves(tensor, cosine, sine):
    half = tensor.shape[-1] // 2
    first = tensor[..., :half]
    second = tensor[..., half:]
    return jnp.concatenate(
        [first * cosine - second * sine, second * cosine + first * sine], axis=-1
    )


def norm_back(upstream, normed, inverse, gain_row):
    scaled = upstream * gain_row
    return inverse * (scaled - normed * jnp.mean(scaled * normed, axis=-1, keepdims=True))


def body(
    inputs,
    lengths,
    cotangent,
    attn_gain,
    w_query,
    key_projection,
    value_projection,
    w_out,
    mlp_gain,
    w_gate,
    w_up,
    w_down,
):
    sections = lax.axis_size("x") * lax.axis_size("c")
    planes = lax.axis_size("z")
    halves = lax.axis_size("y")
    extra = lax.axis_size("e")
    ranks = sections * halves
    layers = sections
    block = inputs.shape[1]
    width = inputs.shape[2]
    rows = w_query.shape[1]
    tokens = block * ranks
    all_tokens = tokens * extra
    head_group = QUERY_HEADS // KEY_VALUE_HEADS
    q_cols = head_group * HEAD_SIZE
    kv_cols = HEAD_SIZE
    ff_cols = FF // ranks
    score_scale = 1.0 / math.sqrt(HEAD_SIZE)

    def swap(array):
        names = ("x", "c", "z")
        pairs = [
            (s * planes + z, z * planes + s) for s in range(sections) for z in range(planes)
        ]
        return lax.ppermute(array, names, pairs)

    def gather_tokens(shard):
        return lax.all_gather(shard, PLANE, axis=0, tiled=True)

    def scatter_tokens(partial):
        return lax.psum_scatter(partial.astype(BF), PLANE, scatter_dimension=0, tiled=True).astype(F32)

    def by_rank(matrix):
        return matrix.reshape(rows, ranks, -1)

    attn_pack = jnp.concatenate(
        [
            by_rank(w_query[0]),
            by_rank(key_projection[0]),
            by_rank(value_projection[0]),
            by_rank(w_out[0].T),
        ],
        axis=2,
    )
    mlp_pack = jnp.concatenate(
        [by_rank(w_gate[0]), by_rank(w_up[0]), by_rank(w_down[0].T)], axis=2
    )

    def exchange(pack):
        moved = lax.all_to_all(
            jnp.swapaxes(pack.astype(BF), 0, 1), PLANE, split_axis=0, concat_axis=0, tiled=True
        )
        return moved.reshape(layers, halves, rows, pack.shape[2])

    def whole(part):
        if extra > 1:
            part = lax.all_gather(part, "e", axis=1, tiled=False)
        return lax.all_gather(part.reshape(-1, part.shape[-1]), "z", axis=0, tiled=True)

    def reduce_rows(grad):
        mine = lax.psum_scatter(grad.astype(BF), "z", scatter_dimension=0, tiled=True)
        mine = mine.reshape(halves, extra, rows, -1)
        if extra > 1:
            return lax.psum_scatter(mine, "e", scatter_dimension=1, tiled=False)
        return mine[:, 0]

    attn_parts = exchange(attn_pack)
    mlp_parts = exchange(mlp_pack)
    gains = jnp.stack([attn_gain[0], mlp_gain[0]]).astype(BF)
    gains = lax.all_gather(gains, ("x", "c", "z", "y", "e"), axis=0, tiled=False)
    gains = gains.reshape(layers, -1, 2, rows).transpose(0, 2, 1, 3).reshape(layers, 2, 1, width)
    gains = gains.astype(F32)

    rank = (lax.axis_index("x") * lax.axis_size("c") + lax.axis_index("c")) * halves + lax.axis_index("y")
    spot = lax.axis_index("e")
    length = lengths[lax.axis_index("z")]

    block_start = (jnp.arange(ranks) * extra + spot) * block
    positions = (block_start[:, None] + jnp.arange(block)[None, :]).reshape(tokens)
    exponents = 2.0 * jnp.arange(HEAD_SIZE // 2).astype(F32) / HEAD_SIZE
    angles = positions.astype(F32)[:, None] * (THETA ** (-exponents))[None, :]
    cosine = jnp.cos(angles)[:, None, :]
    sine = jnp.sin(angles)[:, None, :]
    key_positions = jnp.arange(all_tokens)
    allowed = (key_positions[None, :] <= positions[:, None]) & (key_positions[None, :] < length)
    allowed = allowed[:, None, :]

    def rotated(columns, heads, sign):
        turned = rotate_halves(columns.reshape(tokens, heads, HEAD_SIZE), cosine, sign * sine)
        return turned.reshape(tokens, heads * HEAD_SIZE).astype(BF)

    def all_keys(array):
        if extra == 1:
            return array
        stacked = lax.all_gather(array.reshape(ranks, block, -1), "e", axis=1, tiled=False)
        return stacked.reshape(all_tokens, -1)

    def own_keys(array):
        if extra == 1:
            return array
        stacked = array.astype(BF).reshape(ranks, extra, block, -1)
        return lax.psum_scatter(stacked, "e", scatter_dimension=1, tiled=False).reshape(tokens, -1).astype(F32)

    def attend(q, keys, values):
        scores = jnp.einsum(
            "tgd,nd->tgn", q.reshape(tokens, head_group, HEAD_SIZE), keys, preferred_element_type=F32
        ) * score_scale
        scores = jnp.where(allowed, scores, LOWER_LIMIT)
        top = jnp.max(scores, axis=-1, keepdims=True)
        weights = jnp.where(allowed, jnp.exp(scores - top), 0.0)
        total = jnp.sum(weights, axis=-1, keepdims=True)
        summed = jnp.einsum("tgn,nd->tgd", weights.astype(BF), values, preferred_element_type=F32)
        out = (summed / total).reshape(tokens, q_cols).astype(BF)
        return out, top + jnp.log(total)

    def attend_back(q, keys, values, out, log_total, grad_out):
        q3 = q.reshape(tokens, head_group, HEAD_SIZE)
        g3 = grad_out.reshape(tokens, head_group, HEAD_SIZE)
        scores = jnp.einsum("tgd,nd->tgn", q3, keys, preferred_element_type=F32) * score_scale
        weights = jnp.where(allowed, jnp.exp(jnp.where(allowed, scores, LOWER_LIMIT) - log_total), 0.0)
        delta = jnp.sum(
            g3.astype(F32) * out.reshape(tokens, head_group, HEAD_SIZE).astype(F32), axis=-1, keepdims=True
        )
        weight_grad = jnp.einsum("tgd,nd->tgn", g3, values, preferred_element_type=F32)
        score_grad = (weights * (weight_grad - delta)).astype(BF)
        dq = jnp.einsum("tgn,nd->tgd", score_grad, keys, preferred_element_type=F32) * score_scale
        dk = jnp.einsum("tgn,tgd->nd", score_grad, q3, preferred_element_type=F32) * score_scale
        dv = jnp.einsum("tgn,tgd->nd", weights.astype(BF), g3, preferred_element_type=F32)
        return dq.reshape(tokens, q_cols), dk, dv

    def inverse_of(x):
        return lax.rsqrt(jnp.mean(x * x, axis=-1, keepdims=True) + EPS)

    hidden_state = swap(inputs[0])
    saved = []
    for layer in range(layers):
        attn_w = whole(attn_parts[layer])
        mlp_w = whole(mlp_parts[layer])
        w_qkv, w_o = attn_w[:, : q_cols + 2 * kv_cols], attn_w[:, q_cols + 2 * kv_cols :]
        w_gu, w_d = mlp_w[:, : 2 * ff_cols], mlp_w[:, 2 * ff_cols :]
        h = hidden_state.astype(F32)
        r1 = inverse_of(h)
        a1 = gather_tokens((h * r1 * gains[layer, 0]).astype(BF))
        qkv = dot_nn(a1, w_qkv)
        q = rotated(qkv[:, :q_cols], head_group, 1.0)
        k = all_keys(rotated(qkv[:, q_cols : q_cols + kv_cols], 1, 1.0))
        v = all_keys(qkv[:, q_cols + kv_cols :].astype(BF))
        o, log_total = attend(q, k, v)
        mid = h + scatter_tokens(dot_nt(o, w_o))
        r2 = inverse_of(mid)
        a2 = gather_tokens((mid * r2 * gains[layer, 1]).astype(BF))
        gu = dot_nn(a2, w_gu)
        g, u = gu[:, :ff_cols], gu[:, ff_cols:]
        hid = (jax.nn.silu(g) * u).astype(BF)
        after = mid + scatter_tokens(dot_nt(hid, w_d))
        saved.append(
            (hidden_state, r1, a1, q, k, v, o, log_total, mid, r2, a2, gu.astype(BF), hid, w_qkv, w_o, w_gu, w_d)
        )
        hidden_state = after.astype(BF)
    output = swap(hidden_state)[None]

    my_positions = (rank * extra + spot) * block + jnp.arange(block)
    e = swap(cotangent[0])
    e = jnp.where((my_positions < length)[:, None], e, jnp.zeros_like(e))
    attn_grads = [None] * layers
    mlp_grads = [None] * layers
    gain_grads = [None] * layers
    for layer in reversed(range(layers)):
        (h_low, r1, a1, q, k, v, o, log_total, mid, r2, a2, gu, hid, w_qkv, w_o, w_gu, w_d) = saved[layer]
        e_all = gather_tokens(e)
        dhid = dot_nn(e_all, w_d)
        g, u = gu[:, :ff_cols].astype(F32), gu[:, ff_cols:].astype(F32)
        sig = jax.nn.sigmoid(g)
        dgu = jnp.concatenate([dhid * u * sig * (1.0 + g * (1.0 - sig)), dhid * g * sig], axis=1).astype(BF)
        da2 = scatter_tokens(dot_nt(dgu, w_gu))
        mlp_grads[layer] = reduce_rows(jnp.concatenate([dot_tn(a2, dgu), dot_tn(e_all, hid)], axis=1))
        n2 = mid * r2
        gain2 = jnp.sum(da2 * n2, axis=0)
        dmid = e.astype(F32) + norm_back(da2, n2, r2, gains[layer, 1])
        dat = gather_tokens(dmid.astype(BF))
        dob = dot_nn(dat, w_o).astype(BF)
        dq, dk, dv = attend_back(q, k, v, o, log_total, dob)
        dqkv = jnp.concatenate(
            [rotated(dq, head_group, -1.0), rotated(own_keys(dk), 1, -1.0), own_keys(dv).astype(BF)], axis=1
        )
        da1 = scatter_tokens(dot_nt(dqkv, w_qkv))
        attn_grads[layer] = reduce_rows(jnp.concatenate([dot_tn(a1, dqkv), dot_tn(dat, o)], axis=1))
        n1 = h_low.astype(F32) * r1
        gain1 = jnp.sum(da1 * n1, axis=0)
        gain_grads[layer] = jnp.stack([gain1, gain2])
        e = (dmid + norm_back(da1, n1, r1, gains[layer, 0])).astype(BF)
    input_grad = swap(e)[None]

    def send_home(grads):
        stacked = jnp.stack(grads).reshape(ranks, rows, -1)
        back = lax.all_to_all(stacked, PLANE, split_axis=0, concat_axis=0, tiled=True)
        return back.astype(F32)

    def columns(back, start, count):
        return jnp.swapaxes(back[:, :, start : start + count], 0, 1).reshape(rows, ranks * count)

    attn_back = send_home(attn_grads)
    mlp_back = send_home(mlp_grads)
    gain_all = jnp.stack(gain_grads).reshape(layers, 2, -1, rows).transpose(0, 2, 1, 3).reshape(-1, 2, rows)
    gain_all = lax.psum_scatter(gain_all, ("x", "c", "z", "y", "e"), scatter_dimension=0, tiled=False)
    at = q_cols + 2 * kv_cols
    return (
        output,
        input_grad,
        gain_all[0:1],
        columns(attn_back, 0, q_cols)[None],
        columns(attn_back, q_cols, kv_cols)[None],
        columns(attn_back, q_cols + kv_cols, kv_cols)[None],
        columns(attn_back, at, q_cols).T[None],
        gain_all[1:2],
        columns(mlp_back, 0, ff_cols)[None],
        columns(mlp_back, ff_cols, ff_cols)[None],
        columns(mlp_back, 2 * ff_cols, ff_cols).T[None],
    )


def solution(mesh):
    section, seq = mesh.devices.shape
    halves = KEY_VALUE_HEADS // section
    extra = seq // (section * halves)
    fine = Mesh(
        mesh.devices.reshape(section // 2, 2, section, halves, extra), ("x", "c", "z", "y", "e")
    )
    sec, sq = ("x", "c"), ("z", "y", "e")
    rows3 = P(sec, sq, None)
    cols3 = P(sec, None, sq)
    in_specs = (rows3, P(), rows3, P(sec, sq), rows3, rows3, rows3, cols3, P(sec, sq), rows3, rows3, cols3)
    out_specs = (rows3, rows3, P(sec, sq), rows3, rows3, rows3, cols3, P(sec, sq), rows3, rows3, cols3)
    return jax.shard_map(body, mesh=fine, in_specs=in_specs, out_specs=out_specs, check_vma=False)
```

time: 5880 us -> 3750 us (0.64)
  waiting for transfers between devices: 3460 us -> 2430 us
  other arithmetic: 587 us -> 204 us
  local copies, waits for them, and re-layouts: 492 us -> 110 us
  matrix products: 1010 us -> 687 us
  blocking collectives: 58.3 us -> 265 us
  starting transfers between devices: 220 us -> 31.2 us
    all_gather x35 -> x24, waiting for transfers between devices: 1730 us -> 1090 us  [the longest x16 690 us: gather_tokens(): return lax.all_gather(shard, PLANE, axis=0, tiled=True)]
    reduce_scatter x8 -> x24, waiting for transfers between devices: 1580 us -> 1210 us  [the longest x16 869 us: scatter_tokens(): lax.psum_scatter(partial.astype(BF), PLANE, scatter_dimension=0, tiled=True)]
    dot_general x94 -> x72, matrix products: 1010 us -> 687 us  [the longest x48 342 us: dot(): return lax.dot_general(a, b, (dims, ((), ())), preferred_element_type=F32)]
    dynamic_update_slice x116 -> x0, other arithmetic: 242 us -> none  [put(): lax.dynamic_update_index_in_dim(buffer, jnp.where(is_active, element, pre...]
    dynamic_slice x118 -> x1, local copies, waits for them, and re-layouts: 233 us -> 0.65 us  [body(): length = lengths[lax.axis_index('z')]]
    ppermute x24 -> x4, starting transfers between devices: 217 us -> 17.4 us  [swap(): return lax.ppermute(array, names, pairs)]
    all_to_all x0 -> x2, blocking collectives: none -> 101 us  [exchange(): lax.all_to_all(jnp.swapaxes(pack.astype(BF), 0, 1), PLANE, split_axis=0,...]
    all_gather x1, blocking collectives: 22.2 us -> 118 us  [body(): lax.all_gather(gains, ('x', 'c', 'z', 'y', 'e'), axis=0, tiled=False)]
  transfers between devices with their start and end apart: 67 -> 54, of which waited for: 55 -> 47; matrix products, arithmetic and copies ran while one was open for 16% -> 9% of each run, Pallas kernels for 0% -> 0%
where the time goes in v1:
time: 3750 us; the launch traced here: 3740 us
  waiting for transfers between devices  2430 us (65%)
  matrix products  687 us (18%)
  blocking collectives  265 us (7%)
  other arithmetic  204 us (5%)
  local copies, waits for them, and re-layouts  110 us (3%)
    reduce_scatter x16, waiting for transfers between devices, scatter_tokens(): lax.psum_scatter(partial.astype(BF), PLANE, scatter_dimension=0, tiled=True)  869 us
    all_gather x16, waiting for transfers between devices, gather_tokens(): return lax.all_gather(shard, PLANE, axis=0, tiled=True)  690 us
    all_gather x8, waiting for transfers between devices, whole(): lax.all_gather(part.reshape(-1, part.shape[-1]), 'z', axis=0, tiled=True)  397 us
    reduce_scatter x8, waiting for transfers between devices, reduce_rows(): lax.psum_scatter(grad.astype(BF), 'z', scatter_dimension=0, tiled=True)  345 us
    dot_general x48, matrix products, dot(): return lax.dot_general(a, b, (dims, ((), ())), preferred_element_type=F32)  342 us
    ppermute x4, waiting for transfers between devices, swap(): return lax.ppermute(array, names, pairs)  123 us
    all_gather x1, blocking collectives, body(): lax.all_gather(gains, ('x', 'c', 'z', 'y', 'e'), axis=0, tiled=False)  118 us
    all_to_all x2, blocking collectives, exchange(): lax.all_to_all(jnp.swapaxes(pack.astype(BF), 0, 1), PLANE, split_axis=0,...  101 us
  transfers between devices with their start and end apart: 54, of which 47 were waited for; matrix products, arithmetic and copies ran while one was open for 9% of the time, Pallas kernels for 0%

profile of v1, /device:TPU:2, one launch (start us, length us, event | category | flops | bytes accessed | tf_op | source)
XLA Modules:
  0.0 3743.2 jit_solution(6894624752951356140)
XLA Ops:
  15.4 27.4 all_to_all.20
  49.6 117.5 %all_gather.76 = bf16[32,2,192]{2,1,0:T(2,128)(2,1)S(1)} all-gather(bf16[1,2,192]{2,1,0:T(2,128)(2,1)S(1)} %pad_maximum_fusion.50), channel_id=1, replica_groups=mesh['x'=2,'c'=2,'z'=4,'y'=2,'e'=1] {'x','c','z','y','e'}, dimensions={0}, use_global_device_ids=true | all-gather | bytes 25344 | tf_op jit(solution)/shard_map/all_gather | solution.py:135
  178.1 37.4 all-gather.25.cloned.1.call-done
  285.7 73.4 %all_to_all.21 = bf16[8,192,1536]{2,1,0:T(8,128)(2,1)S(1)} all-to-all(bf16[8,192,1536]{2,1,0:T(8,128)(2,1)S(1)} %copy.126), channel_id=1, replica_groups=mesh['x'=2,'c'=2,'z'=4,'y'=2,'e'=1] {'x','c','y'}, dimensions={0} | all-to-all | bytes 9437184 | tf_op jit(solution)/shard_map/all_to_all | solution.py:115
  377.8 87.7 %all-gather.31.cloned.1.call-done = bf16[1536,1536]{1,0:T(8,128)(2,1)} async-done(((bf16[384,1536]{1,0:T(8,128)(2,1)}), bf16[1536,1536]{1,0:T(8,128)(2,1)}) %all-gather.31.cloned.1.call-update) | async-done | bytes 4718608 | tf_op jit(solution)/shard_map/all_gather | solution.py:123
  465.5 46.4 %all-gather.29.cloned.1.call-done = bf16[2048,1536]{1,0:T(8,128)(2,1)} async-done(((bf16[256,1536]{1,0:T(8,128)(2,1)}), bf16[2048,1536]{1,0:T(8,128)(2,1)}) %all-gather.29.cloned.1.call-update) | async-done | bytes 6291472 | tf_op jit(solution)/shard_map/all_gather | solution.py:93
  533.7 61.0 %reduce-scatter.43.cloned.1.call-done = bf16[256,1536]{1,0:T(8,128)(2,1)} async-done(((bf16[2048,1536]{1,0:T(8,128)(2,1)}), bf16[256,1536]{1,0:T(8,128)(2,1)}) %reduce-scatter.43.cloned.1.call-update) | async-done | bytes 786448 | tf_op jit(solution)/shard_map/reduce_scatter | solution.py:96
  597.6 42.9 %all-gather.35.cloned.1.call-done = bf16[1536,576]{1,0:T(8,128)(2,1)} async-done(((bf16[384,576]{1,0:T(8,128)(2,1)}), bf16[1536,576]{1,0:T(8,128)(2,1)}) %all-gather.35.cloned.1.call-update) | async-done | bytes 1769488 | tf_op jit(solution)/shard_map/all_gather | solution.py:123
  640.5 46.8 %all-gather.33.cloned.1.call-done = bf16[2048,1536]{1,0:T(8,128)(2,1)} async-done(((bf16[256,1536]{1,0:T(8,128)(2,1)}), bf16[2048,1536]{1,0:T(8,128)(2,1)}) %all-gather.33.cloned.1.call-update) | async-done | bytes 6291472 | tf_op jit(solution)/shard_map/all_gather | solution.py:93
  750.8 61.2 %reduce-scatter.45.cloned.1.call-done = bf16[256,1536]{1,0:T(8,128)(2,1)} async-done(((bf16[2048,1536]{1,0:T(8,128)(2,1)}), bf16[256,1536]{1,0:T(8,128)(2,1)}) %reduce-scatter.45.cloned.1.call-update) | async-done | bytes 786448 | tf_op jit(solution)/shard_map/reduce_scatter | solution.py:96
  815.9 87.7 %all-gather.39.cloned.1.call-done = bf16[1536,1536]{1,0:T(8,128)(2,1)} async-done(((bf16[384,1536]{1,0:T(8,128)(2,1)}), bf16[1536,1536]{1,0:T(8,128)(2,1)}) %all-gather.39.cloned.1.call-update) | async-done | bytes 4718608 | tf_op jit(solution)/shard_map/all_gather | solution.py:123
  903.6 46.6 %all-gather.37.cloned.1.call-done = bf16[2048,1536]{1,0:T(8,128)(2,1)} async-done(((bf16[256,1536]{1,0:T(8,128)(2,1)}), bf16[2048,1536]{1,0:T(8,128)(2,1)}) %all-gather.37.cloned.1.call-update) | async-done | bytes 6291472 | tf_op jit(solution)/shard_map/all_gather | solution.py:93
  971.9 61.0 %reduce-scatter.47.cloned.1.call-done = bf16[256,1536]{1,0:T(8,128)(2,1)} async-done(((bf16[2048,1536]{1,0:T(8,128)(2,1)}), bf16[256,1536]{1,0:T(8,128)(2,1)}) %reduce-scatter.47.cloned.1.call-update) | async-done | bytes 786448 | tf_op jit(solution)/shard_map/reduce_scatter | solution.py:96
  1035.7 42.9 %all-gather.43.cloned.1.call-done = bf16[1536,576]{1,0:T(8,128)(2,1)} async-done(((bf16[384,576]{1,0:T(8,128)(2,1)}), bf16[1536,576]{1,0:T(8,128)(2,1)}) %all-gather.43.cloned.1.call-update) | async-done | bytes 1769488 | tf_op jit(solution)/shard_map/all_gather | solution.py:123
  1078.6 46.7 %all-gather.41.cloned.1.call-done = bf16[2048,1536]{1,0:T(8,128)(2,1)} async-done(((bf16[256,1536]{1,0:T(8,128)(2,1)}), bf16[2048,1536]{1,0:T(8,128)(2,1)}) %all-gather.41.cloned.1.call-update) | async-done | bytes 6291472 | tf_op jit(solution)/shard_map/all_gather | solution.py:93
  1189.1 61.2 %reduce-scatter.49.cloned.1.call-done = bf16[256,1536]{1,0:T(8,128)(2,1)} async-done(((bf16[2048,1536]{1,0:T(8,128)(2,1)}), bf16[256,1536]{1,0:T(8,128)(2,1)}) %reduce-scatter.49.cloned.1.call-update) | async-done | bytes 786448 | tf_op jit(solution)/shard_map/reduce_scatter | solution.py:96
  1254.2 87.7 %all-gather.47.cloned.1.call-done = bf16[1536,1536]{1,0:T(8,128)(2,1)} async-done(((bf16[384,1536]{1,0:T(8,128)(2,1)}), bf16[1536,1536]{1,0:T(8,128)(2,1)}) %all-gather.47.cloned.1.call-update) | async-done | bytes 4718608 | tf_op jit(solution)/shard_map/all_gather | solution.py:123
  1342.0 46.4 %all-gather.45.cloned.1.call-done = bf16[2048,1536]{1,0:T(8,128)(2,1)} async-done(((bf16[256,1536]{1,0:T(8,128)(2,1)}), bf16[2048,1536]{1,0:T(8,128)(2,1)}) %all-gather.45.cloned.1.call-update) | async-done | bytes 6291472 | tf_op jit(solution)/shard_map/all_gather | solution.py:93
  1410.1 61.0 %reduce-scatter.51.cloned.1.call-done = bf16[256,1536]{1,0:T(8,128)(2,1)} async-done(((bf16[2048,1536]{1,0:T(8,128)(2,1)}), bf16[256,1536]{1,0:T(8,128)(2,1)}) %reduce-scatter.51.cloned.1.call-update) | async-done | bytes 786448 | tf_op jit(solution)/shard_map/reduce_scatter | solution.py:96
  1474.0 42.9 %all-gather.51.cloned.1.call-done = bf16[1536,576]{1,0:T(8,128)(2,1)} async-done(((bf16[384,576]{1,0:T(8,128)(2,1)}), bf16[1536,576]{1,0:T(8,128)(2,1)}) %all-gather.51.cloned.1.call-update) | async-done | bytes 1769488 | tf_op jit(solution)/shard_map/all_gather | solution.py:123
  1517.0 46.7 %all-gather.49.cloned.1.call-done = bf16[2048,1536]{1,0:T(8,128)(2,1)} async-done(((bf16[256,1536]{1,0:T(8,128)(2,1)}), bf16[2048,1536]{1,0:T(8,128)(2,1)}) %all-gather.49.cloned.1.call-update) | async-done | bytes 6291472 | tf_op jit(solution)/shard_map/all_gather | solution.py:93
  1627.2 61.0 %reduce-scatter.53.cloned.1.call-done = bf16[256,1536]{1,0:T(8,128)(2,1)} async-done(((bf16[2048,1536]{1,0:T(8,128)(2,1)}), bf16[256,1536]{1,0:T(8,128)(2,1)}) %reduce-scatter.53.cloned.1.call-update) | async-done | bytes 786448 | tf_op jit(solution)/shard_map/reduce_scatter | solution.py:96
  1697.2 86.9 %collective-permute-done.2 = bf16[256,1536]{1,0:T(8,128)(2,1)S(1)} collective-permute-done((bf16[256,1536]{1,0:T(8,128)(2,1)S(1)}, bf16[256,1536]{1,0:T(8,128)(2,1)S(1)}, u32[]{:S(2)}, u32[]{:S(2)}) %collective-permute-start.2) | collective-permute-done | bytes 786464 | tf_op jit(solution)/shard_map/ppermute | solution.py:90
  1790.9 65.1 %all-gather.53.cloned.1.call-done = bf16[2048,1536]{1,0:T(8,128)(2,1)} async-done(((bf16[256,1536]{1,0:T(8,128)(2,1)}), bf16[2048,1536]{1,0:T(8,128)(2,1)}) %all-gather.53.cloned.1.call-update) | async-done | bytes 6291472 | tf_op jit(solution)/shard_map/all_gather | solution.py:93
  1868.8 35.2 all-gather.57.cloned.1.call-done
  1925.2 61.8 %reduce-scatter.57.cloned.1.call-done = bf16[256,1536]{1,0:T(8,128)(2,1)} async-done(((bf16[2048,1536]{1,0:T(8,128)(2,1)}), bf16[256,1536]{1,0:T(8,128)(2,1)}) %reduce-scatter.57.cloned.1.call-update) | async-done | bytes 786448 | tf_op jit(solution)/shard_map/reduce_scatter | solution.py:96
  1992.3 45.6 %all-gather.59.cloned.1.call-done = bf16[2048,1536]{1,0:T(8,128)(2,1)} async-done(((bf16[256,1536]{1,0:T(8,128)(2,1)}), bf16[2048,1536]{1,0:T(8,128)(2,1)}) %all-gather.59.cloned.1.call-update) | async-done | bytes 6291472 | tf_op jit(solution)/shard_map/all_gather | solution.py:93
  2116.7 48.9 %reduce-scatter.59.cloned.1.call-done = bf16[256,1536]{1,0:T(8,128)(2,1)} async-done(((bf16[2048,1536]{1,0:T(8,128)(2,1)}), bf16[256,1536]{1,0:T(8,128)(2,1)}) %reduce-scatter.59.cloned.1.call-update) | async-done | bytes 786448 | tf_op jit(solution)/shard_map/reduce_scatter | solution.py:96
  2168.0 63.1 %reduce-scatter.55.cloned.1.call-done = bf16[256,1536]{1,0:T(8,128)(2,1)} async-done(((bf16[2048,1536]{1,0:T(8,128)(2,1)}), bf16[256,1536]{1,0:T(8,128)(2,1)}) %reduce-scatter.55.cloned.1.call-update) | async-done | bytes 786448 | tf_op jit(solution)/shard_map/reduce_scatter | solution.py:96
  2235.5 45.5 %all-gather.61.cloned.1.call-done = bf16[2048,1536]{1,0:T(8,128)(2,1)} async-done(((bf16[256,1536]{1,0:T(8,128)(2,1)}), bf16[2048,1536]{1,0:T(8,128)(2,1)}) %all-gather.61.cloned.1.call-update) | async-done | bytes 6291472 | tf_op jit(solution)/shard_map/all_gather | solution.py:93
  2303.3 61.7 %reduce-scatter.61.cloned.1.call-done = bf16[256,1536]{1,0:T(8,128)(2,1)} async-done(((bf16[2048,1536]{1,0:T(8,128)(2,1)}), bf16[256,1536]{1,0:T(8,128)(2,1)}) %reduce-scatter.61.cloned.1.call-update) | async-done | bytes 786448 | tf_op jit(solution)/shard_map/reduce_scatter | solution.py:96
  2370.5 45.4 %all-gather.63.cloned.1.call-done = bf16[2048,1536]{1,0:T(8,128)(2,1)} async-done(((bf16[256,1536]{1,0:T(8,128)(2,1)}), bf16[2048,1536]{1,0:T(8,128)(2,1)}) %all-gather.63.cloned.1.call-update) | async-done | bytes 6291472 | tf_op jit(solution)/shard_map/all_gather | solution.py:93
  2487.8 61.8 %reduce-scatter.63.cloned.1.call-done = bf16[256,1536]{1,0:T(8,128)(2,1)} async-done(((bf16[2048,1536]{1,0:T(8,128)(2,1)}), bf16[256,1536]{1,0:T(8,128)(2,1)}) %reduce-scatter.63.cloned.1.call-update) | async-done | bytes 786448 | tf_op jit(solution)/shard_map/reduce_scatter | solution.py:96
  2555.6 45.5 %all-gather.65.cloned.1.call-done = bf16[2048,1536]{1,0:T(8,128)(2,1)} async-done(((bf16[256,1536]{1,0:T(8,128)(2,1)}), bf16[2048,1536]{1,0:T(8,128)(2,1)}) %all-gather.65.cloned.1.call-update) | async-done | bytes 6291472 | tf_op jit(solution)/shard_map/all_gather | solution.py:93
  2623.4 61.8 %reduce-scatter.65.cloned.1.call-done = bf16[256,1536]{1,0:T(8,128)(2,1)} async-done(((bf16[2048,1536]{1,0:T(8,128)(2,1)}), bf16[256,1536]{1,0:T(8,128)(2,1)}) %reduce-scatter.65.cloned.1.call-update) | async-done | bytes 786448 | tf_op jit(solution)/shard_map/reduce_scatter | solution.py:96
  2690.6 45.4 %all-gather.67.cloned.1.call-done = bf16[2048,1536]{1,0:T(8,128)(2,1)} async-done(((bf16[256,1536]{1,0:T(8,128)(2,1)}), bf16[2048,1536]{1,0:T(8,128)(2,1)}) %all-gather.67.cloned.1.call-update) | async-done | bytes 6291472 | tf_op jit(solution)/shard_map/all_gather | solution.py:93
  2760.9 24.0 multiply_convert_fusion.1
  2807.6 61.8 %reduce-scatter.67.cloned.1.call-done = bf16[256,1536]{1,0:T(8,128)(2,1)} async-done(((bf16[2048,1536]{1,0:T(8,128)(2,1)}), bf16[256,1536]{1,0:T(8,128)(2,1)}) %reduce-scatter.67.cloned.1.call-update) | async-done | bytes 786448 | tf_op jit(solution)/shard_map/reduce_scatter | solution.py:96
  2875.2 45.5 %all-gather.69.cloned.1.call-done = bf16[2048,1536]{1,0:T(8,128)(2,1)} async-done(((bf16[256,1536]{1,0:T(8,128)(2,1)}), bf16[2048,1536]{1,0:T(8,128)(2,1)}) %all-gather.69.cloned.1.call-update) | async-done | bytes 6291472 | tf_op jit(solution)/shard_map/all_gather | solution.py:93
  2943.0 61.8 %reduce-scatter.69.cloned.1.call-done = bf16[256,1536]{1,0:T(8,128)(2,1)} async-done(((bf16[2048,1536]{1,0:T(8,128)(2,1)}), bf16[256,1536]{1,0:T(8,128)(2,1)}) %reduce-scatter.69.cloned.1.call-update) | async-done | bytes 786448 | tf_op jit(solution)/shard_map/reduce_scatter | solution.py:96
  3232.1 88.2 %reduce-scatter.83.cloned.1.call-done = bf16[384,1536]{1,0:T(8,128)(2,1)} async-done(((bf16[1536,1536]{1,0:T(8,128)(2,1)}), bf16[384,1536]{1,0:T(8,128)(2,1)}) %reduce-scatter.83.cloned.1.call-update) | async-done | bytes 1179664 | tf_op jit(solution)/shard_map/reduce_scatter | solution.py:126
  3320.3 88.1 %reduce-scatter.81.cloned.1.call-done = bf16[384,1536]{1,0:T(8,128)(2,1)} async-done(((bf16[1536,1536]{1,0:T(8,128)(2,1)}), bf16[384,1536]{1,0:T(8,128)(2,1)}) %reduce-scatter.81.cloned.1.call-update) | async-done | bytes 1179664 | tf_op jit(solution)/shard_map/reduce_scatter | solution.py:126
  3417.5 35.9 reduce-scatter.79.cloned.1.call-done
  3453.4 43.6 %reduce-scatter.77.cloned.1.call-done = bf16[384,576]{1,0:T(8,128)(2,1)} async-done(((bf16[1536,576]{1,0:T(8,128)(2,1)}), bf16[384,576]{1,0:T(8,128)(2,1)}) %reduce-scatter.77.cloned.1.call-update) | async-done | bytes 442384 | tf_op jit(solution)/shard_map/reduce_scatter | solution.py:126
  3497.0 43.0 %reduce-scatter.75.cloned.1.call-done = bf16[384,576]{1,0:T(8,128)(2,1)} async-done(((bf16[1536,576]{1,0:T(8,128)(2,1)}), bf16[384,576]{1,0:T(8,128)(2,1)}) %reduce-scatter.75.cloned.1.call-update) | async-done | bytes 442384 | tf_op jit(solution)/shard_map/reduce_scatter | solution.py:126
  3540.0 43.6 %reduce-scatter.73.cloned.1.call-done = bf16[384,576]{1,0:T(8,128)(2,1)} async-done(((bf16[1536,576]{1,0:T(8,128)(2,1)}), bf16[384,576]{1,0:T(8,128)(2,1)}) %reduce-scatter.73.cloned.1.call-update) | async-done | bytes 442384 | tf_op jit(solution)/shard_map/reduce_scatter | solution.py:126
  3595.0 36.2 collective-permute-done.1
  3686.7 46.3 %all-reduce = f32[32,2,192]{2,1,0:T(2,128)S(1)} all-reduce(f32[32,2,192]{2,1,0:T(2,128)S(1)} %copy.146), channel_id=18, replica_groups=mesh['x'=2,'c'=2,'z'=4,'y'=2,'e'=1] {'x','c','z','y','e'}, use_global_device_ids=true, to_apply=%region_52.53.clone | all-reduce | flops 12288 | bytes 98304
  (772 shorter events, 1040.0 us)
Async XLA Ops:
  7.2 170.9 %all-gather.27.cloned.1.call-start = ((), (), s32[]{:S(2)}) async-start(), calls=%async_computation.29 | async-start | bytes 2457600 | tf_op jit(solution)/shard_map/all_gather | solution.py:123
  44.2 171.2 %all-gather.25.cloned.1.call-start = ((), (), s32[]{:S(2)}) async-start(), calls=%async_computation.28 | async-start | bytes 7077888 | tf_op jit(solution)/shard_map/all_gather | solution.py:93
  44.4 123.5 %collective-permute-start = (bf16[256,1536]{1,0:T(8,128)(2,1)S(1)}, bf16[256,1536]{1,0:T(8,128)(2,1)S(1)}, u32[]{:S(2)}, u32[]{:S(2)}) collective-permute-start(bf16[256,1536]{1,0:T(8,128)(2,1)S(1)} %bitcast.381), channel_id=1, source_target_pairs={{0,0},{2,8},{4,16},{6,24},{8,2},{10,10},{12,18},{14,26},{16,4},{18... | collective-permute-start | bytes 2359304 | tf_op jit(solution)/shard_map/ppermute | solution.py:90
  169.4 204.6 %reduce-scatter.41.cloned.1.call-start = ((), (), s32[]{:S(2)}) async-start(), calls=%async_computation.30 | async-start | bytes 7077888 | tf_op jit(solution)/shard_map/reduce_scatter | solution.py:96
  278.1 187.4 %all-gather.31.cloned.1.call-start = ((), (), s32[]{:S(2)}) async-start(), calls=%async_computation.32 | async-start | bytes 5898240 | tf_op jit(solution)/shard_map/all_gather | solution.py:123
  361.4 150.6 %all-gather.29.cloned.1.call-start = ((), (), s32[]{:S(2)}) async-start(), calls=%async_computation.31 | async-start | bytes 7077888 | tf_op jit(solution)/shard_map/all_gather | solution.py:93
  377.8 216.9 %reduce-scatter.43.cloned.1.call-start = ((), (), s32[]{:S(2)}) async-start(), calls=%async_computation.33 | async-start | bytes 7077888 | tf_op jit(solution)/shard_map/reduce_scatter | solution.py:96
  533.6 153.7 %all-gather.33.cloned.1.call-start = ((), (), s32[]{:S(2)}) async-start(), calls=%async_computation.34 | async-start | bytes 7077888 | tf_op jit(solution)/shard_map/all_gather | solution.py:93
  597.5 214.5 %reduce-scatter.45.cloned.1.call-start = ((), (), s32[]{:S(2)}) async-start(), calls=%async_computation.36 | async-start | bytes 7077888 | tf_op jit(solution)/shard_map/reduce_scatter | solution.py:96
  750.2 153.5 %all-gather.39.cloned.1.call-start = ((), (), s32[]{:S(2)}) async-start(), calls=%async_computation.38 | async-start | bytes 5898240 | tf_op jit(solution)/shard_map/all_gather | solution.py:123
  750.8 199.5 %all-gather.37.cloned.1.call-start = ((), (), s32[]{:S(2)}) async-start(), calls=%async_computation.37 | async-start | bytes 7077888 | tf_op jit(solution)/shard_map/all_gather | solution.py:93
  815.9 217.0 %reduce-scatter.47.cloned.1.call-start = ((), (), s32[]{:S(2)}) async-start(), calls=%async_computation.39 | async-start | bytes 7077888 | tf_op jit(solution)/shard_map/reduce_scatter | solution.py:96
  971.8 153.5 %all-gather.41.cloned.1.call-start = ((), (), s32[]{:S(2)}) async-start(), calls=%async_computation.40 | async-start | bytes 7077888 | tf_op jit(solution)/shard_map/all_gather | solution.py:93
  1035.7 214.7 %reduce-scatter.49.cloned.1.call-start = ((), (), s32[]{:S(2)}) async-start(), calls=%async_computation.42 | async-start | bytes 7077888 | tf_op jit(solution)/shard_map/reduce_scatter | solution.py:96
  1188.5 153.4 %all-gather.47.cloned.1.call-start = ((), (), s32[]{:S(2)}) async-start(), calls=%async_computation.44 | async-start | bytes 5898240 | tf_op jit(solution)/shard_map/all_gather | solution.py:123
  1189.1 199.3 %all-gather.45.cloned.1.call-start = ((), (), s32[]{:S(2)}) async-start(), calls=%async_computation.43 | async-start | bytes 7077888 | tf_op jit(solution)/shard_map/all_gather | solution.py:93
  1254.2 217.0 %reduce-scatter.51.cloned.1.call-start = ((), (), s32[]{:S(2)}) async-start(), calls=%async_computation.45 | async-start | bytes 7077888 | tf_op jit(solution)/shard_map/reduce_scatter | solution.py:96
  1409.3 107.6 %all-gather.51.cloned.1.call-start = ((), (), s32[]{:S(2)}) async-start(), calls=%async_computation.47 | async-start | bytes 2457600 | tf_op jit(solution)/shard_map/all_gather | solution.py:123
  1410.1 153.6 %all-gather.49.cloned.1.call-start = ((), (), s32[]{:S(2)}) async-start(), calls=%async_computation.46 | async-start | bytes 7077888 | tf_op jit(solution)/shard_map/all_gather | solution.py:93
  1474.0 214.3 %reduce-scatter.53.cloned.1.call-start = ((), (), s32[]{:S(2)}) async-start(), calls=%async_computation.48 | async-start | bytes 7077888 | tf_op jit(solution)/shard_map/reduce_scatter | solution.py:96
  1626.4 164.4 %all-gather.55.cloned.1.call-start = ((), (), s32[]{:S(2)}) async-start(), calls=%async_computation.50 | async-start | bytes 5898240 | tf_op jit(solution)/shard_map/all_gather | solution.py:123
  1627.2 228.8 %all-gather.53.cloned.1.call-start = ((), (), s32[]{:S(2)}) async-start(), calls=%async_computation.49 | async-start | bytes 7077888 | tf_op jit(solution)/shard_map/all_gather | solution.py:93
  1692.1 211.9 %all-gather.57.cloned.1.call-start = ((), (), s32[]{:S(2)}) async-start(), calls=%async_computation.52 | async-start | bytes 7077888 | tf_op jit(solution)/shard_map/all_gather | solution.py:93
  1785.3 201.7 %reduce-scatter.57.cloned.1.call-start = ((), (), s32[]{:S(2)}) async-start(), calls=%async_computation.53 | async-start | bytes 7077888 | tf_op jit(solution)/shard_map/reduce_scatter | solution.py:96
  1925.2 112.8 %all-gather.59.cloned.1.call-start = ((), (), s32[]{:S(2)}) async-start(), calls=%async_computation.54 | async-start | bytes 7077888 | tf_op jit(solution)/shard_map/all_gather | solution.py:93
  1992.2 173.4 %reduce-scatter.59.cloned.1.call-start = ((), (), s32[]{:S(2)}) async-start(), calls=%async_computation.55 | async-start | bytes 7077888 | tf_op jit(solution)/shard_map/reduce_scatter | solution.py:96
  2103.8 127.4 %reduce-scatter.55.cloned.1.call-start = ((), (), s32[]{:S(2)}) async-start(), calls=%async_computation.51 | async-start | bytes 7077888 | tf_op jit(solution)/shard_map/reduce_scatter | solution.py:96
  2116.7 164.3 %all-gather.61.cloned.1.call-start = ((), (), s32[]{:S(2)}) async-start(), calls=%async_computation.56 | async-start | bytes 7077888 | tf_op jit(solution)/shard_map/all_gather | solution.py:93
  2235.2 129.8 %reduce-scatter.61.cloned.1.call-start = ((), (), s32[]{:S(2)}) async-start(), calls=%async_computation.57 | async-start | bytes 7077888 | tf_op jit(solution)/shard_map/reduce_scatter | solution.py:96
  2303.2 112.7 %all-gather.63.cloned.1.call-start = ((), (), s32[]{:S(2)}) async-start(), calls=%async_computation.58 | async-start | bytes 7077888 | tf_op jit(solution)/shard_map/all_gather | solution.py:93
  2370.1 179.5 %reduce-scatter.63.cloned.1.call-start = ((), (), s32[]{:S(2)}) async-start(), calls=%async_computation.59 | async-start | bytes 7077888 | tf_op jit(solution)/shard_map/reduce_scatter | solution.py:96
  2487.8 113.3 %all-gather.65.cloned.1.call-start = ((), (), s32[]{:S(2)}) async-start(), calls=%async_computation.60 | async-start | bytes 7077888 | tf_op jit(solution)/shard_map/all_gather | solution.py:93
  2555.4 129.8 %reduce-scatter.65.cloned.1.call-start = ((), (), s32[]{:S(2)}) async-start(), calls=%async_computation.61 | async-start | bytes 7077888 | tf_op jit(solution)/shard_map/reduce_scatter | solution.py:96
  2623.3 112.7 %all-gather.67.cloned.1.call-start = ((), (), s32[]{:S(2)}) async-start(), calls=%async_computation.62 | async-start | bytes 7077888 | tf_op jit(solution)/shard_map/all_gather | solution.py:93
  2690.3 179.2 %reduce-scatter.67.cloned.1.call-start = ((), (), s32[]{:S(2)}) async-start(), calls=%async_computation.63 | async-start | bytes 7077888 | tf_op jit(solution)/shard_map/reduce_scatter | solution.py:96
  2807.6 113.1 %all-gather.69.cloned.1.call-start = ((), (), s32[]{:S(2)}) async-start(), calls=%async_computation.64 | async-start | bytes 7077888 | tf_op jit(solution)/shard_map/all_gather | solution.py:93
  2874.9 129.8 %reduce-scatter.69.cloned.1.call-start = ((), (), s32[]{:S(2)}) async-start(), calls=%async_computation.65 | async-start | bytes 7077888 | tf_op jit(solution)/shard_map/reduce_scatter | solution.py:96
  2942.9 209.5 %all-gather.71.cloned.1.call-start = ((), (), s32[]{:S(2)}) async-start(), calls=%async_computation.66 | async-start | bytes 7077888 | tf_op jit(solution)/shard_map/all_gather | solution.py:93
  3010.4 219.1 %reduce-scatter.87.cloned.1.call-start = ((), (), s32[]{:S(2)}) async-start(), calls=%async_computation.75 | async-start | bytes 5898240 | tf_op jit(solution)/shard_map/reduce_scatter | solution.py:126
  3035.9 196.2 %reduce-scatter.85.cloned.1.call-start = ((), (), s32[]{:S(2)}) async-start(), calls=%async_computation.74 | async-start | bytes 5898240 | tf_op jit(solution)/shard_map/reduce_scatter | solution.py:126
  3062.1 258.2 %reduce-scatter.83.cloned.1.call-start = ((), (), s32[]{:S(2)}) async-start(), calls=%async_computation.73 | async-start | bytes 5898240 | tf_op jit(solution)/shard_map/reduce_scatter | solution.py:126
  3088.8 319.6 %reduce-scatter.81.cloned.1.call-start = ((), (), s32[]{:S(2)}) async-start(), calls=%async_computation.72 | async-start | bytes 5898240 | tf_op jit(solution)/shard_map/reduce_scatter | solution.py:126
  3114.7 338.7 %reduce-scatter.79.cloned.1.call-start = ((), (), s32[]{:S(2)}) async-start(), calls=%async_computation.71 | async-start | bytes 2457600 | tf_op jit(solution)/shard_map/reduce_scatter | solution.py:126
  3127.9 369.0 %reduce-scatter.77.cloned.1.call-start = ((), (), s32[]{:S(2)}) async-start(), calls=%async_computation.70 | async-start | bytes 2457600 | tf_op jit(solution)/shard_map/reduce_scatter | solution.py:126
  3140.1 399.8 %reduce-scatter.75.cloned.1.call-start = ((), (), s32[]{:S(2)}) async-start(), calls=%async_computation.69 | async-start | bytes 2457600 | tf_op jit(solution)/shard_map/reduce_scatter | solution.py:126
  3152.4 431.1 %reduce-scatter.73.cloned.1.call-start = ((), (), s32[]{:S(2)}) async-start(), calls=%async_computation.68 | async-start | bytes 2457600 | tf_op jit(solution)/shard_map/reduce_scatter | solution.py:126
  3222.7 443.6 %reduce-scatter.71.cloned.1.call-start = ((), (), s32[]{:S(2)}) async-start(), calls=%async_computation.67 | async-start | bytes 7077888 | tf_op jit(solution)/shard_map/reduce_scatter | solution.py:96
  3412.4 174.4 %all-to-all-start.3 = ((bf16[8,192,1536]{2,1,0:T(8,128)(2,1)}), bf16[8,192,1536]{2,1,0:T(8,128)(2,1)}, u32[]{:S(2)}, u32[]{:S(2)}) async-start(bf16[8,192,1536]{2,1,0:T(8,128)(2,1)} %bitcast.317), calls=%async_computation.19 | async-start | bytes 9437184 | tf_op jit(solution)/shard_map/all_to_all | solution.py:261
  (207 other events, 11692.0 us)
Sparse Core Ops, SparseCore 0:
  44.3 56.4 all-gather.26
  169.5 45.9 all-gather.24
  278.2 95.6 reduce-scatter.40
  376.0 89.4 all-gather.30
  468.0 43.9 all-gather.28
  533.0 61.6 reduce-scatter.42
  596.9 43.5 all-gather.34
  642.9 44.3 all-gather.32
  750.3 61.6 reduce-scatter.44
  814.1 89.5 all-gather.38
  906.3 43.9 all-gather.36
  971.2 61.6 reduce-scatter.46
  1035.0 43.5 all-gather.42
  1081.0 44.3 all-gather.40
  1188.6 61.6 reduce-scatter.48
  1252.4 89.5 all-gather.46
  1344.4 43.9 all-gather.44
  1409.5 61.6 reduce-scatter.50
  1473.3 43.5 all-gather.50
  1519.3 44.3 all-gather.48
  1626.6 61.6 reduce-scatter.52
  1690.5 100.3 all-gather.54
  1793.5 62.4 all-gather.52
  1858.5 45.5 all-gather.56
  1925.3 61.6 reduce-scatter.56
  1992.3 45.5 all-gather.58
  2103.9 61.6 reduce-scatter.58
  2169.4 61.7 reduce-scatter.54
  2235.4 45.5 all-gather.60
  2303.3 61.6 reduce-scatter.60
  2370.3 45.5 all-gather.62
  2487.9 61.6 reduce-scatter.62
  2555.5 45.5 all-gather.64
  2623.4 61.6 reduce-scatter.64
  2690.4 45.5 all-gather.66
  2807.7 61.6 reduce-scatter.66
  2875.1 45.5 all-gather.68
  2943.1 61.6 reduce-scatter.68
  3010.6 45.5 all-gather.70
  3058.6 85.2 reduce-scatter.86
  3146.3 85.7 reduce-scatter.84
  3234.5 85.7 reduce-scatter.82
  3322.6 85.7 reduce-scatter.80
  3411.4 41.9 reduce-scatter.78
  3456.2 40.6 reduce-scatter.76
  3499.2 40.6 reduce-scatter.74
  3542.8 40.6 reduce-scatter.72
  3587.2 79.1 reduce-scatter.70

commit v2 on v1

--- a/solution.py
+++ b/solution.py
@@ -1,8 +1,11 @@
+import functools
 import math
 
 import jax
 import jax.numpy as jnp
 from jax import lax
+from jax.experimental import pallas as pl
+from jax.experimental.pallas import tpu as pltpu
 from jax.sharding import Mesh
 from jax.sharding import PartitionSpec as P
 
@@ -18,12 +21,310 @@
 BF = jnp.bfloat16
 F32 = jnp.float32
 
-PLANE = ("x", "c", "y")
-
-
+LANES = 128
+HALF = HEAD_SIZE // 2
+VMEM_LIMIT = 56 * 1024 * 1024
+MESH = pl.DeviceIdType.MESH
+
+OWN, X, Y, D = (0, 0), (1, 0), (0, 1), (1, 1)
+
+def place():
+    return lax.axis_index("x"), lax.axis_index("c"), lax.axis_index("y")
+
+def flip(index, by):
+    return 1 - index if by else index
+
+def rank_of(here, dx, dc, dy):
+    x, c, y = here
+    return (flip(x, dx) * 2 + flip(c, dc)) * 2 + flip(y, dy)
+
+def greet(here):
+    x, c, y = here
+    barrier = pltpu.get_barrier_semaphore()
+    for peer in ({"x": 1 - x}, {"c": 1 - c}, {"y": 1 - y}):
+        pl.semaphore_signal(barrier, inc=1, device_id=peer, device_id_type=MESH)
+    pl.semaphore_wait(barrier, 3)
+
+def ag_kernel(shard, full, send_sem, recv_sem, local_sem):
+    here = place()
+    x, c, y = here
+    block = shard.shape[0]
+    piece = block // 4
+    to_x, to_y, to_c = {"x": 1 - x}, {"y": 1 - y}, {"c": 1 - c}
+    sent = []
+
+    def slot(role, chunk, count=1):
+        start = rank_of(here, *role) * block + chunk * piece
+        return full.at[pl.ds(pl.multiple_of(start, piece), piece * count)]
+
+    def send(src, dst, peer, role, chunk):
+        copy = pltpu.make_async_remote_copy(
+            src_ref=src, dst_ref=dst, send_sem=send_sem.at[len(sent)],
+            recv_sem=recv_sem.at[role[0] * 4 + role[1] * 2 + role[2], chunk],
+            device_id=peer, device_id_type=MESH)
+        copy.start()
+        sent.append(copy)
+
+    def arrived(role, chunk, count=1):
+        where = slot(role, chunk, count)
+        pltpu.make_async_remote_copy(
+            src_ref=where, dst_ref=where, send_sem=send_sem.at[0],
+            recv_sem=recv_sem.at[role[0] * 4 + role[1] * 2 + role[2], chunk],
+            device_id=to_c, device_id_type=MESH).wait_recv()
+
+    mine = pltpu.make_async_copy(shard, slot((0, 0, 0), 0, 4), local_sem)
+    mine.start()
+    greet(here)
+    own = (0, 0, 0)
+    for cx, cy in ((2, 0), (3, 1), (0, 2), (1, 3)):
+        send(shard.at[pl.ds(cx * piece, piece)], slot(own, cx), to_x, (1, 0, 0), cx)
+        send(shard.at[pl.ds(cy * piece, piece)], slot(own, cy), to_y, (0, 0, 1), cy)
+    send(shard, slot(own, 0, 4), to_c, (0, 1, 0), 0)
+    for cx, cy in ((2, 0), (3, 1), (0, 2), (1, 3)):
+        arrived((1, 0, 0), cx)
+        if cx >= 2:
+            send(slot((1, 0, 0), cx), slot((1, 0, 0), cx), to_y, (1, 0, 1), cx)
+        send(slot((1, 0, 0), cx), slot((1, 0, 0), cx), to_c, (1, 1, 0), cx)
+        arrived((0, 0, 1), cy)
+        if cy < 2:
+            send(slot((0, 0, 1), cy), slot((0, 0, 1), cy), to_x, (1, 0, 1), cy)
+        send(slot((0, 0, 1), cy), slot((0, 0, 1), cy), to_c, (0, 1, 1), cy)
+    for chunk in (0, 2, 1, 3):
+        arrived((1, 0, 1), chunk)
+        send(slot((1, 0, 1), chunk), slot((1, 0, 1), chunk), to_c, (1, 1, 1), chunk)
+    arrived((0, 1, 0), 0, 4)
+    for role in ((1, 1, 0), (0, 1, 1), (1, 1, 1)):
+        for chunk in range(4):
+            arrived(role, chunk)
+    mine.wait()
+    for copy in sent:
+        copy.wait_send()
+
+def gather_tokens(shard):
+    block, width = shard.shape
+    return pl.pallas_call(
+        ag_kernel,
+        out_shape=jax.ShapeDtypeStruct((8 * block, width), shard.dtype),
+        in_specs=[pl.BlockSpec(memory_space=pl.ANY)],
+        out_specs=pl.BlockSpec(memory_space=pl.ANY),
+        scratch_shapes=[pltpu.SemaphoreType.DMA((32,)), pltpu.SemaphoreType.DMA((8, 4)), pltpu.SemaphoreType.DMA],
+        compiler_params=pltpu.CompilerParams(collective_id=0, has_side_effects=True),
+        name="plane_gather",
+        cost_estimate=pl.CostEstimate(flops=0, bytes_accessed=90000000, transcendentals=0),
+    )(shard)
+
+def rs_kernel(partial, out, from_c, acc, via_x, via_y, from_x, from_y, send_sem, recv_sem, local_sem):
+    here = place()
+    x, c, y = here
+    block = out.shape[0]
+    half = block // 2
+    to_x, to_y, to_c = {"x": 1 - x}, {"y": 1 - y}, {"c": 1 - c}
+    order = (D, X, Y, OWN)
+    lower, upper = pl.ds(0, half), pl.ds(half, half)
+    sent = []
+
+    def rows(pos, dc):
+        return partial.at[pl.ds(pl.multiple_of(rank_of(here, pos[0], dc, pos[1]) * block, block), block)]
+
+    def send(src, dst, peer, sem):
+        copy = pltpu.make_async_remote_copy(
+            src_ref=src, dst_ref=dst, send_sem=send_sem.at[len(sent)], recv_sem=recv_sem.at[sem],
+            device_id=peer, device_id_type=MESH)
+        copy.start()
+        sent.append(copy)
+
+    def arrived(where, sem):
+        pltpu.make_async_remote_copy(
+            src_ref=where, dst_ref=where, send_sem=send_sem.at[0], recv_sem=recv_sem.at[sem],
+            device_id=to_c, device_id_type=MESH).wait_recv()
+
+    def add(slot, where, more):
+        acc[slot, where] = (acc[slot, where].astype(F32) + more.astype(F32)).astype(BF)
+
+    loads = []
+    for slot, pos in enumerate(order):
+        load = pltpu.make_async_copy(rows(pos, 0), acc.at[slot], local_sem.at[slot])
+        load.start()
+        loads.append(load)
+    greet(here)
+    for slot, pos in enumerate(order):
+        send(rows(pos, 1), from_c.at[slot], to_c, slot)
+    whole = pl.ds(0, block)
+    for slot in range(3):
+        loads[slot].wait()
+        arrived(from_c.at[slot], slot)
+        add(slot, whole, from_c[slot])
+        if slot == 0:
+            send(acc.at[0, upper], via_x, to_x, 4)
+            send(acc.at[0, lower], via_y, to_y, 5)
+        elif slot == 1:
+            send(acc.at[1, upper], from_x.at[upper], to_x, 6)
+        else:
+            send(acc.at[2, lower], from_y.at[lower], to_y, 7)
+    arrived(via_y, 5)
+    add(1, lower, via_y[...])
+    send(acc.at[1, lower], from_x.at[lower], to_x, 8)
+    arrived(via_x, 4)
+    add(2, upper, via_x[...])
+    send(acc.at[2, upper], from_y.at[upper], to_y, 9)
+    loads[3].wait()
+    arrived(from_c.at[3], 3)
+    out[...] = acc[3].astype(F32) + from_c[3].astype(F32)
+    arrived(from_x.at[upper], 6)
+    arrived(from_y.at[lower], 7)
+    out[upper] = out[upper] + from_x[upper].astype(F32)
+    out[lower] = out[lower] + from_y[lower].astype(F32)
+    arrived(from_x.at[lower], 8)
+    arrived(from_y.at[upper], 9)
+    out[lower] = out[lower] + from_x[lower].astype(F32)
+    out[upper] = out[upper] + from_y[upper].astype(F32)
+    for copy in sent:
+        copy.wait_send()
+
+def scatter_tokens(partial):
+    block, width = partial.shape[0] // 8, partial.shape[1]
+    half = block // 2
+    return pl.pallas_call(
+        rs_kernel,
+        out_shape=jax.ShapeDtypeStruct((block, width), F32),
+        in_specs=[pl.BlockSpec(memory_space=pl.ANY)],
+        out_specs=pl.BlockSpec(memory_space=pltpu.VMEM),
+        scratch_shapes=[
+            pltpu.VMEM((4, block, width), BF), pltpu.VMEM((4, block, width), BF),
+            pltpu.VMEM((half, width), BF), pltpu.VMEM((half, width), BF),
+            pltpu.VMEM((block, width), BF), pltpu.VMEM((block, width), BF),
+            pltpu.SemaphoreType.DMA((10,)), pltpu.SemaphoreType.DMA((10,)), pltpu.SemaphoreType.DMA((4,)),
+        ],
+        compiler_params=pltpu.CompilerParams(collective_id=1, has_side_effects=True, vmem_limit_bytes=VMEM_LIMIT),
+        name="plane_scatter",
+        cost_estimate=pl.CostEstimate(flops=0, bytes_accessed=90000000, transcendentals=0),
+    )(partial)
+
+
+LOWER=-1e30
 def dot(a, b, dims):
     return lax.dot_general(a, b, (dims, ((), ())), preferred_element_type=F32)
 
+def attend_kernel(scale2, bq, bk, bounds, length, q, k, v, qpos, out, lse):
+    groups = q.shape[0]
+    i = pl.program_id(0)
+    rows = groups * bq
+    qs = q[...].reshape(rows, LANES)
+    pos = qpos[0]
+    pos2 = jnp.concatenate([pos] * groups, axis=1)
+    def step(masked, j, state):
+        top, total, acc = state
+        at = pl.ds(pl.multiple_of(j * bk, bk), bk)
+        s = dot(k[at, :], qs, ((1,), (1,)))
+        if masked:
+            kp = j * bk + lax.broadcasted_iota(jnp.int32, (bk, 1), 0)
+            ok = (kp <= pos2) & (kp < length[0])
+            s = jnp.where(ok, s, LOWER)
+        new = jnp.maximum(top, jnp.max(s, axis=0, keepdims=True) * scale2)
+        p = jnp.exp2(s * scale2 - new)
+        alpha = jnp.exp2(top - new)
+        total = total * alpha + jnp.sum(p, axis=0, keepdims=True)
+        acc = acc * alpha + dot(v[at, :], p.astype(BF), ((0,), (0,)))
+        return new, total, acc
+    state = (jnp.full((1, rows), LOWER, F32), jnp.zeros((1, rows), F32), jnp.zeros((LANES, rows), F32))
+    full, end = bounds[0, i], bounds[1, i]
+    state = lax.fori_loop(0, full, functools.partial(step, False), state)
+    top, total, acc = lax.fori_loop(full, end, functools.partial(step, True), state)
+    o = (acc / total).T.astype(BF)
+    for g in range(groups):
+        out[:, g * LANES:(g + 1) * LANES] = o[g * bq:(g + 1) * bq]
+    lse[...] = (top + jnp.log2(total))[None]
+
+def attend(q, k, v, qpos, bounds, length, bq, bk, scale2):
+    groups, tokens, _ = q.shape
+    n = tokens // bq
+    out, lse = pl.pallas_call(
+        functools.partial(attend_kernel, scale2, bq, bk),
+        grid_spec=pltpu.PrefetchScalarGridSpec(
+            num_scalar_prefetch=2, grid=(n,),
+            in_specs=[
+                pl.BlockSpec((groups, bq, LANES), lambda i, *_: (0, i, 0)),
+                pl.BlockSpec(k.shape, lambda i, *_: (0, 0)),
+                pl.BlockSpec(v.shape, lambda i, *_: (0, 0)),
+                pl.BlockSpec((1, 1, bq), lambda i, *_: (i, 0, 0)),
+            ],
+            out_specs=[
+                pl.BlockSpec((bq, groups * LANES), lambda i, *_: (i, 0)),
+                pl.BlockSpec((1, 1, groups * bq), lambda i, *_: (i, 0, 0)),
+            ]),
+        out_shape=[jax.ShapeDtypeStruct((tokens, groups * LANES), BF), jax.ShapeDtypeStruct((n, 1, groups * bq), F32)],
+        compiler_params=pltpu.CompilerParams(vmem_limit_bytes=VMEM_LIMIT),
+        name="attend",
+        cost_estimate=pl.CostEstimate(flops=0, bytes_accessed=45000000, transcendentals=0),
+    )(bounds, length, q, k, v, qpos)
+    return out, lse
+
+def back_kernel(scale, scale2, bq, bk, bounds, length, q, k, v, qpos, o, do, lse, dq, dk, dv):
+    groups = q.shape[0]
+    i = pl.program_id(0)
+    @pl.when(i == 0)
+    def _():
+        dk[...] = jnp.zeros_like(dk)
+        dv[...] = jnp.zeros_like(dv)
+    qs = q[...].reshape(groups * bq, LANES)
+    dos = jnp.concatenate([do[:, g * LANES:(g + 1) * LANES] for g in range(groups)], axis=0)
+    os_ = jnp.concatenate([o[:, g * LANES:(g + 1) * LANES] for g in range(groups)], axis=0)
+    delta = jnp.sum(dos.astype(F32) * os_.astype(F32), axis=1, keepdims=True).reshape(1, groups * bq)
+    lse_row = lse[0]
+    pos = qpos[0]
+    pos2 = jnp.concatenate([pos] * groups, axis=1)
+    def step(masked, j, acc):
+        at = pl.ds(pl.multiple_of(j * bk, bk), bk)
+        kb, vb = k[at, :], v[at, :]
+        s = dot(kb, qs, ((1,), (1,)))
+        p = jnp.exp2(s * scale2 - lse_row)
+        if masked:
+            kp = j * bk + lax.broadcasted_iota(jnp.int32, (bk, 1), 0)
+            ok = (kp <= pos2) & (kp < length[0])
+            p = jnp.where(ok, p, 0.0)
+        dp = dot(vb, dos, ((1,), (1,)))
+        ds = (p * (dp - delta)).astype(BF)
+        dv[at, :] += dot(p.astype(BF), dos, ((1,), (0,)))
+        dk[at, :] += dot(ds, qs, ((1,), (0,))) * scale
+        return acc + dot(ds, kb, ((0,), (0,)))
+    full, end = bounds[0, i], bounds[1, i]
+    acc = jnp.zeros((groups * bq, LANES), F32)
+    acc = lax.fori_loop(0, full, functools.partial(step, False), acc)
+    acc = lax.fori_loop(full, end, functools.partial(step, True), acc) * scale
+    for g in range(groups):
+        dq[:, g * LANES:(g + 1) * LANES] = acc[g * bq:(g + 1) * bq]
+
+def attend_back(q, k, v, qpos_row, o, do, lse, bounds, length, bq, bk, scale, scale2):
+    groups, tokens, _ = q.shape
+    n = tokens // bq
+    wide = pl.BlockSpec((bq, groups * LANES), lambda i, *_: (i, 0))
+    return pl.pallas_call(
+        functools.partial(back_kernel, scale, scale2, bq, bk),
+        grid_spec=pltpu.PrefetchScalarGridSpec(
+            num_scalar_prefetch=2, grid=(n,),
+            in_specs=[
+                pl.BlockSpec((groups, bq, LANES), lambda i, *_: (0, i, 0)),
+                pl.BlockSpec(k.shape, lambda i, *_: (0, 0)),
+                pl.BlockSpec(v.shape, lambda i, *_: (0, 0)),
+                pl.BlockSpec((1, 1, bq), lambda i, *_: (i, 0, 0)),
+                wide, wide,
+                pl.BlockSpec((1, 1, groups * bq), lambda i, *_: (i, 0, 0)),
+            ],
+            out_specs=[wide, pl.BlockSpec(k.shape, lambda i, *_: (0, 0)), pl.BlockSpec(k.shape, lambda i, *_: (0, 0))]),
+        out_shape=[jax.ShapeDtypeStruct((tokens, groups * LANES), F32), jax.ShapeDtypeStruct(k.shape, F32), jax.ShapeDtypeStruct(k.shape, F32)],
+        compiler_params=pltpu.CompilerParams(vmem_limit_bytes=VMEM_LIMIT),
+        name="attend_back",
+        cost_estimate=pl.CostEstimate(flops=0, bytes_accessed=65000000, transcendentals=0),
+    )(bounds, length, q, k, v, qpos_row, o, do, lse)
+
+def bounds_of(positions, length, bq, bk):
+    p = positions.reshape(-1, bq)
+    lo = jnp.minimum(jnp.min(p, axis=1) + 1, length) // bk
+    hi = -(-jnp.minimum(jnp.max(p, axis=1) + 1, length) // bk)
+    return jnp.stack([lo, hi]).astype(jnp.int32)
+
+
+PLANE = ("x", "c", "y")
 
 def dot_nn(a, b):
     return dot(a, b, ((1,), (0,)))
@@ -37,13 +338,22 @@
     return dot(a, b, ((0,), (0,)))
 
 
-def rotate_halves(tensor, cosine, sine):
-    half = tensor.shape[-1] // 2
-    first = tensor[..., :half]
-    second = tensor[..., half:]
-    return jnp.concatenate(
-        [first * cosine - second * sine, second * cosine + first * sine], axis=-1
-    )
+def spread(matrix, heads):
+    split = matrix.reshape(matrix.shape[0], heads, 2, HALF)
+    return jnp.pad(split, ((0, 0), (0, 0), (0, 0), (0, LANES // 2 - HALF))).reshape(-1, heads * LANES)
+
+
+def unspread(matrix, heads):
+    return matrix.reshape(-1, heads, 2, LANES // 2)[..., :HALF].reshape(-1, heads * HEAD_SIZE)
+
+
+def widen(matrix, heads):
+    split = matrix.reshape(matrix.shape[0], heads, HEAD_SIZE)
+    return jnp.pad(split, ((0, 0), (0, 0), (0, LANES - HEAD_SIZE))).reshape(-1, heads * LANES)
+
+
+def narrow(matrix, heads):
+    return matrix.reshape(-1, heads, LANES)[..., :HEAD_SIZE].reshape(-1, heads * HEAD_SIZE)
 
 
 def norm_back(upstream, normed, inverse, gain_row):
@@ -80,7 +390,8 @@
     q_cols = head_group * HEAD_SIZE
     kv_cols = HEAD_SIZE
     ff_cols = FF // ranks
-    score_scale = 1.0 / math.sqrt(HEAD_SIZE)
+    scale = 1.0 / math.sqrt(HEAD_SIZE)
+    scale2 = scale * math.log2(math.e)
 
     def swap(array):
         names = ("x", "c", "z")
@@ -88,12 +399,6 @@
             (s * planes + z, z * planes + s) for s in range(sections) for z in range(planes)
         ]
         return lax.ppermute(array, names, pairs)
-
-    def gather_tokens(shard):
-        return lax.all_gather(shard, PLANE, axis=0, tiled=True)
-
-    def scatter_tokens(partial):
-        return lax.psum_scatter(partial.astype(BF), PLANE, scatter_dimension=0, tiled=True).astype(F32)
 
     def by_rank(matrix):
         return matrix.reshape(rows, ranks, -1)
@@ -144,15 +449,18 @@
     positions = (block_start[:, None] + jnp.arange(block)[None, :]).reshape(tokens)
     exponents = 2.0 * jnp.arange(HEAD_SIZE // 2).astype(F32) / HEAD_SIZE
     angles = positions.astype(F32)[:, None] * (THETA ** (-exponents))[None, :]
-    cosine = jnp.cos(angles)[:, None, :]
-    sine = jnp.sin(angles)[:, None, :]
-    key_positions = jnp.arange(all_tokens)
-    allowed = (key_positions[None, :] <= positions[:, None]) & (key_positions[None, :] < length)
-    allowed = allowed[:, None, :]
-
-    def rotated(columns, heads, sign):
-        turned = rotate_halves(columns.reshape(tokens, heads, HEAD_SIZE), cosine, sign * sine)
-        return turned.reshape(tokens, heads * HEAD_SIZE).astype(BF)
+    table = lambda values: jnp.pad(values, ((0, 0), (0, LANES // 2 - HALF)))
+    cosine = jnp.concatenate([table(jnp.cos(angles))] * 2, axis=1)
+    sine = jnp.concatenate([table(-jnp.sin(angles)), table(jnp.sin(angles))], axis=1)
+    bq = math.gcd(tokens, 512)
+    bk = math.gcd(all_tokens, 512)
+    bounds = bounds_of(positions, length, bq, bk)
+    length1 = length.reshape(1)
+    query_rows = positions.astype(jnp.int32).reshape(-1, 1, bq)
+
+    def rotated(head, sign):
+        turned = jnp.concatenate([head[:, LANES // 2 :], head[:, : LANES // 2]], axis=1)
+        return (head * cosine + turned * (sign * sine)).astype(BF)
 
     def all_keys(array):
         if extra == 1:
@@ -166,33 +474,6 @@
         stacked = array.astype(BF).reshape(ranks, extra, block, -1)
         return lax.psum_scatter(stacked, "e", scatter_dimension=1, tiled=False).reshape(tokens, -1).astype(F32)
 
-    def attend(q, keys, values):
-        scores = jnp.einsum(
-            "tgd,nd->tgn", q.reshape(tokens, head_group, HEAD_SIZE), keys, preferred_element_type=F32
-        ) * score_scale
-        scores = jnp.where(allowed, scores, LOWER_LIMIT)
-        top = jnp.max(scores, axis=-1, keepdims=True)
-        weights = jnp.where(allowed, jnp.exp(scores - top), 0.0)
-        total = jnp.sum(weights, axis=-1, keepdims=True)
-        summed = jnp.einsum("tgn,nd->tgd", weights.astype(BF), values, preferred_element_type=F32)
-        out = (summed / total).reshape(tokens, q_cols).astype(BF)
-        return out, top + jnp.log(total)
-
-    def attend_back(q, keys, values, out, log_total, grad_out):
-        q3 = q.reshape(tokens, head_group, HEAD_SIZE)
-        g3 = grad_out.reshape(tokens, head_group, HEAD_SIZE)
-        scores = jnp.einsum("tgd,nd->tgn", q3, keys, preferred_element_type=F32) * score_scale
-        weights = jnp.where(allowed, jnp.exp(jnp.where(allowed, scores, LOWER_LIMIT) - log_total), 0.0)
-        delta = jnp.sum(
-            g3.astype(F32) * out.reshape(tokens, head_group, HEAD_SIZE).astype(F32), axis=-1, keepdims=True
-        )
-        weight_grad = jnp.einsum("tgd,nd->tgn", g3, values, preferred_element_type=F32)
-        score_grad = (weights * (weight_grad - delta)).astype(BF)
-        dq = jnp.einsum("tgn,nd->tgd", score_grad, keys, preferred_element_type=F32) * score_scale
-        dk = jnp.einsum("tgn,tgd->nd", score_grad, q3, preferred_element_type=F32) * score_scale
-        dv = jnp.einsum("tgn,tgd->nd", weights.astype(BF), g3, preferred_element_type=F32)
-        return dq.reshape(tokens, q_cols), dk, dv
-
     def inverse_of(x):
         return lax.rsqrt(jnp.mean(x * x, axis=-1, keepdims=True) + EPS)
 
@@ -201,23 +482,28 @@
     for layer in range(layers):
         attn_w = whole(attn_parts[layer])
         mlp_w = whole(mlp_parts[layer])
-        w_qkv, w_o = attn_w[:, : q_cols + 2 * kv_cols], attn_w[:, q_cols + 2 * kv_cols :]
+        qk_cols = q_cols + kv_cols
+        w_qkv = jnp.concatenate(
+            [spread(attn_w[:, :qk_cols], head_group + 1), widen(attn_w[:, qk_cols : qk_cols + kv_cols], 1)], axis=1
+        )
+        w_o = widen(attn_w[:, qk_cols + kv_cols :], head_group)
         w_gu, w_d = mlp_w[:, : 2 * ff_cols], mlp_w[:, 2 * ff_cols :]
         h = hidden_state.astype(F32)
         r1 = inverse_of(h)
         a1 = gather_tokens((h * r1 * gains[layer, 0]).astype(BF))
         qkv = dot_nn(a1, w_qkv)
-        q = rotated(qkv[:, :q_cols], head_group, 1.0)
-        k = all_keys(rotated(qkv[:, q_cols : q_cols + kv_cols], 1, 1.0))
-        v = all_keys(qkv[:, q_cols + kv_cols :].astype(BF))
-        o, log_total = attend(q, k, v)
-        mid = h + scatter_tokens(dot_nt(o, w_o))
+        heads = [qkv[:, n * LANES : (n + 1) * LANES] for n in range(head_group + 2)]
+        q = jnp.stack([rotated(head, 1.0) for head in heads[:head_group]])
+        k = all_keys(rotated(heads[head_group], 1.0))
+        v = all_keys(heads[head_group + 1].astype(BF))
+        o, log_total = attend(q, k, v, query_rows, bounds, length1, bq, bk, scale2)
+        mid = h + scatter_tokens(dot_nt(o, w_o).astype(BF))
         r2 = inverse_of(mid)
         a2 = gather_tokens((mid * r2 * gains[layer, 1]).astype(BF))
         gu = dot_nn(a2, w_gu)
         g, u = gu[:, :ff_cols], gu[:, ff_cols:]
         hid = (jax.nn.silu(g) * u).astype(BF)
-        after = mid + scatter_tokens(dot_nt(hid, w_d))
+        after = mid + scatter_tokens(dot_nt(hid, w_d).astype(BF))
         saved.append(
             (hidden_state, r1, a1, q, k, v, o, log_total, mid, r2, a2, gu.astype(BF), hid, w_qkv, w_o, w_gu, w_d)
         )
@@ -237,19 +523,32 @@
         g, u = gu[:, :ff_cols].astype(F32), gu[:, ff_cols:].astype(F32)
         sig = jax.nn.sigmoid(g)
         dgu = jnp.concatenate([dhid * u * sig * (1.0 + g * (1.0 - sig)), dhid * g * sig], axis=1).astype(BF)
-        da2 = scatter_tokens(dot_nt(dgu, w_gu))
+        da2 = scatter_tokens(dot_nt(dgu, w_gu).astype(BF))
         mlp_grads[layer] = reduce_rows(jnp.concatenate([dot_tn(a2, dgu), dot_tn(e_all, hid)], axis=1))
         n2 = mid * r2
         gain2 = jnp.sum(da2 * n2, axis=0)
         dmid = e.astype(F32) + norm_back(da2, n2, r2, gains[layer, 1])
         dat = gather_tokens(dmid.astype(BF))
         dob = dot_nn(dat, w_o).astype(BF)
-        dq, dk, dv = attend_back(q, k, v, o, log_total, dob)
+        dq, dk, dv = attend_back(q, k, v, query_rows, o, dob, log_total, bounds, length1, bq, bk, scale, scale2)
         dqkv = jnp.concatenate(
-            [rotated(dq, head_group, -1.0), rotated(own_keys(dk), 1, -1.0), own_keys(dv).astype(BF)], axis=1
+            [rotated(dq[:, n * LANES : (n + 1) * LANES], -1.0) for n in range(head_group)]
+            + [rotated(own_keys(dk), -1.0), own_keys(dv).astype(BF)],
+            axis=1,
         )
-        da1 = scatter_tokens(dot_nt(dqkv, w_qkv))
-        attn_grads[layer] = reduce_rows(jnp.concatenate([dot_tn(a1, dqkv), dot_tn(dat, o)], axis=1))
+        da1 = scatter_tokens(dot_nt(dqkv, w_qkv).astype(BF))
+        dqkv_w = dot_tn(a1, dqkv).astype(BF)
+        qk_wide = (head_group + 1) * LANES
+        attn_grads[layer] = reduce_rows(
+            jnp.concatenate(
+                [
+                    unspread(dqkv_w[:, :qk_wide], head_group + 1),
+                    narrow(dqkv_w[:, qk_wide:], 1),
+                    narrow(dot_tn(dat, o).astype(BF), head_group),
+                ],
+                axis=1,
+            )
+        )
         n1 = h_low.astype(F32) * r1
         gain1 = jnp.sum(da1 * n1, axis=0)
         gain_grads[layer] = jnp.stack([gain1, gain2])

time: 3750 us -> 2520 us (0.67)
  waiting for transfers between devices: 2430 us -> 342 us
  Pallas kernels: 0 us -> 1220 us
  matrix products: 687 us -> 336 us
  local copies, waits for them, and re-layouts: 110 us -> 204 us
  other arithmetic: 204 us -> 129 us
    pallas_call x0 -> x40, Pallas kernels: none -> 1220 us  [the longest x16 570 us: scatter_tokens(): pl.pallas_call(rs_kernel, out_shape=jax.ShapeDtypeStruct((block, width),...]
    reduce_scatter x16 -> x0, waiting for transfers between devices: 869 us -> none  [scatter_tokens(): lax.psum_scatter(partial.astype(BF), PLANE, scatter_dimension=0, tiled=True)]
    all_gather x16 -> x0, waiting for transfers between devices: 690 us -> none  [gather_tokens(): return lax.all_gather(shard, PLANE, axis=0, tiled=True)]
    all_gather x8, waiting for transfers between devices: 397 us -> 0.11 us  [whole(): lax.all_gather(part.reshape(-1, part.shape[-1]), 'z', axis=0, tiled=True)]
    dot_general x24 -> x0, matrix products: 345 us -> none  [the longest x4 89.6 us: attend_back(): jnp.einsum('tgd,nd->tgn', g3, values, preferred_element_type=F32)]
    ppermute x4, waiting for transfers between devices: 123 us -> 0.01 us  [swap(): return lax.ppermute(array, names, pairs)]
    all_to_all x2 -> x1, blocking collectives: 101 us -> 27.4 us  [exchange(): lax.all_to_all(jnp.swapaxes(pack.astype(BF), 0, 1), PLANE, split_axis=0,...]
    reduce_sum x8 -> x0, other arithmetic: 61.6 us -> none  [the longest x4 60.5 us: attend(): total = jnp.sum(weights, axis=-1, keepdims=True)]
  transfers between devices with their start and end apart: 54 -> 23, of which waited for: 47 -> 5; matrix products, arithmetic and copies ran while one was open for 9% -> 17% of each run, Pallas kernels for 0% -> 33%
where the time goes in v2:
time: 2520 us; the launch traced here: 2510 us
  Pallas kernels  1220 us (48%)
  waiting for transfers between devices  342 us (14%)
  matrix products  336 us (13%)
  blocking collectives  230 us (9%)
  local copies, waits for them, and re-layouts  204 us (8%)
  other arithmetic  129 us (5%)
  starting transfers between devices  34.3 us (1%)
    pallas_call x16, Pallas kernels, scatter_tokens(): pl.pallas_call(rs_kernel, out_shape=jax.ShapeDtypeStruct((block, width),...  570 us
    pallas_call x16, Pallas kernels, gather_tokens(): pl.pallas_call(ag_kernel, out_shape=jax.ShapeDtypeStruct((8 * block, widt...  489 us
    dot_general x48, matrix products, dot(): return lax.dot_general(a, b, (dims, ((), ())), preferred_element_type=F32)  336 us
    reduce_scatter x8, waiting for transfers between devices, reduce_rows(): lax.psum_scatter(grad.astype(BF), 'z', scatter_dimension=0, tiled=True)  285 us
    all_gather x1, blocking collectives, body(): lax.all_gather(gains, ('x', 'c', 'z', 'y', 'e'), axis=0, tiled=False)  155 us
    pallas_call x4, Pallas kernels, attend_back(): pl.pallas_call(functools.partial(back_kernel, scale, scale2, bq, bk), gri...  93.6 us
    unnamed x355, local copies, waits for them, and re-layouts  90.9 us
    pallas_call x4, Pallas kernels, attend(): pl.pallas_call(functools.partial(attend_kernel, scale2, bq, bk), grid_spe...  66.6 us
  transfers between devices with their start and end apart: 23, of which 5 were waited for; matrix products, arithmetic and copies ran while one was open for 17% of the time, Pallas kernels for 33%

profile of v2, /device:TPU:2, one launch (start us, length us, event | category | flops | bytes accessed | tf_op | source)
XLA Modules:
  0.0 2511.3 jit_solution(13590754925360688916)
XLA Ops:
  14.5 27.4 %all_to_all.20 = bf16[8,192,576]{2,1,0:T(8,128)(2,1)S(1)} all-to-all(bf16[8,192,576]{2,1,0:T(8,128)(2,1)S(1)} %maximum_bitcast_fusion.1), channel_id=1, replica_groups=mesh['x'=2,'c'=2,'z'=4,'y'=2,'e'=1] {'x','c','y'}, dimensions={0} | all-to-all | bytes 3538944 | tf_op jit(solution)/shard_map/all_to_all | solution.py:420
  60.1 52.7 %all-to-all-done.1 = bf16[8,192,1536]{2,1,0:T(8,128)(2,1)} async-done(((bf16[8,192,1536]{2,1,0:T(8,128)(2,1)}), bf16[8,192,1536]{2,1,0:T(8,128)(2,1)}, u32[]{:S(2)}, u32[]{:S(2)}) %all-to-all-start.1) | async-done | bytes 4718624 | tf_op jit(solution)/shard_map/all_to_all | solution.py:420
  126.7 155.2 %all_gather.28 = bf16[32,2,192]{2,1,0:T(2,128)(2,1)S(1)} all-gather(bf16[1,2,192]{2,1,0:T(2,128)(2,1)S(1)} %pad_maximum_fusion.51), channel_id=1, replica_groups=mesh['x'=2,'c'=2,'z'=4,'y'=2,'e'=1] {'x','c','z','y','e'}, dimensions={0}, use_global_device_ids=true | all-gather | bytes 25344 | tf_op jit(solution)/shard_map/all_gather | solution.py:440
  292.8 34.1 %plane_gather.24 = bf16[2048,1536]{1,0:T(8,128)(2,1)} custom-call(bf16[256,1536]{1,0:T(8,128)(2,1)} %broadcast_select_fusion.shard), custom_call_target="tpu_custom_call" | custom-call | bytes 90000000 | tf_op jit(solution)/shard_map/plane_gather/pallas_call | solution.py:105
  328.3 30.9 %plane_gather.16 = bf16[2048,1536]{1,0:T(8,128)(2,1)} custom-call(bf16[256,1536]{1,0:T(8,128)(2,1)} %fusion.64.shard), custom_call_target="tpu_custom_call" | custom-call | bytes 90000000 | tf_op jit(solution)/shard_map/plane_gather/pallas_call | solution.py:105
  416.8 16.8 attend.4
  439.3 32.4 %plane_scatter.16 = f32[256,1536]{1,0:T(8,128)} custom-call(bf16[2048,1536]{1,0:T(8,128)(2,1)} %convolution_convert_fusion.3.partial), custom_call_target="tpu_custom_call" | custom-call | bytes 90000000 | tf_op jit(solution)/shard_map/plane_scatter/pallas_call | solution.py:187
  475.7 30.4 %plane_gather.17 = bf16[2048,1536]{1,0:T(8,128)(2,1)} custom-call(bf16[256,1536]{1,0:T(8,128)(2,1)} %multiply_convert_fusion.3.shard), custom_call_target="tpu_custom_call" | custom-call | bytes 90000000 | tf_op jit(solution)/shard_map/plane_gather/pallas_call | solution.py:105
  527.4 32.5 %plane_scatter.17 = f32[256,1536]{1,0:T(8,128)} custom-call(bf16[2048,1536]{1,0:T(8,128)(2,1)} %convolution_convert_fusion.15.partial), custom_call_target="tpu_custom_call" | custom-call | bytes 90000000 | tf_op jit(solution)/shard_map/plane_scatter/pallas_call | solution.py:187
  563.3 30.4 %plane_gather.18 = bf16[2048,1536]{1,0:T(8,128)(2,1)} custom-call(bf16[256,1536]{1,0:T(8,128)(2,1)} %fusion.72.shard), custom_call_target="tpu_custom_call" | custom-call | bytes 90000000 | tf_op jit(solution)/shard_map/plane_gather/pallas_call | solution.py:105
  604.6 16.6 attend.5
  626.9 32.4 %plane_scatter.18 = f32[256,1536]{1,0:T(8,128)} custom-call(bf16[2048,1536]{1,0:T(8,128)(2,1)} %convolution_convert_fusion.2.partial), custom_call_target="tpu_custom_call" | custom-call | bytes 90000000 | tf_op jit(solution)/shard_map/plane_scatter/pallas_call | solution.py:187
  663.2 30.3 %plane_gather.19 = bf16[2048,1536]{1,0:T(8,128)(2,1)} custom-call(bf16[256,1536]{1,0:T(8,128)(2,1)} %multiply_convert_fusion.2.shard), custom_call_target="tpu_custom_call" | custom-call | bytes 90000000 | tf_op jit(solution)/shard_map/plane_gather/pallas_call | solution.py:105
  715.0 32.4 %plane_scatter.19 = f32[256,1536]{1,0:T(8,128)} custom-call(bf16[2048,1536]{1,0:T(8,128)(2,1)} %convolution_convert_fusion.14.partial), custom_call_target="tpu_custom_call" | custom-call | bytes 90000000 | tf_op jit(solution)/shard_map/plane_scatter/pallas_call | solution.py:187
  750.2 30.2 %plane_gather.20 = bf16[2048,1536]{1,0:T(8,128)(2,1)} custom-call(bf16[256,1536]{1,0:T(8,128)(2,1)} %fusion.80.shard), custom_call_target="tpu_custom_call" | custom-call | bytes 90000000 | tf_op jit(solution)/shard_map/plane_gather/pallas_call | solution.py:105
  791.3 16.6 attend.6
  813.6 32.3 %plane_scatter.20 = f32[256,1536]{1,0:T(8,128)} custom-call(bf16[2048,1536]{1,0:T(8,128)(2,1)} %convolution_convert_fusion.1.partial), custom_call_target="tpu_custom_call" | custom-call | bytes 90000000 | tf_op jit(solution)/shard_map/plane_scatter/pallas_call | solution.py:187
  849.9 30.2 %plane_gather.21 = bf16[2048,1536]{1,0:T(8,128)(2,1)} custom-call(bf16[256,1536]{1,0:T(8,128)(2,1)} %multiply_convert_fusion.1.shard), custom_call_target="tpu_custom_call" | custom-call | bytes 90000000 | tf_op jit(solution)/shard_map/plane_gather/pallas_call | solution.py:105
  901.3 32.4 %plane_scatter.21 = f32[256,1536]{1,0:T(8,128)} custom-call(bf16[2048,1536]{1,0:T(8,128)(2,1)} %convolution_convert_fusion.13.partial), custom_call_target="tpu_custom_call" | custom-call | bytes 90000000 | tf_op jit(solution)/shard_map/plane_scatter/pallas_call | solution.py:187
  936.6 30.2 %plane_gather.22 = bf16[2048,1536]{1,0:T(8,128)(2,1)} custom-call(bf16[256,1536]{1,0:T(8,128)(2,1)} %fusion.88.shard), custom_call_target="tpu_custom_call" | custom-call | bytes 90000000 | tf_op jit(solution)/shard_map/plane_gather/pallas_call | solution.py:105
  977.7 16.6 attend.7
  1000.1 32.4 %plane_scatter.22 = f32[256,1536]{1,0:T(8,128)} custom-call(bf16[2048,1536]{1,0:T(8,128)(2,1)} %convolution_convert_fusion.partial), custom_call_target="tpu_custom_call" | custom-call | bytes 90000000 | tf_op jit(solution)/shard_map/plane_scatter/pallas_call | solution.py:187
  1036.4 30.2 %plane_gather.23 = bf16[2048,1536]{1,0:T(8,128)(2,1)} custom-call(bf16[256,1536]{1,0:T(8,128)(2,1)} %multiply_convert_fusion.shard), custom_call_target="tpu_custom_call" | custom-call | bytes 90000000 | tf_op jit(solution)/shard_map/plane_gather/pallas_call | solution.py:105
  1098.4 32.4 %plane_scatter.24 = f32[256,1536]{1,0:T(8,128)} custom-call(bf16[2048,1536]{1,0:T(8,128)(2,1)} %convolution_convert_fusion.11.partial), custom_call_target="tpu_custom_call" | custom-call | bytes 90000000 | tf_op jit(solution)/shard_map/plane_scatter/pallas_call | solution.py:187
  1134.9 30.2 %plane_gather.25 = bf16[2048,1536]{1,0:T(8,128)(2,1)} custom-call(bf16[256,1536]{1,0:T(8,128)(2,1)} %fusion.200.shard), custom_call_target="tpu_custom_call" | custom-call | bytes 90000000 | tf_op jit(solution)/shard_map/plane_gather/pallas_call | solution.py:105
  1173.8 23.4 attend_back.4
  1223.8 32.4 %plane_scatter.23 = f32[256,1536]{1,0:T(8,128)} custom-call(bf16[2048,1536]{1,0:T(8,128)(2,1)} %convolution_convert_fusion.12.partial), custom_call_target="tpu_custom_call" | custom-call | bytes 90000000 | tf_op jit(solution)/shard_map/plane_scatter/pallas_call | solution.py:187
  1256.3 31.8 %plane_scatter.25 = f32[256,1536]{1,0:T(8,128)} custom-call(bf16[2048,1536]{1,0:T(8,128)(2,1)} %convolution_convert_fusion.10.partial), custom_call_target="tpu_custom_call" | custom-call | bytes 90000000 | tf_op jit(solution)/shard_map/plane_scatter/pallas_call | solution.py:187
  1294.3 30.6 %plane_gather.26 = bf16[2048,1536]{1,0:T(8,128)(2,1)} custom-call(bf16[256,1536]{1,0:T(8,128)(2,1)} %get-tuple-element.179.shard), custom_call_target="tpu_custom_call" | custom-call | bytes 90000000 | tf_op jit(solution)/shard_map/plane_gather/pallas_call | solution.py:105
  1347.2 32.4 %plane_scatter.26 = f32[256,1536]{1,0:T(8,128)} custom-call(bf16[2048,1536]{1,0:T(8,128)(2,1)} %convolution_convert_fusion.9.partial), custom_call_target="tpu_custom_call" | custom-call | bytes 90000000 | tf_op jit(solution)/shard_map/plane_scatter/pallas_call | solution.py:187
  1383.6 30.2 %plane_gather.27 = bf16[2048,1536]{1,0:T(8,128)(2,1)} custom-call(bf16[256,1536]{1,0:T(8,128)(2,1)} %fusion.201.shard), custom_call_target="tpu_custom_call" | custom-call | bytes 90000000 | tf_op jit(solution)/shard_map/plane_gather/pallas_call | solution.py:105
  1422.5 23.4 attend_back.5
  1463.1 32.4 %plane_scatter.27 = f32[256,1536]{1,0:T(8,128)} custom-call(bf16[2048,1536]{1,0:T(8,128)(2,1)} %convolution_convert_fusion.8.partial), custom_call_target="tpu_custom_call" | custom-call | bytes 90000000 | tf_op jit(solution)/shard_map/plane_scatter/pallas_call | solution.py:187
  1501.3 30.2 %plane_gather.28 = bf16[2048,1536]{1,0:T(8,128)(2,1)} custom-call(bf16[256,1536]{1,0:T(8,128)(2,1)} %fusion.85.shard), custom_call_target="tpu_custom_call" | custom-call | bytes 90000000 | tf_op jit(solution)/shard_map/plane_gather/pallas_call | solution.py:105
  1554.0 32.4 %plane_scatter.28 = f32[256,1536]{1,0:T(8,128)} custom-call(bf16[2048,1536]{1,0:T(8,128)(2,1)} %convolution_convert_fusion.7.partial), custom_call_target="tpu_custom_call" | custom-call | bytes 90000000 | tf_op jit(solution)/shard_map/plane_scatter/pallas_call | solution.py:187
  1590.4 30.2 %plane_gather.29 = bf16[2048,1536]{1,0:T(8,128)(2,1)} custom-call(bf16[256,1536]{1,0:T(8,128)(2,1)} %fusion.202.shard), custom_call_target="tpu_custom_call" | custom-call | bytes 90000000 | tf_op jit(solution)/shard_map/plane_gather/pallas_call | solution.py:105
  1643.0 23.3 attend_back.6
  1689.9 32.4 %plane_scatter.29 = f32[256,1536]{1,0:T(8,128)} custom-call(bf16[2048,1536]{1,0:T(8,128)(2,1)} %convolution_convert_fusion.6.partial), custom_call_target="tpu_custom_call" | custom-call | bytes 90000000 | tf_op jit(solution)/shard_map/plane_scatter/pallas_call | solution.py:187
  1728.2 30.3 %plane_gather.30 = bf16[2048,1536]{1,0:T(8,128)(2,1)} custom-call(bf16[256,1536]{1,0:T(8,128)(2,1)} %fusion.77.shard), custom_call_target="tpu_custom_call" | custom-call | bytes 90000000 | tf_op jit(solution)/shard_map/plane_gather/pallas_call | solution.py:105
  1781.1 32.4 %plane_scatter.30 = f32[256,1536]{1,0:T(8,128)} custom-call(bf16[2048,1536]{1,0:T(8,128)(2,1)} %convolution_convert_fusion.5.partial), custom_call_target="tpu_custom_call" | custom-call | bytes 90000000 | tf_op jit(solution)/shard_map/plane_scatter/pallas_call | solution.py:187
  1818.1 30.4 %plane_gather.31 = bf16[2048,1536]{1,0:T(8,128)(2,1)} custom-call(bf16[256,1536]{1,0:T(8,128)(2,1)} %fusion.203.shard), custom_call_target="tpu_custom_call" | custom-call | bytes 90000000 | tf_op jit(solution)/shard_map/plane_gather/pallas_call | solution.py:105
  1857.3 23.4 attend_back.7
  2005.4 21.5 reduce-scatter.39.cloned.1.call-done
  2026.8 88.0 %reduce-scatter.37.cloned.1.call-done = bf16[384,1536]{1,0:T(8,128)(2,1)} async-done(((bf16[1536,1536]{1,0:T(8,128)(2,1)}), bf16[384,1536]{1,0:T(8,128)(2,1)}) %reduce-scatter.37.cloned.1.call-update) | async-done | bytes 1179664 | tf_op jit(solution)/shard_map/reduce_scatter | solution.py:431
  2114.8 87.9 %reduce-scatter.35.cloned.1.call-done = bf16[384,1536]{1,0:T(8,128)(2,1)} async-done(((bf16[1536,1536]{1,0:T(8,128)(2,1)}), bf16[384,1536]{1,0:T(8,128)(2,1)}) %reduce-scatter.35.cloned.1.call-update) | async-done | bytes 1179664 | tf_op jit(solution)/shard_map/reduce_scatter | solution.py:431
  2202.8 88.0 %reduce-scatter.33.cloned.1.call-done = bf16[384,1536]{1,0:T(8,128)(2,1)} async-done(((bf16[1536,1536]{1,0:T(8,128)(2,1)}), bf16[384,1536]{1,0:T(8,128)(2,1)}) %reduce-scatter.33.cloned.1.call-update) | async-done | bytes 1179664 | tf_op jit(solution)/shard_map/reduce_scatter | solution.py:431
  2311.5 84.6 %plane_scatter.31 = f32[256,1536]{1,0:T(8,128)} custom-call(bf16[2048,1536]{1,0:T(8,128)(2,1)} %convolution_convert_fusion.4.partial), custom_call_target="tpu_custom_call" | custom-call | bytes 90000000 | tf_op jit(solution)/shard_map/plane_scatter/pallas_call | solution.py:187
  2416.9 46.9 %all-reduce.15 = f32[32,2,192]{2,1,0:T(2,128)} all-reduce(f32[32,2,192]{2,1,0:T(2,128)} %copy.278), channel_id=2, replica_groups=mesh['x'=2,'c'=2,'z'=4,'y'=2,'e'=1] {'x','c','z','y','e'}, use_global_device_ids=true, to_apply=%region_26.27.clone | all-reduce | flops 12288 | bytes 98304
  (685 shorter events, 706.9 us)
Async XLA Ops:
  7.2 352.1 %all-gather.9.cloned.1.call-start = ((), (), s32[]{:S(2)}) async-start(), calls=%async_computation.12 | async-start | bytes 2457600 | tf_op jit(solution)/shard_map/all_gather | solution.py:428
  43.2 333.5 %all-gather.13.cloned.1.call-start = ((), (), s32[]{:S(2)}) async-start(), calls=%async_computation.14 | async-start | bytes 2457600 | tf_op jit(solution)/shard_map/all_gather | solution.py:428
  44.0 334.9 %all-gather.21.cloned.1.call-start = ((), (), s32[]{:S(2)}) async-start(), calls=%async_computation.18 | async-start | bytes 2457600 | tf_op jit(solution)/shard_map/all_gather | solution.py:428
  53.8 59.0 %all-to-all-start.1 = ((bf16[8,192,1536]{2,1,0:T(8,128)(2,1)}), bf16[8,192,1536]{2,1,0:T(8,128)(2,1)}, u32[]{:S(2)}, u32[]{:S(2)}) async-start(bf16[8,192,1536]{2,1,0:T(8,128)(2,1)} %copy.238), calls=%async_computation.1 | async-start | bytes 9437184 | tf_op jit(solution)/shard_map/all_to_all | solution.py:420
  59.5 321.6 %all-gather.17.cloned.1.call-start = ((), (), s32[]{:S(2)}) async-start(), calls=%async_computation.16 | async-start | bytes 2457600 | tf_op jit(solution)/shard_map/all_gather | solution.py:428
  60.1 446.1 %all-gather.11.cloned.1.call-start = ((), (), s32[]{:S(2)}) async-start(), calls=%async_computation.13 | async-start | bytes 5898240 | tf_op jit(solution)/shard_map/all_gather | solution.py:428
  117.4 164.7 %copy-start.142 = (s32[4]{0:T(128)S(1)}, s32[4]{0:T(128)}, u32[]{:S(2)}) copy-start(s32[4]{0:T(128)} %param.13) | copy-start | bytes 52
  117.4 576.1 %all-gather.15.cloned.1.call-start = ((), (), s32[]{:S(2)}) async-start(), calls=%async_computation.15 | async-start | bytes 5898240 | tf_op jit(solution)/shard_map/all_gather | solution.py:428
  118.0 762.1 %all-gather.19.cloned.1.call-start = ((), (), s32[]{:S(2)}) async-start(), calls=%async_computation.17 | async-start | bytes 5898240 | tf_op jit(solution)/shard_map/all_gather | solution.py:428
  118.8 947.9 %all-gather.23.cloned.1.call-start = ((), (), s32[]{:S(2)}) async-start(), calls=%async_computation.19 | async-start | bytes 5898240 | tf_op jit(solution)/shard_map/all_gather | solution.py:428
  118.8 208.1 %collective-permute-start = (bf16[256,1536]{1,0:T(8,128)(2,1)}, bf16[256,1536]{1,0:T(8,128)(2,1)S(1)}, u32[]{:S(2)}, u32[]{:S(2)}) collective-permute-start(bf16[256,1536]{1,0:T(8,128)(2,1)} %bitcast), channel_id=1, source_target_pairs={{0,0},{2,8},{4,16},{6,24},{8,2},{10,10},{12,18},{14,26},{16,4},{18... | collective-permute-start | bytes 2359304 | tf_op jit(solution)/shard_map/ppermute | solution.py:401
  123.5 168.2 %collective-permute-start.2 = (bf16[256,1536]{1,0:T(8,128)(2,1)}, bf16[256,1536]{1,0:T(8,128)(2,1)S(1)}, u32[]{:S(2)}, u32[]{:S(2)}) collective-permute-start(bf16[256,1536]{1,0:T(8,128)(2,1)} %bitcast.56), channel_id=1, source_target_pairs={{0,0},{2,8},{4,16},{6,24},{8,2},{10,10},{12,18},{14,26},{16,4},{18... | collective-permute-start | bytes 2359304 | tf_op jit(solution)/shard_map/ppermute | solution.py:401
  290.5 36.7 %copy-start.113 = (f32[1536]{0:T(1024)}, f32[1536]{0:T(1024)S(1)}, u32[]{:S(2)}) copy-start(f32[1536]{0:T(1024)S(1)} %get-tuple-element.74) | copy-start | bytes 18436
  290.5 183.0 %copy-start.105 = (f32[1536]{0:T(1024)}, f32[1536]{0:T(1024)S(1)}, u32[]{:S(2)}) copy-start(f32[1536]{0:T(1024)S(1)} %get-tuple-element.73) | copy-start | bytes 18436
  290.5 271.1 %copy-start.115 = (f32[1536]{0:T(1024)}, f32[1536]{0:T(1024)S(1)}, u32[]{:S(2)}) copy-start(f32[1536]{0:T(1024)S(1)} %get-tuple-element.72) | copy-start | bytes 18436
  290.5 370.6 %copy-start.108 = (f32[1536]{0:T(1024)}, f32[1536]{0:T(1024)S(1)}, u32[]{:S(2)}) copy-start(f32[1536]{0:T(1024)S(1)} %get-tuple-element.71) | copy-start | bytes 18436
  290.5 458.6 %copy-start.117 = (f32[1536]{0:T(1024)}, f32[1536]{0:T(1024)S(1)}, u32[]{:S(2)}) copy-start(f32[1536]{0:T(1024)S(1)} %get-tuple-element.70) | copy-start | bytes 18436
  290.5 557.2 %copy-start.110 = (f32[1536]{0:T(1024)}, f32[1536]{0:T(1024)S(1)}, u32[]{:S(2)}) copy-start(f32[1536]{0:T(1024)S(1)} %get-tuple-element.69) | copy-start | bytes 18436
  291.1 35.8 %copy-start.137 = (pred[256]{0:T(512)(128)(4,1)}, pred[256]{0:T(512)(128)(4,1)S(1)}, u32[]{:S(2)}) copy-start(pred[256]{0:T(512)(128)(4,1)S(1)} %add_compare_fusion) | copy-start | bytes 772
  291.7 35.2 %copy-start.44 = (bf16[256,1536]{1,0:T(8,128)(2,1)}, bf16[256,1536]{1,0:T(8,128)(2,1)S(1)}, u32[]{:S(2)}) copy-start(bf16[256,1536]{1,0:T(8,128)(2,1)S(1)} %collective-permute-done.2) | copy-start | bytes 2359300
  326.9 144.8 %copy-start.25 = (bf16[256,1536]{1,0:T(8,128)(2,1)}, bf16[256,1536]{1,0:T(8,128)(2,1)S(1)}, u32[]{:S(2)}) copy-start(bf16[256,1536]{1,0:T(8,128)(2,1)S(1)} %collective-permute-done) | copy-start | bytes 2359300
  359.2 1638.8 %reduce-scatter.31.cloned.1.call-start = ((), (), s32[]{:S(2)}) async-start(), calls=%async_computation.23 | async-start | bytes 2457600 | tf_op jit(solution)/shard_map/reduce_scatter | solution.py:431
  473.4 32.7 %copy-start.122 = (f32[256]{0:T(256)}, f32[256]{0:T(256)S(1)}, u32[]{:S(2)}) copy-start(f32[256]{0:T(256)S(1)} %add_rsqrt_fusion.6) | copy-start | bytes 3076
  527.4 32.5 %copy-start.1 = (f32[256,1536]{1,0:T(8,128)S(1)}, f32[256,1536]{1,0:T(8,128)}, u32[]{:S(2)}) copy-start(f32[256,1536]{1,0:T(8,128)} %copy-done) | copy-start | bytes 4718596
  561.5 97.8 %copy-start.27 = (bf16[256,1536]{1,0:T(8,128)(2,1)}, bf16[256,1536]{1,0:T(8,128)(2,1)S(1)}, u32[]{:S(2)}) copy-start(bf16[256,1536]{1,0:T(8,128)(2,1)S(1)} %get-tuple-element.88) | copy-start | bytes 2359300
  661.0 32.5 %copy-start.125 = (f32[256]{0:T(256)}, f32[256]{0:T(256)S(1)}, u32[]{:S(2)}) copy-start(f32[256]{0:T(256)S(1)} %add_rsqrt_fusion.4) | copy-start | bytes 3076
  749.0 96.9 %copy-start.29 = (bf16[256,1536]{1,0:T(8,128)(2,1)}, bf16[256,1536]{1,0:T(8,128)(2,1)S(1)}, u32[]{:S(2)}) copy-start(bf16[256,1536]{1,0:T(8,128)(2,1)S(1)} %get-tuple-element.84) | copy-start | bytes 2359300
  1256.2 34.5 %copy-start.22 = (f32[256,1536]{1,0:T(8,128)S(1)}, f32[256,1536]{1,0:T(8,128)}, u32[]{:S(2)}) copy-start(f32[256,1536]{1,0:T(8,128)} %plane_scatter.24) | copy-start | bytes 4718596
  1256.3 34.5 %copy-start.55 = (f32[256,1536]{1,0:T(8,128)S(1)}, f32[256,1536]{1,0:T(8,128)}, u32[]{:S(2)}) copy-start(f32[256,1536]{1,0:T(8,128)} %plane_scatter.23) | copy-start | bytes 4718596
  1463.0 32.5 %copy-start.30 = (bf16[256,1536]{1,0:T(8,128)(2,1)S(1)}, bf16[256,1536]{1,0:T(8,128)(2,1)}, u32[]{:S(2)}) copy-start(bf16[256,1536]{1,0:T(8,128)(2,1)} %copy-done.29) | copy-start | bytes 2359300
  1463.1 32.5 %copy-start.118 = (f32[1536]{0:T(1024)S(1)}, f32[1536]{0:T(1024)}, u32[]{:S(2)}) copy-start(f32[1536]{0:T(1024)} %copy-done.117) | copy-start | bytes 18436
  1463.1 35.1 %copy-start.20 = (f32[256,1536]{1,0:T(8,128)S(1)}, f32[256,1536]{1,0:T(8,128)}, u32[]{:S(2)}) copy-start(f32[256,1536]{1,0:T(8,128)} %plane_scatter.26) | copy-start | bytes 4718596
  1635.9 362.2 %reduce-scatter.29.cloned.1.call-start = ((), (), s32[]{:S(2)}) async-start(), calls=%async_computation.22 | async-start | bytes 2457600 | tf_op jit(solution)/shard_map/reduce_scatter | solution.py:431
  1689.9 35.1 %copy-start.18 = (f32[256,1536]{1,0:T(8,128)S(1)}, f32[256,1536]{1,0:T(8,128)}, u32[]{:S(2)}) copy-start(f32[256,1536]{1,0:T(8,128)} %plane_scatter.28) | copy-start | bytes 4718596
  1758.5 239.6 %reduce-scatter.27.cloned.1.call-start = ((), (), s32[]{:S(2)}) async-start(), calls=%async_computation.21 | async-start | bytes 2457600 | tf_op jit(solution)/shard_map/reduce_scatter | solution.py:431
  1857.2 140.9 %reduce-scatter.25.cloned.1.call-start = ((), (), s32[]{:S(2)}) async-start(), calls=%async_computation.20 | async-start | bytes 2457600 | tf_op jit(solution)/shard_map/reduce_scatter | solution.py:431
  1894.1 132.7 %reduce-scatter.39.cloned.1.call-start = ((), (), s32[]{:S(2)}) async-start(), calls=%async_computation.27 | async-start | bytes 5898240 | tf_op jit(solution)/shard_map/reduce_scatter | solution.py:431
  1919.6 195.2 %reduce-scatter.37.cloned.1.call-start = ((), (), s32[]{:S(2)}) async-start(), calls=%async_computation.26 | async-start | bytes 5898240 | tf_op jit(solution)/shard_map/reduce_scatter | solution.py:431
  1945.5 257.3 %reduce-scatter.35.cloned.1.call-start = ((), (), s32[]{:S(2)}) async-start(), calls=%async_computation.25 | async-start | bytes 5898240 | tf_op jit(solution)/shard_map/reduce_scatter | solution.py:431
  1972.1 318.6 %reduce-scatter.33.cloned.1.call-start = ((), (), s32[]{:S(2)}) async-start(), calls=%async_computation.24 | async-start | bytes 5898240 | tf_op jit(solution)/shard_map/reduce_scatter | solution.py:431
  2001.3 293.6 %all-to-all-start.2 = ((bf16[8,192,576]{2,1,0:T(8,128)(2,1)}), bf16[8,192,576]{2,1,0:T(8,128)(2,1)S(1)}, u32[]{:S(2)}, u32[]{:S(2)}) async-start(bf16[8,192,576]{2,1,0:T(8,128)(2,1)} %bitcast.288), calls=%async_computation.2 | async-start | bytes 3932160 | tf_op jit(solution)/shard_map/all_to_all | solution.py:560
  2294.9 183.3 %all-to-all-start.3 = ((bf16[8,192,1536]{2,1,0:T(8,128)(2,1)}), bf16[8,192,1536]{2,1,0:T(8,128)(2,1)}, u32[]{:S(2)}, u32[]{:S(2)}) async-start(bf16[8,192,1536]{2,1,0:T(8,128)(2,1)} %bitcast.285), calls=%async_computation.3 | async-start | bytes 9437184 | tf_op jit(solution)/shard_map/all_to_all | solution.py:560
  2300.1 165.0 %collective-permute-start.1 = (bf16[256,1536]{1,0:T(8,128)(2,1)}, bf16[256,1536]{1,0:T(8,128)(2,1)}, u32[]{:S(2)}, u32[]{:S(2)}) collective-permute-start(bf16[256,1536]{1,0:T(8,128)(2,1)} %get-tuple-element.180), channel_id=1, source_target_pairs={{0,0},{2,8},{4,16},{6,24},{8,2},{10,10},{12,18},{14,26},{16,4},{18... | collective-permute-start | bytes 2359304 | tf_op jit(solution)/shard_map/ppermute | solution.py:401
  2311.4 84.6 %copy-start.26 = (bf16[256,1536]{1,0:T(8,128)(2,1)S(1)}, bf16[256,1536]{1,0:T(8,128)(2,1)}, u32[]{:S(2)}) copy-start(bf16[256,1536]{1,0:T(8,128)(2,1)} %copy-done.25) | copy-start | bytes 2359300
  2311.4 84.6 %copy-start.114 = (f32[1536]{0:T(1024)S(1)}, f32[1536]{0:T(1024)}, u32[]{:S(2)}) copy-start(f32[1536]{0:T(1024)} %copy-done.113) | copy-start | bytes 18436
  2311.4 84.6 %copy-start.130 = (f32[256]{0:T(256)S(1)}, f32[256]{0:T(256)}, u32[]{:S(2)}) copy-start(f32[256]{0:T(256)} %copy-done.129) | copy-start | bytes 3076
  2311.4 87.3 %copy-start.16 = (f32[256,1536]{1,0:T(8,128)S(1)}, f32[256,1536]{1,0:T(8,128)}, u32[]{:S(2)}) copy-start(f32[256,1536]{1,0:T(8,128)} %plane_scatter.30) | copy-start | bytes 4718596
  2401.1 64.0 %collective-permute-start.3 = (bf16[256,1536]{1,0:T(8,128)(2,1)S(1)}, bf16[256,1536]{1,0:T(8,128)(2,1)S(1)}, u32[]{:S(2)}, u32[]{:S(2)}) collective-permute-start(bf16[256,1536]{1,0:T(8,128)(2,1)S(1)} %fusion.69), channel_id=1, source_target_pairs={{0,0},{2,8},{4,16},{6,24},{8,2},{10,10},{12,18},{14,26},{16,4},{18... | collective-permute-start | bytes 2359304 | tf_op jit(solution)/shard_map/ppermute | solution.py:401
  (145 other events, 1207.2 us)
Sparse Core Ops, SparseCore 0:
  43.3 44.1 all-gather.8
  89.1 42.3 all-gather.12
  133.7 77.3 all-gather.20
  213.1 59.7 all-gather.16
  274.9 88.2 all-gather.10
  365.1 87.8 all-gather.14
  455.1 87.8 all-gather.18
  545.2 87.8 all-gather.22
  1636.0 39.1 reduce-scatter.30
  1758.6 39.2 reduce-scatter.28
  1857.4 39.1 reduce-scatter.26
  1899.3 40.6 reduce-scatter.24
  1942.3 84.4 reduce-scatter.38
  2029.0 85.7 reduce-scatter.36
  2117.0 85.7 reduce-scatter.34
  2204.9 85.7 reduce-scatter.32

commit v3 on v2

v3 whole, which is shorter than its diff:
```python
import functools
import math

import jax
import jax.numpy as jnp
from jax import lax
from jax.experimental import pallas as pl
from jax.experimental.pallas import tpu as pltpu
from jax.sharding import Mesh
from jax.sharding import PartitionSpec as P

QUERY_HEADS = 16
KEY_VALUE_HEADS = 8
HEAD_SIZE = 96
FF = 4096

EPS = 1e-05
THETA = 100000.0
LOWER_LIMIT = -1e30

BF = jnp.bfloat16
F32 = jnp.float32

LANES = 128
HALF = HEAD_SIZE // 2
VMEM_LIMIT = 56 * 1024 * 1024


def dot(a, b, dims):
    return lax.dot_general(a, b, (dims, ((), ())), preferred_element_type=F32)


def dot_nn(a, b):
    return dot(a, b, ((1,), (0,)))


def dot_nt(a, b):
    return dot(a, b, ((1,), (1,)))


def dot_tn(a, b):
    return dot(a, b, ((0,), (0,)))


MESH = pl.DeviceIdType.MESH

OWN, X, Y, D = (0, 0), (1, 0), (0, 1), (1, 1)


def place():
    return lax.axis_index("x"), lax.axis_index("c"), lax.axis_index("y")


def flip(index, by):
    return 1 - index if by else index


def rank_of(here, dx, dc, dy):
    x, c, y = here
    return (flip(x, dx) * 2 + flip(c, dc)) * 2 + flip(y, dy)


def greet(here):
    x, c, y = here
    barrier = pltpu.get_barrier_semaphore()
    for peer in ({"x": 1 - x}, {"c": 1 - c}, {"y": 1 - y}):
        pl.semaphore_signal(barrier, inc=1, device_id=peer, device_id_type=MESH)
    pl.semaphore_wait(barrier, 3)


class Sender:
    def __init__(self, here, send_sem, recv_sem):
        x, c, y = here
        self.peers = {"x": {"x": 1 - x}, "c": {"c": 1 - c}, "y": {"y": 1 - y}}
        self.send_sem, self.recv_sem = send_sem, recv_sem
        self.sent = []

    def copy(self, src, dst, index, to, number):
        return pltpu.make_async_remote_copy(
            src_ref=src,
            dst_ref=dst,
            send_sem=self.send_sem.at[number],
            recv_sem=self.recv_sem.at[index],
            device_id=self.peers[to],
            device_id_type=MESH,
        )

    def send(self, src, dst, index, to):
        started = self.copy(src, dst, index, to, len(self.sent))
        started.start()
        self.sent.append(started)

    def arrived(self, where, index):
        self.copy(where, where, index, "c", 0).wait_recv()

    def drain(self):
        for started in self.sent:
            started.wait_send()


def run_gather(here, full, sems, on_block):
    block = full.shape[1]
    piece = block // 4
    net = Sender(here, *sems)

    def index(role, chunk):
        return (role[0] * 4 + role[1] * 2 + role[2]) * 4 + chunk

    def slot(role, chunk, count=1):
        return full.at[rank_of(here, *role), pl.ds(chunk * piece, piece * count)]

    def send(role, chunk, to, as_role, count=1):
        where = slot(role, chunk, count)
        net.send(where, where, index(as_role, chunk), to)

    def arrived(role, chunk, count=1):
        net.arrived(slot(role, chunk, count), index(role, chunk))

    def whole(role):
        for chunk in range(4):
            arrived(role, chunk)

    def done(role):
        on_block(rank_of(here, *role))

    own, at_x, at_y, at_d, at_c = (0, 0, 0), (1, 0, 0), (0, 0, 1), (1, 0, 1), (0, 1, 0)
    xc, yc, dc = (1, 1, 0), (0, 1, 1), (1, 1, 1)
    for cx, cy in ((2, 0), (3, 1), (0, 2), (1, 3)):
        send(own, cx, "x", at_x)
        send(own, cy, "y", at_y)
    send(own, 0, "c", at_c, 4)

    def pass_on(cx, cy):
        arrived(at_x, cx)
        if cx >= 2:
            send(at_x, cx, "y", at_d)
        send(at_x, cx, "c", xc)
        arrived(at_y, cy)
        if cy < 2:
            send(at_y, cy, "x", at_d)
        send(at_y, cy, "c", yc)

    def pass_last(chunks):
        for chunk in chunks:
            arrived(at_d, chunk)
            send(at_d, chunk, "c", dc)

    done(own)
    pass_on(2, 0)
    arrived(at_c, 0, 4)
    done(at_c)
    pass_on(3, 1)
    pass_on(0, 2)
    pass_on(1, 3)
    done(at_x)
    done(at_y)
    pass_last((0, 2))
    whole(xc)
    done(xc)
    whole(yc)
    done(yc)
    pass_last((1, 3))
    done(at_d)
    whole(dc)
    done(dc)
    return net


def run_scatter(here, parts, total, bufs, sems, fill=None, beside=None):
    from_c, via_x, via_y, from_x, from_y = bufs
    block = parts.shape[1]
    half = block // 2
    net = Sender(here, *sems)
    order = (D, X, Y, OWN)
    lower, upper = pl.ds(0, half), pl.ds(half, half)

    def rank(n, dc):
        return rank_of(here, order[n][0], dc, order[n][1])

    def make(r):
        if fill is not None:
            fill(r)

    def sibling(n):
        r = rank(n, 1)
        make(r)
        net.send(parts.at[r], from_c.at[n], n, "c")

    def add(n, where, more):
        r = rank(n, 0)
        parts[r, where] = (parts[r, where].astype(F32) + more.astype(F32)).astype(BF)

    def mine(n, where):
        return parts.at[rank(n, 0), where]

    def combine(n):
        net.arrived(from_c.at[n], n)
        if n < 3:
            add(n, pl.ds(0, block), from_c[n])

    sibling(0)
    make(rank(0, 0))
    sibling(1)
    sibling(2)
    combine(0)
    net.send(mine(0, upper), via_x, 4, "x")
    net.send(mine(0, lower), via_y, 5, "y")
    make(rank(1, 0))
    combine(1)
    net.send(mine(1, upper), from_x.at[upper], 6, "x")
    make(rank(2, 0))
    combine(2)
    net.send(mine(2, lower), from_y.at[lower], 7, "y")
    sibling(3)
    make(rank(3, 0))
    combine(3)
    total[...] = parts[rank(3, 0)].astype(F32) + from_c[3].astype(F32)
    if beside is not None:
        beside(0)
    net.arrived(via_y, 5)
    add(1, lower, via_y[...])
    net.send(mine(1, lower), from_x.at[lower], 8, "x")
    net.arrived(via_x, 4)
    add(2, upper, via_x[...])
    net.send(mine(2, upper), from_y.at[upper], 9, "y")
    if beside is not None:
        beside(1)
    net.arrived(from_x.at[upper], 6)
    net.arrived(from_y.at[lower], 7)
    total[upper] += from_x[upper].astype(F32)
    total[lower] += from_y[lower].astype(F32)
    net.arrived(from_x.at[lower], 8)
    net.arrived(from_y.at[upper], 9)
    total[lower] += from_x[lower].astype(F32)
    total[upper] += from_y[upper].astype(F32)
    return net


def gather_sems():
    return [pltpu.SemaphoreType.DMA((32,)), pltpu.SemaphoreType.DMA((32,))]


def scatter_scratch(block, width):
    half = block // 2
    return [
        pltpu.VMEM((4, block, width), BF),
        pltpu.VMEM((half, width), BF),
        pltpu.VMEM((half, width), BF),
        pltpu.VMEM((block, width), BF),
        pltpu.VMEM((block, width), BF),
        pltpu.SemaphoreType.DMA((10,)),
        pltpu.SemaphoreType.DMA((10,)),
    ]


class Loads:
    def __init__(self, sem):
        self.sem = sem
        self.count = 0

    def start(self, src, dst):
        copy = pltpu.make_async_copy(src, dst, self.sem.at[self.count])
        self.count += 1
        copy.start()
        return copy


def inverse_of(x):
    return lax.rsqrt(jnp.mean(x * x, axis=-1, keepdims=True) + EPS)


def turn(head, cosine, sine):
    return head * cosine + pltpu.roll(head, LANES // 2, 1) * sine


def plane_call(kernel, name, number, out_shape, out_specs, in_specs, scratch, time_us, *operands):
    return pl.pallas_call(
        kernel,
        out_shape=out_shape,
        in_specs=in_specs,
        out_specs=out_specs,
        scratch_shapes=scratch,
        compiler_params=pltpu.CompilerParams(
            collective_id=number, has_side_effects=True, vmem_limit_bytes=VMEM_LIMIT
        ),
        cost_estimate=pl.CostEstimate(flops=0, bytes_accessed=time_us * 3000000, transcendentals=0),
        name=name,
    )(*operands)


ANYWHERE = pl.BlockSpec(memory_space=pl.ANY)
IN_VMEM = pl.BlockSpec(memory_space=pltpu.VMEM)


def attn_in_kernel(heads, h, gain, w_hbm, cosine, sine, a1_out, q_out, k_out, v_out, full, w, send, recv, local):
    here = place()
    loads = Loads(local)
    w_load = loads.start(w_hbm, w)
    x = h[...].astype(F32)
    full[rank_of(here, 0, 0, 0)] = (x * inverse_of(x) * gain[...]).astype(BF)
    greet(here)
    saves = []

    def on_block(r):
        if not saves:
            w_load.wait()
        saves.append(loads.start(full.at[r], a1_out.at[r]))
        qkv = dot_nn(full[r], w[...])
        cos, sin = cosine[r], sine[r]
        part = lambda n: qkv[:, n * LANES : (n + 1) * LANES]
        for n in range(heads):
            q_out[n, r] = turn(part(n), cos, sin).astype(BF)
        k_out[r] = turn(part(heads), cos, sin).astype(BF)
        v_out[r] = part(heads + 1).astype(BF)

    net = run_gather(here, full, (send, recv), on_block)
    net.drain()
    for save in saves:
        save.wait()


def attn_in(h, gain, w, cosine, sine, heads):
    block, width = h.shape
    cols = w.shape[1]
    return plane_call(
        functools.partial(attn_in_kernel, heads),
        "attn_in",
        0,
        [
            jax.ShapeDtypeStruct((8, block, width), BF),
            jax.ShapeDtypeStruct((heads, 8, block, LANES), BF),
            jax.ShapeDtypeStruct((8, block, LANES), BF),
            jax.ShapeDtypeStruct((8, block, LANES), BF),
        ],
        [ANYWHERE, IN_VMEM, IN_VMEM, IN_VMEM],
        [IN_VMEM, IN_VMEM, ANYWHERE, IN_VMEM, IN_VMEM],
        [pltpu.VMEM((8, block, width), BF), pltpu.VMEM((width, cols), BF)]
        + gather_sems()
        + [pltpu.SemaphoreType.DMA((9,))],
        34,
        h, gain, w, cosine, sine,
    )


def mlp_kernel(
    ff, h, o, gain, wo_hbm, wgu_hbm, wd_hbm, mid_out, a2_out, gu_out, hid_out, next_out,
    full, parts, gu, hid, wo, wgu, wd, total,
    from_c, via_x, via_y, from_x, from_y, send1, recv1, send2, recv2,
    from_c3, via_x3, via_y3, from_x3, from_y3, send3, recv3, local,
):
    here = place()
    loads = Loads(local)
    wo_load = loads.start(wo_hbm, wo)
    wgu_load = loads.start(wgu_hbm, wgu)
    wd_load = loads.start(wd_hbm, wd)
    greet(here)
    wo_load.wait()

    def fill(r):
        parts[r] = dot_nt(o[r], wo[...]).astype(BF)

    bufs = (from_c, via_x, via_y, from_x, from_y)
    net1 = run_scatter(here, parts, total, bufs, (send1, recv1), fill)
    mid = h[...].astype(F32) + total[...]
    mid_out[...] = mid
    full[rank_of(here, 0, 0, 0)] = (mid * inverse_of(mid) * gain[...]).astype(BF)
    net1.drain()
    saves = []

    def on_block(r):
        if not saves:
            wgu_load.wait()
            wd_load.wait()
        saves.append(loads.start(full.at[r], a2_out.at[r]))
        a2 = full[r]
        g = dot_nn(a2, wgu[:, :ff])
        u = dot_nn(a2, wgu[:, ff:])
        gu[r, :, :ff] = g.astype(BF)
        gu[r, :, ff:] = u.astype(BF)
        low = (g * (1.0 / (1.0 + jnp.exp(-g))) * u).astype(BF)
        hid[r] = low
        saves.append(loads.start(gu.at[r], gu_out.at[r]))
        saves.append(loads.start(hid.at[r], hid_out.at[r]))
        parts[r] = dot_nt(low, wd[...]).astype(BF)

    net2 = run_gather(here, full, (send2, recv2), on_block)
    bufs3 = (from_c3, via_x3, via_y3, from_x3, from_y3)
    net3 = run_scatter(here, parts, total, bufs3, (send3, recv3))
    next_out[...] = (mid_out[...] + total[...]).astype(BF)
    net2.drain()
    net3.drain()
    for save in saves:
        save.wait()


def mlp(h, o, gain, wo, wgu, wd):
    block, width = h.shape
    ff = wd.shape[1]
    return plane_call(
        functools.partial(mlp_kernel, ff),
        "mlp",
        1,
        [
            jax.ShapeDtypeStruct((block, width), F32),
            jax.ShapeDtypeStruct((8, block, width), BF),
            jax.ShapeDtypeStruct((8, block, 2 * ff), BF),
            jax.ShapeDtypeStruct((8, block, ff), BF),
            jax.ShapeDtypeStruct((block, width), BF),
        ],
        [IN_VMEM, ANYWHERE, ANYWHERE, ANYWHERE, IN_VMEM],
        [IN_VMEM, IN_VMEM, IN_VMEM, ANYWHERE, ANYWHERE, ANYWHERE],
        [
            pltpu.VMEM((8, block, width), BF),
            pltpu.VMEM((8, block, width), BF),
            pltpu.VMEM((8, block, 2 * ff), BF),
            pltpu.VMEM((8, block, ff), BF),
            pltpu.VMEM(wo.shape, BF),
            pltpu.VMEM(wgu.shape, BF),
            pltpu.VMEM(wd.shape, BF),
            pltpu.VMEM((block, width), F32),
        ]
        + scatter_scratch(block, width)
        + gather_sems()
        + scatter_scratch(block, width)
        + [pltpu.SemaphoreType.DMA((27,))],
        96,
        h, o, gain, wo, wgu, wd,
    )


def norm_back(upstream, normed, inverse, gain_row):
    scaled = upstream * gain_row
    return inverse * (scaled - normed * jnp.mean(scaled * normed, axis=-1, keepdims=True))


def mlp_back_kernel(
    ff, e, mid, gain, gu_hbm, wd_hbm, wgu_hbm, wo_hbm, e_out, dgu_out, dmid_out, gain_out, dat_out, dob_out,
    full, full2, parts, gu, wd, wgu, wo, total, send1, recv1,
    from_c, via_x, via_y, from_x, from_y, send2, recv2, send3, recv3, local,
):
    here = place()
    loads = Loads(local)
    wd_load = loads.start(wd_hbm, wd)
    gu_load = loads.start(gu_hbm, gu)
    wgu_load = loads.start(wgu_hbm, wgu)
    wo_load = loads.start(wo_hbm, wo)
    own = rank_of(here, 0, 0, 0)
    full[own] = e[...]
    greet(here)
    saves = []

    def on_block(r):
        first = not saves
        if first:
            wd_load.wait()
            gu_load.wait()
        saves.append(loads.start(full.at[r], e_out.at[r]))
        dhid = dot_nn(full[r], wd[...])
        g = gu[r, :, :ff].astype(F32)
        u = gu[r, :, ff:].astype(F32)
        sig = 1.0 / (1.0 + jnp.exp(-g))
        du = dhid * g * sig
        dg = dhid * u * sig * (1.0 + g * (1.0 - sig))
        gu[r, :, :ff] = dg.astype(BF)
        gu[r, :, ff:] = du.astype(BF)
        saves.append(loads.start(gu.at[r], dgu_out.at[r]))
        if first:
            wgu_load.wait()
        parts[r] = dot_nt(gu[r], wgu[...]).astype(BF)

    net1 = run_gather(here, full, (send1, recv1), on_block)
    net2 = run_scatter(here, parts, total, (from_c, via_x, via_y, from_x, from_y), (send2, recv2))
    da2 = total[...]
    m = mid[...]
    r2 = inverse_of(m)
    n2 = m * r2
    gain_out[...] = jnp.sum(da2 * n2, axis=0, keepdims=True)
    dmid = e[...].astype(F32) + norm_back(da2, n2, r2, gain[...])
    dmid_out[...] = dmid
    full2[own] = dmid.astype(BF)
    wo_load.wait()

    def on_second(r):
        saves.append(loads.start(full2.at[r], dat_out.at[r]))
        dob_out[r] = dot_nn(full2[r], wo[...]).astype(BF)

    net3 = run_gather(here, full2, (send3, recv3), on_second)
    for net in (net1, net2, net3):
        net.drain()
    for save in saves:
        save.wait()


def mlp_back(e, mid, gain, gu, wd, wgu, wo):
    block, width = e.shape
    ff = wd.shape[1]
    cols = wo.shape[1]
    return plane_call(
        functools.partial(mlp_back_kernel, ff),
        "mlp_back",
        2,
        [
            jax.ShapeDtypeStruct((8, block, width), BF),
            jax.ShapeDtypeStruct((8, block, 2 * ff), BF),
            jax.ShapeDtypeStruct((block, width), F32),
            jax.ShapeDtypeStruct((1, width), F32),
            jax.ShapeDtypeStruct((8, block, width), BF),
            jax.ShapeDtypeStruct((8, block, cols), BF),
        ],
        [ANYWHERE, ANYWHERE, IN_VMEM, IN_VMEM, ANYWHERE, IN_VMEM],
        [IN_VMEM, IN_VMEM, IN_VMEM, ANYWHERE, ANYWHERE, ANYWHERE, ANYWHERE],
        [
            pltpu.VMEM((8, block, width), BF),
            pltpu.VMEM((8, block, width), BF),
            pltpu.VMEM((8, block, width), BF),
            pltpu.VMEM((8, block, 2 * ff), BF),
            pltpu.VMEM(wd.shape, BF),
            pltpu.VMEM(wgu.shape, BF),
            pltpu.VMEM(wo.shape, BF),
            pltpu.VMEM((block, width), F32),
        ]
        + gather_sems()
        + scatter_scratch(block, width)
        + gather_sems()
        + [pltpu.SemaphoreType.DMA((28,))],
        100,
        e, mid, gain, gu, wd, wgu, wo,
    )


def attn_back_kernel(
    h, dmid, gain, dq, dk, dv, cosine, sine, w_hbm, dqkv_out, e_out, gain_out,
    parts, w, total, from_c, via_x, via_y, from_x, from_y, send, recv, local,
):
    here = place()
    w_load = Loads(local).start(w_hbm, w)
    greet(here)
    w_load.wait()
    q_cols = dq.shape[2]

    def fill(r):
        dqkv_out[r, :, :q_cols] = dq[r]
        dqkv_out[r, :, q_cols : q_cols + LANES] = turn(dk[r], cosine[r], -sine[r]).astype(BF)
        dqkv_out[r, :, q_cols + LANES :] = dv[r].astype(BF)
        parts[r] = dot_nt(dqkv_out[r], w[...]).astype(BF)

    net = run_scatter(here, parts, total, (from_c, via_x, via_y, from_x, from_y), (send, recv), fill)
    da1 = total[...]
    x = h[...].astype(F32)
    r1 = inverse_of(x)
    n1 = x * r1
    gain_out[...] = jnp.sum(da1 * n1, axis=0, keepdims=True)
    e_out[...] = (dmid[...] + norm_back(da1, n1, r1, gain[...])).astype(BF)
    net.drain()


def attn_back(h, dmid, gain, dq, dk, dv, cosine, sine, w):
    block, width = h.shape
    cols = w.shape[1]
    return plane_call(
        attn_back_kernel,
        "attn_back",
        3,
        [
            jax.ShapeDtypeStruct((8, block, cols), BF),
            jax.ShapeDtypeStruct((block, width), BF),
            jax.ShapeDtypeStruct((1, width), F32),
        ],
        [IN_VMEM, IN_VMEM, IN_VMEM],
        [IN_VMEM] * 8 + [ANYWHERE],
        [pltpu.VMEM((8, block, width), BF), pltpu.VMEM(w.shape, BF), pltpu.VMEM((block, width), F32)]
        + scatter_scratch(block, width)
        + [pltpu.SemaphoreType.DMA((1,))],
        36,
        h, dmid, gain, dq, dk, dv, cosine, sine, w,
    )


LOWER=-1e30
def dot(a, b, dims):
    return lax.dot_general(a, b, (dims, ((), ())), preferred_element_type=F32)

def attend_kernel(scale2, bq, bk, bounds, length, q, k, v, qpos, out, lse):
    groups = q.shape[0]
    i = pl.program_id(0)
    rows = groups * bq
    qs = q[...].reshape(rows, LANES)
    pos = qpos[0]
    pos2 = jnp.concatenate([pos] * groups, axis=1)
    def step(masked, j, state):
        top, total, acc = state
        at = pl.ds(pl.multiple_of(j * bk, bk), bk)
        s = dot(k[at, :], qs, ((1,), (1,)))
        if masked:
            kp = j * bk + lax.broadcasted_iota(jnp.int32, (bk, 1), 0)
            ok = (kp <= pos2) & (kp < length[0])
            s = jnp.where(ok, s, LOWER)
        new = jnp.maximum(top, jnp.max(s, axis=0, keepdims=True) * scale2)
        p = jnp.exp2(s * scale2 - new)
        alpha = jnp.exp2(top - new)
        total = total * alpha + jnp.sum(p, axis=0, keepdims=True)
        acc = acc * alpha + dot(v[at, :], p.astype(BF), ((0,), (0,)))
        return new, total, acc
    state = (jnp.full((1, rows), LOWER, F32), jnp.zeros((1, rows), F32), jnp.zeros((LANES, rows), F32))
    full, end = bounds[0, i], bounds[1, i]
    state = lax.fori_loop(0, full, functools.partial(step, False), state)
    top, total, acc = lax.fori_loop(full, end, functools.partial(step, True), state)
    o = (acc / total).T.astype(BF)
    for g in range(groups):
        out[:, g * LANES:(g + 1) * LANES] = o[g * bq:(g + 1) * bq]
    lse[...] = (top + jnp.log2(total))[None]

def attend(q, k, v, qpos, bounds, length, bq, bk, scale2):
    groups, tokens, _ = q.shape
    n = tokens // bq
    out, lse = pl.pallas_call(
        functools.partial(attend_kernel, scale2, bq, bk),
        grid_spec=pltpu.PrefetchScalarGridSpec(
            num_scalar_prefetch=2, grid=(n,),
            in_specs=[
                pl.BlockSpec((groups, bq, LANES), lambda i, *_: (0, i, 0)),
                pl.BlockSpec(k.shape, lambda i, *_: (0, 0)),
                pl.BlockSpec(v.shape, lambda i, *_: (0, 0)),
                pl.BlockSpec((1, 1, bq), lambda i, *_: (i, 0, 0)),
            ],
            out_specs=[
                pl.BlockSpec((bq, groups * LANES), lambda i, *_: (i, 0)),
                pl.BlockSpec((1, 1, groups * bq), lambda i, *_: (i, 0, 0)),
            ]),
        out_shape=[jax.ShapeDtypeStruct((tokens, groups * LANES), BF), jax.ShapeDtypeStruct((n, 1, groups * bq), F32)],
        compiler_params=pltpu.CompilerParams(vmem_limit_bytes=VMEM_LIMIT),
        name="attend",
        cost_estimate=pl.CostEstimate(flops=0, bytes_accessed=45000000, transcendentals=0),
    )(bounds, length, q, k, v, qpos)
    return out, lse

def back_kernel(scale, scale2, bq, bk, bounds, length, q, k, v, qpos, o, do, lse, cosine, sine, dq, dk, dv):
    groups = q.shape[0]
    i = pl.program_id(0)
    @pl.when(i == 0)
    def _():
        dk[...] = jnp.zeros_like(dk)
        dv[...] = jnp.zeros_like(dv)
    qs = q[...].reshape(groups * bq, LANES)
    dos = jnp.concatenate([do[:, g * LANES:(g + 1) * LANES] for g in range(groups)], axis=0)
    os_ = jnp.concatenate([o[:, g * LANES:(g + 1) * LANES] for g in range(groups)], axis=0)
    delta = jnp.sum(dos.astype(F32) * os_.astype(F32), axis=1, keepdims=True).reshape(1, groups * bq)
    lse_row = lse[0]
    pos = qpos[0]
    pos2 = jnp.concatenate([pos] * groups, axis=1)
    def step(masked, j, acc):
        at = pl.ds(pl.multiple_of(j * bk, bk), bk)
        kb, vb = k[at, :], v[at, :]
        s = dot(kb, qs, ((1,), (1,)))
        p = jnp.exp2(s * scale2 - lse_row)
        if masked:
            kp = j * bk + lax.broadcasted_iota(jnp.int32, (bk, 1), 0)
            ok = (kp <= pos2) & (kp < length[0])
            p = jnp.where(ok, p, 0.0)
        dp = dot(vb, dos, ((1,), (1,)))
        ds = (p * (dp - delta)).astype(BF)
        dv[at, :] += dot(p.astype(BF), dos, ((1,), (0,)))
        dk[at, :] += dot(ds, qs, ((1,), (0,))) * scale
        return acc + dot(ds, kb, ((0,), (0,)))
    full, end = bounds[0, i], bounds[1, i]
    acc = jnp.zeros((groups * bq, LANES), F32)
    acc = lax.fori_loop(0, full, functools.partial(step, False), acc)
    acc = lax.fori_loop(full, end, functools.partial(step, True), acc) * scale
    for g in range(groups):
        dq[:, g * LANES:(g + 1) * LANES] = turn(acc[g * bq:(g + 1) * bq], cosine[...], -sine[...]).astype(BF)

def attend_back(q, k, v, qpos_row, o, do, lse, cosine, sine, bounds, length, bq, bk, scale, scale2):
    groups, tokens, _ = q.shape
    n = tokens // bq
    wide = pl.BlockSpec((bq, groups * LANES), lambda i, *_: (i, 0))
    return pl.pallas_call(
        functools.partial(back_kernel, scale, scale2, bq, bk),
        grid_spec=pltpu.PrefetchScalarGridSpec(
            num_scalar_prefetch=2, grid=(n,),
            in_specs=[
                pl.BlockSpec((groups, bq, LANES), lambda i, *_: (0, i, 0)),
                pl.BlockSpec(k.shape, lambda i, *_: (0, 0)),
                pl.BlockSpec(v.shape, lambda i, *_: (0, 0)),
                pl.BlockSpec((1, 1, bq), lambda i, *_: (i, 0, 0)),
                wide, wide,
                pl.BlockSpec((1, 1, groups * bq), lambda i, *_: (i, 0, 0)),
                pl.BlockSpec((bq, LANES), lambda i, *_: (i, 0)),
                pl.BlockSpec((bq, LANES), lambda i, *_: (i, 0)),
            ],
            out_specs=[wide, pl.BlockSpec(k.shape, lambda i, *_: (0, 0)), pl.BlockSpec(k.shape, lambda i, *_: (0, 0))]),
        out_shape=[jax.ShapeDtypeStruct((tokens, groups * LANES), BF), jax.ShapeDtypeStruct(k.shape, F32), jax.ShapeDtypeStruct(k.shape, F32)],
        compiler_params=pltpu.CompilerParams(vmem_limit_bytes=VMEM_LIMIT),
        name="attend_back",
        cost_estimate=pl.CostEstimate(flops=0, bytes_accessed=65000000, transcendentals=0),
    )(bounds, length, q, k, v, qpos_row, o, do, lse, cosine, sine)

def bounds_of(positions, length, bq, bk):
    p = positions.reshape(-1, bq)
    lo = jnp.minimum(jnp.min(p, axis=1) + 1, length) // bk
    hi = -(-jnp.minimum(jnp.max(p, axis=1) + 1, length) // bk)
    return jnp.stack([lo, hi]).astype(jnp.int32)


PLANE = ("x", "c", "y")

def spread(matrix, heads):
    split = matrix.reshape(matrix.shape[0], heads, 2, HALF)
    return jnp.pad(split, ((0, 0), (0, 0), (0, 0), (0, LANES // 2 - HALF))).reshape(-1, heads * LANES)


def unspread(matrix, heads):
    return matrix.reshape(-1, heads, 2, LANES // 2)[..., :HALF].reshape(-1, heads * HEAD_SIZE)


def widen(matrix, heads):
    split = matrix.reshape(matrix.shape[0], heads, HEAD_SIZE)
    return jnp.pad(split, ((0, 0), (0, 0), (0, LANES - HEAD_SIZE))).reshape(-1, heads * LANES)


def narrow(matrix, heads):
    return matrix.reshape(-1, heads, LANES)[..., :HEAD_SIZE].reshape(-1, heads * HEAD_SIZE)


def together(*arrays):
    return lax.optimization_barrier(arrays)


def body(
    inputs,
    lengths,
    cotangent,
    attn_gain,
    w_query,
    key_projection,
    value_projection,
    w_out,
    mlp_gain,
    w_gate,
    w_up,
    w_down,
):
    sections = lax.axis_size("x") * lax.axis_size("c")
    planes = lax.axis_size("z")
    halves = lax.axis_size("y")
    extra = lax.axis_size("e")
    ranks = sections * halves
    layers = sections
    block = inputs.shape[1]
    width = inputs.shape[2]
    rows = w_query.shape[1]
    tokens = block * ranks
    all_tokens = tokens * extra
    head_group = QUERY_HEADS // KEY_VALUE_HEADS
    q_cols = head_group * HEAD_SIZE
    kv_cols = HEAD_SIZE
    ff_cols = FF // ranks
    scale = 1.0 / math.sqrt(HEAD_SIZE)
    scale2 = scale * math.log2(math.e)

    def swap(array):
        names = ("x", "c", "z")
        pairs = [
            (s * planes + z, z * planes + s) for s in range(sections) for z in range(planes)
        ]
        return lax.ppermute(array, names, pairs)

    def by_rank(matrix):
        return matrix.reshape(rows, ranks, -1)

    attn_pack = jnp.concatenate(
        [
            by_rank(w_query[0]),
            by_rank(key_projection[0]),
            by_rank(value_projection[0]),
            by_rank(w_out[0].T),
            jnp.broadcast_to(jnp.stack([attn_gain[0], mlp_gain[0]], axis=1)[:, None, :], (rows, ranks, 2)),
        ],
        axis=2,
    )
    mlp_pack = jnp.concatenate(
        [by_rank(w_gate[0]), by_rank(w_up[0]), by_rank(w_down[0].T)], axis=2
    )

    def exchange(pack):
        moved = lax.all_to_all(
            jnp.swapaxes(pack.astype(BF), 0, 1), PLANE, split_axis=0, concat_axis=0, tiled=True
        )
        return moved.reshape(layers, halves, rows, pack.shape[2])

    def whole(part):
        if extra > 1:
            part = lax.all_gather(part, "e", axis=1, tiled=False)
        return lax.all_gather(part.reshape(-1, part.shape[-1]), "z", axis=0, tiled=True)

    def reduce_rows(grad):
        mine = lax.psum_scatter(grad.astype(BF), "z", scatter_dimension=0, tiled=True)
        mine = mine.reshape(halves, extra, rows, -1)
        if extra > 1:
            return lax.psum_scatter(mine, "e", scatter_dimension=1, tiled=False)
        return mine[:, 0]

    attn_parts = exchange(attn_pack)
    mlp_parts = exchange(mlp_pack)

    rank = (lax.axis_index("x") * lax.axis_size("c") + lax.axis_index("c")) * halves + lax.axis_index("y")
    spot = lax.axis_index("e")
    length = lengths[lax.axis_index("z")]

    block_start = (jnp.arange(ranks) * extra + spot) * block
    positions = (block_start[:, None] + jnp.arange(block)[None, :]).reshape(tokens)
    exponents = 2.0 * jnp.arange(HEAD_SIZE // 2).astype(F32) / HEAD_SIZE
    angles = positions.astype(F32)[:, None] * (THETA ** (-exponents))[None, :]
    table = lambda values: jnp.pad(values, ((0, 0), (0, LANES // 2 - HALF)))
    cosine = jnp.concatenate([table(jnp.cos(angles))] * 2, axis=1)
    sine = jnp.concatenate([table(-jnp.sin(angles)), table(jnp.sin(angles))], axis=1)
    bq = math.gcd(tokens, 512)
    bk = math.gcd(all_tokens, 512)
    bounds = bounds_of(positions, length, bq, bk)
    length1 = length.reshape(1)
    query_rows = positions.astype(jnp.int32).reshape(-1, 1, bq)

    def all_keys(array):
        if extra == 1:
            return array
        stacked = lax.all_gather(array.reshape(ranks, block, -1), "e", axis=1, tiled=False)
        return stacked.reshape(all_tokens, -1)

    def own_keys(array):
        if extra == 1:
            return array
        stacked = array.astype(BF).reshape(ranks, extra, block, -1)
        return lax.psum_scatter(stacked, "e", scatter_dimension=1, tiled=False).reshape(tokens, -1).astype(F32)

    cosine3 = cosine.reshape(ranks, block, LANES)
    sine3 = sine.reshape(ranks, block, LANES)

    def flat(array):
        return array.reshape(tokens, array.shape[-1])

    hidden_state = swap(inputs[0])
    qk_cols = q_cols + kv_cols
    qkv_cols = qk_cols + kv_cols
    saved = []
    gu_parts = [part[..., : 2 * ff_cols] for part in mlp_parts]
    d_parts = [part[..., 2 * ff_cols :] for part in mlp_parts]
    attn_w, gu_part, d_part = together(whole(attn_parts[0]), gu_parts[0], d_parts[0])
    w_gu, w_d = whole(gu_part), whole(d_part)
    for layer in range(layers):
        w_qkv = jnp.concatenate(
            [spread(attn_w[:, :qk_cols], head_group + 1), widen(attn_w[:, qk_cols:qkv_cols], 1)], axis=1
        )
        w_o = widen(attn_w[:, qkv_cols : qkv_cols + q_cols], head_group)
        gains = attn_w[:, qkv_cols + q_cols :].astype(F32).T
        gain1, gain2 = gains[0:1], gains[1:2]
        a1, q, k, v = attn_in(hidden_state, gain1, w_qkv, cosine3, sine3, head_group)
        q, k, v = q.reshape(head_group, tokens, LANES), all_keys(flat(k)), all_keys(flat(v))
        o, log_total = attend(q, k, v, query_rows, bounds, length1, bq, bk, scale2)
        if layer + 1 < layers:
            o, attn_part, gu_part = together(o, attn_parts[layer + 1], gu_parts[layer + 1])
            attn_w, next_gu = whole(attn_part), whole(gu_part)
        mid, a2, gu, hid, after_mlp = mlp(
            hidden_state, o.reshape(ranks, block, -1), gain2, w_o, w_gu, w_d
        )
        saved.append(
            (hidden_state, a1, q, k, v, o, log_total, mid, a2, gu, hid, w_qkv, w_o, w_gu, w_d, gain1, gain2)
        )
        hidden_state = after_mlp
        if layer + 1 < layers:
            hidden_state, attn_w, w_gu, d_part = together(hidden_state, attn_w, next_gu, d_parts[layer + 1])
            w_d = whole(d_part)
    output = swap(hidden_state)[None]

    my_positions = (rank * extra + spot) * block + jnp.arange(block)
    e = swap(cotangent[0])
    e = jnp.where((my_positions < length)[:, None], e, jnp.zeros_like(e))
    attn_grads = [None] * layers
    gu_grads = [None] * layers
    d_grads = [None] * layers
    for layer in reversed(range(layers)):
        (h, a1, q, k, v, o, log_total, mid, a2, gu, hid, w_qkv, w_o, w_gu, w_d, gain1, gain2) = saved[layer]
        e_all, dgu, dmid, gain2_grad, dat, dob = mlp_back(e, mid, gain2, gu, w_d, w_gu, w_o)
        gu_sums = dot_tn(flat(a2), flat(dgu)).astype(BF)
        d_sums = dot_tn(flat(e_all), flat(hid)).astype(BF)
        dob, gu_sums, d_sums = together(dob, gu_sums, d_sums)
        if layer + 1 < layers:
            dob, attn_grads[layer + 1], d_grads[layer + 1] = together(
                dob, attn_grads[layer + 1], d_grads[layer + 1]
            )
        gu_grads[layer] = reduce_rows(gu_sums)
        if layer == 0:
            d_grads[layer] = reduce_rows(d_sums)
        dq, dk, dv = attend_back(
            q, k, v, query_rows, o, flat(dob), log_total, cosine, sine, bounds, length1, bq, bk, scale, scale2
        )
        dk, dv = own_keys(dk), own_keys(dv)
        dqkv, e, gain1_grad = attn_back(
            h, dmid, gain1, *(array.reshape(ranks, block, -1) for array in (dq, dk, dv)), cosine3, sine3, w_qkv
        )
        dqkv_w = dot_tn(flat(a1), flat(dqkv)).astype(BF)
        qk_wide = (head_group + 1) * LANES
        attn_sums = jnp.concatenate(
            [
                unspread(dqkv_w[:, :qk_wide], head_group + 1),
                narrow(dqkv_w[:, qk_wide:], 1),
                narrow(dot_tn(flat(dat), o).astype(BF), head_group),
                jnp.concatenate([gain1_grad, gain2_grad], axis=0).T.astype(BF),
            ],
            axis=1,
        )
        if layer > 0:
            e, attn_sums, d_sums, gu_grads[layer] = together(e, attn_sums, d_sums, gu_grads[layer])
            d_grads[layer] = reduce_rows(d_sums)
        else:
            e, attn_sums, gu_grads[layer], d_grads[layer] = together(e, attn_sums, gu_grads[layer], d_grads[layer])
        attn_grads[layer] = reduce_rows(attn_sums)
    input_grad = swap(e)[None]

    def send_home(grads):
        stacked = jnp.stack(grads).reshape(ranks, rows, -1)
        back = lax.all_to_all(stacked, PLANE, split_axis=0, concat_axis=0, tiled=True)
        return back.astype(F32)

    def columns(back, start, count):
        return jnp.swapaxes(back[:, :, start : start + count], 0, 1).reshape(rows, ranks * count)

    mlp_back_home = send_home([jnp.concatenate(pair, axis=2) for pair in zip(gu_grads, d_grads)])
    attn_back_home = send_home(attn_grads)
    at = q_cols + 2 * kv_cols
    gain_sums = jnp.sum(attn_back_home[:, :, at + q_cols :], axis=0)
    return (
        output,
        input_grad,
        gain_sums[:, 0][None],
        columns(attn_back_home, 0, q_cols)[None],
        columns(attn_back_home, q_cols, kv_cols)[None],
        columns(attn_back_home, q_cols + kv_cols, kv_cols)[None],
        columns(attn_back_home, at, q_cols).T[None],
        gain_sums[:, 1][None],
        columns(mlp_back_home, 0, ff_cols)[None],
        columns(mlp_back_home, ff_cols, ff_cols)[None],
        columns(mlp_back_home, 2 * ff_cols, ff_cols).T[None],
    )


def solution(mesh):
    section, seq = mesh.devices.shape
    halves = KEY_VALUE_HEADS // section
    extra = seq // (section * halves)
    fine = Mesh(
        mesh.devices.reshape(section // 2, 2, section, halves, extra), ("x", "c", "z", "y", "e")
    )
    sec, sq = ("x", "c"), ("z", "y", "e")
    rows3 = P(sec, sq, None)
    cols3 = P(sec, None, sq)
    in_specs = (rows3, P(), rows3, P(sec, sq), rows3, rows3, rows3, cols3, P(sec, sq), rows3, rows3, cols3)
    out_specs = (rows3, rows3, P(sec, sq), rows3, rows3, rows3, cols3, P(sec, sq), rows3, rows3, cols3)
    return jax.shard_map(body, mesh=fine, in_specs=in_specs, out_specs=out_specs, check_vma=False)
```

time: 2520 us -> 1850 us (0.73)
  blocking collectives: 230 us -> 0 us
  matrix products: 336 us -> 119 us
  local copies, waits for them, and re-layouts: 204 us -> 107 us
  other arithmetic: 129 us -> 49.6 us
  Pallas kernels: 1220 us -> 1160 us
    dot_general x48 -> x16, matrix products: 336 us -> 119 us  [dot(): return lax.dot_general(a, b, (dims, ((), ())), preferred_element_type=F32)]
    reduce_scatter x8 -> x12, waiting for transfers between devices: 285 us -> 98.6 us  [reduce_rows(): lax.psum_scatter(grad.astype(BF), 'z', scatter_dimension=0, tiled=True)]
    all_gather x1 -> x0, blocking collectives: 155 us -> none  [body(): lax.all_gather(gains, ('x', 'c', 'z', 'y', 'e'), axis=0, tiled=False)]
    ppermute x4, waiting for transfers between devices: 0.01 us -> 108 us  [swap(): return lax.ppermute(array, names, pairs)]
    unnamed x355 -> x96, local copies, waits for them, and re-layouts: 90.9 us -> 23.5 us
    all_gather x8 -> x12, waiting for transfers between devices: 0.11 us -> 63.2 us  [whole(): lax.all_gather(part.reshape(-1, part.shape[-1]), 'z', axis=0, tiled=True)]
    convert_element_type x33 -> x4, other arithmetic: 49.6 us -> 0.08 us  [body(): jnp.concatenate([gain1_grad, gain2_grad], axis=0).T.astype(BF)]
    unnamed x1 -> x0, blocking collectives: 46.9 us -> none
  transfers between devices with their start and end apart: 23 -> 32, of which waited for: 5 -> 14; matrix products, arithmetic and copies ran while one was open for 17% -> 12% of each run, Pallas kernels for 33% -> 53%
where the time goes in v3:
time: 1850 us; the launch traced here: 1840 us
  Pallas kernels  1160 us (63%)
  waiting for transfers between devices  345 us (19%)
  matrix products  119 us (6%)
  local copies, waits for them, and re-layouts  107 us (6%)
  other arithmetic  49.6 us (3%)
  starting transfers between devices  43.7 us (2%)
    pallas_call x16, Pallas kernels, plane_call(): pl.pallas_call(kernel, out_shape=out_shape, in_specs=in_specs, out_specs=...  1060 us
    dot_general x16, matrix products, dot(): return lax.dot_general(a, b, (dims, ((), ())), preferred_element_type=F32)  119 us
    ppermute x4, waiting for transfers between devices, swap(): return lax.ppermute(array, names, pairs)  108 us
    reduce_scatter x12, waiting for transfers between devices, reduce_rows(): lax.psum_scatter(grad.astype(BF), 'z', scatter_dimension=0, tiled=True)  98.6 us
    all_to_all x2, waiting for transfers between devices, exchange(): lax.all_to_all(jnp.swapaxes(pack.astype(BF), 0, 1), PLANE, split_axis=0,...  65.4 us
    all_gather x12, waiting for transfers between devices, whole(): lax.all_gather(part.reshape(-1, part.shape[-1]), 'z', axis=0, tiled=True)  63.2 us
    pallas_call x4, Pallas kernels, attend_back(): pl.pallas_call(functools.partial(back_kernel, scale, scale2, bq, bk), gri...  57.7 us
    pallas_call x4, Pallas kernels, attend(): pl.pallas_call(functools.partial(attend_kernel, scale2, bq, bk), grid_spe...  39.1 us
  transfers between devices with their start and end apart: 32, of which 14 were waited for; matrix products, arithmetic and copies ran while one was open for 12% of the time, Pallas kernels for 53%

profile of v3, /device:TPU:2, one launch (start us, length us, event | category | flops | bytes accessed | tf_op | source)
XLA Modules:
  0.0 1841.0 jit_solution(12717128467648919238)
XLA Ops:
  31.6 13.5 all-to-all-done
  51.8 51.9 %all-to-all-done.1 = bf16[8,192,1536]{2,1,0:T(8,128)(2,1)} async-done(((bf16[8,192,1536]{2,1,0:T(8,128)(2,1)}), bf16[8,192,1536]{2,1,0:T(8,128)(2,1)}, u32[]{:S(2)}, u32[]{:S(2)}) %all-to-all-start.1) | async-done | bytes 4718624 | tf_op jit(solution)/shard_map/all_to_all | solution.py:785
  134.3 42.4 %collective-permute-done.h = bf16[256,1536]{1,0:T(8,128)(2,1)S(1)} collective-permute-done((bf16[256,1536]{1,0:T(8,128)(2,1)}, bf16[256,1536]{1,0:T(8,128)(2,1)S(1)}, u32[]{:S(2)}, u32[]{:S(2)}) %collective-permute-start) | collective-permute-done | bytes 786464 | tf_op jit(solution)/shard_map/ppermute | solution.py:765
  177.6 33.0 %attn_in.4 = (bf16[8,256,1536]{2,1,0:T(8,128)(2,1)}, bf16[2,8,256,128]{3,2,1,0:T(8,128)(2,1)}, bf16[8,256,128]{2,1,0:T(8,128)(2,1)}, bf16[8,256,128]{2,1,0:T(8,128)(2,1)}) custom-call(bf16[256,1536]{1,0:T(8,128)(2,1)} %copy-done, f32[1,1536]{1,0:T(1,128)} %copy.267.gain, bf16[1536,512]{1,0:T(8,128)(2,1)} %pad_maximum_fusion.6.w_hbm, ...), custom_call_target="tpu_custom_call" | custom-call | bytes 102000000 | tf_op jit(solution)/shard_map/attn_in/pallas_call | solution.py:277
  210.6 9.8 attend.4
  223.6 15.4 all-gather.15.cloned.1.call-done.wgu_hbm
  239.0 96.6 %mlp.4 = (f32[256,1536]{1,0:T(8,128)}, bf16[8,256,1536]{2,1,0:T(8,128)(2,1)}, bf16[8,256,1024]{2,1,0:T(8,128)(2,1)}, bf16[8,256,512]{2,1,0:T(8,128)(2,1)}, bf16[256,1536]{1,0:T(8,128)(2,1)}) custom-call(bf16[256,1536]{1,0:T(8,128)(2,1)} %copy-done, bf16[8,256,256]{2,1,0:T(8,128)(2,1)} %bitcast.341, f32[1,1536]{1,0:T(1,128)} %copy.270.gain, ...), custom_call_target="tpu_custom_call" | custom-call | bytes 288000000 | tf_op jit(solution)/shard_map/mlp/pallas_call | solution.py:277
  335.6 10.8 all-gather.21.cloned.1.call-done.wgu_hbm
  354.2 33.9 %attn_in.5 = (bf16[8,256,1536]{2,1,0:T(8,128)(2,1)}, bf16[2,8,256,128]{3,2,1,0:T(8,128)(2,1)}, bf16[8,256,128]{2,1,0:T(8,128)(2,1)}, bf16[8,256,128]{2,1,0:T(8,128)(2,1)}) custom-call(bf16[256,1536]{1,0:T(8,128)(2,1)} %get-tuple-element.175.h, f32[1,1536]{1,0:T(1,128)} %copy.273.gain, bf16[1536,512]{1,0:T(8,128)(2,1)} %pad_maximum_fusion.7.w_hbm, ...), custom_call_target="tpu_custom_call" | custom-call | bytes 102000000 | tf_op jit(solution)/shard_map/attn_in/pallas_call | solution.py:277
  388.1 9.7 attend.5
  401.2 96.0 %mlp.5 = (f32[256,1536]{1,0:T(8,128)}, bf16[8,256,1536]{2,1,0:T(8,128)(2,1)}, bf16[8,256,1024]{2,1,0:T(8,128)(2,1)}, bf16[8,256,512]{2,1,0:T(8,128)(2,1)}, bf16[256,1536]{1,0:T(8,128)(2,1)}) custom-call(bf16[256,1536]{1,0:T(8,128)(2,1)} %get-tuple-element.175.h, bf16[8,256,256]{2,1,0:T(8,128)(2,1)} %bitcast.342, f32[1,1536]{1,0:T(1,128)} %copy.276.gain, ...), custom_call_target="tpu_custom_call" | custom-call | bytes 288000000 | tf_op jit(solution)/shard_map/mlp/pallas_call | solution.py:277
  497.3 13.5 all-gather.27.cloned.1.call-done.wgu_hbm
  518.5 34.1 %attn_in.6 = (bf16[8,256,1536]{2,1,0:T(8,128)(2,1)}, bf16[2,8,256,128]{3,2,1,0:T(8,128)(2,1)}, bf16[8,256,128]{2,1,0:T(8,128)(2,1)}, bf16[8,256,128]{2,1,0:T(8,128)(2,1)}) custom-call(bf16[256,1536]{1,0:T(8,128)(2,1)} %get-tuple-element.187.h, f32[1,1536]{1,0:T(1,128)} %copy.279.gain, bf16[1536,512]{1,0:T(8,128)(2,1)} %pad_maximum_fusion.8.w_hbm, ...), custom_call_target="tpu_custom_call" | custom-call | bytes 102000000 | tf_op jit(solution)/shard_map/attn_in/pallas_call | solution.py:277
  552.6 9.8 attend.6
  563.2 9.3 collective-permute-start.2
  575.5 103.5 %mlp.6 = (f32[256,1536]{1,0:T(8,128)}, bf16[8,256,1536]{2,1,0:T(8,128)(2,1)}, bf16[8,256,1024]{2,1,0:T(8,128)(2,1)}, bf16[8,256,512]{2,1,0:T(8,128)(2,1)}, bf16[256,1536]{1,0:T(8,128)(2,1)}) custom-call(bf16[256,1536]{1,0:T(8,128)(2,1)} %get-tuple-element.187.h, bf16[8,256,256]{2,1,0:T(8,128)(2,1)} %bitcast.343, f32[1,1536]{1,0:T(1,128)} %copy.282.gain, ...), custom_call_target="tpu_custom_call" | custom-call | bytes 288000000 | tf_op jit(solution)/shard_map/mlp/pallas_call | solution.py:277
  679.0 23.4 %all-gather.33.cloned.1.call-done.wgu_hbm = bf16[1536,1024]{1,0:T(8,128)(2,1)} async-done(((bf16[384,1024]{1,0:T(8,128)(2,1)}), bf16[1536,1024]{1,0:T(8,128)(2,1)}) %all-gather.33.cloned.1.call-update) | async-done | bytes 3145744 | tf_op jit(solution)/shard_map/all_gather | solution.py:793
  718.7 33.8 %attn_in.7 = (bf16[8,256,1536]{2,1,0:T(8,128)(2,1)}, bf16[2,8,256,128]{3,2,1,0:T(8,128)(2,1)}, bf16[8,256,128]{2,1,0:T(8,128)(2,1)}, bf16[8,256,128]{2,1,0:T(8,128)(2,1)}) custom-call(bf16[256,1536]{1,0:T(8,128)(2,1)} %get-tuple-element.199.h, f32[1,1536]{1,0:T(1,128)} %copy.285.gain, bf16[1536,512]{1,0:T(8,128)(2,1)} %pad_maximum_fusion.9.w_hbm, ...), custom_call_target="tpu_custom_call" | custom-call | bytes 102000000 | tf_op jit(solution)/shard_map/attn_in/pallas_call | solution.py:277
  752.5 9.8 attend.7
  762.4 95.8 %mlp.7 = (f32[256,1536]{1,0:T(8,128)}, bf16[8,256,1536]{2,1,0:T(8,128)(2,1)}, bf16[8,256,1024]{2,1,0:T(8,128)(2,1)}, bf16[8,256,512]{2,1,0:T(8,128)(2,1)}, bf16[256,1536]{1,0:T(8,128)(2,1)}) custom-call(bf16[256,1536]{1,0:T(8,128)(2,1)} %get-tuple-element.199.h, bf16[8,256,256]{2,1,0:T(8,128)(2,1)} %bitcast.344, f32[1,1536]{1,0:T(1,128)} %copy.288.gain, ...), custom_call_target="tpu_custom_call" | custom-call | bytes 288000000 | tf_op jit(solution)/shard_map/mlp/pallas_call | solution.py:277
  858.2 95.4 %mlp_back.4 = (bf16[8,256,1536]{2,1,0:T(8,128)(2,1)}, bf16[8,256,1024]{2,1,0:T(8,128)(2,1)}, f32[256,1536]{1,0:T(8,128)}, f32[1,1536]{1,0:T(1,128)}, bf16[8,256,...) custom-call(bf16[256,1536]{1,0:T(8,128)(2,1)} %broadcast_select_fusion.e, f32[256,1536]{1,0:T(8,128)} %get-tuple-element.208.mid, ...), custom_call_target="tpu_custom_call" | custom-call | bytes 300000000 | tf_op jit(solution)/shard_map/mlp_back/pallas_call | solution.py:277
  953.6 7.4 fusion
  961.0 11.4 bitcast_convert_fusion.3
  978.3 14.6 attend_back.4
  992.9 38.7 %attn_back.4 = (bf16[8,256,512]{2,1,0:T(8,128)(2,1)}, bf16[256,1536]{1,0:T(8,128)(2,1)}, f32[1,1536]{1,0:T(1,128)}) custom-call(bf16[256,1536]{1,0:T(8,128)(2,1)} %get-tuple-element.199.h, f32[256,1536]{1,0:T(8,128)} %get-tuple-element.210.dmid, f32[1,1536]{1,0:T(1,128)} %copy.285.gain, bf16[8,256,256]{2,1,0:T(8,128)(2,1)} %bitcast.408, ...), custom_call_target="tpu_custom_call" | custom-call | bytes 108000000 | tf_op jit(solution)/shard_map/attn_back/pallas_call | solution.py:277
  1040.7 95.5 %mlp_back.5 = (bf16[8,256,1536]{2,1,0:T(8,128)(2,1)}, bf16[8,256,1024]{2,1,0:T(8,128)(2,1)}, f32[256,1536]{1,0:T(8,128)}, f32[1,1536]{1,0:T(1,128)}, bf16[8,256,...) custom-call(bf16[256,1536]{1,0:T(8,128)(2,1)} %get-tuple-element.229.e, f32[256,1536]{1,0:T(8,128)} %get-tuple-element.230.mid, ...), custom_call_target="tpu_custom_call" | custom-call | bytes 300000000 | tf_op jit(solution)/shard_map/mlp_back/pallas_call | solution.py:277
  1136.3 7.4 fusion.2
  1143.7 11.3 bitcast_convert_fusion.2
  1161.0 14.5 attend_back.5
  1175.4 38.5 %attn_back.5 = (bf16[8,256,512]{2,1,0:T(8,128)(2,1)}, bf16[256,1536]{1,0:T(8,128)(2,1)}, f32[1,1536]{1,0:T(1,128)}) custom-call(bf16[256,1536]{1,0:T(8,128)(2,1)} %get-tuple-element.187.h, f32[256,1536]{1,0:T(8,128)} %get-tuple-element.232.dmid, f32[1,1536]{1,0:T(1,128)} %copy.279.gain, bf16[8,256,256]{2,1,0:T(8,128)(2,1)} %bitcast.402, ...), custom_call_target="tpu_custom_call" | custom-call | bytes 108000000 | tf_op jit(solution)/shard_map/attn_back/pallas_call | solution.py:277
  1214.6 6.9 fusion.3
  1222.0 7.0 reduce-scatter.25.cloned.1.call-done
  1231.6 96.2 %mlp_back.6 = (bf16[8,256,1536]{2,1,0:T(8,128)(2,1)}, bf16[8,256,1024]{2,1,0:T(8,128)(2,1)}, f32[256,1536]{1,0:T(8,128)}, f32[1,1536]{1,0:T(1,128)}, bf16[8,256,...) custom-call(bf16[256,1536]{1,0:T(8,128)(2,1)} %get-tuple-element.254.e, f32[256,1536]{1,0:T(8,128)} %get-tuple-element.255.mid, ...), custom_call_target="tpu_custom_call" | custom-call | bytes 300000000 | tf_op jit(solution)/shard_map/mlp_back/pallas_call | solution.py:277
  1327.8 7.4 fusion.4
  1335.2 11.2 bitcast_convert_fusion.1
  1352.4 14.2 attend_back.6
  1366.7 38.8 %attn_back.6 = (bf16[8,256,512]{2,1,0:T(8,128)(2,1)}, bf16[256,1536]{1,0:T(8,128)(2,1)}, f32[1,1536]{1,0:T(1,128)}) custom-call(bf16[256,1536]{1,0:T(8,128)(2,1)} %get-tuple-element.175.h, f32[256,1536]{1,0:T(8,128)} %get-tuple-element.257.dmid, f32[1,1536]{1,0:T(1,128)} %copy.273.gain, bf16[8,256,256]{2,1,0:T(8,128)(2,1)} %bitcast.405, ...), custom_call_target="tpu_custom_call" | custom-call | bytes 108000000 | tf_op jit(solution)/shard_map/attn_back/pallas_call | solution.py:277
  1413.4 9.2 reduce-scatter.29.cloned.1.call-done
  1425.4 95.9 %mlp_back.7 = (bf16[8,256,1536]{2,1,0:T(8,128)(2,1)}, bf16[8,256,1024]{2,1,0:T(8,128)(2,1)}, f32[256,1536]{1,0:T(8,128)}, f32[1,1536]{1,0:T(1,128)}, bf16[8,256,...) custom-call(bf16[256,1536]{1,0:T(8,128)(2,1)} %get-tuple-element.279.e, f32[256,1536]{1,0:T(8,128)} %get-tuple-element.280.mid, ...), custom_call_target="tpu_custom_call" | custom-call | bytes 300000000 | tf_op jit(solution)/shard_map/mlp_back/pallas_call | solution.py:277
  1521.3 7.4 fusion.6
  1528.7 11.2 bitcast_convert_fusion
  1550.1 14.5 attend_back.7
  1564.5 38.3 %attn_back.7 = (bf16[8,256,512]{2,1,0:T(8,128)(2,1)}, bf16[256,1536]{1,0:T(8,128)(2,1)}, f32[1,1536]{1,0:T(1,128)}) custom-call(bf16[256,1536]{1,0:T(8,128)(2,1)} %copy-done, f32[256,1536]{1,0:T(8,128)} %get-tuple-element.282.dmid, f32[1,1536]{1,0:T(1,128)} %copy.267.gain, bf16[8,256,256]{2,1,0:T(8,128)(2,1)} %bitcast.399, f32[8,256,128]{2,1,0:T(8,128)} %bitcast.400, ...), custom_call_target="tpu_custom_call" | custom-call | bytes 108000000 | tf_op jit(solution)/shard_map/attn_back/pallas_call | solution.py:277
  1603.5 6.9 fusion.7
  1613.0 39.8 %reduce-scatter.33.cloned.1.call-done = bf16[384,1024]{1,0:T(8,128)(2,1)} async-done(((bf16[1536,1024]{1,0:T(8,128)(2,1)}), bf16[384,1024]{1,0:T(8,128)(2,1)}) %reduce-scatter.33.cloned.1.call-update) | async-done | bytes 786448 | tf_op jit(solution)/shard_map/reduce_scatter | solution.py:796
  1664.8 42.4 %reduce-scatter.43.cloned.1.call-done = bf16[384,578]{1,0:T(8,128)(2,1)} async-done(((bf16[1536,578]{1,0:T(8,128)(2,1)}), bf16[384,578]{1,0:T(8,128)(2,1)}) %reduce-scatter.43.cloned.1.call-update) | async-done | bytes 443920 | tf_op jit(solution)/shard_map/reduce_scatter | solution.py:796
  1728.2 49.9 %collective-permute-done.1 = bf16[256,1536]{1,0:T(8,128)(2,1)S(1)} collective-permute-done((bf16[256,1536]{1,0:T(8,128)(2,1)S(1)}, bf16[256,1536]{1,0:T(8,128)(2,1)S(1)}, u32[]{:S(2)}, u32[]{:S(2)}) %collective-permute-start.1) | collective-permute-done | bytes 786464 | tf_op jit(solution)/shard_map/ppermute | solution.py:765
  1778.1 16.1 collective-permute-done.3
  (348 shorter events, 230.9 us)
Async XLA Ops:
  17.2 27.9 %all-to-all-start = ((bf16[8,192,578]{2,1,0:T(8,128)(2,1)}), bf16[8,192,578]{2,1,0:T(8,128)(2,1)S(1)}, u32[]{:S(2)}, u32[]{:S(2)}) async-start(bf16[8,192,578]{2,1,0:T(8,128)(2,1)} %bitcast.8), calls=%async_computation | async-start | bytes 3932160 | tf_op jit(solution)/shard_map/all_to_all | solution.py:785
  45.2 58.5 %all-to-all-start.1 = ((bf16[8,192,1536]{2,1,0:T(8,128)(2,1)}), bf16[8,192,1536]{2,1,0:T(8,128)(2,1)}, u32[]{:S(2)}, u32[]{:S(2)}) async-start(bf16[8,192,1536]{2,1,0:T(8,128)(2,1)} %maximum_bitcast_fusion), calls=%async_computation.1 | async-start | bytes 9437184 | tf_op jit(solution)/shard_map/all_to_all | solution.py:785
  50.4 59.5 %all-gather.13.cloned.1.call-start = ((), (), s32[]{:S(2)}) async-start(), calls=%async_computation.16 | async-start | bytes 2457600 | tf_op jit(solution)/shard_map/all_gather | solution.py:793
  51.7 171.8 %all-gather.17.cloned.1.call-start = ((), (), s32[]{:S(2)}) async-start(), calls=%async_computation.18 | async-start | bytes 1966080 | tf_op jit(solution)/shard_map/all_gather | solution.py:793
  109.9 129.0 %all-gather.15.cloned.1.call-start = ((), (), s32[]{:S(2)}) async-start(), calls=%async_computation.17 | async-start | bytes 3932160 | tf_op jit(solution)/shard_map/all_gather | solution.py:793
  110.6 224.9 %all-gather.19.cloned.1.call-start = ((), (), s32[]{:S(2)}) async-start(), calls=%async_computation.19 | async-start | bytes 2457600 | tf_op jit(solution)/shard_map/all_gather | solution.py:793
  110.7 66.0 %collective-permute-start = (bf16[256,1536]{1,0:T(8,128)(2,1)}, bf16[256,1536]{1,0:T(8,128)(2,1)S(1)}, u32[]{:S(2)}, u32[]{:S(2)}) collective-permute-start(bf16[256,1536]{1,0:T(8,128)(2,1)} %bitcast), channel_id=1, source_target_pairs={{0,0},{2,8},{4,16},{6,24},{8,2},{10,10},{12,18},{14,26},{16,4},{18... | collective-permute-start | bytes 2359304 | tf_op jit(solution)/shard_map/ppermute | solution.py:765
  220.4 126.0 %all-gather.21.cloned.1.call-start = ((), (), s32[]{:S(2)}) async-start(), calls=%async_computation.20 | async-start | bytes 3932160 | tf_op jit(solution)/shard_map/all_gather | solution.py:793
  221.0 180.2 %all-gather.23.cloned.1.call-start = ((), (), s32[]{:S(2)}) async-start(), calls=%async_computation.21 | async-start | bytes 1966080 | tf_op jit(solution)/shard_map/all_gather | solution.py:793
  335.6 10.9 slice-start.4
  346.4 150.8 %all-gather.25.cloned.1.call-start = ((), (), s32[]{:S(2)}) async-start(), calls=%async_computation.22 | async-start | bytes 2457600 | tf_op jit(solution)/shard_map/all_gather | solution.py:793
  388.1 10.8 slice-start.5
  397.9 112.9 %all-gather.27.cloned.1.call-start = ((), (), s32[]{:S(2)}) async-start(), calls=%async_computation.23 | async-start | bytes 3932160 | tf_op jit(solution)/shard_map/all_gather | solution.py:793
  398.6 176.9 %all-gather.29.cloned.1.call-start = ((), (), s32[]{:S(2)}) async-start(), calls=%async_computation.24 | async-start | bytes 1966080 | tf_op jit(solution)/shard_map/all_gather | solution.py:793
  497.2 13.6 slice-start.6
  510.8 168.2 %all-gather.31.cloned.1.call-start = ((), (), s32[]{:S(2)}) async-start(), calls=%async_computation.25 | async-start | bytes 2457600 | tf_op jit(solution)/shard_map/all_gather | solution.py:793
  552.6 20.6 %slice-start.7 = ((bf16[1536,578]{1,0:T(8,128)(2,1)}), bf16[1536,192]{1,0:T(8,128)(2,1)S(1)}, s32[]{:S(2)}) async-start(bf16[1536,578]{1,0:T(8,128)(2,1)} %all-gather.25.cloned.1.call-done), calls=%async_computation.47 | async-start | bytes 1572864 | tf_op jit(solution)/shard_map/slice | solution.py:852
  562.4 140.1 %all-gather.33.cloned.1.call-start = ((), (), s32[]{:S(2)}) async-start(), calls=%async_computation.26 | async-start | bytes 3932160 | tf_op jit(solution)/shard_map/all_gather | solution.py:793
  563.1 199.3 %all-gather.35.cloned.1.call-start = ((), (), s32[]{:S(2)}) async-start(), calls=%async_computation.27 | async-start | bytes 1966080 | tf_op jit(solution)/shard_map/all_gather | solution.py:793
  563.2 139.3 %collective-permute-start.2 = (bf16[256,1536]{1,0:T(8,128)(2,1)}, bf16[256,1536]{1,0:T(8,128)(2,1)}, u32[]{:S(2)}, u32[]{:S(2)}) collective-permute-start(bf16[256,1536]{1,0:T(8,128)(2,1)} %bitcast.445), channel_id=1, source_target_pairs={{0,0},{2,8},{4,16},{6,24},{8,2},{10,10},{12,18},{14,26},{16,4},{18... | collective-permute-start | bytes 2359304 | tf_op jit(solution)/shard_map/ppermute | solution.py:765
  702.5 335.4 %reduce-scatter.21.cloned.1.call-start = ((), (), s32[]{:S(2)}) async-start(), calls=%async_computation.28 | async-start | bytes 3932160 | tf_op jit(solution)/shard_map/reduce_scatter | solution.py:796
  858.2 95.4 %copy-start.36 = (bf16[8,256,512]{2,1,0:T(8,128)(2,1)S(1)}, bf16[8,256,512]{2,1,0:T(8,128)(2,1)}, u32[]{:S(2)}) copy-start(bf16[8,256,512]{2,1,0:T(8,128)(2,1)} %get-tuple-element.215) | copy-start | bytes 6291460
  972.4 188.5 %reduce-scatter.23.cloned.1.call-start = ((), (), s32[]{:S(2)}) async-start(), calls=%async_computation.29 | async-start | bytes 1966080 | tf_op jit(solution)/shard_map/reduce_scatter | solution.py:796
  978.3 54.0 %slice-start.8 = ((s8[6291456]{0:T(1024)(128)(4,1)}), s8[4194304]{0:T(1024)(128)(4,1)S(1)}, s32[]{:S(2)}) async-start(s8[6291456]{0:T(1024)(128)(4,1)} %bitcast.439), calls=%async_computation.48 | async-start | bytes 8388608
  992.9 39.4 %copy-start.29 = (f32[1,1536]{1,0:T(1,128)S(1)}, f32[1,1536]{1,0:T(1,128)}, u32[]{:S(2)}) copy-start(f32[1,1536]{1,0:T(1,128)} %get-tuple-element.226) | copy-start | bytes 18436
  992.9 39.5 %slice-start.9 = ((s8[6291456]{0:T(1024)(128)(4,1)}), s8[2097152]{0:T(1024)(128)(4,1)S(1)}, s32[]{:S(2)}) async-start(s8[6291456]{0:T(1024)(128)(4,1)} %bitcast.439), calls=%async_computation.49 | async-start | bytes 4194304
  1037.9 123.1 %reduce-scatter.37.cloned.1.call-start = ((), (), s32[]{:S(2)}) async-start(), calls=%async_computation.36 | async-start | bytes 2457600 | tf_op jit(solution)/shard_map/reduce_scatter | solution.py:796
  1040.2 188.8 %reduce-scatter.25.cloned.1.call-start = ((), (), s32[]{:S(2)}) async-start(), calls=%async_computation.30 | async-start | bytes 3932160 | tf_op jit(solution)/shard_map/reduce_scatter | solution.py:796
  1040.7 95.5 %copy-start.35 = (bf16[8,256,512]{2,1,0:T(8,128)(2,1)S(1)}, bf16[8,256,512]{2,1,0:T(8,128)(2,1)}, u32[]{:S(2)}) copy-start(bf16[8,256,512]{2,1,0:T(8,128)(2,1)} %get-tuple-element.237) | copy-start | bytes 6291460
  1155.0 197.4 %reduce-scatter.27.cloned.1.call-start = ((), (), s32[]{:S(2)}) async-start(), calls=%async_computation.31 | async-start | bytes 1966080 | tf_op jit(solution)/shard_map/reduce_scatter | solution.py:796
  1229.0 123.4 %reduce-scatter.39.cloned.1.call-start = ((), (), s32[]{:S(2)}) async-start(), calls=%async_computation.37 | async-start | bytes 2457600 | tf_op jit(solution)/shard_map/reduce_scatter | solution.py:796
  1231.4 191.2 %reduce-scatter.29.cloned.1.call-start = ((), (), s32[]{:S(2)}) async-start(), calls=%async_computation.32 | async-start | bytes 3932160 | tf_op jit(solution)/shard_map/reduce_scatter | solution.py:796
  1231.6 96.2 %copy-start.34 = (bf16[8,256,512]{2,1,0:T(8,128)(2,1)S(1)}, bf16[8,256,512]{2,1,0:T(8,128)(2,1)}, u32[]{:S(2)}) copy-start(bf16[8,256,512]{2,1,0:T(8,128)(2,1)} %get-tuple-element.262) | copy-start | bytes 6291460
  1346.5 203.6 %reduce-scatter.31.cloned.1.call-start = ((), (), s32[]{:S(2)}) async-start(), calls=%async_computation.33 | async-start | bytes 1966080 | tf_op jit(solution)/shard_map/reduce_scatter | solution.py:796
  1422.6 127.5 %reduce-scatter.41.cloned.1.call-start = ((), (), s32[]{:S(2)}) async-start(), calls=%async_computation.38 | async-start | bytes 2457600 | tf_op jit(solution)/shard_map/reduce_scatter | solution.py:796
  1424.9 188.0 %reduce-scatter.35.cloned.1.call-start = ((), (), s32[]{:S(2)}) async-start(), calls=%async_computation.35 | async-start | bytes 1966080 | tf_op jit(solution)/shard_map/reduce_scatter | solution.py:796
  1425.4 95.9 %copy-start.33 = (bf16[8,256,512]{2,1,0:T(8,128)(2,1)S(1)}, bf16[8,256,512]{2,1,0:T(8,128)(2,1)}, u32[]{:S(2)}) copy-start(bf16[8,256,512]{2,1,0:T(8,128)(2,1)} %get-tuple-element.287) | copy-start | bytes 6291460
  1540.0 112.8 %reduce-scatter.33.cloned.1.call-start = ((), (), s32[]{:S(2)}) async-start(), calls=%async_computation.34 | async-start | bytes 3932160 | tf_op jit(solution)/shard_map/reduce_scatter | solution.py:796
  1657.2 58.3 %all-to-all-start.3 = ((bf16[8,192,1536]{2,1,0:T(8,128)(2,1)}), bf16[8,192,1536]{2,1,0:T(8,128)(2,1)}, u32[]{:S(2)}, u32[]{:S(2)}) async-start(bf16[8,192,1536]{2,1,0:T(8,128)(2,1)} %bitcast.322), calls=%async_computation.11 | async-start | bytes 9437184 | tf_op jit(solution)/shard_map/all_to_all | solution.py:920
  1662.3 44.9 %copy-start.23 = (bf16[384,578]{1,0:T(8,128)(2,1)S(1)}, bf16[384,578]{1,0:T(8,128)(2,1)}, u32[]{:S(2)}) copy-start(bf16[384,578]{1,0:T(8,128)(2,1)} %reduce-scatter.37.cloned.1.call-done) | copy-start | bytes 1331716
  1662.3 44.9 %copy-start.24 = (bf16[384,578]{1,0:T(8,128)(2,1)S(1)}, bf16[384,578]{1,0:T(8,128)(2,1)}, u32[]{:S(2)}) copy-start(bf16[384,578]{1,0:T(8,128)(2,1)} %reduce-scatter.39.cloned.1.call-done) | copy-start | bytes 1331716
  1662.3 44.9 %copy-start.25 = (bf16[384,578]{1,0:T(8,128)(2,1)S(1)}, bf16[384,578]{1,0:T(8,128)(2,1)}, u32[]{:S(2)}) copy-start(bf16[384,578]{1,0:T(8,128)(2,1)} %reduce-scatter.41.cloned.1.call-done) | copy-start | bytes 1331716
  1662.3 44.9 %reduce-scatter.43.cloned.1.call-start = ((), (), s32[]{:S(2)}) async-start(), calls=%async_computation.39 | async-start | bytes 2457600 | tf_op jit(solution)/shard_map/reduce_scatter | solution.py:796
  1710.0 14.4 copy-start.38
  1715.6 102.6 %all-to-all-start.2 = ((bf16[8,192,578]{2,1,0:T(8,128)(2,1)}), bf16[8,192,578]{2,1,0:T(8,128)(2,1)}, u32[]{:S(2)}, u32[]{:S(2)}) async-start(bf16[8,192,578]{2,1,0:T(8,128)(2,1)} %bitcast.148), calls=%async_computation.10 | async-start | bytes 3932160 | tf_op jit(solution)/shard_map/all_to_all | solution.py:920
  1720.5 57.6 %collective-permute-start.1 = (bf16[256,1536]{1,0:T(8,128)(2,1)S(1)}, bf16[256,1536]{1,0:T(8,128)(2,1)S(1)}, u32[]{:S(2)}, u32[]{:S(2)}) collective-permute-start(bf16[256,1536]{1,0:T(8,128)(2,1)S(1)} %copy-done.37), channel_id=1, source_target_pairs={{0,0},{2,8},{4,16},{6,24},{8,2},{10,10},{12,18},{14,26},{16,4},{18... | collective-permute-start | bytes 2359304 | tf_op jit(solution)/shard_map/ppermute | solution.py:765
  1724.5 69.7 %collective-permute-start.3 = (bf16[256,1536]{1,0:T(8,128)(2,1)S(1)}, bf16[256,1536]{1,0:T(8,128)(2,1)S(1)}, u32[]{:S(2)}, u32[]{:S(2)}) collective-permute-start(bf16[256,1536]{1,0:T(8,128)(2,1)S(1)} %copy-done.38), channel_id=1, source_target_pairs={{0,0},{2,8},{4,16},{6,24},{8,2},{10,10},{12,18},{14,26},{16,4},{18... | collective-permute-start | bytes 2359304 | tf_op jit(solution)/shard_map/ppermute | solution.py:765
  1778.1 16.1 copy-start.17
  (34 other events, 105.3 us)
Sparse Core Ops, SparseCore 0:
  53.4 44.7 all-gather.12
  110.0 52.1 all-gather.16
  163.8 75.0 all-gather.14
  240.4 42.1 all-gather.18
  284.0 62.3 all-gather.20
  347.8 35.7 all-gather.22
  398.0 48.1 all-gather.24
  448.4 62.3 all-gather.26
  512.3 35.7 all-gather.28
  562.5 57.1 all-gather.30
  621.9 80.5 all-gather.32
  703.9 35.7 all-gather.34
  972.5 64.9 reduce-scatter.20
  1039.7 46.4 reduce-scatter.22
  1088.9 40.3 reduce-scatter.36
  1155.1 73.8 reduce-scatter.24
  1231.2 48.8 reduce-scatter.26
  1282.8 40.4 reduce-scatter.38
  1346.6 75.9 reduce-scatter.28
  1424.7 48.3 reduce-scatter.30
  1476.0 40.4 reduce-scatter.40
  1540.1 50.4 reduce-scatter.34
  1593.5 59.2 reduce-scatter.32
  1665.7 41.4 reduce-scatter.42

commit v4 on v3

--- a/solution.py
+++ b/solution.py
@@ -60,12 +60,66 @@
     return (flip(x, dx) * 2 + flip(c, dc)) * 2 + flip(y, dy)
 
 
-def greet(here):
+class Swap:
+    def __init__(self, here, moving, moved, sem):
+        x, c, _ = here
+        z = lax.axis_index("z")
+        section = x * 2 + c
+        self.away = section != z
+        self.partner = {"x": z // 2, "c": lax.rem(z, 2), "z": section}
+        self.remote = pltpu.make_async_remote_copy(
+            src_ref=moving,
+            dst_ref=moved,
+            send_sem=sem.at[0],
+            recv_sem=sem.at[1],
+            device_id=self.partner,
+            device_id_type=MESH,
+        )
+        self.local = pltpu.make_async_copy(moving, moved, sem.at[2])
+
+    def greet(self, barrier):
+        @pl.when(self.away)
+        def _():
+            pl.semaphore_signal(barrier, inc=1, device_id=self.partner, device_id_type=MESH)
+
+    def either(self, remote, local):
+        pl.when(self.away)(remote)
+        pl.when(jnp.logical_not(self.away))(local)
+
+    def start(self):
+        self.either(lambda: self.remote.start(), lambda: self.local.start())
+
+    def met(self, barrier, count):
+        self.either(lambda: pl.semaphore_wait(barrier, count + 1), lambda: pl.semaphore_wait(barrier, count))
+
+    def wait(self):
+        self.either(lambda: self.remote.wait(), lambda: self.local.wait())
+
+
+def with_swap(kernel, inputs, outputs):
+    def wrapped(*refs):
+        last = inputs + 1 + outputs
+        kernel(
+            *refs[:inputs],
+            *refs[inputs + 1 : last],
+            *refs[last + 1 : -1],
+            swap=(refs[inputs], refs[last], refs[-1]),
+        )
+
+    return wrapped
+
+
+def greet(here, swap=None):
     x, c, y = here
     barrier = pltpu.get_barrier_semaphore()
     for peer in ({"x": 1 - x}, {"c": 1 - c}, {"y": 1 - y}):
         pl.semaphore_signal(barrier, inc=1, device_id=peer, device_id_type=MESH)
-    pl.semaphore_wait(barrier, 3)
+    if swap is None:
+        pl.semaphore_wait(barrier, 3)
+    else:
+        swap.greet(barrier)
+        swap.met(barrier, 3)
+        swap.start()
 
 
 class Sender:
@@ -269,11 +323,46 @@
     return lax.rsqrt(jnp.mean(x * x, axis=-1, keepdims=True) + EPS)
 
 
+def lane(x):
+    return lax.broadcasted_iota(jnp.int32, x.shape, 1)
+
+
 def turn(head, cosine, sine):
     return head * cosine + pltpu.roll(head, LANES // 2, 1) * sine
 
 
-def plane_call(kernel, name, number, out_shape, out_specs, in_specs, scratch, time_us, *operands):
+def open_halves(head):
+    return jnp.where(lane(head) < LANES // 2, head, pltpu.roll(head, LANES // 2 - HALF, 1))
+
+
+def close_halves(head):
+    low = lane(head) < LANES // 2
+    return jnp.where(low, head, 0.0) + pltpu.roll(jnp.where(low, 0.0, head), LANES // 2 + HALF, 1)
+
+
+def four_heads(a, b, c):
+    at = lane(a)
+    return (
+        a,
+        pltpu.roll(jnp.where(at >= 96, a, b), 32, 1),
+        pltpu.roll(jnp.where(at >= 64, b, c), 64, 1),
+        pltpu.roll(c, 96, 1),
+    )
+
+
+def three_lanes(heads):
+    at = lane(heads[0])
+    b, c, d = pltpu.roll(heads[1], 96, 1), pltpu.roll(heads[2], 64, 1), pltpu.roll(heads[3], 32, 1)
+    return jnp.where(at < 96, heads[0], b), jnp.where(at < 64, b, c), jnp.where(at < 32, c, d)
+
+
+def plane_call(kernel, name, number, out_shape, out_specs, in_specs, scratch, time_us, *operands, moving=None):
+    if moving is not None:
+        kernel = with_swap(kernel, len(in_specs), len(out_specs))
+        out_shape = out_shape + [jax.ShapeDtypeStruct(moving.shape, moving.dtype)]
+        in_specs, out_specs = in_specs + [ANYWHERE], out_specs + [ANYWHERE]
+        scratch = scratch + [pltpu.SemaphoreType.DMA((3,))]
+        operands = operands + (moving,)
     return pl.pallas_call(
         kernel,
         out_shape=out_shape,
@@ -290,28 +379,34 @@
 
 ANYWHERE = pl.BlockSpec(memory_space=pl.ANY)
 IN_VMEM = pl.BlockSpec(memory_space=pltpu.VMEM)
-
-
-def attn_in_kernel(heads, h, gain, w_hbm, cosine, sine, a1_out, q_out, k_out, v_out, full, w, send, recv, local):
+QKV = 4 * HEAD_SIZE
+OUT = 2 * HEAD_SIZE
+GAIN_AT = QKV + OUT
+PACK = -(-(GAIN_AT + 2) // LANES) * LANES
+
+
+def attn_in_kernel(h, w_hbm, cosine, sine, a1_out, q_out, k_out, v_out, gain_out, full, w, send, recv, local):
     here = place()
     loads = Loads(local)
     w_load = loads.start(w_hbm, w)
     x = h[...].astype(F32)
-    full[rank_of(here, 0, 0, 0)] = (x * inverse_of(x) * gain[...]).astype(BF)
+    n1 = x * inverse_of(x)
+    w_load.wait()
+    rows = w[:, PACK - LANES :].astype(F32).T
+    gain_out[...] = rows[GAIN_AT - PACK + LANES : GAIN_AT - PACK + LANES + 2]
+    full[rank_of(here, 0, 0, 0)] = (n1 * gain_out[0:1, :]).astype(BF)
     greet(here)
     saves = []
 
     def on_block(r):
-        if not saves:
-            w_load.wait()
         saves.append(loads.start(full.at[r], a1_out.at[r]))
-        qkv = dot_nn(full[r], w[...])
+        qkv = dot_nn(full[r], w[:, :QKV])
+        heads = four_heads(*(qkv[:, n * LANES : (n + 1) * LANES] for n in range(3)))
         cos, sin = cosine[r], sine[r]
-        part = lambda n: qkv[:, n * LANES : (n + 1) * LANES]
-        for n in range(heads):
-            q_out[n, r] = turn(part(n), cos, sin).astype(BF)
-        k_out[r] = turn(part(heads), cos, sin).astype(BF)
-        v_out[r] = part(heads + 1).astype(BF)
+        for n in range(2):
+            q_out[n, r] = turn(open_halves(heads[n]), cos, sin).astype(BF)
+        k_out[r] = turn(open_halves(heads[2]), cos, sin).astype(BF)
+        v_out[r] = jnp.where(lane(heads[3]) < HEAD_SIZE, heads[3], 0.0).astype(BF)
 
     net = run_gather(here, full, (send, recv), on_block)
     net.drain()
@@ -319,69 +414,71 @@
         save.wait()
 
 
-def attn_in(h, gain, w, cosine, sine, heads):
+def attn_in(h, w, cosine, sine):
     block, width = h.shape
-    cols = w.shape[1]
     return plane_call(
-        functools.partial(attn_in_kernel, heads),
+        attn_in_kernel,
         "attn_in",
         0,
         [
             jax.ShapeDtypeStruct((8, block, width), BF),
-            jax.ShapeDtypeStruct((heads, 8, block, LANES), BF),
+            jax.ShapeDtypeStruct((2, 8, block, LANES), BF),
             jax.ShapeDtypeStruct((8, block, LANES), BF),
             jax.ShapeDtypeStruct((8, block, LANES), BF),
+            jax.ShapeDtypeStruct((2, width), F32),
         ],
-        [ANYWHERE, IN_VMEM, IN_VMEM, IN_VMEM],
-        [IN_VMEM, IN_VMEM, ANYWHERE, IN_VMEM, IN_VMEM],
-        [pltpu.VMEM((8, block, width), BF), pltpu.VMEM((width, cols), BF)]
+        [ANYWHERE, IN_VMEM, IN_VMEM, IN_VMEM, IN_VMEM],
+        [IN_VMEM, ANYWHERE, IN_VMEM, IN_VMEM],
+        [pltpu.VMEM((8, block, width), BF), pltpu.VMEM(w.shape, BF)]
         + gather_sems()
         + [pltpu.SemaphoreType.DMA((9,))],
         34,
-        h, gain, w, cosine, sine,
+        h, w, cosine, sine,
     )
 
 
 def mlp_kernel(
-    ff, h, o, gain, wo_hbm, wgu_hbm, wd_hbm, mid_out, a2_out, gu_out, hid_out, next_out,
-    full, parts, gu, hid, wo, wgu, wd, total,
+    ff, h, o, gain, wa_hbm, w1_hbm, w2_hbm, mid_out, a2_out, gu_out, hid_out, next_out,
+    full, parts, gu, hid, wa, wm, total,
     from_c, via_x, via_y, from_x, from_y, send1, recv1, send2, recv2,
-    from_c3, via_x3, via_y3, from_x3, from_y3, send3, recv3, local,
+    from_c3, via_x3, via_y3, from_x3, from_y3, send3, recv3, local, swap=None,
 ):
     here = place()
+    swap = swap and Swap(here, *swap)
     loads = Loads(local)
-    wo_load = loads.start(wo_hbm, wo)
-    wgu_load = loads.start(wgu_hbm, wgu)
-    wd_load = loads.start(wd_hbm, wd)
-    greet(here)
-    wo_load.wait()
+    wa_load = loads.start(wa_hbm, wa)
+    split = w1_hbm.shape[1]
+    w1_load = loads.start(w1_hbm, wm.at[:, pl.ds(0, split)])
+    w2_load = loads.start(w2_hbm, wm.at[:, pl.ds(split, 3 * ff - split)])
+    greet(here, swap)
+    wa_load.wait()
 
     def fill(r):
-        parts[r] = dot_nt(o[r], wo[...]).astype(BF)
+        parts[r] = dot_nt(o[r], wa[:, QKV:GAIN_AT]).astype(BF)
 
     bufs = (from_c, via_x, via_y, from_x, from_y)
     net1 = run_scatter(here, parts, total, bufs, (send1, recv1), fill)
     mid = h[...].astype(F32) + total[...]
     mid_out[...] = mid
-    full[rank_of(here, 0, 0, 0)] = (mid * inverse_of(mid) * gain[...]).astype(BF)
+    full[rank_of(here, 0, 0, 0)] = (mid * inverse_of(mid) * gain[1:2, :]).astype(BF)
     net1.drain()
     saves = []
 
     def on_block(r):
         if not saves:
-            wgu_load.wait()
-            wd_load.wait()
+            w1_load.wait()
+            w2_load.wait()
         saves.append(loads.start(full.at[r], a2_out.at[r]))
         a2 = full[r]
-        g = dot_nn(a2, wgu[:, :ff])
-        u = dot_nn(a2, wgu[:, ff:])
+        g = dot_nn(a2, wm[:, :ff])
+        u = dot_nn(a2, wm[:, ff : 2 * ff])
         gu[r, :, :ff] = g.astype(BF)
         gu[r, :, ff:] = u.astype(BF)
         low = (g * (1.0 / (1.0 + jnp.exp(-g))) * u).astype(BF)
         hid[r] = low
         saves.append(loads.start(gu.at[r], gu_out.at[r]))
         saves.append(loads.start(hid.at[r], hid_out.at[r]))
-        parts[r] = dot_nt(low, wd[...]).astype(BF)
+        parts[r] = dot_nt(low, wm[:, 2 * ff :]).astype(BF)
 
     net2 = run_gather(here, full, (send2, recv2), on_block)
     bufs3 = (from_c3, via_x3, via_y3, from_x3, from_y3)
@@ -391,15 +488,17 @@
     net3.drain()
     for save in saves:
         save.wait()
-
-
-def mlp(h, o, gain, wo, wgu, wd):
+    if swap is not None:
+        swap.wait()
+
+
+def mlp(h, o, gain, wa, w1, w2, moving=None):
     block, width = h.shape
-    ff = wd.shape[1]
+    ff = (w1.shape[1] + w2.shape[1]) // 3
     return plane_call(
         functools.partial(mlp_kernel, ff),
         "mlp",
-        1,
+        1 if moving is None else 8,
         [
             jax.ShapeDtypeStruct((block, width), F32),
             jax.ShapeDtypeStruct((8, block, width), BF),
@@ -414,9 +513,8 @@
             pltpu.VMEM((8, block, width), BF),
             pltpu.VMEM((8, block, 2 * ff), BF),
             pltpu.VMEM((8, block, ff), BF),
-            pltpu.VMEM(wo.shape, BF),
-            pltpu.VMEM(wgu.shape, BF),
-            pltpu.VMEM(wd.shape, BF),
+            pltpu.VMEM(wa.shape, BF),
+            pltpu.VMEM((width, 3 * ff), BF),
             pltpu.VMEM((block, width), F32),
         ]
         + scatter_scratch(block, width)
@@ -424,7 +522,8 @@
         + scatter_scratch(block, width)
         + [pltpu.SemaphoreType.DMA((27,))],
         96,
-        h, o, gain, wo, wgu, wd,
+        h, o, gain, wa, w1, w2,
+        moving=moving,
     )
 
 
@@ -433,29 +532,37 @@
     return inverse * (scaled - normed * jnp.mean(scaled * normed, axis=-1, keepdims=True))
 
 
+def flat_tn(a, cols, b):
+    total = dot_tn(a[0, :, cols], b[0])
+    for n in range(1, a.shape[0]):
+        total = total + dot_tn(a[n, :, cols], b[n])
+    return total
+
+
 def mlp_back_kernel(
-    ff, e, mid, gain, gu_hbm, wd_hbm, wgu_hbm, wo_hbm, e_out, dgu_out, dmid_out, gain_out, dat_out, dob_out,
-    full, full2, parts, gu, wd, wgu, wo, total, send1, recv1,
-    from_c, via_x, via_y, from_x, from_y, send2, recv2, send3, recv3, local,
+    ff, step, e, mid, gain, gu_hbm, hid_hbm, a2_hbm, w1_hbm, w2_hbm, wa_hbm, dmid_out, gain_out, dat_out, dob_out,
+    gu_sums, d_sums, full, full2, parts, a2, gu, hid, wm, wa, total, stage, send1, recv1,
+    from_c, via_x, via_y, from_x, from_y, send2, recv2, send3, recv3, local, swap=None,
 ):
     here = place()
+    swap = swap and Swap(here, *swap)
     loads = Loads(local)
-    wd_load = loads.start(wd_hbm, wd)
+    split = w1_hbm.shape[1]
+    w2_load = loads.start(w2_hbm, wm.at[:, pl.ds(split, 3 * ff - split)])
     gu_load = loads.start(gu_hbm, gu)
-    wgu_load = loads.start(wgu_hbm, wgu)
-    wo_load = loads.start(wo_hbm, wo)
+    w1_load = loads.start(w1_hbm, wm.at[:, pl.ds(0, split)])
+    wa_load = loads.start(wa_hbm, wa)
+    a2_load = loads.start(a2_hbm, a2)
+    hid_load = loads.start(hid_hbm, hid)
     own = rank_of(here, 0, 0, 0)
     full[own] = e[...]
-    greet(here)
-    saves = []
+    greet(here, swap)
+    w2_load.wait()
+    gu_load.wait()
+    w1_load.wait()
 
     def on_block(r):
-        first = not saves
-        if first:
-            wd_load.wait()
-            gu_load.wait()
-        saves.append(loads.start(full.at[r], e_out.at[r]))
-        dhid = dot_nn(full[r], wd[...])
+        dhid = dot_nn(full[r], wm[:, 2 * ff :])
         g = gu[r, :, :ff].astype(F32)
         u = gu[r, :, ff:].astype(F32)
         sig = 1.0 / (1.0 + jnp.exp(-g))
@@ -463,117 +570,262 @@
         dg = dhid * u * sig * (1.0 + g * (1.0 - sig))
         gu[r, :, :ff] = dg.astype(BF)
         gu[r, :, ff:] = du.astype(BF)
-        saves.append(loads.start(gu.at[r], dgu_out.at[r]))
-        if first:
-            wgu_load.wait()
-        parts[r] = dot_nt(gu[r], wgu[...]).astype(BF)
+        parts[r] = dot_nt(gu[r], wm[:, : 2 * ff]).astype(BF)
 
     net1 = run_gather(here, full, (send1, recv1), on_block)
-    net2 = run_scatter(here, parts, total, (from_c, via_x, via_y, from_x, from_y), (send2, recv2))
+    a2_load.wait()
+    hid_load.wait()
+    sums = []
+    count = full.shape[2] // step
+
+    def beside(turn_number):
+        half = (count + 1) // 2
+        for number in range(turn_number * half, min((turn_number + 1) * half, count)):
+            if number >= 2:
+                for save in sums[number - 2]:
+                    save.wait()
+            at = slice(number * step, (number + 1) * step)
+            held = stage.at[number % 2]
+            held[:, : 2 * ff] = flat_tn(a2, at, gu).astype(BF)
+            held[:, 2 * ff :] = flat_tn(full, at, hid).astype(BF)
+            rows = pl.ds(number * step, step)
+            sums.append(
+                [
+                    loads.start(held.at[:, pl.ds(0, 2 * ff)], gu_sums.at[rows]),
+                    loads.start(held.at[:, pl.ds(2 * ff, ff)], d_sums.at[rows]),
+                ]
+            )
+
+    net2 = run_scatter(
+        here, parts, total, (from_c, via_x, via_y, from_x, from_y), (send2, recv2), beside=beside
+    )
     da2 = total[...]
     m = mid[...]
     r2 = inverse_of(m)
     n2 = m * r2
     gain_out[...] = jnp.sum(da2 * n2, axis=0, keepdims=True)
-    dmid = e[...].astype(F32) + norm_back(da2, n2, r2, gain[...])
+    dmid = e[...].astype(F32) + norm_back(da2, n2, r2, gain[1:2, :])
     dmid_out[...] = dmid
     full2[own] = dmid.astype(BF)
-    wo_load.wait()
+    wa_load.wait()
+    saves = []
 
     def on_second(r):
         saves.append(loads.start(full2.at[r], dat_out.at[r]))
-        dob_out[r] = dot_nn(full2[r], wo[...]).astype(BF)
+        dob_out[r] = dot_nn(full2[r], wa[:, QKV:PACK]).astype(BF)
 
     net3 = run_gather(here, full2, (send3, recv3), on_second)
     for net in (net1, net2, net3):
         net.drain()
-    for save in saves:
+    for save in saves + sums[-2] + sums[-1]:
         save.wait()
-
-
-def mlp_back(e, mid, gain, gu, wd, wgu, wo):
+    if swap is not None:
+        swap.wait()
+
+
+def mlp_back(e, mid, gain, gu, hid, a2, w1, w2, wa, moving=None):
     block, width = e.shape
-    ff = wd.shape[1]
-    cols = wo.shape[1]
+    ff = hid.shape[2]
+    cols = PACK - QKV
+    step = math.gcd(width, 256)
     return plane_call(
-        functools.partial(mlp_back_kernel, ff),
+        functools.partial(mlp_back_kernel, ff, step),
         "mlp_back",
-        2,
+        2 if moving is None else 9,
         [
-            jax.ShapeDtypeStruct((8, block, width), BF),
-            jax.ShapeDtypeStruct((8, block, 2 * ff), BF),
             jax.ShapeDtypeStruct((block, width), F32),
             jax.ShapeDtypeStruct((1, width), F32),
             jax.ShapeDtypeStruct((8, block, width), BF),
             jax.ShapeDtypeStruct((8, block, cols), BF),
+            jax.ShapeDtypeStruct((width, 2 * ff), BF),
+            jax.ShapeDtypeStruct((width, ff), BF),
         ],
-        [ANYWHERE, ANYWHERE, IN_VMEM, IN_VMEM, ANYWHERE, IN_VMEM],
-        [IN_VMEM, IN_VMEM, IN_VMEM, ANYWHERE, ANYWHERE, ANYWHERE, ANYWHERE],
+        [IN_VMEM, IN_VMEM, ANYWHERE, IN_VMEM, ANYWHERE, ANYWHERE],
+        [IN_VMEM, IN_VMEM, IN_VMEM] + [ANYWHERE] * 6,
         [
             pltpu.VMEM((8, block, width), BF),
             pltpu.VMEM((8, block, width), BF),
             pltpu.VMEM((8, block, width), BF),
+            pltpu.VMEM((8, block, width), BF),
             pltpu.VMEM((8, block, 2 * ff), BF),
-            pltpu.VMEM(wd.shape, BF),
-            pltpu.VMEM(wgu.shape, BF),
-            pltpu.VMEM(wo.shape, BF),
+            pltpu.VMEM((8, block, ff), BF),
+            pltpu.VMEM((width, 3 * ff), BF),
+            pltpu.VMEM(wa.shape, BF),
             pltpu.VMEM((block, width), F32),
+            pltpu.VMEM((2, step, 3 * ff), BF),
         ]
         + gather_sems()
         + scatter_scratch(block, width)
         + gather_sems()
-        + [pltpu.SemaphoreType.DMA((28,))],
+        + [pltpu.SemaphoreType.DMA((14 + 2 * (width // step),))],
         100,
-        e, mid, gain, gu, wd, wgu, wo,
+        e, mid, gain, gu, hid, a2, w1, w2, wa,
+        moving=moving,
     )
 
 
 def attn_back_kernel(
-    h, dmid, gain, dq, dk, dv, cosine, sine, w_hbm, dqkv_out, e_out, gain_out,
-    parts, w, total, from_c, via_x, via_y, from_x, from_y, send, recv, local,
+    step, h, dmid, gain, gain2_grad, dq, dk, dv, cosine, sine, o, a1_hbm, dat_hbm, w_hbm, e_out, sums,
+    parts, a1, dat, w, dqkv, gain_rows, total, from_c, via_x, via_y, from_x, from_y, send, recv, local,
 ):
     here = place()
-    w_load = Loads(local).start(w_hbm, w)
+    loads = Loads(local)
+    w_load = loads.start(w_hbm, w)
+    a1_load = loads.start(a1_hbm, a1)
+    dat_load = loads.start(dat_hbm, dat)
     greet(here)
     w_load.wait()
-    q_cols = dq.shape[2]
 
     def fill(r):
-        dqkv_out[r, :, :q_cols] = dq[r]
-        dqkv_out[r, :, q_cols : q_cols + LANES] = turn(dk[r], cosine[r], -sine[r]).astype(BF)
-        dqkv_out[r, :, q_cols + LANES :] = dv[r].astype(BF)
-        parts[r] = dot_nt(dqkv_out[r], w[...]).astype(BF)
-
-    net = run_scatter(here, parts, total, (from_c, via_x, via_y, from_x, from_y), (send, recv), fill)
+        heads = [dq[r, :, n * LANES : (n + 1) * LANES].astype(F32) for n in range(2)]
+        heads.append(turn(dk[r], cosine[r], -sine[r]))
+        lanes = three_lanes([close_halves(head) for head in heads] + [dv[r]])
+        for n in range(3):
+            dqkv[r, :, n * LANES : (n + 1) * LANES] = lanes[n].astype(BF)
+        parts[r] = dot_nt(dqkv[r], w[:, :QKV]).astype(BF)
+
+    count = a1.shape[2] // step
+
+    def beside(turn_number):
+        if turn_number == 0:
+            a1_load.wait()
+            dat_load.wait()
+        half = (count + 1) // 2
+        for number in range(turn_number * half, min((turn_number + 1) * half, count)):
+            at = slice(number * step, (number + 1) * step)
+            sums[at, :QKV] = flat_tn(a1, at, dqkv).astype(BF)
+            sums[at, QKV:GAIN_AT] = flat_tn(dat, at, o).astype(BF)
+
+    net = run_scatter(
+        here, parts, total, (from_c, via_x, via_y, from_x, from_y), (send, recv), fill, beside
+    )
     da1 = total[...]
     x = h[...].astype(F32)
     r1 = inverse_of(x)
     n1 = x * r1
-    gain_out[...] = jnp.sum(da1 * n1, axis=0, keepdims=True)
-    e_out[...] = (dmid[...] + norm_back(da1, n1, r1, gain[...])).astype(BF)
+    e_out[...] = (dmid[...] + norm_back(da1, n1, r1, gain[0:1, :])).astype(BF)
+    gain_rows[...] = jnp.zeros_like(gain_rows)
+    first = GAIN_AT - PACK + LANES
+    gain_rows[first : first + 1, :] = jnp.sum(da1 * n1, axis=0, keepdims=True)
+    gain_rows[first + 1 : first + 2, :] = gain2_grad[...]
+    columns = gain_rows[...].T
+    last = sums[:, PACK - LANES :].astype(F32)
+    sums[:, PACK - LANES :] = jnp.where(lane(last) < first, last, columns).astype(BF)
     net.drain()
 
 
-def attn_back(h, dmid, gain, dq, dk, dv, cosine, sine, w):
+def attn_back(h, dmid, gain, gain2_grad, dq, dk, dv, cosine, sine, o, a1, dat, w):
     block, width = h.shape
-    cols = w.shape[1]
+    step = math.gcd(width, 256)
     return plane_call(
-        attn_back_kernel,
+        functools.partial(attn_back_kernel, step),
         "attn_back",
         3,
         [
-            jax.ShapeDtypeStruct((8, block, cols), BF),
             jax.ShapeDtypeStruct((block, width), BF),
-            jax.ShapeDtypeStruct((1, width), F32),
+            jax.ShapeDtypeStruct((width, PACK), BF),
         ],
-        [IN_VMEM, IN_VMEM, IN_VMEM],
-        [IN_VMEM] * 8 + [ANYWHERE],
-        [pltpu.VMEM((8, block, width), BF), pltpu.VMEM(w.shape, BF), pltpu.VMEM((block, width), F32)]
+        [IN_VMEM, IN_VMEM],
+        [IN_VMEM] * 10 + [ANYWHERE] * 3,
+        [
+            pltpu.VMEM((8, block, width), BF),
+            pltpu.VMEM((8, block, width), BF),
+            pltpu.VMEM((8, block, width), BF),
+            pltpu.VMEM(w.shape, BF),
+            pltpu.VMEM((8, block, QKV), BF),
+            pltpu.VMEM((LANES, width), F32),
+            pltpu.VMEM((block, width), F32),
+        ]
         + scatter_scratch(block, width)
-        + [pltpu.SemaphoreType.DMA((1,))],
+        + [pltpu.SemaphoreType.DMA((3,))],
         36,
-        h, dmid, gain, dq, dk, dv, cosine, sine, w,
+        h, dmid, gain, gain2_grad, dq, dk, dv, cosine, sine, o, a1, dat, w,
     )
+
+
+def exchange_kernel(blocks, got, send_sem, recv_sem, local, swap=None):
+    here = place()
+    x, c, y = here
+    swap = swap and Swap(here, *swap)
+    masks = [(dx, dc, dy) for dx in range(2) for dc in range(2) for dy in range(2)][1:]
+    peer = lambda mask: {"x": flip(x, mask[0]), "c": flip(c, mask[1]), "y": flip(y, mask[2])}
+    own = rank_of(here, 0, 0, 0)
+    mine = pltpu.make_async_copy(blocks.at[own], got.at[own], local)
+    mine.start()
+    barrier = pltpu.get_barrier_semaphore()
+    for mask in masks:
+        pl.semaphore_signal(barrier, inc=1, device_id=peer(mask), device_id_type=MESH)
+    if swap is None:
+        pl.semaphore_wait(barrier, 7)
+    else:
+        swap.greet(barrier)
+        swap.met(barrier, 7)
+        swap.start()
+
+    def copy(n, src, dst):
+        return pltpu.make_async_remote_copy(
+            src_ref=src,
+            dst_ref=dst,
+            send_sem=send_sem.at[n],
+            recv_sem=recv_sem.at[n],
+            device_id=peer(masks[n]),
+            device_id_type=MESH,
+        )
+
+    copies = [copy(n, blocks.at[rank_of(here, *mask)], got.at[own]) for n, mask in enumerate(masks)]
+    for started in copies:
+        started.start()
+    mine.wait()
+    for n, mask in enumerate(masks):
+        where = got.at[rank_of(here, *mask)]
+        copy(n, where, where).wait_recv()
+    for started in copies:
+        started.wait_send()
+    if swap is not None:
+        swap.wait()
+
+
+def exchange(number, blocks, moving=None):
+    return plane_call(
+        exchange_kernel,
+        "exchange",
+        number,
+        [jax.ShapeDtypeStruct(blocks.shape, BF)],
+        [ANYWHERE],
+        [ANYWHERE],
+        [pltpu.SemaphoreType.DMA((7,)), pltpu.SemaphoreType.DMA((7,)), pltpu.SemaphoreType.DMA],
+        blocks.size // 40000,
+        blocks,
+        moving=moving,
+    )
+
+
+def finish_kernel(ff, got, gate, up, down):
+    gate[...] = got[0, :, :ff].astype(F32)
+    up[...] = got[0, :, ff : 2 * ff].astype(F32)
+    down[...] = got[0, :, 2 * ff :].astype(F32).T
+
+
+def finish(got):
+    ranks, rows, cols = got.shape
+    ff = cols // 3
+    return pl.pallas_call(
+        functools.partial(finish_kernel, ff),
+        grid=(ranks,),
+        out_shape=[
+            jax.ShapeDtypeStruct((rows, ranks * ff), F32),
+            jax.ShapeDtypeStruct((rows, ranks * ff), F32),
+            jax.ShapeDtypeStruct((ranks * ff, rows), F32),
+        ],
+        in_specs=[pl.BlockSpec((1, rows, cols), lambda i: (i, 0, 0))],
+        out_specs=[
+            pl.BlockSpec((rows, ff), lambda i: (0, i)),
+            pl.BlockSpec((rows, ff), lambda i: (0, i)),
+            pl.BlockSpec((ff, rows), lambda i: (i, 0)),
+        ],
+        compiler_params=pltpu.CompilerParams(vmem_limit_bytes=VMEM_LIMIT),
+        name="finish",
+    )(got)
 
 
 LOWER=-1e30
@@ -605,9 +857,10 @@
     full, end = bounds[0, i], bounds[1, i]
     state = lax.fori_loop(0, full, functools.partial(step, False), state)
     top, total, acc = lax.fori_loop(full, end, functools.partial(step, True), state)
-    o = (acc / total).T.astype(BF)
-    for g in range(groups):
-        out[:, g * LANES:(g + 1) * LANES] = o[g * bq:(g + 1) * bq]
+    o = (acc / total).T
+    first, second = o[:bq], pltpu.roll(o[bq:], HEAD_SIZE, 1)
+    out[:, :LANES] = jnp.where(lane(first) < HEAD_SIZE, first, second).astype(BF)
+    out[:, LANES:] = second[:, : OUT - LANES].astype(BF)
     lse[...] = (top + jnp.log2(total))[None]
 
 def attend(q, k, v, qpos, bounds, length, bq, bk, scale2):
@@ -624,10 +877,10 @@
                 pl.BlockSpec((1, 1, bq), lambda i, *_: (i, 0, 0)),
             ],
             out_specs=[
-                pl.BlockSpec((bq, groups * LANES), lambda i, *_: (i, 0)),
+                pl.BlockSpec((bq, OUT), lambda i, *_: (i, 0)),
                 pl.BlockSpec((1, 1, groups * bq), lambda i, *_: (i, 0, 0)),
             ]),
-        out_shape=[jax.ShapeDtypeStruct((tokens, groups * LANES), BF), jax.ShapeDtypeStruct((n, 1, groups * bq), F32)],
+        out_shape=[jax.ShapeDtypeStruct((tokens, OUT), BF), jax.ShapeDtypeStruct((n, 1, groups * bq), F32)],
         compiler_params=pltpu.CompilerParams(vmem_limit_bytes=VMEM_LIMIT),
         name="attend",
         cost_estimate=pl.CostEstimate(flops=0, bytes_accessed=45000000, transcendentals=0),
@@ -642,9 +895,15 @@
         dk[...] = jnp.zeros_like(dk)
         dv[...] = jnp.zeros_like(dv)
     qs = q[...].reshape(groups * bq, LANES)
-    dos = jnp.concatenate([do[:, g * LANES:(g + 1) * LANES] for g in range(groups)], axis=0)
-    os_ = jnp.concatenate([o[:, g * LANES:(g + 1) * LANES] for g in range(groups)], axis=0)
-    delta = jnp.sum(dos.astype(F32) * os_.astype(F32), axis=1, keepdims=True).reshape(1, groups * bq)
+    do0, do1 = do[:, :LANES].astype(F32), do[:, LANES : 2 * LANES].astype(F32)
+    at = lane(do0)
+    do1 = pltpu.roll(jnp.where(at >= HEAD_SIZE, do0, do1), LANES - HEAD_SIZE, 1)
+    wide = jnp.concatenate([jnp.where(at < HEAD_SIZE, do0, 0.0), jnp.where(at < HEAD_SIZE, do1, 0.0)], axis=0)
+    dos = wide.astype(BF)
+    o0 = o[:, :LANES].astype(F32)
+    o1 = jnp.concatenate([o[:, LANES:].astype(F32), jnp.zeros((bq, 2 * LANES - OUT), F32)], axis=1)
+    o1 = pltpu.roll(jnp.where(at >= HEAD_SIZE, o0, o1), LANES - HEAD_SIZE, 1)
+    delta = jnp.sum(wide * jnp.concatenate([o0, o1], axis=0), axis=1, keepdims=True).reshape(1, groups * bq)
     lse_row = lse[0]
     pos = qpos[0]
     pos2 = jnp.concatenate([pos] * groups, axis=1)
@@ -673,6 +932,7 @@
     groups, tokens, _ = q.shape
     n = tokens // bq
     wide = pl.BlockSpec((bq, groups * LANES), lambda i, *_: (i, 0))
+    narrow = pl.BlockSpec((bq, OUT), lambda i, *_: (i, 0))
     return pl.pallas_call(
         functools.partial(back_kernel, scale, scale2, bq, bk),
         grid_spec=pltpu.PrefetchScalarGridSpec(
@@ -682,7 +942,7 @@
                 pl.BlockSpec(k.shape, lambda i, *_: (0, 0)),
                 pl.BlockSpec(v.shape, lambda i, *_: (0, 0)),
                 pl.BlockSpec((1, 1, bq), lambda i, *_: (i, 0, 0)),
-                wide, wide,
+                narrow, wide,
                 pl.BlockSpec((1, 1, groups * bq), lambda i, *_: (i, 0, 0)),
                 pl.BlockSpec((bq, LANES), lambda i, *_: (i, 0)),
                 pl.BlockSpec((bq, LANES), lambda i, *_: (i, 0)),
@@ -702,24 +962,6 @@
 
 
 PLANE = ("x", "c", "y")
-
-def spread(matrix, heads):
-    split = matrix.reshape(matrix.shape[0], heads, 2, HALF)
-    return jnp.pad(split, ((0, 0), (0, 0), (0, 0), (0, LANES // 2 - HALF))).reshape(-1, heads * LANES)
-
-
-def unspread(matrix, heads):
-    return matrix.reshape(-1, heads, 2, LANES // 2)[..., :HALF].reshape(-1, heads * HEAD_SIZE)
-
-
-def widen(matrix, heads):
-    split = matrix.reshape(matrix.shape[0], heads, HEAD_SIZE)
-    return jnp.pad(split, ((0, 0), (0, 0), (0, LANES - HEAD_SIZE))).reshape(-1, heads * LANES)
-
-
-def narrow(matrix, heads):
-    return matrix.reshape(-1, heads, LANES)[..., :HEAD_SIZE].reshape(-1, heads * HEAD_SIZE)
-
 
 def together(*arrays):
     return lax.optimization_barrier(arrays)
@@ -757,13 +999,6 @@
     scale = 1.0 / math.sqrt(HEAD_SIZE)
     scale2 = scale * math.log2(math.e)
 
-    def swap(array):
-        names = ("x", "c", "z")
-        pairs = [
-            (s * planes + z, z * planes + s) for s in range(sections) for z in range(planes)
-        ]
-        return lax.ppermute(array, names, pairs)
-
     def by_rank(matrix):
         return matrix.reshape(rows, ranks, -1)
 
@@ -774,6 +1009,7 @@
             by_rank(value_projection[0]),
             by_rank(w_out[0].T),
             jnp.broadcast_to(jnp.stack([attn_gain[0], mlp_gain[0]], axis=1)[:, None, :], (rows, ranks, 2)),
+            jnp.zeros((rows, ranks, PACK - GAIN_AT - 2), F32),
         ],
         axis=2,
     )
@@ -781,26 +1017,32 @@
         [by_rank(w_gate[0]), by_rank(w_up[0]), by_rank(w_down[0].T)], axis=2
     )
 
-    def exchange(pack):
-        moved = lax.all_to_all(
-            jnp.swapaxes(pack.astype(BF), 0, 1), PLANE, split_axis=0, concat_axis=0, tiled=True
-        )
-        return moved.reshape(layers, halves, rows, pack.shape[2])
+    def by_layer(got):
+        return got.reshape(layers, halves, rows, -1)
+
+    def ready(pack):
+        return jnp.swapaxes(pack.astype(BF), 0, 1)
 
     def whole(part):
         if extra > 1:
             part = lax.all_gather(part, "e", axis=1, tiled=False)
         return lax.all_gather(part.reshape(-1, part.shape[-1]), "z", axis=0, tiled=True)
 
-    def reduce_rows(grad):
-        mine = lax.psum_scatter(grad.astype(BF), "z", scatter_dimension=0, tiled=True)
+    def reduce_rows(sums):
+        mine = lax.psum_scatter(sums, "z", scatter_dimension=0, tiled=True)
         mine = mine.reshape(halves, extra, rows, -1)
         if extra > 1:
             return lax.psum_scatter(mine, "e", scatter_dimension=1, tiled=False)
         return mine[:, 0]
 
-    attn_parts = exchange(attn_pack)
-    mlp_parts = exchange(mlp_pack)
+    cut = 3 * ff_cols * 7 // 12 // LANES * LANES
+    mlp_blocks = ready(mlp_pack)
+    (attn_got,) = exchange(4, ready(attn_pack))
+    first_blocks, attn_got = together(mlp_blocks[..., :cut], attn_got)
+    (first_got,) = exchange(5, first_blocks)
+    second_blocks, first_got = together(mlp_blocks[..., cut:], first_got)
+    second_got, hidden_state = exchange(6, second_blocks, inputs[0])
+    attn_parts, first_parts, second_parts = by_layer(attn_got), by_layer(first_got), by_layer(second_got)
 
     rank = (lax.axis_index("x") * lax.axis_size("c") + lax.axis_index("c")) * halves + lax.axis_index("y")
     spot = lax.axis_index("e")
@@ -837,54 +1079,43 @@
     def flat(array):
         return array.reshape(tokens, array.shape[-1])
 
-    hidden_state = swap(inputs[0])
-    qk_cols = q_cols + kv_cols
-    qkv_cols = qk_cols + kv_cols
     saved = []
-    gu_parts = [part[..., : 2 * ff_cols] for part in mlp_parts]
-    d_parts = [part[..., 2 * ff_cols :] for part in mlp_parts]
-    attn_w, gu_part, d_part = together(whole(attn_parts[0]), gu_parts[0], d_parts[0])
-    w_gu, w_d = whole(gu_part), whole(d_part)
+    attn_w, w_1 = whole(attn_parts[0]), whole(first_parts[0])
+    w_2 = whole(second_parts[0])
     for layer in range(layers):
-        w_qkv = jnp.concatenate(
-            [spread(attn_w[:, :qk_cols], head_group + 1), widen(attn_w[:, qk_cols:qkv_cols], 1)], axis=1
-        )
-        w_o = widen(attn_w[:, qkv_cols : qkv_cols + q_cols], head_group)
-        gains = attn_w[:, qkv_cols + q_cols :].astype(F32).T
-        gain1, gain2 = gains[0:1], gains[1:2]
-        a1, q, k, v = attn_in(hidden_state, gain1, w_qkv, cosine3, sine3, head_group)
+        a1, q, k, v, gain = attn_in(hidden_state, attn_w, cosine3, sine3)
         q, k, v = q.reshape(head_group, tokens, LANES), all_keys(flat(k)), all_keys(flat(v))
         o, log_total = attend(q, k, v, query_rows, bounds, length1, bq, bk, scale2)
         if layer + 1 < layers:
-            o, attn_part, gu_part = together(o, attn_parts[layer + 1], gu_parts[layer + 1])
-            attn_w, next_gu = whole(attn_part), whole(gu_part)
-        mid, a2, gu, hid, after_mlp = mlp(
-            hidden_state, o.reshape(ranks, block, -1), gain2, w_o, w_gu, w_d
+            o, attn_part, first_part = together(o, attn_parts[layer + 1], first_parts[layer + 1])
+            next_attn, next_1 = whole(attn_part), whole(first_part)
+        mid, a2, gu, hid, after_mlp, *moved = mlp(
+            hidden_state, o.reshape(ranks, block, -1), gain, attn_w, w_1, w_2,
+            cotangent[0] if layer + 1 == layers else None,
         )
-        saved.append(
-            (hidden_state, a1, q, k, v, o, log_total, mid, a2, gu, hid, w_qkv, w_o, w_gu, w_d, gain1, gain2)
-        )
+        saved.append((hidden_state, a1, q, k, v, o, log_total, mid, a2, gu, hid, attn_w, w_1, w_2, gain))
         hidden_state = after_mlp
         if layer + 1 < layers:
-            hidden_state, attn_w, w_gu, d_part = together(hidden_state, attn_w, next_gu, d_parts[layer + 1])
-            w_d = whole(d_part)
-    output = swap(hidden_state)[None]
+            hidden_state, attn_w, w_1, second_part = together(hidden_state, next_attn, next_1, second_parts[layer + 1])
+            w_2 = whole(second_part)
+    output = hidden_state
 
     my_positions = (rank * extra + spot) * block + jnp.arange(block)
-    e = swap(cotangent[0])
+    (e,) = moved
     e = jnp.where((my_positions < length)[:, None], e, jnp.zeros_like(e))
     attn_grads = [None] * layers
     gu_grads = [None] * layers
     d_grads = [None] * layers
     for layer in reversed(range(layers)):
-        (h, a1, q, k, v, o, log_total, mid, a2, gu, hid, w_qkv, w_o, w_gu, w_d, gain1, gain2) = saved[layer]
-        e_all, dgu, dmid, gain2_grad, dat, dob = mlp_back(e, mid, gain2, gu, w_d, w_gu, w_o)
-        gu_sums = dot_tn(flat(a2), flat(dgu)).astype(BF)
-        d_sums = dot_tn(flat(e_all), flat(hid)).astype(BF)
-        dob, gu_sums, d_sums = together(dob, gu_sums, d_sums)
+        (h, a1, q, k, v, o, log_total, mid, a2, gu, hid, attn_w, w_1, w_2, gain) = saved[layer]
+        dmid, gain2, dat, dob, gu_sums, d_sums, *moved = mlp_back(
+            e, mid, gain, gu, hid, a2, w_1, w_2, attn_w, output if layer + 1 == layers else None
+        )
+        if moved:
+            (output,) = moved
         if layer + 1 < layers:
-            dob, attn_grads[layer + 1], d_grads[layer + 1] = together(
-                dob, attn_grads[layer + 1], d_grads[layer + 1]
+            dob, gu_sums, d_sums, attn_grads[layer + 1], d_grads[layer + 1] = together(
+                dob, gu_sums, d_sums, attn_grads[layer + 1], d_grads[layer + 1]
             )
         gu_grads[layer] = reduce_rows(gu_sums)
         if layer == 0:
@@ -893,19 +1124,9 @@
             q, k, v, query_rows, o, flat(dob), log_total, cosine, sine, bounds, length1, bq, bk, scale, scale2
         )
         dk, dv = own_keys(dk), own_keys(dv)
-        dqkv, e, gain1_grad = attn_back(
-            h, dmid, gain1, *(array.reshape(ranks, block, -1) for array in (dq, dk, dv)), cosine3, sine3, w_qkv
-        )
-        dqkv_w = dot_tn(flat(a1), flat(dqkv)).astype(BF)
-        qk_wide = (head_group + 1) * LANES
-        attn_sums = jnp.concatenate(
-            [
-                unspread(dqkv_w[:, :qk_wide], head_group + 1),
-                narrow(dqkv_w[:, qk_wide:], 1),
-                narrow(dot_tn(flat(dat), o).astype(BF), head_group),
-                jnp.concatenate([gain1_grad, gain2_grad], axis=0).T.astype(BF),
-            ],
-            axis=1,
+        e, attn_sums = attn_back(
+            h, dmid, gain, gain2, *(array.reshape(ranks, block, -1) for array in (dq, dk, dv)), cosine3, sine3,
+            o.reshape(ranks, block, -1), a1, dat, attn_w,
         )
         if layer > 0:
             e, attn_sums, d_sums, gu_grads[layer] = together(e, attn_sums, d_sums, gu_grads[layer])
@@ -913,32 +1134,33 @@
         else:
             e, attn_sums, gu_grads[layer], d_grads[layer] = together(e, attn_sums, gu_grads[layer], d_grads[layer])
         attn_grads[layer] = reduce_rows(attn_sums)
-    input_grad = swap(e)[None]
-
-    def send_home(grads):
-        stacked = jnp.stack(grads).reshape(ranks, rows, -1)
-        back = lax.all_to_all(stacked, PLANE, split_axis=0, concat_axis=0, tiled=True)
-        return back.astype(F32)
-
-    def columns(back, start, count):
-        return jnp.swapaxes(back[:, :, start : start + count], 0, 1).reshape(rows, ranks * count)
-
-    mlp_back_home = send_home([jnp.concatenate(pair, axis=2) for pair in zip(gu_grads, d_grads)])
-    attn_back_home = send_home(attn_grads)
-    at = q_cols + 2 * kv_cols
-    gain_sums = jnp.sum(attn_back_home[:, :, at + q_cols :], axis=0)
+
+    def by_place(grads):
+        return jnp.stack(grads).reshape(ranks, rows, -1)
+
+    mlp_blocks = by_place([jnp.concatenate(pair, axis=2) for pair in zip(gu_grads, d_grads)])
+    mlp_home, input_grad = exchange(7, mlp_blocks, e)
+    attn_blocks, mlp_home = together(by_place(attn_grads), mlp_home)
+    (attn_home,) = exchange(10, attn_blocks)
+    grad_gate, grad_up, grad_down = finish(mlp_home)
+    attn_home = attn_home.astype(F32)
+    gain_sums = jnp.sum(attn_home[:, :, GAIN_AT : GAIN_AT + 2], axis=0)
+
+    def columns(start, count):
+        return jnp.swapaxes(attn_home[:, :, start : start + count], 0, 1).reshape(rows, ranks * count)
+
     return (
-        output,
-        input_grad,
+        output[None],
+        input_grad[None],
         gain_sums[:, 0][None],
-        columns(attn_back_home, 0, q_cols)[None],
-        columns(attn_back_home, q_cols, kv_cols)[None],
-        columns(attn_back_home, q_cols + kv_cols, kv_cols)[None],
-        columns(attn_back_home, at, q_cols).T[None],
+        columns(0, q_cols)[None],
+        columns(q_cols, kv_cols)[None],
+        columns(q_cols + kv_cols, kv_cols)[None],
+        jnp.swapaxes(attn_home[:, :, QKV:GAIN_AT], 1, 2).reshape(ranks * OUT, rows)[None],
         gain_sums[:, 1][None],
-        columns(mlp_back_home, 0, ff_cols)[None],
-        columns(mlp_back_home, ff_cols, ff_cols)[None],
-        columns(mlp_back_home, 2 * ff_cols, ff_cols).T[None],
+        grad_gate[None],
+        grad_up[None],
+        grad_down[None],
     )
 
 

time: 1850 us -> 1660 us (0.90)
  Pallas kernels: 1160 us -> 1420 us
  waiting for transfers between devices: 345 us -> 150 us
  matrix products: 119 us -> 0 us
  local copies, waits for them, and re-layouts: 107 us -> 46.9 us
  starting transfers between devices: 43.7 us -> 2.44 us
  other arithmetic: 49.6 us -> 22.3 us
    pallas_call x16 -> x21, Pallas kernels: 1060 us -> 1310 us  [plane_call(): pl.pallas_call(kernel, out_shape=out_shape, in_specs=in_specs, out_specs=...]
    dot_general x16 -> x0, matrix products: 119 us -> none  [dot(): return lax.dot_general(a, b, (dims, ((), ())), preferred_element_type=F32)]
    ppermute x4 -> x0, waiting for transfers between devices: 108 us -> none  [swap(): return lax.ppermute(array, names, pairs)]
    all_to_all x4 -> x0, waiting for transfers between devices: 70.9 us -> none  [the longest x2 65.4 us: exchange(): lax.all_to_all(jnp.swapaxes(pack.astype(BF), 0, 1), PLANE, split_axis=0,...]
    slice x50 -> x4, local copies, waits for them, and re-layouts: 31.4 us -> 9.41 us  [the longest x1 2.99 us: body(): second_blocks, first_got = together(mlp_blocks[..., cut:], first_got)]
    ppermute x4 -> x0, starting transfers between devices: 21.9 us -> none  [swap(): return lax.ppermute(array, names, pairs)]
    reduce_scatter x12, waiting for transfers between devices: 98.6 us -> 76.9 us  [reduce_rows(): mine = lax.psum_scatter(sums, 'z', scatter_dimension=0, tiled=True)]
    all_to_all x4 -> x0, starting transfers between devices: 19.5 us -> none  [the longest x2 10 us: send_home(): lax.all_to_all(stacked, PLANE, split_axis=0, concat_axis=0, tiled=True)]
  transfers between devices with their start and end apart: 32 -> 24, of which waited for: 14 -> 8; matrix products, arithmetic and copies ran while one was open for 12% -> 1% of each run, Pallas kernels for 53% -> 68%
where the time goes in v4:
time: 1660 us; the launch traced here: 1650 us
  Pallas kernels  1420 us (86%)
  waiting for transfers between devices  150 us (9%)
  local copies, waits for them, and re-layouts  46.9 us (3%)
  other arithmetic  22.3 us (1%)
    pallas_call x21, Pallas kernels, plane_call(): pl.pallas_call(kernel, out_shape=out_shape, in_specs=in_specs, out_specs=...  1310 us
    reduce_scatter x12, waiting for transfers between devices, reduce_rows(): mine = lax.psum_scatter(sums, 'z', scatter_dimension=0, tiled=True)  76.9 us
    all_gather x12, waiting for transfers between devices, whole(): lax.all_gather(part.reshape(-1, part.shape[-1]), 'z', axis=0, tiled=True)  69 us
    pallas_call x4, Pallas kernels, attend_back(): pl.pallas_call(functools.partial(back_kernel, scale, scale2, bq, bk), gri...  58.9 us
    pallas_call x4, Pallas kernels, attend(): pl.pallas_call(functools.partial(attend_kernel, scale2, bq, bk), grid_spe...  40.1 us
  transfers between devices with their start and end apart: 24, of which 8 were waited for; matrix products, arithmetic and copies ran while one was open for 1% of the time, Pallas kernels for 68%

profile of v4, /device:TPU:2, one launch (start us, length us, event | category | flops | bytes accessed | tf_op | source)
XLA Modules:
  0.0 1654.4 jit_solution(6903218825857279597)
XLA Ops:
  13.6 4.2 concatenate.27
  17.8 25.1 %exchange.5 = bf16[8,192,640]{2,1,0:T(8,128)(2,1)} custom-call(bf16[8,192,640]{2,1,0:T(8,128)(2,1)} %bitcast.161), custom_call_target="tpu_custom_call" | custom-call | bytes 72000000 | tf_op jit(solution)/shard_map/exchange/pallas_call | solution.py:366
  49.2 1.9 slice.97.blocks
  53.7 3.0 slice.96.refs_0_
  56.7 33.4 %exchange.6 = bf16[8,192,896]{2,1,0:T(8,128)(2,1)} custom-call(bf16[8,192,896]{2,1,0:T(8,128)(2,1)} %slice.97.blocks), custom_call_target="tpu_custom_call" | custom-call | bytes 102000000 | tf_op jit(solution)/shard_map/exchange/pallas_call | solution.py:366
  90.1 42.0 %exchange.7 = (bf16[8,192,640]{2,1,0:T(8,128)(2,1)}, bf16[256,1536]{1,0:T(8,128)(2,1)}) custom-call(bf16[8,192,640]{2,1,0:T(8,128)(2,1)} %slice.96.refs_0_, bf16[256,1536]{1,0:T(8,128)(2,1)} %bitcast.225), custom_call_target="tpu_custom_call" | custom-call | bytes 72000000 | tf_op jit(solution)/shard_map/exchange/pallas_call | solution.py:366
  132.1 3.0 fusion.5
  137.9 3.7 fusion
  143.8 1.9 select_maximum_fusion
  145.8 35.5 %attn_in.4 = (bf16[8,256,1536]{2,1,0:T(8,128)(2,1)}, bf16[2,8,256,128]{3,2,1,0:T(8,128)(2,1)}, bf16[8,256,128]{2,1,0:T(8,128)(2,1)}, bf16[8,256,128]{2,1,0:T(8,128)(2,1)}, f32[2,1536]{1,0:T(2,128)}) custom-call(bf16[256,1536]{1,0:T(8,128)(2,1)} %get-tuple-element.172.h, bf16[1536,640]{1,0:T(8,128)(2,1)} %all-gather.13.cloned.1.call-done.w_hbm.wa_hbm, ...), custom_call_target="tpu_custom_call" | custom-call | bytes 102000000 | tf_op jit(solution)/shard_map/attn_in/pallas_call | solution.py:366
  181.3 10.0 attend.4
  192.5 44.7 %all-gather.15.cloned.1.call-done.w1_hbm = bf16[1536,896]{1,0:T(8,128)(2,1)} async-done(((bf16[384,896]{1,0:T(8,128)(2,1)}), bf16[1536,896]{1,0:T(8,128)(2,1)}) %all-gather.15.cloned.1.call-update) | async-done | bytes 2752528 | tf_op jit(solution)/shard_map/all_gather | solution.py:1029
  237.2 97.3 %mlp.4 = (f32[256,1536]{1,0:T(8,128)}, bf16[8,256,1536]{2,1,0:T(8,128)(2,1)}, bf16[8,256,1024]{2,1,0:T(8,128)(2,1)}, bf16[8,256,512]{2,1,0:T(8,128)(2,1)}, bf16[256,1536]{1,0:T(8,128)(2,1)}) custom-call(bf16[256,1536]{1,0:T(8,128)(2,1)} %get-tuple-element.172.h, bf16[8,256,192]{2,1,0:T(8,128)(2,1)} %bitcast.153, f32[2,1536]{1,0:T(2,128)} %get-tuple-element.180.gain, ...), custom_call_target="tpu_custom_call" | custom-call | bytes 288000000 | tf_op jit(solution)/shard_map/mlp/pallas_call | solution.py:366
  334.5 4.3 all-gather.21.cloned.1.call-done.w1_hbm
  338.9 35.5 %attn_in.5 = (bf16[8,256,1536]{2,1,0:T(8,128)(2,1)}, bf16[2,8,256,128]{3,2,1,0:T(8,128)(2,1)}, bf16[8,256,128]{2,1,0:T(8,128)(2,1)}, bf16[8,256,128]{2,1,0:T(8,128)(2,1)}, f32[2,1536]{1,0:T(2,128)}) custom-call(bf16[256,1536]{1,0:T(8,128)(2,1)} %get-tuple-element.185.h, bf16[1536,640]{1,0:T(8,128)(2,1)} %all-gather.19.cloned.1.call-done.w_hbm.wa_hbm, ...), custom_call_target="tpu_custom_call" | custom-call | bytes 102000000 | tf_op jit(solution)/shard_map/attn_in/pallas_call | solution.py:366
  374.4 10.0 attend.5
  385.7 96.2 %mlp.5 = (f32[256,1536]{1,0:T(8,128)}, bf16[8,256,1536]{2,1,0:T(8,128)(2,1)}, bf16[8,256,1024]{2,1,0:T(8,128)(2,1)}, bf16[8,256,512]{2,1,0:T(8,128)(2,1)}, bf16[256,1536]{1,0:T(8,128)(2,1)}) custom-call(bf16[256,1536]{1,0:T(8,128)(2,1)} %get-tuple-element.185.h, bf16[8,256,192]{2,1,0:T(8,128)(2,1)} %bitcast.155, f32[2,1536]{1,0:T(2,128)} %get-tuple-element.192.gain, ...), custom_call_target="tpu_custom_call" | custom-call | bytes 288000000 | tf_op jit(solution)/shard_map/mlp/pallas_call | solution.py:366
  481.9 9.9 all-gather.27.cloned.1.call-done.w1_hbm
  491.9 35.6 %attn_in.6 = (bf16[8,256,1536]{2,1,0:T(8,128)(2,1)}, bf16[2,8,256,128]{3,2,1,0:T(8,128)(2,1)}, bf16[8,256,128]{2,1,0:T(8,128)(2,1)}, bf16[8,256,128]{2,1,0:T(8,128)(2,1)}, f32[2,1536]{1,0:T(2,128)}) custom-call(bf16[256,1536]{1,0:T(8,128)(2,1)} %get-tuple-element.198.h, bf16[1536,640]{1,0:T(8,128)(2,1)} %all-gather.25.cloned.1.call-done.w_hbm.wa_hbm, ...), custom_call_target="tpu_custom_call" | custom-call | bytes 102000000 | tf_op jit(solution)/shard_map/attn_in/pallas_call | solution.py:366
  527.5 10.0 attend.6
  538.7 96.1 %mlp.6 = (f32[256,1536]{1,0:T(8,128)}, bf16[8,256,1536]{2,1,0:T(8,128)(2,1)}, bf16[8,256,1024]{2,1,0:T(8,128)(2,1)}, bf16[8,256,512]{2,1,0:T(8,128)(2,1)}, bf16[256,1536]{1,0:T(8,128)(2,1)}) custom-call(bf16[256,1536]{1,0:T(8,128)(2,1)} %get-tuple-element.198.h, bf16[8,256,192]{2,1,0:T(8,128)(2,1)} %bitcast.157, f32[2,1536]{1,0:T(2,128)} %get-tuple-element.205.gain, ...), custom_call_target="tpu_custom_call" | custom-call | bytes 288000000 | tf_op jit(solution)/shard_map/mlp/pallas_call | solution.py:366
  634.9 10.0 all-gather.33.cloned.1.call-done.refs_4_.refs_6_
  645.6 35.6 %attn_in.7 = (bf16[8,256,1536]{2,1,0:T(8,128)(2,1)}, bf16[2,8,256,128]{3,2,1,0:T(8,128)(2,1)}, bf16[8,256,128]{2,1,0:T(8,128)(2,1)}, bf16[8,256,128]{2,1,0:T(8,128)(2,1)}, f32[2,1536]{1,0:T(2,128)}) custom-call(bf16[256,1536]{1,0:T(8,128)(2,1)} %get-tuple-element.211.h.refs_0_, bf16[1536,640]{1,0:T(8,128)(2,1)} %all-gather.31.cloned.1.call-done.w_hbm.refs_3_.refs_8_, ...), custom_call_target="tpu_custom_call" | custom-call | bytes 102000000 | tf_op jit(solution)/shard_map/attn_in/pallas_call | solution.py:366
  681.2 10.0 attend.7
  691.2 113.4 %mlp.7 = (f32[256,1536]{1,0:T(8,128)}, bf16[8,256,1536]{2,1,0:T(8,128)(2,1)}, bf16[8,256,1024]{2,1,0:T(8,128)(2,1)}, bf16[8,256,512]{2,1,0:T(8,128)(2,1)}, bf16[...) custom-call(bf16[256,1536]{1,0:T(8,128)(2,1)} %get-tuple-element.211.h.refs_0_, bf16[8,256,192]{2,1,0:T(8,128)(2,1)} %bitcast.159, ...), custom_call_target="tpu_custom_call" | custom-call | bytes 288000000 | tf_op jit(solution)/shard_map/mlp/pallas_call | solution.py:366
  804.6 2.1 broadcast_select_fusion.refs_0_
  806.8 115.1 %mlp_back.4 = (f32[256,1536]{1,0:T(8,128)}, f32[1,1536]{1,0:T(1,128)}, bf16[8,256,1536]{2,1,0:T(8,128)(2,1)}, bf16[8,256,256]{2,1,0:T(8,128)(2,1)}, bf16[1536,10...) custom-call(bf16[256,1536]{1,0:T(8,128)(2,1)} %broadcast_select_fusion.refs_0_, ...), custom_call_target="tpu_custom_call" | custom-call | bytes 300000000 | tf_op jit(solution)/shard_map/mlp_back/pallas_call | solution.py:366
  921.9 14.7 attend_back.4
  936.6 40.2 %attn_back.4 = (bf16[256,1536]{1,0:T(8,128)(2,1)}, bf16[1536,640]{1,0:T(8,128)(2,1)}) custom-call(bf16[256,1536]{1,0:T(8,128)(2,1)} %get-tuple-element.211.h.refs_0_, f32[256,1536]{1,0:T(8,128)} %get-tuple-element.227.dmid, f32[2,1536]{1,0:T(2,128)} %get-tuple-element.217.refs_2_.gain, f32[1,1536]{1,0:T(1,128)} %get-tuple-element.228.gain2_grad, ...), custom_call_target="tpu_custom_call" | custom-call | bytes 108000000 | tf_op jit(solution)/shard_map/attn_back/pallas_call | solution.py:366
  976.8 10.7 reduce-scatter.13.cloned.1.call-done
  988.2 98.0 %mlp_back.5 = (f32[256,1536]{1,0:T(8,128)}, f32[1,1536]{1,0:T(1,128)}, bf16[8,256,1536]{2,1,0:T(8,128)(2,1)}, bf16[8,256,256]{2,1,0:T(8,128)(2,1)}, bf16[1536,10...) custom-call(bf16[256,1536]{1,0:T(8,128)(2,1)} %get-tuple-element.240.e, f32[256,1536]{1,0:T(8,128)} %get-tuple-element.241.mid, ...), custom_call_target="tpu_custom_call" | custom-call | bytes 300000000 | tf_op jit(solution)/shard_map/mlp_back/pallas_call | solution.py:366
  1086.3 14.9 attend_back.5
  1101.2 39.4 %attn_back.5 = (bf16[256,1536]{1,0:T(8,128)(2,1)}, bf16[1536,640]{1,0:T(8,128)(2,1)}) custom-call(bf16[256,1536]{1,0:T(8,128)(2,1)} %get-tuple-element.198.h, f32[256,1536]{1,0:T(8,128)} %get-tuple-element.245.dmid, f32[2,1536]{1,0:T(2,128)} %get-tuple-element.205.gain, f32[1,1536]{1,0:T(1,128)} %get-tuple-element.246.gain2_grad, ...), custom_call_target="tpu_custom_call" | custom-call | bytes 108000000 | tf_op jit(solution)/shard_map/attn_back/pallas_call | solution.py:366
  1140.6 10.0 reduce-scatter.19.cloned.1.call-done
  1151.3 97.9 %mlp_back.6 = (f32[256,1536]{1,0:T(8,128)}, f32[1,1536]{1,0:T(1,128)}, bf16[8,256,1536]{2,1,0:T(8,128)(2,1)}, bf16[8,256,256]{2,1,0:T(8,128)(2,1)}, bf16[1536,10...) custom-call(bf16[256,1536]{1,0:T(8,128)(2,1)} %get-tuple-element.263.e, f32[256,1536]{1,0:T(8,128)} %get-tuple-element.264.mid, ...), custom_call_target="tpu_custom_call" | custom-call | bytes 300000000 | tf_op jit(solution)/shard_map/mlp_back/pallas_call | solution.py:366
  1249.3 14.6 attend_back.6
  1264.0 39.6 %attn_back.6 = (bf16[256,1536]{1,0:T(8,128)(2,1)}, bf16[1536,640]{1,0:T(8,128)(2,1)}) custom-call(bf16[256,1536]{1,0:T(8,128)(2,1)} %get-tuple-element.185.h, f32[256,1536]{1,0:T(8,128)} %get-tuple-element.268.dmid, f32[2,1536]{1,0:T(2,128)} %get-tuple-element.192.gain, f32[1,1536]{1,0:T(1,128)} %get-tuple-element.269.gain2_grad, ...), custom_call_target="tpu_custom_call" | custom-call | bytes 108000000 | tf_op jit(solution)/shard_map/attn_back/pallas_call | solution.py:366
  1303.6 10.0 reduce-scatter.25.cloned.1.call-done
  1314.5 97.9 %mlp_back.7 = (f32[256,1536]{1,0:T(8,128)}, f32[1,1536]{1,0:T(1,128)}, bf16[8,256,1536]{2,1,0:T(8,128)(2,1)}, bf16[8,256,256]{2,1,0:T(8,128)(2,1)}, bf16[1536,10...) custom-call(bf16[256,1536]{1,0:T(8,128)(2,1)} %get-tuple-element.286.e, f32[256,1536]{1,0:T(8,128)} %get-tuple-element.287.mid, ...), custom_call_target="tpu_custom_call" | custom-call | bytes 300000000 | tf_op jit(solution)/shard_map/mlp_back/pallas_call | solution.py:366
  1413.3 14.7 attend_back.7
  1427.9 39.4 %attn_back.7 = (bf16[256,1536]{1,0:T(8,128)(2,1)}, bf16[1536,640]{1,0:T(8,128)(2,1)}) custom-call(bf16[256,1536]{1,0:T(8,128)(2,1)} %get-tuple-element.172.h, f32[256,1536]{1,0:T(8,128)} %get-tuple-element.291.dmid, f32[2,1536]{1,0:T(2,128)} %get-tuple-element.180.gain, f32[1,1536]{1,0:T(1,128)} %get-tuple-element.292.gain2_grad, ...), custom_call_target="tpu_custom_call" | custom-call | bytes 108000000 | tf_op jit(solution)/shard_map/attn_back/pallas_call | solution.py:366
  1467.4 45.9 %reduce-scatter.31.cloned.1.call-done = bf16[384,1024]{1,0:T(8,128)(2,1)} async-done(((bf16[1536,1024]{1,0:T(8,128)(2,1)}), bf16[384,1024]{1,0:T(8,128)(2,1)}) %reduce-scatter.31.cloned.1.call-update) | async-done | bytes 786448 | tf_op jit(solution)/shard_map/reduce_scatter | solution.py:1032
  1516.0 2.5 pad_maximum_fusion
  1518.5 71.5 %exchange.8 = (bf16[8,192,1536]{2,1,0:T(8,128)(2,1)}, bf16[256,1536]{1,0:T(8,128)(2,1)}) custom-call(bf16[8,192,1536]{2,1,0:T(8,128)(2,1)} %bitcast.152, bf16[256,1536]{1,0:T(8,128)(2,1)} %get-tuple-element.317.refs_1_), custom_call_target="tpu_custom_call" | custom-call | bytes 174000000 | tf_op jit(solution)/shard_map/exchange/pallas_call | solution.py:366
  1590.1 2.6 pad_maximum_fusion.1
  1592.7 25.0 %exchange.9 = bf16[8,192,640]{2,1,0:T(8,128)(2,1)} custom-call(bf16[8,192,640]{2,1,0:T(8,128)(2,1)} %bitcast.162), custom_call_target="tpu_custom_call" | custom-call | bytes 72000000 | tf_op jit(solution)/shard_map/exchange/pallas_call | solution.py:366
  1631.6 7.9 finish.1
  1639.5 5.3 copy.49
  (172 shorter events, 46.3 us)
Async XLA Ops:
  7.2 2.6 copy-start.14
  7.2 138.6 %all-gather.13.cloned.1.call-start = ((), (), s32[]{:S(2)}) async-start(), calls=%async_computation.12 | async-start | bytes 2457600 | tf_op jit(solution)/shard_map/all_gather | solution.py:1029
  9.3 1.3 copy-start.7
  17.8 25.1 %copy-start.3 = (f32[1,192,4096]{2,1,0:T(8,128)S(1)}, f32[1,192,4096]{2,1,0:T(8,128)}, u32[]{:S(2)}) copy-start(f32[1,192,4096]{2,1,0:T(8,128)} %param.21) | copy-start | bytes 9437188
  43.8 1.9 copy-start.4
  46.5 1.9 copy-start.5
  49.1 3.1 copy-start
  49.2 3.1 copy-start.2
  53.6 138.8 %all-gather.17.cloned.1.call-start = ((), (), s32[]{:S(2)}) async-start(), calls=%async_computation.14 | async-start | bytes 2457600 | tf_op jit(solution)/shard_map/all_gather | solution.py:1029
  132.1 3.1 copy-start.1
  135.1 2.2 copy-start.22
  135.1 102.1 %all-gather.15.cloned.1.call-start = ((), (), s32[]{:S(2)}) async-start(), calls=%async_computation.13 | async-start | bytes 3440640 | tf_op jit(solution)/shard_map/all_gather | solution.py:1029
  136.8 197.7 %all-gather.19.cloned.1.call-start = ((), (), s32[]{:S(2)}) async-start(), calls=%async_computation.15 | async-start | bytes 2457600 | tf_op jit(solution)/shard_map/all_gather | solution.py:1029
  191.4 147.5 %all-gather.21.cloned.1.call-start = ((), (), s32[]{:S(2)}) async-start(), calls=%async_computation.16 | async-start | bytes 3440640 | tf_op jit(solution)/shard_map/all_gather | solution.py:1029
  191.9 193.8 %all-gather.23.cloned.1.call-start = ((), (), s32[]{:S(2)}) async-start(), calls=%async_computation.17 | async-start | bytes 2457600 | tf_op jit(solution)/shard_map/all_gather | solution.py:1029
  338.9 143.1 %all-gather.25.cloned.1.call-start = ((), (), s32[]{:S(2)}) async-start(), calls=%async_computation.18 | async-start | bytes 2457600 | tf_op jit(solution)/shard_map/all_gather | solution.py:1029
  384.5 107.4 %all-gather.27.cloned.1.call-start = ((), (), s32[]{:S(2)}) async-start(), calls=%async_computation.19 | async-start | bytes 3440640 | tf_op jit(solution)/shard_map/all_gather | solution.py:1029
  385.2 153.5 %all-gather.29.cloned.1.call-start = ((), (), s32[]{:S(2)}) async-start(), calls=%async_computation.20 | async-start | bytes 2457600 | tf_op jit(solution)/shard_map/all_gather | solution.py:1029
  491.9 143.0 %all-gather.31.cloned.1.call-start = ((), (), s32[]{:S(2)}) async-start(), calls=%async_computation.21 | async-start | bytes 2457600 | tf_op jit(solution)/shard_map/all_gather | solution.py:1029
  537.5 107.3 %all-gather.33.cloned.1.call-start = ((), (), s32[]{:S(2)}) async-start(), calls=%async_computation.22 | async-start | bytes 3440640 | tf_op jit(solution)/shard_map/all_gather | solution.py:1029
  538.2 153.0 %all-gather.35.cloned.1.call-start = ((), (), s32[]{:S(2)}) async-start(), calls=%async_computation.23 | async-start | bytes 2457600 | tf_op jit(solution)/shard_map/all_gather | solution.py:1029
  644.9 342.7 %reduce-scatter.13.cloned.1.call-start = ((), (), s32[]{:S(2)}) async-start(), calls=%async_computation.24 | async-start | bytes 3932160 | tf_op jit(solution)/shard_map/reduce_scatter | solution.py:1032
  921.9 164.4 %reduce-scatter.17.cloned.1.call-start = ((), (), s32[]{:S(2)}) async-start(), calls=%async_computation.26 | async-start | bytes 1966080 | tf_op jit(solution)/shard_map/reduce_scatter | solution.py:1032
  987.6 98.7 %reduce-scatter.15.cloned.1.call-start = ((), (), s32[]{:S(2)}) async-start(), calls=%async_computation.25 | async-start | bytes 2457600 | tf_op jit(solution)/shard_map/reduce_scatter | solution.py:1032
  988.2 162.5 %reduce-scatter.19.cloned.1.call-start = ((), (), s32[]{:S(2)}) async-start(), calls=%async_computation.27 | async-start | bytes 3932160 | tf_op jit(solution)/shard_map/reduce_scatter | solution.py:1032
  1086.3 162.9 %reduce-scatter.23.cloned.1.call-start = ((), (), s32[]{:S(2)}) async-start(), calls=%async_computation.29 | async-start | bytes 1966080 | tf_op jit(solution)/shard_map/reduce_scatter | solution.py:1032
  1150.7 98.6 %reduce-scatter.21.cloned.1.call-start = ((), (), s32[]{:S(2)}) async-start(), calls=%async_computation.28 | async-start | bytes 2457600 | tf_op jit(solution)/shard_map/reduce_scatter | solution.py:1032
  1151.2 162.4 %reduce-scatter.25.cloned.1.call-start = ((), (), s32[]{:S(2)}) async-start(), calls=%async_computation.30 | async-start | bytes 3932160 | tf_op jit(solution)/shard_map/reduce_scatter | solution.py:1032
  1249.3 163.2 %reduce-scatter.29.cloned.1.call-start = ((), (), s32[]{:S(2)}) async-start(), calls=%async_computation.32 | async-start | bytes 1966080 | tf_op jit(solution)/shard_map/reduce_scatter | solution.py:1032
  1313.7 98.8 %reduce-scatter.27.cloned.1.call-start = ((), (), s32[]{:S(2)}) async-start(), calls=%async_computation.31 | async-start | bytes 2457600 | tf_op jit(solution)/shard_map/reduce_scatter | solution.py:1032
  1314.4 153.0 %reduce-scatter.33.cloned.1.call-start = ((), (), s32[]{:S(2)}) async-start(), calls=%async_computation.34 | async-start | bytes 1966080 | tf_op jit(solution)/shard_map/reduce_scatter | solution.py:1032
  1412.5 100.9 %reduce-scatter.31.cloned.1.call-start = ((), (), s32[]{:S(2)}) async-start(), calls=%async_computation.33 | async-start | bytes 3932160 | tf_op jit(solution)/shard_map/reduce_scatter | solution.py:1032
  1413.2 176.8 %reduce-scatter.35.cloned.1.call-start = ((), (), s32[]{:S(2)}) async-start(), calls=%async_computation.35 | async-start | bytes 2457600 | tf_op jit(solution)/shard_map/reduce_scatter | solution.py:1032
  1467.4 46.0 %copy-start.10 = (bf16[384,1024]{1,0:T(8,128)(2,1)S(1)}, bf16[384,1024]{1,0:T(8,128)(2,1)}, u32[]{:S(2)}) copy-start(bf16[384,1024]{1,0:T(8,128)(2,1)} %reduce-scatter.13.cloned.1.call-done) | copy-start | bytes 2359300
  1467.4 46.0 %copy-start.18 = (bf16[384,512]{1,0:T(8,128)(2,1)S(1)}, bf16[384,512]{1,0:T(8,128)(2,1)}, u32[]{:S(2)}) copy-start(bf16[384,512]{1,0:T(8,128)(2,1)} %reduce-scatter.17.cloned.1.call-done) | copy-start | bytes 1179652
  1513.4 1.1 copy-start.11
  1513.4 1.2 copy-start.19
  1513.4 1.5 copy-start.12
  1513.4 1.5 copy-start.20
  1514.6 1.2 copy-start.13
  1514.6 1.3 copy-start.21
  1518.5 71.6 %copy-start.15 = (bf16[384,640]{1,0:T(8,128)(2,1)S(1)}, bf16[384,640]{1,0:T(8,128)(2,1)}, u32[]{:S(2)}) copy-start(bf16[384,640]{1,0:T(8,128)(2,1)} %reduce-scatter.15.cloned.1.call-done) | copy-start | bytes 1474564
  1518.5 71.6 %copy-start.16 = (bf16[384,640]{1,0:T(8,128)(2,1)S(1)}, bf16[384,640]{1,0:T(8,128)(2,1)}, u32[]{:S(2)}) copy-start(bf16[384,640]{1,0:T(8,128)(2,1)} %reduce-scatter.21.cloned.1.call-done) | copy-start | bytes 1474564
  1518.5 71.6 %copy-start.17 = (bf16[384,640]{1,0:T(8,128)(2,1)S(1)}, bf16[384,640]{1,0:T(8,128)(2,1)}, u32[]{:S(2)}) copy-start(bf16[384,640]{1,0:T(8,128)(2,1)} %reduce-scatter.27.cloned.1.call-done) | copy-start | bytes 1474564
  1624.9 2.8 copy-start.6
  1639.5 5.3 copy-start.8
  1644.8 1.4 copy-start.9
Sparse Core Ops, SparseCore 0:
  53.8 44.7 all-gather.12
  135.2 43.8 all-gather.16
  181.3 55.8 all-gather.14
  238.6 42.3 all-gather.18
  283.0 55.8 all-gather.20
  340.3 42.2 all-gather.22
  384.7 49.0 all-gather.24
  436.0 55.8 all-gather.26
  493.4 42.2 all-gather.28
  537.7 49.0 all-gather.30
  589.0 55.8 all-gather.32
  646.3 42.2 all-gather.34
  922.0 65.5 reduce-scatter.12
  989.7 36.9 reduce-scatter.16
  1028.8 40.4 reduce-scatter.14
  1086.4 64.1 reduce-scatter.18
  1152.8 36.9 reduce-scatter.22
  1192.0 40.4 reduce-scatter.20
  1249.4 64.2 reduce-scatter.24
  1315.8 36.9 reduce-scatter.28
  1355.2 40.4 reduce-scatter.26
  1412.6 39.1 reduce-scatter.32
  1454.1 59.2 reduce-scatter.30
  1515.5 64.7 reduce-scatter.34

commit v5 on v4

--- a/solution.py
+++ b/solution.py
@@ -51,6 +51,15 @@
     return lax.axis_index("x"), lax.axis_index("c"), lax.axis_index("y")
 
 
+def xor(a, b):
+    return a + b - 2 * a * b
+
+
+def token_place():
+    x, c, y = place()
+    return xor(x, lax.rem(lax.axis_index("z"), 2)), c, y
+
+
 def flip(index, by):
     return 1 - index if by else index
 
@@ -61,18 +70,20 @@
 
 
 class Swap:
-    def __init__(self, here, moving, moved, sem):
-        x, c, _ = here
+    def __init__(self, homeward, moving, moved, sem):
+        x, c, _ = place()
         z = lax.axis_index("z")
-        section = x * 2 + c
-        self.away = section != z
-        self.partner = {"x": z // 2, "c": lax.rem(z, 2), "z": section}
+        low = lax.rem(z, 2)
+        out = {"x": xor(z // 2, c), "c": low, "z": x * 2 + c}
+        back = {"x": z // 2, "c": low, "z": 2 * xor(x, low) + c}
+        target, self.source = (back, out) if homeward else (out, back)
+        self.away = (target["x"] != x) | (target["c"] != c) | (target["z"] != z)
         self.remote = pltpu.make_async_remote_copy(
             src_ref=moving,
             dst_ref=moved,
             send_sem=sem.at[0],
             recv_sem=sem.at[1],
-            device_id=self.partner,
+            device_id=target,
             device_id_type=MESH,
         )
         self.local = pltpu.make_async_copy(moving, moved, sem.at[2])
@@ -80,7 +91,7 @@
     def greet(self, barrier):
         @pl.when(self.away)
         def _():
-            pl.semaphore_signal(barrier, inc=1, device_id=self.partner, device_id_type=MESH)
+            pl.semaphore_signal(barrier, inc=1, device_id=self.source, device_id_type=MESH)
 
     def either(self, remote, local):
         pl.when(self.away)(remote)
@@ -109,8 +120,8 @@
     return wrapped
 
 
-def greet(here, swap=None):
-    x, c, y = here
+def greet(swap=None):
+    x, c, y = place()
     barrier = pltpu.get_barrier_semaphore()
     for peer in ({"x": 1 - x}, {"c": 1 - c}, {"y": 1 - y}):
         pl.semaphore_signal(barrier, inc=1, device_id=peer, device_id_type=MESH)
@@ -123,8 +134,8 @@
 
 
 class Sender:
-    def __init__(self, here, send_sem, recv_sem):
-        x, c, y = here
+    def __init__(self, send_sem, recv_sem):
+        x, c, y = place()
         self.peers = {"x": {"x": 1 - x}, "c": {"c": 1 - c}, "y": {"y": 1 - y}}
         self.send_sem, self.recv_sem = send_sem, recv_sem
         self.sent = []
@@ -152,10 +163,10 @@
             started.wait_send()
 
 
-def run_gather(here, full, sems, on_block):
+def run_gather(here, full, sems, on_block, before_last=None):
     block = full.shape[1]
     piece = block // 4
-    net = Sender(here, *sems)
+    net = Sender(*sems)
 
     def index(role, chunk):
         return (role[0] * 4 + role[1] * 2 + role[2]) * 4 + chunk
@@ -213,6 +224,8 @@
     done(xc)
     whole(yc)
     done(yc)
+    if before_last is not None:
+        before_last()
     pass_last((1, 3))
     done(at_d)
     whole(dc)
@@ -220,74 +233,89 @@
     return net
 
 
-def run_scatter(here, parts, total, bufs, sems, fill=None, beside=None):
-    from_c, via_x, via_y, from_x, from_y = bufs
-    block = parts.shape[1]
-    half = block // 2
-    net = Sender(here, *sems)
+class Scatter:
     order = (D, X, Y, OWN)
-    lower, upper = pl.ds(0, half), pl.ds(half, half)
-
-    def rank(n, dc):
-        return rank_of(here, order[n][0], dc, order[n][1])
-
-    def make(r):
-        if fill is not None:
-            fill(r)
-
-    def sibling(n):
-        r = rank(n, 1)
-        make(r)
-        net.send(parts.at[r], from_c.at[n], n, "c")
-
-    def add(n, where, more):
-        r = rank(n, 0)
-        parts[r, where] = (parts[r, where].astype(F32) + more.astype(F32)).astype(BF)
-
-    def mine(n, where):
-        return parts.at[rank(n, 0), where]
-
-    def combine(n):
-        net.arrived(from_c.at[n], n)
+
+    def __init__(self, here, parts, total, bufs, sems, fill=None):
+        self.here, self.parts, self.total, self.fill = here, parts, total, fill
+        self.from_c, self.via_x, self.via_y, self.from_x, self.from_y = bufs
+        half = parts.shape[1] // 2
+        self.lower, self.upper = pl.ds(0, half), pl.ds(half, half)
+        self.net = Sender(*sems)
+
+    def rank(self, n, dc):
+        return rank_of(self.here, self.order[n][0], dc, self.order[n][1])
+
+    def make(self, r):
+        if self.fill is not None:
+            self.fill(r)
+
+    def sibling(self, n):
+        r = self.rank(n, 1)
+        self.make(r)
+        self.net.send(self.parts.at[r], self.from_c.at[n], n, "c")
+
+    def add(self, n, where, more):
+        r = self.rank(n, 0)
+        self.parts[r, where] = (self.parts[r, where].astype(F32) + more.astype(F32)).astype(BF)
+
+    def mine(self, n, where):
+        return self.parts.at[self.rank(n, 0), where]
+
+    def combine(self, n):
+        self.make(self.rank(n, 0))
+        self.net.arrived(self.from_c.at[n], n)
         if n < 3:
-            add(n, pl.ds(0, block), from_c[n])
-
-    sibling(0)
-    make(rank(0, 0))
-    sibling(1)
-    sibling(2)
-    combine(0)
-    net.send(mine(0, upper), via_x, 4, "x")
-    net.send(mine(0, lower), via_y, 5, "y")
-    make(rank(1, 0))
-    combine(1)
-    net.send(mine(1, upper), from_x.at[upper], 6, "x")
-    make(rank(2, 0))
-    combine(2)
-    net.send(mine(2, lower), from_y.at[lower], 7, "y")
-    sibling(3)
-    make(rank(3, 0))
-    combine(3)
-    total[...] = parts[rank(3, 0)].astype(F32) + from_c[3].astype(F32)
-    if beside is not None:
-        beside(0)
-    net.arrived(via_y, 5)
-    add(1, lower, via_y[...])
-    net.send(mine(1, lower), from_x.at[lower], 8, "x")
-    net.arrived(via_x, 4)
-    add(2, upper, via_x[...])
-    net.send(mine(2, upper), from_y.at[upper], 9, "y")
-    if beside is not None:
-        beside(1)
-    net.arrived(from_x.at[upper], 6)
-    net.arrived(from_y.at[lower], 7)
-    total[upper] += from_x[upper].astype(F32)
-    total[lower] += from_y[lower].astype(F32)
-    net.arrived(from_x.at[lower], 8)
-    net.arrived(from_y.at[upper], 9)
-    total[lower] += from_x[lower].astype(F32)
-    total[upper] += from_y[upper].astype(F32)
-    return net
+            self.add(n, pl.ds(0, self.parts.shape[1]), self.from_c[n])
+
+    def to_diagonal(self):
+        self.combine(0)
+        self.net.send(self.mine(0, self.upper), self.via_x, 4, "x")
+        self.net.send(self.mine(0, self.lower), self.via_y, 5, "y")
+
+    def to_neighbours(self):
+        self.combine(1)
+        self.net.send(self.mine(1, self.upper), self.from_x.at[self.upper], 6, "x")
+        self.combine(2)
+        self.net.send(self.mine(2, self.lower), self.from_y.at[self.lower], 7, "y")
+
+    def early(self):
+        for n in (1, 2, 3):
+            self.sibling(n)
+        self.to_neighbours()
+
+    def run(self, beside=None, early_done=False):
+        net, total, lower, upper = self.net, self.total, self.lower, self.upper
+        self.sibling(0)
+        if early_done:
+            self.to_diagonal()
+        else:
+            self.sibling(1)
+            self.sibling(2)
+            self.to_diagonal()
+            self.to_neighbours()
+            self.sibling(3)
+        self.combine(3)
+        total[...] = self.parts[self.rank(3, 0)].astype(F32) + self.from_c[3].astype(F32)
+        if beside is not None:
+            beside(0)
+        net.arrived(self.via_y, 5)
+        self.add(1, lower, self.via_y[...])
+        net.send(self.mine(1, lower), self.from_x.at[lower], 8, "x")
+        net.arrived(self.via_x, 4)
+        self.add(2, upper, self.via_x[...])
+        net.send(self.mine(2, upper), self.from_y.at[upper], 9, "y")
+        if beside is not None:
+            beside(1)
+        net.arrived(self.from_x.at[upper], 6)
+        net.arrived(self.from_y.at[lower], 7)
+        total[upper] += self.from_x[upper].astype(F32)
+        total[lower] += self.from_y[lower].astype(F32)
+        net.arrived(self.from_x.at[lower], 8)
+        net.arrived(self.from_y.at[upper], 9)
+        total[lower] += self.from_x[lower].astype(F32)
+        total[upper] += self.from_y[upper].astype(F32)
+        return net
 
 
 def gather_sems():
@@ -386,7 +414,7 @@
 
 
 def attn_in_kernel(h, w_hbm, cosine, sine, a1_out, q_out, k_out, v_out, gain_out, full, w, send, recv, local):
-    here = place()
+    here = token_place()
     loads = Loads(local)
     w_load = loads.start(w_hbm, w)
     x = h[...].astype(F32)
@@ -395,7 +423,7 @@
     rows = w[:, PACK - LANES :].astype(F32).T
     gain_out[...] = rows[GAIN_AT - PACK + LANES : GAIN_AT - PACK + LANES + 2]
     full[rank_of(here, 0, 0, 0)] = (n1 * gain_out[0:1, :]).astype(BF)
-    greet(here)
+    greet()
     saves = []
 
     def on_block(r):
@@ -438,26 +466,26 @@
 
 
 def mlp_kernel(
-    ff, h, o, gain, wa_hbm, w1_hbm, w2_hbm, mid_out, a2_out, gu_out, hid_out, next_out,
+    ff, homeward, h, o, gain, wa_hbm, w1_hbm, w2_hbm, mid_out, a2_out, gu_out, hid_out, next_out,
     full, parts, gu, hid, wa, wm, total,
     from_c, via_x, via_y, from_x, from_y, send1, recv1, send2, recv2,
     from_c3, via_x3, via_y3, from_x3, from_y3, send3, recv3, local, swap=None,
 ):
-    here = place()
-    swap = swap and Swap(here, *swap)
+    here = token_place()
+    swap = swap and Swap(homeward, *swap)
     loads = Loads(local)
     wa_load = loads.start(wa_hbm, wa)
     split = w1_hbm.shape[1]
     w1_load = loads.start(w1_hbm, wm.at[:, pl.ds(0, split)])
     w2_load = loads.start(w2_hbm, wm.at[:, pl.ds(split, 3 * ff - split)])
-    greet(here, swap)
+    greet(swap)
     wa_load.wait()
 
     def fill(r):
         parts[r] = dot_nt(o[r], wa[:, QKV:GAIN_AT]).astype(BF)
 
     bufs = (from_c, via_x, via_y, from_x, from_y)
-    net1 = run_scatter(here, parts, total, bufs, (send1, recv1), fill)
+    net1 = Scatter(here, parts, total, bufs, (send1, recv1), fill).run()
     mid = h[...].astype(F32) + total[...]
     mid_out[...] = mid
     full[rank_of(here, 0, 0, 0)] = (mid * inverse_of(mid) * gain[1:2, :]).astype(BF)
@@ -480,9 +508,10 @@
         saves.append(loads.start(hid.at[r], hid_out.at[r]))
         parts[r] = dot_nt(low, wm[:, 2 * ff :]).astype(BF)
 
-    net2 = run_gather(here, full, (send2, recv2), on_block)
     bufs3 = (from_c3, via_x3, via_y3, from_x3, from_y3)
-    net3 = run_scatter(here, parts, total, bufs3, (send3, recv3))
+    scatter = Scatter(here, parts, total, bufs3, (send3, recv3))
+    net2 = run_gather(here, full, (send2, recv2), on_block, scatter.early)
+    net3 = scatter.run(early_done=True)
     next_out[...] = (mid_out[...] + total[...]).astype(BF)
     net2.drain()
     net3.drain()
@@ -496,7 +525,7 @@
     block, width = h.shape
     ff = (w1.shape[1] + w2.shape[1]) // 3
     return plane_call(
-        functools.partial(mlp_kernel, ff),
+        functools.partial(mlp_kernel, ff, False),
         "mlp",
         1 if moving is None else 8,
         [
@@ -540,23 +569,23 @@
 
 
 def mlp_back_kernel(
-    ff, step, e, mid, gain, gu_hbm, hid_hbm, a2_hbm, w1_hbm, w2_hbm, wa_hbm, dmid_out, gain_out, dat_out, dob_out,
+    ff, step, homeward, e, mid, gain, gu_hbm, hid_hbm, a2_hbm, w1_hbm, w2_hbm, wa_hbm, dmid_out, gain_out, dat_out, dob_out,
     gu_sums, d_sums, full, full2, parts, a2, gu, hid, wm, wa, total, stage, send1, recv1,
-    from_c, via_x, via_y, from_x, from_y, send2, recv2, send3, recv3, local, swap=None,
+    from_c, via_x, via_y, from_x, from_y, send2, recv2, send3, recv3, local, swap=None, alone=False,
 ):
-    here = place()
-    swap = swap and Swap(here, *swap)
+    here = token_place()
+    swap = swap and Swap(homeward, *swap)
     loads = Loads(local)
     split = w1_hbm.shape[1]
     w2_load = loads.start(w2_hbm, wm.at[:, pl.ds(split, 3 * ff - split)])
     gu_load = loads.start(gu_hbm, gu)
     w1_load = loads.start(w1_hbm, wm.at[:, pl.ds(0, split)])
-    wa_load = loads.start(wa_hbm, wa)
+    wa_load = None if alone else loads.start(wa_hbm, wa)
     a2_load = loads.start(a2_hbm, a2)
     hid_load = loads.start(hid_hbm, hid)
     own = rank_of(here, 0, 0, 0)
     full[own] = e[...]
-    greet(here, swap)
+    greet(swap)
     w2_load.wait()
     gu_load.wait()
     w1_load.wait()
@@ -572,7 +601,8 @@
         gu[r, :, ff:] = du.astype(BF)
         parts[r] = dot_nt(gu[r], wm[:, : 2 * ff]).astype(BF)
 
-    net1 = run_gather(here, full, (send1, recv1), on_block)
+    scatter = Scatter(here, parts, total, (from_c, via_x, via_y, from_x, from_y), (send2, recv2))
+    net1 = run_gather(here, full, (send1, recv1), on_block, scatter.early)
     a2_load.wait()
     hid_load.wait()
     sums = []
@@ -596,9 +626,7 @@
                 ]
             )
 
-    net2 = run_scatter(
-        here, parts, total, (from_c, via_x, via_y, from_x, from_y), (send2, recv2), beside=beside
-    )
+    net2 = scatter.run(beside, True)
     da2 = total[...]
     m = mid[...]
     r2 = inverse_of(m)
@@ -606,21 +634,104 @@
     gain_out[...] = jnp.sum(da2 * n2, axis=0, keepdims=True)
     dmid = e[...].astype(F32) + norm_back(da2, n2, r2, gain[1:2, :])
     dmid_out[...] = dmid
-    full2[own] = dmid.astype(BF)
-    wa_load.wait()
-    saves = []
-
-    def on_second(r):
-        saves.append(loads.start(full2.at[r], dat_out.at[r]))
-        dob_out[r] = dot_nn(full2[r], wa[:, QKV:PACK]).astype(BF)
-
-    net3 = run_gather(here, full2, (send3, recv3), on_second)
-    for net in (net1, net2, net3):
+    saves = [save for pair in sums[-2:] for save in pair]
+    nets = [net1, net2]
+    if alone:
+        dat_out[...] = dmid.astype(BF)
+    else:
+        full2[own] = dmid.astype(BF)
+        wa_load.wait()
+
+        def on_second(r):
+            saves.append(loads.start(full2.at[r], dat_out.at[r]))
+            dob_out[r] = dot_nn(full2[r], wa[:, QKV:PACK]).astype(BF)
+
+        nets.append(run_gather(here, full2, (send3, recv3), on_second))
+    for net in nets:
         net.drain()
-    for save in saves + sums[-2] + sums[-1]:
+    for save in saves:
         save.wait()
     if swap is not None:
         swap.wait()
+
+
+def dat_kernel(dat, wa_hbm, dat_out, dob_out, full, wa, send, recv, local):
+    here = token_place()
+    loads = Loads(local)
+    wa_load = loads.start(wa_hbm, wa)
+    full[rank_of(here, 0, 0, 0)] = dat[...]
+    greet()
+    wa_load.wait()
+    saves = []
+
+    def on_block(r):
+        saves.append(loads.start(full.at[r], dat_out.at[r]))
+        dob_out[r] = dot_nn(full[r], wa[:, QKV:PACK]).astype(BF)
+
+    run_gather(here, full, (send, recv), on_block).drain()
+    for save in saves:
+        save.wait()
+
+
+def dat_gather(dat, wa):
+    block, width = dat.shape
+    return plane_call(
+        dat_kernel,
+        "dat_gather",
+        12,
+        [jax.ShapeDtypeStruct((8, block, width), BF), jax.ShapeDtypeStruct((8, block, PACK - QKV), BF)],
+        [ANYWHERE, IN_VMEM],
+        [IN_VMEM, ANYWHERE],
+        [pltpu.VMEM((8, block, width), BF), pltpu.VMEM(wa.shape, BF)] + gather_sems() + [pltpu.SemaphoreType.DMA((9,))],
+        32,
+        dat, wa,
+    )
+
+
+def mlp_back_alone_kernel(
+    ff, step, homeward, e, mid, gain, gu_hbm, hid_hbm, a2_hbm, w1_hbm, w2_hbm, dmid_out, gain_out, dat_out,
+    gu_sums, d_sums, full, parts, a2, gu, hid, wm, total, stage, *rest
+):
+    mlp_back_kernel(
+        ff, step, homeward, e, mid, gain, gu_hbm, hid_hbm, a2_hbm, w1_hbm, w2_hbm, None, dmid_out, gain_out,
+        dat_out, None, gu_sums, d_sums, full, None, parts, a2, gu, hid, wm, None, total, stage,
+        *rest[:-1], None, None, rest[-1], alone=True,
+    )
+
+
+def mlp_back_alone(e, mid, gain, gu, hid, a2, w1, w2):
+    block, width = e.shape
+    ff = hid.shape[2]
+    step = math.gcd(width, 256)
+    return plane_call(
+        functools.partial(mlp_back_alone_kernel, ff, step, True),
+        "mlp_back_alone",
+        11,
+        [
+            jax.ShapeDtypeStruct((block, width), F32),
+            jax.ShapeDtypeStruct((1, width), F32),
+            jax.ShapeDtypeStruct((block, width), BF),
+            jax.ShapeDtypeStruct((width, 2 * ff), BF),
+            jax.ShapeDtypeStruct((width, ff), BF),
+        ],
+        [IN_VMEM, IN_VMEM, IN_VMEM, ANYWHERE, ANYWHERE],
+        [IN_VMEM, IN_VMEM, IN_VMEM] + [ANYWHERE] * 5,
+        [
+            pltpu.VMEM((8, block, width), BF),
+            pltpu.VMEM((8, block, width), BF),
+            pltpu.VMEM((8, block, width), BF),
+            pltpu.VMEM((8, block, 2 * ff), BF),
+            pltpu.VMEM((8, block, ff), BF),
+            pltpu.VMEM((width, 3 * ff), BF),
+            pltpu.VMEM((block, width), F32),
+            pltpu.VMEM((2, step, 3 * ff), BF),
+        ]
+        + gather_sems()
+        + scatter_scratch(block, width)
+        + [pltpu.SemaphoreType.DMA((5 + 2 * (width // step),))],
+        68,
+        e, mid, gain, gu, hid, a2, w1, w2,
+    )
 
 
 def mlp_back(e, mid, gain, gu, hid, a2, w1, w2, wa, moving=None):
@@ -629,7 +740,7 @@
     cols = PACK - QKV
     step = math.gcd(width, 256)
     return plane_call(
-        functools.partial(mlp_back_kernel, ff, step),
+        functools.partial(mlp_back_kernel, ff, step, True),
         "mlp_back",
         2 if moving is None else 9,
         [
@@ -668,12 +779,12 @@
     step, h, dmid, gain, gain2_grad, dq, dk, dv, cosine, sine, o, a1_hbm, dat_hbm, w_hbm, e_out, sums,
     parts, a1, dat, w, dqkv, gain_rows, total, from_c, via_x, via_y, from_x, from_y, send, recv, local,
 ):
-    here = place()
+    here = token_place()
     loads = Loads(local)
     w_load = loads.start(w_hbm, w)
     a1_load = loads.start(a1_hbm, a1)
     dat_load = loads.start(dat_hbm, dat)
-    greet(here)
+    greet()
     w_load.wait()
 
     def fill(r):
@@ -696,9 +807,7 @@
             sums[at, :QKV] = flat_tn(a1, at, dqkv).astype(BF)
             sums[at, QKV:GAIN_AT] = flat_tn(dat, at, o).astype(BF)
 
-    net = run_scatter(
-        here, parts, total, (from_c, via_x, via_y, from_x, from_y), (send, recv), fill, beside
-    )
+    net = Scatter(here, parts, total, (from_c, via_x, via_y, from_x, from_y), (send, recv), fill).run(beside)
     da1 = total[...]
     x = h[...].astype(F32)
     r1 = inverse_of(x)
@@ -743,10 +852,10 @@
     )
 
 
-def exchange_kernel(blocks, got, send_sem, recv_sem, local, swap=None):
+def exchange_kernel(homeward, blocks, got, send_sem, recv_sem, local, swap=None):
     here = place()
     x, c, y = here
-    swap = swap and Swap(here, *swap)
+    swap = swap and Swap(homeward, *swap)
     masks = [(dx, dc, dy) for dx in range(2) for dc in range(2) for dy in range(2)][1:]
     peer = lambda mask: {"x": flip(x, mask[0]), "c": flip(c, mask[1]), "y": flip(y, mask[2])}
     own = rank_of(here, 0, 0, 0)
@@ -785,9 +894,9 @@
         swap.wait()
 
 
-def exchange(number, blocks, moving=None):
+def exchange(number, blocks, moving=None, homeward=False):
     return plane_call(
-        exchange_kernel,
+        functools.partial(exchange_kernel, homeward),
         "exchange",
         number,
         [jax.ShapeDtypeStruct(blocks.shape, BF)],
@@ -803,7 +912,7 @@
 def finish_kernel(ff, got, gate, up, down):
     gate[...] = got[0, :, :ff].astype(F32)
     up[...] = got[0, :, ff : 2 * ff].astype(F32)
-    down[...] = got[0, :, 2 * ff :].astype(F32).T
+    down[...] = got[0, :, 2 * ff :].astype(F32)
 
 
 def finish(got):
@@ -812,17 +921,9 @@
     return pl.pallas_call(
         functools.partial(finish_kernel, ff),
         grid=(ranks,),
-        out_shape=[
-            jax.ShapeDtypeStruct((rows, ranks * ff), F32),
-            jax.ShapeDtypeStruct((rows, ranks * ff), F32),
-            jax.ShapeDtypeStruct((ranks * ff, rows), F32),
-        ],
+        out_shape=[jax.ShapeDtypeStruct((rows, ranks * ff), F32)] * 3,
         in_specs=[pl.BlockSpec((1, rows, cols), lambda i: (i, 0, 0))],
-        out_specs=[
-            pl.BlockSpec((rows, ff), lambda i: (0, i)),
-            pl.BlockSpec((rows, ff), lambda i: (0, i)),
-            pl.BlockSpec((ff, rows), lambda i: (i, 0)),
-        ],
+        out_specs=[pl.BlockSpec((rows, ff), lambda i: (0, i))] * 3,
         compiler_params=pltpu.CompilerParams(vmem_limit_bytes=VMEM_LIMIT),
         name="finish",
     )(got)
@@ -1044,7 +1145,8 @@
     second_got, hidden_state = exchange(6, second_blocks, inputs[0])
     attn_parts, first_parts, second_parts = by_layer(attn_got), by_layer(first_got), by_layer(second_got)
 
-    rank = (lax.axis_index("x") * lax.axis_size("c") + lax.axis_index("c")) * halves + lax.axis_index("y")
+    token_x, token_c, token_y = token_place()
+    rank = (token_x * 2 + token_c) * halves + token_y
     spot = lax.axis_index("e")
     length = lengths[lax.axis_index("z")]
 
@@ -1081,7 +1183,8 @@
 
     saved = []
     attn_w, w_1 = whole(attn_parts[0]), whole(first_parts[0])
-    w_2 = whole(second_parts[0])
+    hidden_state, attn_w, w_1, second_part = together(hidden_state, attn_w, w_1, second_parts[0])
+    w_2 = whole(second_part)
     for layer in range(layers):
         a1, q, k, v, gain = attn_in(hidden_state, attn_w, cosine3, sine3)
         q, k, v = q.reshape(head_group, tokens, LANES), all_keys(flat(k)), all_keys(flat(v))
@@ -1108,12 +1211,19 @@
     d_grads = [None] * layers
     for layer in reversed(range(layers)):
         (h, a1, q, k, v, o, log_total, mid, a2, gu, hid, attn_w, w_1, w_2, gain) = saved[layer]
-        dmid, gain2, dat, dob, gu_sums, d_sums, *moved = mlp_back(
-            e, mid, gain, gu, hid, a2, w_1, w_2, attn_w, output if layer + 1 == layers else None
-        )
-        if moved:
-            (output,) = moved
-        if layer + 1 < layers:
+        if layer > 0:
+            dmid, gain2, dat, dob, gu_sums, d_sums, *moved = mlp_back(
+                e, mid, gain, gu, hid, a2, w_1, w_2, attn_w, output if layer + 1 == layers else None
+            )
+            if moved:
+                (output,) = moved
+        else:
+            dmid, gain2, dat, gu_sums, d_sums = mlp_back_alone(e, mid, gain, gu, hid, a2, w_1, w_2)
+            dat, gu_sums, d_sums, attn_grads[1], d_grads[1] = together(
+                dat, gu_sums, d_sums, attn_grads[1], d_grads[1]
+            )
+            dat, dob = dat_gather(dat, attn_w)
+        if 0 < layer < layers - 1:
             dob, gu_sums, d_sums, attn_grads[layer + 1], d_grads[layer + 1] = together(
                 dob, gu_sums, d_sums, attn_grads[layer + 1], d_grads[layer + 1]
             )
@@ -1139,7 +1249,7 @@
         return jnp.stack(grads).reshape(ranks, rows, -1)
 
     mlp_blocks = by_place([jnp.concatenate(pair, axis=2) for pair in zip(gu_grads, d_grads)])
-    mlp_home, input_grad = exchange(7, mlp_blocks, e)
+    mlp_home, input_grad = exchange(7, mlp_blocks, e, True)
     attn_blocks, mlp_home = together(by_place(attn_grads), mlp_home)
     (attn_home,) = exchange(10, attn_blocks)
     grad_gate, grad_up, grad_down = finish(mlp_home)
@@ -1156,11 +1266,11 @@
         columns(0, q_cols)[None],
         columns(q_cols, kv_cols)[None],
         columns(q_cols + kv_cols, kv_cols)[None],
-        jnp.swapaxes(attn_home[:, :, QKV:GAIN_AT], 1, 2).reshape(ranks * OUT, rows)[None],
+        columns(QKV, OUT).T[None],
         gain_sums[:, 1][None],
         grad_gate[None],
         grad_up[None],
-        grad_down[None],
+        grad_down.T[None],
     )
 
 

time: 1660 us -> 1620 us (0.976)
  waiting for transfers between devices: 150 us -> 38.5 us
  Pallas kernels: 1420 us -> 1480 us
    reduce_scatter x12, waiting for transfers between devices: 76.9 us -> 12.9 us  [reduce_rows(): mine = lax.psum_scatter(sums, 'z', scatter_dimension=0, tiled=True)]
    all_gather x12, waiting for transfers between devices: 69 us -> 21.1 us  [whole(): lax.all_gather(part.reshape(-1, part.shape[-1]), 'z', axis=0, tiled=True)]
    pallas_call x4, Pallas kernels: 58.9 us -> 91.8 us  [attend_back(): pl.pallas_call(functools.partial(back_kernel, scale, scale2, bq, bk), gri...]
    pallas_call x4, Pallas kernels: 40.1 us -> 62.9 us  [attend(): pl.pallas_call(functools.partial(attend_kernel, scale2, bq, bk), grid_spe...]
    pallas_call x21 -> x22, Pallas kernels: 1310 us -> 1320 us  [plane_call(): pl.pallas_call(kernel, out_shape=out_shape, in_specs=in_specs, out_specs=...]
  transfers between devices with their start and end apart: 24 -> 24, of which waited for: 8 -> 5; matrix products, arithmetic and copies ran while one was open for 1% -> 1% of each run, Pallas kernels for 68% -> 75%
where the time goes in v5:
time: 1620 us; the launch traced here: 1610 us
  Pallas kernels  1480 us (91%)
  local copies, waits for them, and re-layouts  43.1 us (3%)
  waiting for transfers between devices  38.5 us (2%)
  other arithmetic  22.3 us (1%)
    pallas_call x22, Pallas kernels, plane_call(): pl.pallas_call(kernel, out_shape=out_shape, in_specs=in_specs, out_specs=...  1320 us
    pallas_call x4, Pallas kernels, attend_back(): pl.pallas_call(functools.partial(back_kernel, scale, scale2, bq, bk), gri...  91.8 us
    pallas_call x4, Pallas kernels, attend(): pl.pallas_call(functools.partial(attend_kernel, scale2, bq, bk), grid_spe...  62.9 us
  transfers between devices with their start and end apart: 24, of which 5 were waited for; matrix products, arithmetic and copies ran while one was open for 1% of the time, Pallas kernels for 75%

profile of v5, /device:TPU:2, one launch (start us, length us, event | category | flops | bytes accessed | tf_op | source)
XLA Modules:
  0.0 1606.0 jit_solution(10481015809841005839)
XLA Ops:
  13.6 4.2 concatenate.27
  17.8 25.1 %exchange.5 = bf16[8,192,640]{2,1,0:T(8,128)(2,1)} custom-call(bf16[8,192,640]{2,1,0:T(8,128)(2,1)} %bitcast.164), custom_call_target="tpu_custom_call" | custom-call | bytes 72000000 | tf_op jit(solution)/shard_map/exchange/pallas_call | solution.py:394
  49.2 1.9 slice.97.blocks
  53.6 3.0 slice.96.refs_0_
  56.6 33.4 %exchange.6 = bf16[8,192,896]{2,1,0:T(8,128)(2,1)} custom-call(bf16[8,192,896]{2,1,0:T(8,128)(2,1)} %slice.97.blocks), custom_call_target="tpu_custom_call" | custom-call | bytes 102000000 | tf_op jit(solution)/shard_map/exchange/pallas_call | solution.py:394
  90.1 3.3 fusion.4
  93.5 78.3 %exchange.7 = (bf16[8,192,640]{2,1,0:T(8,128)(2,1)}, bf16[256,1536]{1,0:T(8,128)(2,1)}) custom-call(bf16[8,192,640]{2,1,0:T(8,128)(2,1)} %slice.96.refs_0_, bf16[256,1536]{1,0:T(8,128)(2,1)} %bitcast.228), custom_call_target="tpu_custom_call" | custom-call | bytes 72000000 | tf_op jit(solution)/shard_map/exchange/pallas_call | solution.py:394
  171.7 2.8 fusion.5
  175.6 3.7 fusion
  181.6 1.9 select_maximum_fusion
  183.5 38.2 %attn_in.4 = (bf16[8,256,1536]{2,1,0:T(8,128)(2,1)}, bf16[2,8,256,128]{3,2,1,0:T(8,128)(2,1)}, bf16[8,256,128]{2,1,0:T(8,128)(2,1)}, bf16[8,256,128]{2,1,0:T(8,128)(2,1)}, f32[2,1536]{1,0:T(2,128)}) custom-call(bf16[256,1536]{1,0:T(8,128)(2,1)} %get-tuple-element.181.h, bf16[1536,640]{1,0:T(8,128)(2,1)} %all-gather.13.cloned.1.call-done.w_hbm.wa_hbm, ...), custom_call_target="tpu_custom_call" | custom-call | bytes 102000000 | tf_op jit(solution)/shard_map/attn_in/pallas_call | solution.py:394
  221.7 15.7 attend.4
  238.6 94.1 %mlp.4 = (f32[256,1536]{1,0:T(8,128)}, bf16[8,256,1536]{2,1,0:T(8,128)(2,1)}, bf16[8,256,1024]{2,1,0:T(8,128)(2,1)}, bf16[8,256,512]{2,1,0:T(8,128)(2,1)}, bf16[256,1536]{1,0:T(8,128)(2,1)}) custom-call(bf16[256,1536]{1,0:T(8,128)(2,1)} %get-tuple-element.181.h, bf16[8,256,192]{2,1,0:T(8,128)(2,1)} %bitcast.156, f32[2,1536]{1,0:T(2,128)} %get-tuple-element.188.gain, ...), custom_call_target="tpu_custom_call" | custom-call | bytes 288000000 | tf_op jit(solution)/shard_map/mlp/pallas_call | solution.py:394
  332.7 7.5 all-gather.21.cloned.1.call-done.w1_hbm
  340.2 35.5 %attn_in.5 = (bf16[8,256,1536]{2,1,0:T(8,128)(2,1)}, bf16[2,8,256,128]{3,2,1,0:T(8,128)(2,1)}, bf16[8,256,128]{2,1,0:T(8,128)(2,1)}, bf16[8,256,128]{2,1,0:T(8,128)(2,1)}, f32[2,1536]{1,0:T(2,128)}) custom-call(bf16[256,1536]{1,0:T(8,128)(2,1)} %get-tuple-element.194.h, bf16[1536,640]{1,0:T(8,128)(2,1)} %all-gather.19.cloned.1.call-done.w_hbm.wa_hbm, ...), custom_call_target="tpu_custom_call" | custom-call | bytes 102000000 | tf_op jit(solution)/shard_map/attn_in/pallas_call | solution.py:394
  375.8 15.7 attend.5
  392.7 93.8 %mlp.5 = (f32[256,1536]{1,0:T(8,128)}, bf16[8,256,1536]{2,1,0:T(8,128)(2,1)}, bf16[8,256,1024]{2,1,0:T(8,128)(2,1)}, bf16[8,256,512]{2,1,0:T(8,128)(2,1)}, bf16[256,1536]{1,0:T(8,128)(2,1)}) custom-call(bf16[256,1536]{1,0:T(8,128)(2,1)} %get-tuple-element.194.h, bf16[8,256,192]{2,1,0:T(8,128)(2,1)} %bitcast.158, f32[2,1536]{1,0:T(2,128)} %get-tuple-element.201.gain, ...), custom_call_target="tpu_custom_call" | custom-call | bytes 288000000 | tf_op jit(solution)/shard_map/mlp/pallas_call | solution.py:394
  486.6 6.7 all-gather.27.cloned.1.call-done.w1_hbm
  493.3 35.5 %attn_in.6 = (bf16[8,256,1536]{2,1,0:T(8,128)(2,1)}, bf16[2,8,256,128]{3,2,1,0:T(8,128)(2,1)}, bf16[8,256,128]{2,1,0:T(8,128)(2,1)}, bf16[8,256,128]{2,1,0:T(8,128)(2,1)}, f32[2,1536]{1,0:T(2,128)}) custom-call(bf16[256,1536]{1,0:T(8,128)(2,1)} %get-tuple-element.207.h, bf16[1536,640]{1,0:T(8,128)(2,1)} %all-gather.25.cloned.1.call-done.w_hbm.wa_hbm, ...), custom_call_target="tpu_custom_call" | custom-call | bytes 102000000 | tf_op jit(solution)/shard_map/attn_in/pallas_call | solution.py:394
  528.9 15.7 attend.6
  545.8 93.8 %mlp.6 = (f32[256,1536]{1,0:T(8,128)}, bf16[8,256,1536]{2,1,0:T(8,128)(2,1)}, bf16[8,256,1024]{2,1,0:T(8,128)(2,1)}, bf16[8,256,512]{2,1,0:T(8,128)(2,1)}, bf16[256,1536]{1,0:T(8,128)(2,1)}) custom-call(bf16[256,1536]{1,0:T(8,128)(2,1)} %get-tuple-element.207.h, bf16[8,256,192]{2,1,0:T(8,128)(2,1)} %bitcast.160, f32[2,1536]{1,0:T(2,128)} %get-tuple-element.214.gain, ...), custom_call_target="tpu_custom_call" | custom-call | bytes 288000000 | tf_op jit(solution)/shard_map/mlp/pallas_call | solution.py:394
  639.7 6.8 all-gather.33.cloned.1.call-done.refs_4_.refs_6_
  647.2 35.6 %attn_in.7 = (bf16[8,256,1536]{2,1,0:T(8,128)(2,1)}, bf16[2,8,256,128]{3,2,1,0:T(8,128)(2,1)}, bf16[8,256,128]{2,1,0:T(8,128)(2,1)}, bf16[8,256,128]{2,1,0:T(8,128)(2,1)}, f32[2,1536]{1,0:T(2,128)}) custom-call(bf16[256,1536]{1,0:T(8,128)(2,1)} %get-tuple-element.220.h.refs_0_, bf16[1536,640]{1,0:T(8,128)(2,1)} %all-gather.31.cloned.1.call-done.w_hbm.refs_3_.refs_8_, ...), custom_call_target="tpu_custom_call" | custom-call | bytes 102000000 | tf_op jit(solution)/shard_map/attn_in/pallas_call | solution.py:394
  682.8 15.7 attend.7
  698.5 110.7 %mlp.7 = (f32[256,1536]{1,0:T(8,128)}, bf16[8,256,1536]{2,1,0:T(8,128)(2,1)}, bf16[8,256,1024]{2,1,0:T(8,128)(2,1)}, bf16[8,256,512]{2,1,0:T(8,128)(2,1)}, bf16[...) custom-call(bf16[256,1536]{1,0:T(8,128)(2,1)} %get-tuple-element.220.h.refs_0_, bf16[8,256,192]{2,1,0:T(8,128)(2,1)} %bitcast.162, ...), custom_call_target="tpu_custom_call" | custom-call | bytes 288000000 | tf_op jit(solution)/shard_map/mlp/pallas_call | solution.py:394
  809.2 2.1 broadcast_select_fusion.refs_0_
  811.4 104.0 %mlp_back.3 = (f32[256,1536]{1,0:T(8,128)}, f32[1,1536]{1,0:T(1,128)}, bf16[8,256,1536]{2,1,0:T(8,128)(2,1)}, bf16[8,256,256]{2,1,0:T(8,128)(2,1)}, bf16[1536,10...) custom-call(bf16[256,1536]{1,0:T(8,128)(2,1)} %broadcast_select_fusion.refs_0_, ...), custom_call_target="tpu_custom_call" | custom-call | bytes 300000000 | tf_op jit(solution)/shard_map/mlp_back/pallas_call | solution.py:394
  915.4 22.9 %attend_back.4 = (bf16[2048,256]{1,0:T(8,128)(2,1)}, f32[2048,128]{1,0:T(8,128)}, f32[2048,128]{1,0:T(8,128)}) custom-call(s32[2,4]{1,0:T(2,128)} %pad_add_fusion.bounds, s32[1]{0:T(128)} %dynamic_slice.3.length, bf16[2,2048,128]{2,1,0:T(8,128)(2,1)} %bitcast.179, bf16[2048,128]{1,0:T(8,128)(2,1)} %bitcast.197, bf16[2048,128]{1,0:T(8,128)(2,1)} %bitcast.199, ...), custom_call_target="tpu_custom_call" | custom-call | bytes 65000000 | tf_op jit(solution)/shard_map/attend_back/pallas_call | solution.py:1037
  938.4 40.2 %attn_back.4 = (bf16[256,1536]{1,0:T(8,128)(2,1)}, bf16[1536,640]{1,0:T(8,128)(2,1)}) custom-call(bf16[256,1536]{1,0:T(8,128)(2,1)} %get-tuple-element.220.h.refs_0_, f32[256,1536]{1,0:T(8,128)} %get-tuple-element.236.dmid, f32[2,1536]{1,0:T(2,128)} %get-tuple-element.226.refs_2_.gain, f32[1,1536]{1,0:T(1,128)} %get-tuple-element.237.gain2_grad, ...), custom_call_target="tpu_custom_call" | custom-call | bytes 108000000 | tf_op jit(solution)/shard_map/attn_back/pallas_call | solution.py:394
  979.3 97.7 %mlp_back.4 = (f32[256,1536]{1,0:T(8,128)}, f32[1,1536]{1,0:T(1,128)}, bf16[8,256,1536]{2,1,0:T(8,128)(2,1)}, bf16[8,256,256]{2,1,0:T(8,128)(2,1)}, bf16[1536,10...) custom-call(bf16[256,1536]{1,0:T(8,128)(2,1)} %get-tuple-element.249.e, f32[256,1536]{1,0:T(8,128)} %get-tuple-element.250.mid, ...), custom_call_target="tpu_custom_call" | custom-call | bytes 300000000 | tf_op jit(solution)/shard_map/mlp_back/pallas_call | solution.py:394
  1077.1 23.1 %attend_back.5 = (bf16[2048,256]{1,0:T(8,128)(2,1)}, f32[2048,128]{1,0:T(8,128)}, f32[2048,128]{1,0:T(8,128)}) custom-call(s32[2,4]{1,0:T(2,128)} %pad_add_fusion.bounds, s32[1]{0:T(128)} %dynamic_slice.3.length, bf16[2,2048,128]{2,1,0:T(8,128)(2,1)} %bitcast.177, bf16[2048,128]{1,0:T(8,128)(2,1)} %bitcast.193, bf16[2048,128]{1,0:T(8,128)(2,1)} %bitcast.195, ...), custom_call_target="tpu_custom_call" | custom-call | bytes 65000000 | tf_op jit(solution)/shard_map/attend_back/pallas_call | solution.py:1037
  1100.2 40.0 %attn_back.5 = (bf16[256,1536]{1,0:T(8,128)(2,1)}, bf16[1536,640]{1,0:T(8,128)(2,1)}) custom-call(bf16[256,1536]{1,0:T(8,128)(2,1)} %get-tuple-element.207.h, f32[256,1536]{1,0:T(8,128)} %get-tuple-element.254.dmid, f32[2,1536]{1,0:T(2,128)} %get-tuple-element.214.gain, f32[1,1536]{1,0:T(1,128)} %get-tuple-element.255.gain2_grad, ...), custom_call_target="tpu_custom_call" | custom-call | bytes 108000000 | tf_op jit(solution)/shard_map/attn_back/pallas_call | solution.py:394
  1140.9 97.3 %mlp_back.5 = (f32[256,1536]{1,0:T(8,128)}, f32[1,1536]{1,0:T(1,128)}, bf16[8,256,1536]{2,1,0:T(8,128)(2,1)}, bf16[8,256,256]{2,1,0:T(8,128)(2,1)}, bf16[1536,10...) custom-call(bf16[256,1536]{1,0:T(8,128)(2,1)} %get-tuple-element.272.e, f32[256,1536]{1,0:T(8,128)} %get-tuple-element.273.mid, ...), custom_call_target="tpu_custom_call" | custom-call | bytes 300000000 | tf_op jit(solution)/shard_map/mlp_back/pallas_call | solution.py:394
  1238.3 22.9 %attend_back.6 = (bf16[2048,256]{1,0:T(8,128)(2,1)}, f32[2048,128]{1,0:T(8,128)}, f32[2048,128]{1,0:T(8,128)}) custom-call(s32[2,4]{1,0:T(2,128)} %pad_add_fusion.bounds, s32[1]{0:T(128)} %dynamic_slice.3.length, bf16[2,2048,128]{2,1,0:T(8,128)(2,1)} %bitcast.175, bf16[2048,128]{1,0:T(8,128)(2,1)} %bitcast.189, bf16[2048,128]{1,0:T(8,128)(2,1)} %bitcast.191, ...), custom_call_target="tpu_custom_call" | custom-call | bytes 65000000 | tf_op jit(solution)/shard_map/attend_back/pallas_call | solution.py:1037
  1261.2 39.8 %attn_back.6 = (bf16[256,1536]{1,0:T(8,128)(2,1)}, bf16[1536,640]{1,0:T(8,128)(2,1)}) custom-call(bf16[256,1536]{1,0:T(8,128)(2,1)} %get-tuple-element.194.h, f32[256,1536]{1,0:T(8,128)} %get-tuple-element.277.dmid, f32[2,1536]{1,0:T(2,128)} %get-tuple-element.201.gain, f32[1,1536]{1,0:T(1,128)} %get-tuple-element.278.gain2_grad, ...), custom_call_target="tpu_custom_call" | custom-call | bytes 108000000 | tf_op jit(solution)/shard_map/attn_back/pallas_call | solution.py:394
  1301.8 67.3 %mlp_back_alone.1 = (f32[256,1536]{1,0:T(8,128)}, f32[1,1536]{1,0:T(1,128)}, bf16[256,1536]{1,0:T(8,128)(2,1)}, bf16[1536,1024]{1,0:T(8,128)(2,1)}, bf16[1536,512]{1,0:T(8,128)(2,1)}) custom-call(bf16[256,1536]{1,0:T(8,128)(2,1)} %get-tuple-element.295.e, f32[256,1536]{1,0:T(8,128)} %get-tuple-element.296.mid, f32[2,1536]{1,0:T(2,128)} %get-tuple-element.188.gain, ...), custom_call_target="tpu_custom_call" | custom-call | bytes 204000000 | tf_op jit(solution)/shard_map/mlp_back_alone/pallas_call | solution.py:394
  1369.2 10.9 reduce-scatter.27.cloned.1.call-done
  1380.9 33.1 %dat_gather.1 = (bf16[8,256,1536]{2,1,0:T(8,128)(2,1)}, bf16[8,256,256]{2,1,0:T(8,128)(2,1)}) custom-call(bf16[256,1536]{1,0:T(8,128)(2,1)} %get-tuple-element.307.dat, bf16[1536,640]{1,0:T(8,128)(2,1)} %all-gather.13.cloned.1.call-done.w_hbm.wa_hbm), custom_call_target="tpu_custom_call" | custom-call | bytes 96000000 | tf_op jit(solution)/shard_map/dat_gather/pallas_call | solution.py:394
  1414.0 22.9 %attend_back.7 = (bf16[2048,256]{1,0:T(8,128)(2,1)}, f32[2048,128]{1,0:T(8,128)}, f32[2048,128]{1,0:T(8,128)}) custom-call(s32[2,4]{1,0:T(2,128)} %pad_add_fusion.bounds, s32[1]{0:T(128)} %dynamic_slice.3.length, bf16[2,2048,128]{2,1,0:T(8,128)(2,1)} %bitcast.173, bf16[2048,128]{1,0:T(8,128)(2,1)} %bitcast.185, bf16[2048,128]{1,0:T(8,128)(2,1)} %bitcast.187, ...), custom_call_target="tpu_custom_call" | custom-call | bytes 65000000 | tf_op jit(solution)/shard_map/attend_back/pallas_call | solution.py:1037
  1436.9 39.8 %attn_back.7 = (bf16[256,1536]{1,0:T(8,128)(2,1)}, bf16[1536,640]{1,0:T(8,128)(2,1)}) custom-call(bf16[256,1536]{1,0:T(8,128)(2,1)} %get-tuple-element.181.h, f32[256,1536]{1,0:T(8,128)} %get-tuple-element.300.dmid, f32[2,1536]{1,0:T(2,128)} %get-tuple-element.188.gain, f32[1,1536]{1,0:T(1,128)} %get-tuple-element.301.gain2_grad, ...), custom_call_target="tpu_custom_call" | custom-call | bytes 108000000 | tf_op jit(solution)/shard_map/attn_back/pallas_call | solution.py:394
  1476.8 1.8 reduce-scatter.31.cloned.1.call-done
  1481.2 2.5 pad_maximum_fusion
  1483.7 63.0 %exchange.8 = (bf16[8,192,1536]{2,1,0:T(8,128)(2,1)}, bf16[256,1536]{1,0:T(8,128)(2,1)}) custom-call(bf16[8,192,1536]{2,1,0:T(8,128)(2,1)} %bitcast.155, bf16[256,1536]{1,0:T(8,128)(2,1)} %get-tuple-element.327.refs_1_), custom_call_target="tpu_custom_call" | custom-call | bytes 174000000 | tf_op jit(solution)/shard_map/exchange/pallas_call | solution.py:394
  1546.7 2.6 pad_maximum_fusion.1
  1549.3 25.5 %exchange.9 = bf16[8,192,640]{2,1,0:T(8,128)(2,1)} custom-call(bf16[8,192,640]{2,1,0:T(8,128)(2,1)} %bitcast.165), custom_call_target="tpu_custom_call" | custom-call | bytes 72000000 | tf_op jit(solution)/shard_map/exchange/pallas_call | solution.py:394
  1574.8 1.8 convert_element_type.41
  1582.0 1.7 copy.45
  1588.8 7.6 finish.1
  (170 shorter events, 41.3 us)
Async XLA Ops:
  7.2 2.6 copy-start.13
  7.2 167.3 %all-gather.13.cloned.1.call-start = ((), (), s32[]{:S(2)}) async-start(), calls=%async_computation.12 | async-start | bytes 2457600 | tf_op jit(solution)/shard_map/all_gather | solution.py:1130
  9.3 1.3 copy-start.6
  17.8 25.1 %copy-start.2 = (f32[1,192,4096]{2,1,0:T(8,128)S(1)}, f32[1,192,4096]{2,1,0:T(8,128)}, u32[]{:S(2)}) copy-start(f32[1,192,4096]{2,1,0:T(8,128)} %param.21) | copy-start | bytes 9437188
  43.8 1.9 copy-start.3
  46.5 1.9 copy-start.4
  49.1 3.1 copy-start
  49.2 3.1 copy-start.1
  53.6 120.9 %all-gather.15.cloned.1.call-start = ((), (), s32[]{:S(2)}) async-start(), calls=%async_computation.13 | async-start | bytes 3440640 | tf_op jit(solution)/shard_map/all_gather | solution.py:1130
  93.4 145.2 %all-gather.17.cloned.1.call-start = ((), (), s32[]{:S(2)}) async-start(), calls=%async_computation.14 | async-start | bytes 2457600 | tf_op jit(solution)/shard_map/all_gather | solution.py:1130
  171.7 3.3 copy-start.21
  174.6 158.1 %all-gather.19.cloned.1.call-start = ((), (), s32[]{:S(2)}) async-start(), calls=%async_computation.15 | async-start | bytes 2457600 | tf_op jit(solution)/shard_map/all_gather | solution.py:1130
  237.5 102.7 %all-gather.21.cloned.1.call-start = ((), (), s32[]{:S(2)}) async-start(), calls=%async_computation.16 | async-start | bytes 3440640 | tf_op jit(solution)/shard_map/all_gather | solution.py:1130
  238.0 154.7 %all-gather.23.cloned.1.call-start = ((), (), s32[]{:S(2)}) async-start(), calls=%async_computation.17 | async-start | bytes 2457600 | tf_op jit(solution)/shard_map/all_gather | solution.py:1130
  340.2 146.4 %all-gather.25.cloned.1.call-start = ((), (), s32[]{:S(2)}) async-start(), calls=%async_computation.18 | async-start | bytes 2457600 | tf_op jit(solution)/shard_map/all_gather | solution.py:1130
  391.5 101.7 %all-gather.27.cloned.1.call-start = ((), (), s32[]{:S(2)}) async-start(), calls=%async_computation.19 | async-start | bytes 3440640 | tf_op jit(solution)/shard_map/all_gather | solution.py:1130
  392.3 153.6 %all-gather.29.cloned.1.call-start = ((), (), s32[]{:S(2)}) async-start(), calls=%async_computation.20 | async-start | bytes 2457600 | tf_op jit(solution)/shard_map/all_gather | solution.py:1130
  493.3 146.4 %all-gather.31.cloned.1.call-start = ((), (), s32[]{:S(2)}) async-start(), calls=%async_computation.21 | async-start | bytes 2457600 | tf_op jit(solution)/shard_map/all_gather | solution.py:1130
  544.6 101.8 %all-gather.33.cloned.1.call-start = ((), (), s32[]{:S(2)}) async-start(), calls=%async_computation.22 | async-start | bytes 3440640 | tf_op jit(solution)/shard_map/all_gather | solution.py:1130
  545.4 153.1 %all-gather.35.cloned.1.call-start = ((), (), s32[]{:S(2)}) async-start(), calls=%async_computation.23 | async-start | bytes 2457600 | tf_op jit(solution)/shard_map/all_gather | solution.py:1130
  646.5 332.1 %reduce-scatter.13.cloned.1.call-start = ((), (), s32[]{:S(2)}) async-start(), calls=%async_computation.24 | async-start | bytes 3932160 | tf_op jit(solution)/shard_map/reduce_scatter | solution.py:1133
  915.4 161.6 %reduce-scatter.17.cloned.1.call-start = ((), (), s32[]{:S(2)}) async-start(), calls=%async_computation.26 | async-start | bytes 1966080 | tf_op jit(solution)/shard_map/reduce_scatter | solution.py:1133
  978.6 98.4 %reduce-scatter.15.cloned.1.call-start = ((), (), s32[]{:S(2)}) async-start(), calls=%async_computation.25 | async-start | bytes 2457600 | tf_op jit(solution)/shard_map/reduce_scatter | solution.py:1133
  979.2 161.0 %reduce-scatter.19.cloned.1.call-start = ((), (), s32[]{:S(2)}) async-start(), calls=%async_computation.27 | async-start | bytes 3932160 | tf_op jit(solution)/shard_map/reduce_scatter | solution.py:1133
  1077.0 161.2 %reduce-scatter.23.cloned.1.call-start = ((), (), s32[]{:S(2)}) async-start(), calls=%async_computation.29 | async-start | bytes 1966080 | tf_op jit(solution)/shard_map/reduce_scatter | solution.py:1133
  1140.3 98.0 %reduce-scatter.21.cloned.1.call-start = ((), (), s32[]{:S(2)}) async-start(), calls=%async_computation.28 | async-start | bytes 2457600 | tf_op jit(solution)/shard_map/reduce_scatter | solution.py:1133
  1140.8 160.2 %reduce-scatter.25.cloned.1.call-start = ((), (), s32[]{:S(2)}) async-start(), calls=%async_computation.30 | async-start | bytes 3932160 | tf_op jit(solution)/shard_map/reduce_scatter | solution.py:1133
  1238.3 130.9 %reduce-scatter.29.cloned.1.call-start = ((), (), s32[]{:S(2)}) async-start(), calls=%async_computation.32 | async-start | bytes 1966080 | tf_op jit(solution)/shard_map/reduce_scatter | solution.py:1133
  1301.1 79.1 %reduce-scatter.27.cloned.1.call-start = ((), (), s32[]{:S(2)}) async-start(), calls=%async_computation.31 | async-start | bytes 2457600 | tf_op jit(solution)/shard_map/reduce_scatter | solution.py:1133
  1301.8 175.0 %reduce-scatter.33.cloned.1.call-start = ((), (), s32[]{:S(2)}) async-start(), calls=%async_computation.34 | async-start | bytes 1966080 | tf_op jit(solution)/shard_map/reduce_scatter | solution.py:1133
  1380.1 98.4 %reduce-scatter.31.cloned.1.call-start = ((), (), s32[]{:S(2)}) async-start(), calls=%async_computation.33 | async-start | bytes 3932160 | tf_op jit(solution)/shard_map/reduce_scatter | solution.py:1133
  1380.9 165.8 %reduce-scatter.35.cloned.1.call-start = ((), (), s32[]{:S(2)}) async-start(), calls=%async_computation.35 | async-start | bytes 2457600 | tf_op jit(solution)/shard_map/reduce_scatter | solution.py:1133
  1476.8 1.8 copy-start.9
  1476.8 1.8 copy-start.17
  1478.6 1.1 copy-start.10
  1478.6 1.2 copy-start.18
  1478.6 1.5 copy-start.11
  1478.6 1.5 copy-start.19
  1479.8 1.2 copy-start.12
  1479.8 1.3 copy-start.20
  1483.7 63.0 %copy-start.14 = (bf16[384,640]{1,0:T(8,128)(2,1)S(1)}, bf16[384,640]{1,0:T(8,128)(2,1)}, u32[]{:S(2)}) copy-start(bf16[384,640]{1,0:T(8,128)(2,1)} %reduce-scatter.15.cloned.1.call-done) | copy-start | bytes 1474564
  1483.7 63.0 %copy-start.15 = (bf16[384,640]{1,0:T(8,128)(2,1)S(1)}, bf16[384,640]{1,0:T(8,128)(2,1)}, u32[]{:S(2)}) copy-start(bf16[384,640]{1,0:T(8,128)(2,1)} %reduce-scatter.21.cloned.1.call-done) | copy-start | bytes 1474564
  1483.7 63.0 %copy-start.16 = (bf16[384,640]{1,0:T(8,128)(2,1)S(1)}, bf16[384,640]{1,0:T(8,128)(2,1)}, u32[]{:S(2)}) copy-start(bf16[384,640]{1,0:T(8,128)(2,1)} %reduce-scatter.27.cloned.1.call-done) | copy-start | bytes 1474564
  1582.0 2.8 copy-start.5
  1588.8 7.6 copy-start.7
  1596.4 1.4 copy-start.8
Sparse Core Ops, SparseCore 0:
  53.7 44.7 all-gather.12
  100.6 58.4 all-gather.14
  174.7 47.6 all-gather.16
  237.6 44.6 all-gather.18
  284.3 55.8 all-gather.20
  341.6 42.2 all-gather.22
  391.6 43.5 all-gather.24
  437.4 55.8 all-gather.26
  494.8 42.2 all-gather.28
  544.8 43.6 all-gather.30
  590.6 55.8 all-gather.32
  647.9 42.2 all-gather.34
  915.5 59.3 reduce-scatter.12
  978.8 33.5 reduce-scatter.16
  1014.5 40.3 reduce-scatter.14
  1077.2 58.5 reduce-scatter.18
  1140.4 34.5 reduce-scatter.22
  1177.2 40.4 reduce-scatter.20
  1238.4 59.9 reduce-scatter.24
  1301.2 36.0 reduce-scatter.28
  1339.6 40.4 reduce-scatter.26
  1382.4 34.5 reduce-scatter.32
  1419.3 59.2 reduce-scatter.30
  1480.7 56.6 reduce-scatter.34

commit v6 on v5

--- a/solution.py
+++ b/solution.py
@@ -570,7 +570,7 @@
 
 def mlp_back_kernel(
     ff, step, homeward, e, mid, gain, gu_hbm, hid_hbm, a2_hbm, w1_hbm, w2_hbm, wa_hbm, dmid_out, gain_out, dat_out, dob_out,
-    gu_sums, d_sums, full, full2, parts, a2, gu, hid, wm, wa, total, stage, send1, recv1,
+    first_sums, second_sums, full, full2, parts, a2, gu, hid, wm, wa, total, stage, send1, recv1,
     from_c, via_x, via_y, from_x, from_y, send2, recv2, send3, recv3, local, swap=None, alone=False,
 ):
     here = token_place()
@@ -607,6 +607,7 @@
     hid_load.wait()
     sums = []
     count = full.shape[2] // step
+    middle = first_sums.shape[1]
 
     def beside(turn_number):
         half = (count + 1) // 2
@@ -621,8 +622,8 @@
             rows = pl.ds(number * step, step)
             sums.append(
                 [
-                    loads.start(held.at[:, pl.ds(0, 2 * ff)], gu_sums.at[rows]),
-                    loads.start(held.at[:, pl.ds(2 * ff, ff)], d_sums.at[rows]),
+                    loads.start(held.at[:, pl.ds(0, middle)], first_sums.at[rows]),
+                    loads.start(held.at[:, pl.ds(middle, 3 * ff - middle)], second_sums.at[rows]),
                 ]
             )
 
@@ -690,11 +691,11 @@
 
 def mlp_back_alone_kernel(
     ff, step, homeward, e, mid, gain, gu_hbm, hid_hbm, a2_hbm, w1_hbm, w2_hbm, dmid_out, gain_out, dat_out,
-    gu_sums, d_sums, full, parts, a2, gu, hid, wm, total, stage, *rest
+    first_sums, second_sums, full, parts, a2, gu, hid, wm, total, stage, *rest
 ):
     mlp_back_kernel(
         ff, step, homeward, e, mid, gain, gu_hbm, hid_hbm, a2_hbm, w1_hbm, w2_hbm, None, dmid_out, gain_out,
-        dat_out, None, gu_sums, d_sums, full, None, parts, a2, gu, hid, wm, None, total, stage,
+        dat_out, None, first_sums, second_sums, full, None, parts, a2, gu, hid, wm, None, total, stage,
         *rest[:-1], None, None, rest[-1], alone=True,
     )
 
@@ -711,8 +712,8 @@
             jax.ShapeDtypeStruct((block, width), F32),
             jax.ShapeDtypeStruct((1, width), F32),
             jax.ShapeDtypeStruct((block, width), BF),
-            jax.ShapeDtypeStruct((width, 2 * ff), BF),
-            jax.ShapeDtypeStruct((width, ff), BF),
+            jax.ShapeDtypeStruct((width, 3 * ff // 2), BF),
+            jax.ShapeDtypeStruct((width, 3 * ff // 2), BF),
         ],
         [IN_VMEM, IN_VMEM, IN_VMEM, ANYWHERE, ANYWHERE],
         [IN_VMEM, IN_VMEM, IN_VMEM] + [ANYWHERE] * 5,
@@ -748,8 +749,8 @@
             jax.ShapeDtypeStruct((1, width), F32),
             jax.ShapeDtypeStruct((8, block, width), BF),
             jax.ShapeDtypeStruct((8, block, cols), BF),
-            jax.ShapeDtypeStruct((width, 2 * ff), BF),
-            jax.ShapeDtypeStruct((width, ff), BF),
+            jax.ShapeDtypeStruct((width, 3 * ff // 2), BF),
+            jax.ShapeDtypeStruct((width, 3 * ff // 2), BF),
         ],
         [IN_VMEM, IN_VMEM, ANYWHERE, IN_VMEM, ANYWHERE, ANYWHERE],
         [IN_VMEM, IN_VMEM, IN_VMEM] + [ANYWHERE] * 6,
@@ -926,6 +927,47 @@
         out_specs=[pl.BlockSpec((rows, ff), lambda i: (0, i))] * 3,
         compiler_params=pltpu.CompilerParams(vmem_limit_bytes=VMEM_LIMIT),
         name="finish",
+    )(got)
+
+
+def finish_attn_kernel(got, query, key, value, out, gains):
+    ranks = got.shape[0]
+
+    def lanes(t, n):
+        return got[t, :, n * LANES : (n + 1) * LANES].astype(F32)
+
+    groups = [four_heads(*(lanes(t, n) for n in range(3))) for t in range(ranks)]
+
+    def write(ref, heads):
+        for n in range(0, len(heads), 4):
+            for j, part in enumerate(three_lanes(heads[n : n + 4])):
+                at = n * HEAD_SIZE + j * LANES
+                ref[:, at : at + LANES] = part
+
+    write(query, [head for group in groups for head in group[:2]])
+    write(key, [group[2] for group in groups])
+    write(value, [group[3] for group in groups])
+    out_heads = []
+    total = None
+    for t in range(ranks):
+        a, b = lanes(t, 3), lanes(t, 4)
+        out_heads += [a, pltpu.roll(jnp.where(lane(a) >= HEAD_SIZE, a, b), LANES - HEAD_SIZE, 1)]
+        total = b if total is None else total + b
+    write(out, out_heads)
+    first = GAIN_AT - PACK + LANES
+    gains[...] = total.T[first : first + 2]
+
+
+def finish_attn(got):
+    ranks, rows, _ = got.shape
+    wide, narrow = jax.ShapeDtypeStruct((rows, ranks * OUT), F32), jax.ShapeDtypeStruct((rows, ranks * HEAD_SIZE), F32)
+    return pl.pallas_call(
+        finish_attn_kernel,
+        out_shape=[wide, narrow, narrow, wide, jax.ShapeDtypeStruct((2, rows), F32)],
+        in_specs=[IN_VMEM],
+        out_specs=[IN_VMEM] * 5,
+        compiler_params=pltpu.CompilerParams(vmem_limit_bytes=VMEM_LIMIT),
+        name="finish_attn",
     )(got)
 
 
@@ -1136,13 +1178,13 @@
             return lax.psum_scatter(mine, "e", scatter_dimension=1, tiled=False)
         return mine[:, 0]
 
-    cut = 3 * ff_cols * 7 // 12 // LANES * LANES
+    cut = 3 * ff_cols // 2
     mlp_blocks = ready(mlp_pack)
-    (attn_got,) = exchange(4, ready(attn_pack))
+    attn_got, hidden_state = exchange(4, ready(attn_pack), inputs[0])
     first_blocks, attn_got = together(mlp_blocks[..., :cut], attn_got)
     (first_got,) = exchange(5, first_blocks)
     second_blocks, first_got = together(mlp_blocks[..., cut:], first_got)
-    second_got, hidden_state = exchange(6, second_blocks, inputs[0])
+    (second_got,) = exchange(6, second_blocks)
     attn_parts, first_parts, second_parts = by_layer(attn_got), by_layer(first_got), by_layer(second_got)
 
     token_x, token_c, token_y = token_place()
@@ -1207,29 +1249,29 @@
     (e,) = moved
     e = jnp.where((my_positions < length)[:, None], e, jnp.zeros_like(e))
     attn_grads = [None] * layers
-    gu_grads = [None] * layers
-    d_grads = [None] * layers
+    first_grads = [None] * layers
+    second_grads = [None] * layers
     for layer in reversed(range(layers)):
         (h, a1, q, k, v, o, log_total, mid, a2, gu, hid, attn_w, w_1, w_2, gain) = saved[layer]
         if layer > 0:
-            dmid, gain2, dat, dob, gu_sums, d_sums, *moved = mlp_back(
+            dmid, gain2, dat, dob, first_sums, second_sums, *moved = mlp_back(
                 e, mid, gain, gu, hid, a2, w_1, w_2, attn_w, output if layer + 1 == layers else None
             )
             if moved:
                 (output,) = moved
         else:
-            dmid, gain2, dat, gu_sums, d_sums = mlp_back_alone(e, mid, gain, gu, hid, a2, w_1, w_2)
-            dat, gu_sums, d_sums, attn_grads[1], d_grads[1] = together(
-                dat, gu_sums, d_sums, attn_grads[1], d_grads[1]
+            dmid, gain2, dat, first_sums, second_sums = mlp_back_alone(e, mid, gain, gu, hid, a2, w_1, w_2)
+            dat, first_sums, second_sums, attn_grads[1], second_grads[1] = together(
+                dat, first_sums, second_sums, attn_grads[1], second_grads[1]
             )
             dat, dob = dat_gather(dat, attn_w)
         if 0 < layer < layers - 1:
-            dob, gu_sums, d_sums, attn_grads[layer + 1], d_grads[layer + 1] = together(
-                dob, gu_sums, d_sums, attn_grads[layer + 1], d_grads[layer + 1]
+            dob, first_sums, second_sums, attn_grads[layer + 1], second_grads[layer + 1] = together(
+                dob, first_sums, second_sums, attn_grads[layer + 1], second_grads[layer + 1]
             )
-        gu_grads[layer] = reduce_rows(gu_sums)
+        first_grads[layer] = reduce_rows(first_sums)
         if layer == 0:
-            d_grads[layer] = reduce_rows(d_sums)
+            second_grads[layer] = reduce_rows(second_sums)
         dq, dk, dv = attend_back(
             q, k, v, query_rows, o, flat(dob), log_total, cosine, sine, bounds, length1, bq, bk, scale, scale2
         )
@@ -1239,35 +1281,30 @@
             o.reshape(ranks, block, -1), a1, dat, attn_w,
         )
         if layer > 0:
-            e, attn_sums, d_sums, gu_grads[layer] = together(e, attn_sums, d_sums, gu_grads[layer])
-            d_grads[layer] = reduce_rows(d_sums)
+            e, attn_sums, second_sums, first_grads[layer] = together(e, attn_sums, second_sums, first_grads[layer])
+            second_grads[layer] = reduce_rows(second_sums)
         else:
-            e, attn_sums, gu_grads[layer], d_grads[layer] = together(e, attn_sums, gu_grads[layer], d_grads[layer])
+            e, attn_sums, first_grads[layer], second_grads[layer] = together(e, attn_sums, first_grads[layer], second_grads[layer])
         attn_grads[layer] = reduce_rows(attn_sums)
 
     def by_place(grads):
         return jnp.stack(grads).reshape(ranks, rows, -1)
 
-    mlp_blocks = by_place([jnp.concatenate(pair, axis=2) for pair in zip(gu_grads, d_grads)])
-    mlp_home, input_grad = exchange(7, mlp_blocks, e, True)
+    mlp_blocks = by_place([jnp.concatenate(pair, axis=2) for pair in zip(first_grads, second_grads)])
+    (mlp_home,) = exchange(7, mlp_blocks)
     attn_blocks, mlp_home = together(by_place(attn_grads), mlp_home)
-    (attn_home,) = exchange(10, attn_blocks)
+    attn_home, input_grad = exchange(10, attn_blocks, e, True)
     grad_gate, grad_up, grad_down = finish(mlp_home)
-    attn_home = attn_home.astype(F32)
-    gain_sums = jnp.sum(attn_home[:, :, GAIN_AT : GAIN_AT + 2], axis=0)
-
-    def columns(start, count):
-        return jnp.swapaxes(attn_home[:, :, start : start + count], 0, 1).reshape(rows, ranks * count)
-
+    grad_query, grad_key, grad_value, grad_out, gain_sums = finish_attn(attn_home)
     return (
         output[None],
         input_grad[None],
-        gain_sums[:, 0][None],
-        columns(0, q_cols)[None],
-        columns(q_cols, kv_cols)[None],
-        columns(q_cols + kv_cols, kv_cols)[None],
-        columns(QKV, OUT).T[None],
-        gain_sums[:, 1][None],
+        gain_sums[0:1],
+        grad_query[None],
+        grad_key[None],
+        grad_value[None],
+        grad_out.T[None],
+        gain_sums[1:2],
         grad_gate[None],
         grad_up[None],
         grad_down.T[None],

time: 1620 us -> 1600 us (0.988)
  Pallas kernels: 1480 us -> 1390 us
  waiting for transfers between devices: 38.5 us -> 121 us
    reduce_scatter x12, waiting for transfers between devices: 12.9 us -> 67.4 us  [reduce_rows(): mine = lax.psum_scatter(sums, 'z', scatter_dimension=0, tiled=True)]
    pallas_call x22, Pallas kernels: 1320 us -> 1280 us  [plane_call(): pl.pallas_call(kernel, out_shape=out_shape, in_specs=in_specs, out_specs=...]
    pallas_call x4, Pallas kernels: 91.8 us -> 58.9 us  [attend_back(): pl.pallas_call(functools.partial(back_kernel, scale, scale2, bq, bk), gri...]
    all_gather x12, waiting for transfers between devices: 21.1 us -> 48.8 us  [whole(): lax.all_gather(part.reshape(-1, part.shape[-1]), 'z', axis=0, tiled=True)]
    pallas_call x4, Pallas kernels: 62.9 us -> 40.1 us  [attend(): pl.pallas_call(functools.partial(attend_kernel, scale2, bq, bk), grid_spe...]
  transfers between devices with their start and end apart: 24 -> 24, of which waited for: 5 -> 13; matrix products, arithmetic and copies ran while one was open for 1% -> 1% of each run, Pallas kernels for 75% -> 69%
where the time goes in v6:
time: 1600 us; the launch traced here: 1580 us
  Pallas kernels  1390 us (87%)
  waiting for transfers between devices  121 us (8%)
  local copies, waits for them, and re-layouts  29 us (2%)
  other arithmetic  22.3 us (1%)
    pallas_call x22, Pallas kernels, plane_call(): pl.pallas_call(kernel, out_shape=out_shape, in_specs=in_specs, out_specs=...  1280 us
    reduce_scatter x12, waiting for transfers between devices, reduce_rows(): mine = lax.psum_scatter(sums, 'z', scatter_dimension=0, tiled=True)  67.4 us
    pallas_call x4, Pallas kernels, attend_back(): pl.pallas_call(functools.partial(back_kernel, scale, scale2, bq, bk), gri...  58.9 us
    all_gather x12, waiting for transfers between devices, whole(): lax.all_gather(part.reshape(-1, part.shape[-1]), 'z', axis=0, tiled=True)  48.8 us
    pallas_call x4, Pallas kernels, attend(): pl.pallas_call(functools.partial(attend_kernel, scale2, bq, bk), grid_spe...  40.1 us
  transfers between devices with their start and end apart: 24, of which 13 were waited for; matrix products, arithmetic and copies ran while one was open for 1% of the time, Pallas kernels for 69%

profile of v6, /device:TPU:2, one launch (start us, length us, event | category | flops | bytes accessed | tf_op | source)
XLA Modules:
  0.0 1582.9 jit_solution(16836126876846928889)
XLA Ops:
  21.5 2.7 fusion.4
  24.3 4.2 concatenate.26
  28.5 42.9 %exchange.5 = (bf16[8,192,640]{2,1,0:T(8,128)(2,1)}, bf16[256,1536]{1,0:T(8,128)(2,1)}) custom-call(bf16[8,192,640]{2,1,0:T(8,128)(2,1)} %bitcast.157, bf16[256,1536]{1,0:T(8,128)(2,1)} %bitcast.220), custom_call_target="tpu_custom_call" | custom-call | bytes 72000000 | tf_op jit(solution)/shard_map/exchange/pallas_call | solution.py:394
  71.5 2.8 fusion.7
  74.3 29.3 %exchange.6 = bf16[8,192,768]{2,1,0:T(8,128)(2,1)} custom-call(bf16[8,192,768]{2,1,0:T(8,128)(2,1)} %get-tuple-element.183.blocks), custom_call_target="tpu_custom_call" | custom-call | bytes 87000000 | tf_op jit(solution)/shard_map/exchange/pallas_call | solution.py:394
  103.6 3.0 fusion.6
  106.8 29.4 %exchange.7 = bf16[8,192,768]{2,1,0:T(8,128)(2,1)} custom-call(bf16[8,192,768]{2,1,0:T(8,128)(2,1)} %get-tuple-element.185.blocks), custom_call_target="tpu_custom_call" | custom-call | bytes 87000000 | tf_op jit(solution)/shard_map/exchange/pallas_call | solution.py:394
  136.2 3.0 fusion.5
  139.3 29.9 %all-gather.15.cloned.1.call-done.w1_hbm = bf16[1536,768]{1,0:T(8,128)(2,1)} async-done(((bf16[384,768]{1,0:T(8,128)(2,1)}), bf16[1536,768]{1,0:T(8,128)(2,1)}) %all-gather.15.cloned.1.call-update) | async-done | bytes 2359312 | tf_op jit(solution)/shard_map/all_gather | solution.py:1172
  170.2 3.7 fusion
  178.1 35.7 %attn_in.4 = (bf16[8,256,1536]{2,1,0:T(8,128)(2,1)}, bf16[2,8,256,128]{3,2,1,0:T(8,128)(2,1)}, bf16[8,256,128]{2,1,0:T(8,128)(2,1)}, bf16[8,256,128]{2,1,0:T(8,128)(2,1)}, f32[2,1536]{1,0:T(2,128)}) custom-call(bf16[256,1536]{1,0:T(8,128)(2,1)} %get-tuple-element.186.h, bf16[1536,640]{1,0:T(8,128)(2,1)} %all-gather.13.cloned.1.call-done.w_hbm.wa_hbm, ...), custom_call_target="tpu_custom_call" | custom-call | bytes 102000000 | tf_op jit(solution)/shard_map/attn_in/pallas_call | solution.py:394
  213.8 10.0 attend.4
  225.0 93.8 %mlp.4 = (f32[256,1536]{1,0:T(8,128)}, bf16[8,256,1536]{2,1,0:T(8,128)(2,1)}, bf16[8,256,1024]{2,1,0:T(8,128)(2,1)}, bf16[8,256,512]{2,1,0:T(8,128)(2,1)}, bf16[256,1536]{1,0:T(8,128)(2,1)}) custom-call(bf16[256,1536]{1,0:T(8,128)(2,1)} %get-tuple-element.186.h, bf16[8,256,192]{2,1,0:T(8,128)(2,1)} %bitcast.149, f32[2,1536]{1,0:T(2,128)} %get-tuple-element.193.gain, ...), custom_call_target="tpu_custom_call" | custom-call | bytes 288000000 | tf_op jit(solution)/shard_map/mlp/pallas_call | solution.py:394
  318.9 4.3 all-gather.21.cloned.1.call-done.w1_hbm
  323.2 35.5 %attn_in.5 = (bf16[8,256,1536]{2,1,0:T(8,128)(2,1)}, bf16[2,8,256,128]{3,2,1,0:T(8,128)(2,1)}, bf16[8,256,128]{2,1,0:T(8,128)(2,1)}, bf16[8,256,128]{2,1,0:T(8,128)(2,1)}, f32[2,1536]{1,0:T(2,128)}) custom-call(bf16[256,1536]{1,0:T(8,128)(2,1)} %get-tuple-element.199.h, bf16[1536,640]{1,0:T(8,128)(2,1)} %all-gather.19.cloned.1.call-done.w_hbm.wa_hbm, ...), custom_call_target="tpu_custom_call" | custom-call | bytes 102000000 | tf_op jit(solution)/shard_map/attn_in/pallas_call | solution.py:394
  358.7 10.0 attend.5
  370.0 4.5 all-gather.23.cloned.1.call-done.w2_hbm
  374.5 95.7 %mlp.5 = (f32[256,1536]{1,0:T(8,128)}, bf16[8,256,1536]{2,1,0:T(8,128)(2,1)}, bf16[8,256,1024]{2,1,0:T(8,128)(2,1)}, bf16[8,256,512]{2,1,0:T(8,128)(2,1)}, bf16[256,1536]{1,0:T(8,128)(2,1)}) custom-call(bf16[256,1536]{1,0:T(8,128)(2,1)} %get-tuple-element.199.h, bf16[8,256,192]{2,1,0:T(8,128)(2,1)} %bitcast.151, f32[2,1536]{1,0:T(2,128)} %get-tuple-element.206.gain, ...), custom_call_target="tpu_custom_call" | custom-call | bytes 288000000 | tf_op jit(solution)/shard_map/mlp/pallas_call | solution.py:394
  470.9 35.5 %attn_in.6 = (bf16[8,256,1536]{2,1,0:T(8,128)(2,1)}, bf16[2,8,256,128]{3,2,1,0:T(8,128)(2,1)}, bf16[8,256,128]{2,1,0:T(8,128)(2,1)}, bf16[8,256,128]{2,1,0:T(8,128)(2,1)}, f32[2,1536]{1,0:T(2,128)}) custom-call(bf16[256,1536]{1,0:T(8,128)(2,1)} %get-tuple-element.212.h, bf16[1536,640]{1,0:T(8,128)(2,1)} %all-gather.25.cloned.1.call-done.w_hbm.wa_hbm, ...), custom_call_target="tpu_custom_call" | custom-call | bytes 102000000 | tf_op jit(solution)/shard_map/attn_in/pallas_call | solution.py:394
  506.5 10.0 attend.6
  517.7 4.1 all-gather.29.cloned.1.call-done.w2_hbm
  521.8 95.7 %mlp.6 = (f32[256,1536]{1,0:T(8,128)}, bf16[8,256,1536]{2,1,0:T(8,128)(2,1)}, bf16[8,256,1024]{2,1,0:T(8,128)(2,1)}, bf16[8,256,512]{2,1,0:T(8,128)(2,1)}, bf16[256,1536]{1,0:T(8,128)(2,1)}) custom-call(bf16[256,1536]{1,0:T(8,128)(2,1)} %get-tuple-element.212.h, bf16[8,256,192]{2,1,0:T(8,128)(2,1)} %bitcast.153, f32[2,1536]{1,0:T(2,128)} %get-tuple-element.219.gain, ...), custom_call_target="tpu_custom_call" | custom-call | bytes 288000000 | tf_op jit(solution)/shard_map/mlp/pallas_call | solution.py:394
  619.3 35.6 %attn_in.7 = (bf16[8,256,1536]{2,1,0:T(8,128)(2,1)}, bf16[2,8,256,128]{3,2,1,0:T(8,128)(2,1)}, bf16[8,256,128]{2,1,0:T(8,128)(2,1)}, bf16[8,256,128]{2,1,0:T(8,128)(2,1)}, f32[2,1536]{1,0:T(2,128)}) custom-call(bf16[256,1536]{1,0:T(8,128)(2,1)} %get-tuple-element.225.h.refs_0_, bf16[1536,640]{1,0:T(8,128)(2,1)} %all-gather.31.cloned.1.call-done.w_hbm.refs_3_.refs_8_, ...), custom_call_target="tpu_custom_call" | custom-call | bytes 102000000 | tf_op jit(solution)/shard_map/attn_in/pallas_call | solution.py:394
  654.9 10.0 attend.7
  665.0 4.4 all-gather.35.cloned.1.call-done.refs_5_.refs_7_
  669.3 110.3 %mlp.7 = (f32[256,1536]{1,0:T(8,128)}, bf16[8,256,1536]{2,1,0:T(8,128)(2,1)}, bf16[8,256,1024]{2,1,0:T(8,128)(2,1)}, bf16[8,256,512]{2,1,0:T(8,128)(2,1)}, bf16[...) custom-call(bf16[256,1536]{1,0:T(8,128)(2,1)} %get-tuple-element.225.h.refs_0_, bf16[8,256,192]{2,1,0:T(8,128)(2,1)} %bitcast.155, ...), custom_call_target="tpu_custom_call" | custom-call | bytes 288000000 | tf_op jit(solution)/shard_map/mlp/pallas_call | solution.py:394
  781.7 103.7 %mlp_back.3 = (f32[256,1536]{1,0:T(8,128)}, f32[1,1536]{1,0:T(1,128)}, bf16[8,256,1536]{2,1,0:T(8,128)(2,1)}, bf16[8,256,256]{2,1,0:T(8,128)(2,1)}, bf16[1536,76...) custom-call(bf16[256,1536]{1,0:T(8,128)(2,1)} %broadcast_select_fusion.refs_0_, ...), custom_call_target="tpu_custom_call" | custom-call | bytes 300000000 | tf_op jit(solution)/shard_map/mlp_back/pallas_call | solution.py:394
  885.5 14.7 attend_back.4
  900.2 40.1 %attn_back.4 = (bf16[256,1536]{1,0:T(8,128)(2,1)}, bf16[1536,640]{1,0:T(8,128)(2,1)}) custom-call(bf16[256,1536]{1,0:T(8,128)(2,1)} %get-tuple-element.225.h.refs_0_, f32[256,1536]{1,0:T(8,128)} %get-tuple-element.241.dmid, f32[2,1536]{1,0:T(2,128)} %get-tuple-element.231.refs_2_.gain, f32[1,1536]{1,0:T(1,128)} %get-tuple-element.242.gain2_grad, ...), custom_call_target="tpu_custom_call" | custom-call | bytes 108000000 | tf_op jit(solution)/shard_map/attn_back/pallas_call | solution.py:394
  941.0 96.8 %mlp_back.4 = (f32[256,1536]{1,0:T(8,128)}, f32[1,1536]{1,0:T(1,128)}, bf16[8,256,1536]{2,1,0:T(8,128)(2,1)}, bf16[8,256,256]{2,1,0:T(8,128)(2,1)}, bf16[1536,76...) custom-call(bf16[256,1536]{1,0:T(8,128)(2,1)} %get-tuple-element.254.e, f32[256,1536]{1,0:T(8,128)} %get-tuple-element.255.mid, ...), custom_call_target="tpu_custom_call" | custom-call | bytes 300000000 | tf_op jit(solution)/shard_map/mlp_back/pallas_call | solution.py:394
  1039.9 14.9 attend_back.5
  1054.9 39.3 %attn_back.5 = (bf16[256,1536]{1,0:T(8,128)(2,1)}, bf16[1536,640]{1,0:T(8,128)(2,1)}) custom-call(bf16[256,1536]{1,0:T(8,128)(2,1)} %get-tuple-element.212.h, f32[256,1536]{1,0:T(8,128)} %get-tuple-element.259.dmid, f32[2,1536]{1,0:T(2,128)} %get-tuple-element.219.gain, f32[1,1536]{1,0:T(1,128)} %get-tuple-element.260.gain2_grad, ...), custom_call_target="tpu_custom_call" | custom-call | bytes 108000000 | tf_op jit(solution)/shard_map/attn_back/pallas_call | solution.py:394
  1096.4 95.8 %mlp_back.5 = (f32[256,1536]{1,0:T(8,128)}, f32[1,1536]{1,0:T(1,128)}, bf16[8,256,1536]{2,1,0:T(8,128)(2,1)}, bf16[8,256,256]{2,1,0:T(8,128)(2,1)}, bf16[1536,76...) custom-call(bf16[256,1536]{1,0:T(8,128)(2,1)} %get-tuple-element.277.e, f32[256,1536]{1,0:T(8,128)} %get-tuple-element.278.mid, ...), custom_call_target="tpu_custom_call" | custom-call | bytes 300000000 | tf_op jit(solution)/shard_map/mlp_back/pallas_call | solution.py:394
  1192.3 10.3 reduce-scatter.23.cloned.1.call-done
  1202.6 14.6 attend_back.6
  1217.2 39.6 %attn_back.6 = (bf16[256,1536]{1,0:T(8,128)(2,1)}, bf16[1536,640]{1,0:T(8,128)(2,1)}) custom-call(bf16[256,1536]{1,0:T(8,128)(2,1)} %get-tuple-element.199.h, f32[256,1536]{1,0:T(8,128)} %get-tuple-element.282.dmid, f32[2,1536]{1,0:T(2,128)} %get-tuple-element.206.gain, f32[1,1536]{1,0:T(1,128)} %get-tuple-element.283.gain2_grad, ...), custom_call_target="tpu_custom_call" | custom-call | bytes 108000000 | tf_op jit(solution)/shard_map/attn_back/pallas_call | solution.py:394
  1259.2 66.5 %mlp_back_alone.1 = (f32[256,1536]{1,0:T(8,128)}, f32[1,1536]{1,0:T(1,128)}, bf16[256,1536]{1,0:T(8,128)(2,1)}, bf16[1536,768]{1,0:T(8,128)(2,1)}, bf16[1536,768]{1,0:T(8,128)(2,1)}) custom-call(bf16[256,1536]{1,0:T(8,128)(2,1)} %get-tuple-element.300.e, f32[256,1536]{1,0:T(8,128)} %get-tuple-element.301.mid, f32[2,1536]{1,0:T(2,128)} %get-tuple-element.193.gain, ...), custom_call_target="tpu_custom_call" | custom-call | bytes 204000000 | tf_op jit(solution)/shard_map/mlp_back_alone/pallas_call | solution.py:394
  1325.7 40.5 %reduce-scatter.29.cloned.1.call-done = bf16[384,768]{1,0:T(8,128)(2,1)} async-done(((bf16[1536,768]{1,0:T(8,128)(2,1)}), bf16[384,768]{1,0:T(8,128)(2,1)}) %reduce-scatter.29.cloned.1.call-update) | async-done | bytes 589840 | tf_op jit(solution)/shard_map/reduce_scatter | solution.py:1175
  1367.0 33.1 %dat_gather.1 = (bf16[8,256,1536]{2,1,0:T(8,128)(2,1)}, bf16[8,256,256]{2,1,0:T(8,128)(2,1)}) custom-call(bf16[256,1536]{1,0:T(8,128)(2,1)} %get-tuple-element.312.dat, bf16[1536,640]{1,0:T(8,128)(2,1)} %all-gather.13.cloned.1.call-done.w_hbm.wa_hbm), custom_call_target="tpu_custom_call" | custom-call | bytes 96000000 | tf_op jit(solution)/shard_map/dat_gather/pallas_call | solution.py:394
  1400.1 14.7 attend_back.7
  1414.8 39.8 %attn_back.7 = (bf16[256,1536]{1,0:T(8,128)(2,1)}, bf16[1536,640]{1,0:T(8,128)(2,1)}) custom-call(bf16[256,1536]{1,0:T(8,128)(2,1)} %get-tuple-element.186.h, f32[256,1536]{1,0:T(8,128)} %get-tuple-element.305.dmid, f32[2,1536]{1,0:T(2,128)} %get-tuple-element.193.gain, f32[1,1536]{1,0:T(1,128)} %get-tuple-element.306.gain2_grad, ...), custom_call_target="tpu_custom_call" | custom-call | bytes 108000000 | tf_op jit(solution)/shard_map/attn_back/pallas_call | solution.py:394
  1454.7 11.3 reduce-scatter.33.cloned.1.call-done
  1467.7 2.5 pad_maximum_fusion
  1470.2 54.5 %exchange.8.got = bf16[8,192,1536]{2,1,0:T(8,128)(2,1)} custom-call(bf16[8,192,1536]{2,1,0:T(8,128)(2,1)} %bitcast.148), custom_call_target="tpu_custom_call" | custom-call | bytes 174000000 | tf_op jit(solution)/shard_map/exchange/pallas_call | solution.py:394
  1524.8 2.6 pad_maximum_fusion.1
  1527.4 33.4 %exchange.9 = (bf16[8,192,640]{2,1,0:T(8,128)(2,1)}, bf16[256,1536]{1,0:T(8,128)(2,1)}) custom-call(bf16[8,192,640]{2,1,0:T(8,128)(2,1)} %bitcast.158, bf16[256,1536]{1,0:T(8,128)(2,1)} %get-tuple-element.337.refs_1_), custom_call_target="tpu_custom_call" | custom-call | bytes 72000000 | tf_op jit(solution)/shard_map/exchange/pallas_call | solution.py:394
  1560.9 4.0 finish_attn.1
  1566.2 7.6 finish.1
  (150 shorter events, 40.7 us)
Async XLA Ops:
  7.2 2.7 copy-start.5
  7.2 132.1 %all-gather.13.cloned.1.call-start = ((), (), s32[]{:S(2)}) async-start(), calls=%async_computation.12 | async-start | bytes 2457600 | tf_op jit(solution)/shard_map/all_gather | solution.py:1172
  8.1 2.3 copy-start.2
  16.1 1.9 copy-start
  18.9 1.9 copy-start.1
  74.3 94.8 %all-gather.15.cloned.1.call-start = ((), (), s32[]{:S(2)}) async-start(), calls=%async_computation.13 | async-start | bytes 2949120 | tf_op jit(solution)/shard_map/all_gather | solution.py:1172
  106.7 118.3 %all-gather.17.cloned.1.call-start = ((), (), s32[]{:S(2)}) async-start(), calls=%async_computation.14 | async-start | bytes 2949120 | tf_op jit(solution)/shard_map/all_gather | solution.py:1172
  136.2 33.4 %copy-start.17 = (s32[4]{0:T(128)S(1)}, s32[4]{0:T(128)}, u32[]{:S(2)}) copy-start(s32[4]{0:T(128)} %param.13) | copy-start | bytes 52
  169.1 149.7 %all-gather.19.cloned.1.call-start = ((), (), s32[]{:S(2)}) async-start(), calls=%async_computation.15 | async-start | bytes 2457600 | tf_op jit(solution)/shard_map/all_gather | solution.py:1172
  223.9 99.3 %all-gather.21.cloned.1.call-start = ((), (), s32[]{:S(2)}) async-start(), calls=%async_computation.16 | async-start | bytes 2949120 | tf_op jit(solution)/shard_map/all_gather | solution.py:1172
  224.4 150.0 %all-gather.23.cloned.1.call-start = ((), (), s32[]{:S(2)}) async-start(), calls=%async_computation.17 | async-start | bytes 2949120 | tf_op jit(solution)/shard_map/all_gather | solution.py:1172
  323.2 147.0 %all-gather.25.cloned.1.call-start = ((), (), s32[]{:S(2)}) async-start(), calls=%async_computation.18 | async-start | bytes 2457600 | tf_op jit(solution)/shard_map/all_gather | solution.py:1172
  368.8 102.1 %all-gather.27.cloned.1.call-start = ((), (), s32[]{:S(2)}) async-start(), calls=%async_computation.19 | async-start | bytes 2949120 | tf_op jit(solution)/shard_map/all_gather | solution.py:1172
  369.5 152.3 %all-gather.29.cloned.1.call-start = ((), (), s32[]{:S(2)}) async-start(), calls=%async_computation.20 | async-start | bytes 2949120 | tf_op jit(solution)/shard_map/all_gather | solution.py:1172
  470.9 146.7 %all-gather.31.cloned.1.call-start = ((), (), s32[]{:S(2)}) async-start(), calls=%async_computation.21 | async-start | bytes 2457600 | tf_op jit(solution)/shard_map/all_gather | solution.py:1172
  516.5 102.1 %all-gather.33.cloned.1.call-start = ((), (), s32[]{:S(2)}) async-start(), calls=%async_computation.22 | async-start | bytes 2949120 | tf_op jit(solution)/shard_map/all_gather | solution.py:1172
  517.2 152.1 %all-gather.35.cloned.1.call-start = ((), (), s32[]{:S(2)}) async-start(), calls=%async_computation.23 | async-start | bytes 2949120 | tf_op jit(solution)/shard_map/all_gather | solution.py:1172
  618.6 321.8 %reduce-scatter.13.cloned.1.call-start = ((), (), s32[]{:S(2)}) async-start(), calls=%async_computation.24 | async-start | bytes 2949120 | tf_op jit(solution)/shard_map/reduce_scatter | solution.py:1175
  885.5 152.3 %reduce-scatter.15.cloned.1.call-start = ((), (), s32[]{:S(2)}) async-start(), calls=%async_computation.25 | async-start | bytes 2457600 | tf_op jit(solution)/shard_map/reduce_scatter | solution.py:1175
  940.4 99.5 %reduce-scatter.17.cloned.1.call-start = ((), (), s32[]{:S(2)}) async-start(), calls=%async_computation.26 | async-start | bytes 2949120 | tf_op jit(solution)/shard_map/reduce_scatter | solution.py:1175
  941.0 154.8 %reduce-scatter.19.cloned.1.call-start = ((), (), s32[]{:S(2)}) async-start(), calls=%async_computation.27 | async-start | bytes 2949120 | tf_op jit(solution)/shard_map/reduce_scatter | solution.py:1175
  1039.9 152.4 %reduce-scatter.21.cloned.1.call-start = ((), (), s32[]{:S(2)}) async-start(), calls=%async_computation.28 | async-start | bytes 2457600 | tf_op jit(solution)/shard_map/reduce_scatter | solution.py:1175
  1095.8 106.8 %reduce-scatter.23.cloned.1.call-start = ((), (), s32[]{:S(2)}) async-start(), calls=%async_computation.29 | async-start | bytes 2949120 | tf_op jit(solution)/shard_map/reduce_scatter | solution.py:1175
  1096.4 162.0 %reduce-scatter.25.cloned.1.call-start = ((), (), s32[]{:S(2)}) async-start(), calls=%async_computation.30 | async-start | bytes 2949120 | tf_op jit(solution)/shard_map/reduce_scatter | solution.py:1175
  1202.6 123.1 %reduce-scatter.27.cloned.1.call-start = ((), (), s32[]{:S(2)}) async-start(), calls=%async_computation.31 | async-start | bytes 2457600 | tf_op jit(solution)/shard_map/reduce_scatter | solution.py:1175
  1258.4 107.8 %reduce-scatter.29.cloned.1.call-start = ((), (), s32[]{:S(2)}) async-start(), calls=%async_computation.32 | async-start | bytes 2949120 | tf_op jit(solution)/shard_map/reduce_scatter | solution.py:1175
  1259.1 195.5 %reduce-scatter.31.cloned.1.call-start = ((), (), s32[]{:S(2)}) async-start(), calls=%async_computation.33 | async-start | bytes 2949120 | tf_op jit(solution)/shard_map/reduce_scatter | solution.py:1175
  1366.2 99.7 %reduce-scatter.33.cloned.1.call-start = ((), (), s32[]{:S(2)}) async-start(), calls=%async_computation.34 | async-start | bytes 2949120 | tf_op jit(solution)/shard_map/reduce_scatter | solution.py:1175
  1367.0 157.8 %reduce-scatter.35.cloned.1.call-start = ((), (), s32[]{:S(2)}) async-start(), calls=%async_computation.35 | async-start | bytes 2457600 | tf_op jit(solution)/shard_map/reduce_scatter | solution.py:1175
  1454.6 11.4 copy-start.6
  1454.6 11.4 copy-start.7
  1454.6 11.5 copy-start.8
  1454.6 11.5 copy-start.9
  1466.0 1.1 copy-start.10
  1466.0 1.2 copy-start.11
  1466.1 1.3 copy-start.12
  1466.1 1.5 copy-start.13
  1470.2 54.6 %copy-start.14 = (bf16[384,640]{1,0:T(8,128)(2,1)S(1)}, bf16[384,640]{1,0:T(8,128)(2,1)}, u32[]{:S(2)}) copy-start(bf16[384,640]{1,0:T(8,128)(2,1)} %reduce-scatter.15.cloned.1.call-done) | copy-start | bytes 1474564
  1470.2 54.6 %copy-start.15 = (bf16[384,640]{1,0:T(8,128)(2,1)S(1)}, bf16[384,640]{1,0:T(8,128)(2,1)}, u32[]{:S(2)}) copy-start(bf16[384,640]{1,0:T(8,128)(2,1)} %reduce-scatter.21.cloned.1.call-done) | copy-start | bytes 1474564
  1470.2 54.6 %copy-start.16 = (bf16[384,640]{1,0:T(8,128)(2,1)S(1)}, bf16[384,640]{1,0:T(8,128)(2,1)}, u32[]{:S(2)}) copy-start(bf16[384,640]{1,0:T(8,128)(2,1)} %reduce-scatter.27.cloned.1.call-done) | copy-start | bytes 1474564
  1566.2 7.7 copy-start.3
  1566.2 8.5 copy-start.4
Sparse Core Ops, SparseCore 0:
  74.4 43.1 all-gather.12
  119.7 49.3 all-gather.14
  171.3 49.2 all-gather.16
  224.0 47.7 all-gather.18
  273.8 49.3 all-gather.20
  325.1 49.2 all-gather.22
  376.0 43.2 all-gather.24
  421.5 49.3 all-gather.26
  472.4 49.3 all-gather.28
  523.2 43.8 all-gather.30
  569.2 49.3 all-gather.32
  620.0 49.2 all-gather.34
  885.6 49.5 reduce-scatter.12
  940.5 49.8 reduce-scatter.14
  992.6 47.2 reduce-scatter.16
  1042.0 53.6 reduce-scatter.18
  1097.9 55.1 reduce-scatter.20
  1155.2 47.2 reduce-scatter.22
  1204.8 53.4 reduce-scatter.24
  1260.5 56.0 reduce-scatter.26
  1318.9 47.2 reduce-scatter.28
  1368.5 47.5 reduce-scatter.30
  1418.4 47.5 reduce-scatter.32
  1468.1 40.9 reduce-scatter.34

commit v7 on v6

--- a/solution.py
+++ b/solution.py
@@ -57,7 +57,13 @@
 
 def token_place():
     x, c, y = place()
-    return xor(x, lax.rem(lax.axis_index("z"), 2)), c, y
+    z = lax.axis_index("z")
+    return xor(x, xor(lax.rem(z, 2), z // 2)), c, y
+
+
+def micro_of_plane():
+    z = lax.axis_index("z")
+    return lax.rem(z, 2) * 2 + z // 2
 
 
 def flip(index, by):
@@ -74,8 +80,9 @@
         x, c, _ = place()
         z = lax.axis_index("z")
         low = lax.rem(z, 2)
-        out = {"x": xor(z // 2, c), "c": low, "z": x * 2 + c}
-        back = {"x": z // 2, "c": low, "z": 2 * xor(x, low) + c}
+        high = z // 2
+        out = {"x": xor(high, xor(x, c)), "c": low, "z": c * 2 + x}
+        back = {"x": low, "c": high, "z": 2 * xor(x, xor(low, high)) + c}
         target, self.source = (back, out) if homeward else (out, back)
         self.away = (target["x"] != x) | (target["c"] != c) | (target["z"] != z)
         self.remote = pltpu.make_async_remote_copy(
@@ -569,9 +576,9 @@
 
 
 def mlp_back_kernel(
-    ff, step, homeward, e, mid, gain, gu_hbm, hid_hbm, a2_hbm, w1_hbm, w2_hbm, wa_hbm, dmid_out, gain_out, dat_out, dob_out,
-    first_sums, second_sums, full, full2, parts, a2, gu, hid, wm, wa, total, stage, send1, recv1,
-    from_c, via_x, via_y, from_x, from_y, send2, recv2, send3, recv3, local, swap=None, alone=False,
+    ff, step, homeward, e, mid, gain, gu_hbm, hid_hbm, a2_hbm, w1_hbm, w2_hbm, dmid_out, gain_out, dat_out, sums_out,
+    full, parts, a2, gu, hid, wm, total, stage, send1, recv1,
+    from_c, via_x, via_y, from_x, from_y, send2, recv2, local, swap=None,
 ):
     here = token_place()
     swap = swap and Swap(homeward, *swap)
@@ -580,7 +587,6 @@
     w2_load = loads.start(w2_hbm, wm.at[:, pl.ds(split, 3 * ff - split)])
     gu_load = loads.start(gu_hbm, gu)
     w1_load = loads.start(w1_hbm, wm.at[:, pl.ds(0, split)])
-    wa_load = None if alone else loads.start(wa_hbm, wa)
     a2_load = loads.start(a2_hbm, a2)
     hid_load = loads.start(hid_hbm, hid)
     own = rank_of(here, 0, 0, 0)
@@ -607,25 +613,17 @@
     hid_load.wait()
     sums = []
     count = full.shape[2] // step
-    middle = first_sums.shape[1]
 
     def beside(turn_number):
         half = (count + 1) // 2
         for number in range(turn_number * half, min((turn_number + 1) * half, count)):
             if number >= 2:
-                for save in sums[number - 2]:
-                    save.wait()
+                sums[number - 2].wait()
             at = slice(number * step, (number + 1) * step)
             held = stage.at[number % 2]
             held[:, : 2 * ff] = flat_tn(a2, at, gu).astype(BF)
             held[:, 2 * ff :] = flat_tn(full, at, hid).astype(BF)
-            rows = pl.ds(number * step, step)
-            sums.append(
-                [
-                    loads.start(held.at[:, pl.ds(0, middle)], first_sums.at[rows]),
-                    loads.start(held.at[:, pl.ds(middle, 3 * ff - middle)], second_sums.at[rows]),
-                ]
-            )
+            sums.append(loads.start(held, sums_out.at[pl.ds(number * step, step)]))
 
     net2 = scatter.run(beside, True)
     da2 = total[...]
@@ -635,22 +633,10 @@
     gain_out[...] = jnp.sum(da2 * n2, axis=0, keepdims=True)
     dmid = e[...].astype(F32) + norm_back(da2, n2, r2, gain[1:2, :])
     dmid_out[...] = dmid
-    saves = [save for pair in sums[-2:] for save in pair]
-    nets = [net1, net2]
-    if alone:
-        dat_out[...] = dmid.astype(BF)
-    else:
-        full2[own] = dmid.astype(BF)
-        wa_load.wait()
-
-        def on_second(r):
-            saves.append(loads.start(full2.at[r], dat_out.at[r]))
-            dob_out[r] = dot_nn(full2[r], wa[:, QKV:PACK]).astype(BF)
-
-        nets.append(run_gather(here, full2, (send3, recv3), on_second))
-    for net in nets:
-        net.drain()
-    for save in saves:
+    dat_out[...] = dmid.astype(BF)
+    net1.drain()
+    net2.drain()
+    for save in sums[-2:]:
         save.wait()
     if swap is not None:
         swap.wait()
@@ -689,33 +675,21 @@
     )
 
 
-def mlp_back_alone_kernel(
-    ff, step, homeward, e, mid, gain, gu_hbm, hid_hbm, a2_hbm, w1_hbm, w2_hbm, dmid_out, gain_out, dat_out,
-    first_sums, second_sums, full, parts, a2, gu, hid, wm, total, stage, *rest
-):
-    mlp_back_kernel(
-        ff, step, homeward, e, mid, gain, gu_hbm, hid_hbm, a2_hbm, w1_hbm, w2_hbm, None, dmid_out, gain_out,
-        dat_out, None, first_sums, second_sums, full, None, parts, a2, gu, hid, wm, None, total, stage,
-        *rest[:-1], None, None, rest[-1], alone=True,
-    )
-
-
-def mlp_back_alone(e, mid, gain, gu, hid, a2, w1, w2):
+def mlp_back(e, mid, gain, gu, hid, a2, w1, w2, moving=None):
     block, width = e.shape
     ff = hid.shape[2]
     step = math.gcd(width, 256)
     return plane_call(
-        functools.partial(mlp_back_alone_kernel, ff, step, True),
-        "mlp_back_alone",
-        11,
+        functools.partial(mlp_back_kernel, ff, step, True),
+        "mlp_back",
+        2 if moving is None else 9,
         [
             jax.ShapeDtypeStruct((block, width), F32),
             jax.ShapeDtypeStruct((1, width), F32),
             jax.ShapeDtypeStruct((block, width), BF),
-            jax.ShapeDtypeStruct((width, 3 * ff // 2), BF),
-            jax.ShapeDtypeStruct((width, 3 * ff // 2), BF),
+            jax.ShapeDtypeStruct((width, 3 * ff), BF),
         ],
-        [IN_VMEM, IN_VMEM, IN_VMEM, ANYWHERE, ANYWHERE],
+        [IN_VMEM, IN_VMEM, IN_VMEM, ANYWHERE],
         [IN_VMEM, IN_VMEM, IN_VMEM] + [ANYWHERE] * 5,
         [
             pltpu.VMEM((8, block, width), BF),
@@ -729,49 +703,9 @@
         ]
         + gather_sems()
         + scatter_scratch(block, width)
-        + [pltpu.SemaphoreType.DMA((5 + 2 * (width // step),))],
+        + [pltpu.SemaphoreType.DMA((5 + width // step,))],
         68,
         e, mid, gain, gu, hid, a2, w1, w2,
-    )
-
-
-def mlp_back(e, mid, gain, gu, hid, a2, w1, w2, wa, moving=None):
-    block, width = e.shape
-    ff = hid.shape[2]
-    cols = PACK - QKV
-    step = math.gcd(width, 256)
-    return plane_call(
-        functools.partial(mlp_back_kernel, ff, step, True),
-        "mlp_back",
-        2 if moving is None else 9,
-        [
-            jax.ShapeDtypeStruct((block, width), F32),
-            jax.ShapeDtypeStruct((1, width), F32),
-            jax.ShapeDtypeStruct((8, block, width), BF),
-            jax.ShapeDtypeStruct((8, block, cols), BF),
-            jax.ShapeDtypeStruct((width, 3 * ff // 2), BF),
-            jax.ShapeDtypeStruct((width, 3 * ff // 2), BF),
-        ],
-        [IN_VMEM, IN_VMEM, ANYWHERE, IN_VMEM, ANYWHERE, ANYWHERE],
-        [IN_VMEM, IN_VMEM, IN_VMEM] + [ANYWHERE] * 6,
-        [
-            pltpu.VMEM((8, block, width), BF),
-            pltpu.VMEM((8, block, width), BF),
-            pltpu.VMEM((8, block, width), BF),
-            pltpu.VMEM((8, block, width), BF),
-            pltpu.VMEM((8, block, 2 * ff), BF),
-            pltpu.VMEM((8, block, ff), BF),
-            pltpu.VMEM((width, 3 * ff), BF),
-            pltpu.VMEM(wa.shape, BF),
-            pltpu.VMEM((block, width), F32),
-            pltpu.VMEM((2, step, 3 * ff), BF),
-        ]
-        + gather_sems()
-        + scatter_scratch(block, width)
-        + gather_sems()
-        + [pltpu.SemaphoreType.DMA((14 + 2 * (width // step),))],
-        100,
-        e, mid, gain, gu, hid, a2, w1, w2, wa,
         moving=moving,
     )
 
@@ -1183,14 +1117,11 @@
     attn_got, hidden_state = exchange(4, ready(attn_pack), inputs[0])
     first_blocks, attn_got = together(mlp_blocks[..., :cut], attn_got)
     (first_got,) = exchange(5, first_blocks)
-    second_blocks, first_got = together(mlp_blocks[..., cut:], first_got)
-    (second_got,) = exchange(6, second_blocks)
-    attn_parts, first_parts, second_parts = by_layer(attn_got), by_layer(first_got), by_layer(second_got)
 
     token_x, token_c, token_y = token_place()
     rank = (token_x * 2 + token_c) * halves + token_y
     spot = lax.axis_index("e")
-    length = lengths[lax.axis_index("z")]
+    length = lengths[micro_of_plane()]
 
     block_start = (jnp.arange(ranks) * extra + spot) * block
     positions = (block_start[:, None] + jnp.arange(block)[None, :]).reshape(tokens)
@@ -1219,6 +1150,12 @@
 
     cosine3 = cosine.reshape(ranks, block, LANES)
     sine3 = sine.reshape(ranks, block, LANES)
+
+    second_blocks, first_got, cosine, sine, cosine3, sine3, bounds, query_rows = together(
+        mlp_blocks[..., cut:], first_got, cosine, sine, cosine3, sine3, bounds, query_rows
+    )
+    (second_got,) = exchange(6, second_blocks)
+    attn_parts, first_parts, second_parts = by_layer(attn_got), by_layer(first_got), by_layer(second_got)
 
     def flat(array):
         return array.reshape(tokens, array.shape[-1])
@@ -1249,29 +1186,18 @@
     (e,) = moved
     e = jnp.where((my_positions < length)[:, None], e, jnp.zeros_like(e))
     attn_grads = [None] * layers
-    first_grads = [None] * layers
-    second_grads = [None] * layers
+    mlp_grads = [None] * layers
     for layer in reversed(range(layers)):
         (h, a1, q, k, v, o, log_total, mid, a2, gu, hid, attn_w, w_1, w_2, gain) = saved[layer]
-        if layer > 0:
-            dmid, gain2, dat, dob, first_sums, second_sums, *moved = mlp_back(
-                e, mid, gain, gu, hid, a2, w_1, w_2, attn_w, output if layer + 1 == layers else None
-            )
-            if moved:
-                (output,) = moved
+        dmid, gain2, dat, mlp_sums, *moved = mlp_back(
+            e, mid, gain, gu, hid, a2, w_1, w_2, output if layer + 1 == layers else None
+        )
+        if moved:
+            (output,) = moved
         else:
-            dmid, gain2, dat, first_sums, second_sums = mlp_back_alone(e, mid, gain, gu, hid, a2, w_1, w_2)
-            dat, first_sums, second_sums, attn_grads[1], second_grads[1] = together(
-                dat, first_sums, second_sums, attn_grads[1], second_grads[1]
-            )
-            dat, dob = dat_gather(dat, attn_w)
-        if 0 < layer < layers - 1:
-            dob, first_sums, second_sums, attn_grads[layer + 1], second_grads[layer + 1] = together(
-                dob, first_sums, second_sums, attn_grads[layer + 1], second_grads[layer + 1]
-            )
-        first_grads[layer] = reduce_rows(first_sums)
-        if layer == 0:
-            second_grads[layer] = reduce_rows(second_sums)
+            dat, mlp_sums, attn_grads[layer + 1] = together(dat, mlp_sums, attn_grads[layer + 1])
+        mlp_grads[layer] = reduce_rows(mlp_sums)
+        dat, dob = dat_gather(dat, attn_w)
         dq, dk, dv = attend_back(
             q, k, v, query_rows, o, flat(dob), log_total, cosine, sine, bounds, length1, bq, bk, scale, scale2
         )
@@ -1280,18 +1206,13 @@
             h, dmid, gain, gain2, *(array.reshape(ranks, block, -1) for array in (dq, dk, dv)), cosine3, sine3,
             o.reshape(ranks, block, -1), a1, dat, attn_w,
         )
-        if layer > 0:
-            e, attn_sums, second_sums, first_grads[layer] = together(e, attn_sums, second_sums, first_grads[layer])
-            second_grads[layer] = reduce_rows(second_sums)
-        else:
-            e, attn_sums, first_grads[layer], second_grads[layer] = together(e, attn_sums, first_grads[layer], second_grads[layer])
+        e, attn_sums, mlp_grads[layer] = together(e, attn_sums, mlp_grads[layer])
         attn_grads[layer] = reduce_rows(attn_sums)
 
     def by_place(grads):
         return jnp.stack(grads).reshape(ranks, rows, -1)
 
-    mlp_blocks = by_place([jnp.concatenate(pair, axis=2) for pair in zip(first_grads, second_grads)])
-    (mlp_home,) = exchange(7, mlp_blocks)
+    (mlp_home,) = exchange(7, by_place(mlp_grads))
     attn_blocks, mlp_home = together(by_place(attn_grads), mlp_home)
     attn_home, input_grad = exchange(10, attn_blocks, e, True)
     grad_gate, grad_up, grad_down = finish(mlp_home)

time: 1600 us -> 1570 us (0.981)
  waiting for transfers between devices: 121 us -> 27.3 us
  Pallas kernels: 1390 us -> 1460 us
    reduce_scatter x12 -> x8, waiting for transfers between devices: 67.4 us -> 0.17 us  [reduce_rows(): mine = lax.psum_scatter(sums, 'z', scatter_dimension=0, tiled=True)]
    pallas_call x4, Pallas kernels: 58.9 us -> 91.8 us  [attend_back(): pl.pallas_call(functools.partial(back_kernel, scale, scale2, bq, bk), gri...]
    all_gather x12, waiting for transfers between devices: 48.8 us -> 25 us  [whole(): lax.all_gather(part.reshape(-1, part.shape[-1]), 'z', axis=0, tiled=True)]
    pallas_call x4, Pallas kernels: 40.1 us -> 62.9 us  [attend(): pl.pallas_call(functools.partial(attend_kernel, scale2, bq, bk), grid_spe...]
    pallas_call x22 -> x25, Pallas kernels: 1280 us -> 1290 us  [plane_call(): pl.pallas_call(kernel, out_shape=out_shape, in_specs=in_specs, out_specs=...]
  transfers between devices with their start and end apart: 24 -> 20, of which waited for: 13 -> 4; matrix products, arithmetic and copies ran while one was open for 1% -> 1% of each run, Pallas kernels for 69% -> 76%
where the time goes in v7:
time: 1570 us; the launch traced here: 1560 us
  Pallas kernels  1460 us (93%)
  local copies, waits for them, and re-layouts  28.3 us (2%)
  waiting for transfers between devices  27.3 us (2%)
  other arithmetic  21.7 us (1%)
    pallas_call x25, Pallas kernels, plane_call(): pl.pallas_call(kernel, out_shape=out_shape, in_specs=in_specs, out_specs=...  1290 us
    pallas_call x4, Pallas kernels, attend_back(): pl.pallas_call(functools.partial(back_kernel, scale, scale2, bq, bk), gri...  91.8 us
    pallas_call x4, Pallas kernels, attend(): pl.pallas_call(functools.partial(attend_kernel, scale2, bq, bk), grid_spe...  62.9 us
  transfers between devices with their start and end apart: 20, of which 4 were waited for; matrix products, arithmetic and copies ran while one was open for 1% of the time, Pallas kernels for 76%

profile of v7, /device:TPU:2, one launch (start us, length us, event | category | flops | bytes accessed | tf_op | source)
XLA Modules:
  0.0 1556.7 jit_solution(1981330412961659603)
XLA Ops:
  13.2 2.1 convert.43
  16.5 1.4 copy-done.1
  21.3 2.7 fusion.4
  24.1 4.2 concatenate.14
  28.4 42.9 %exchange.5 = (bf16[8,192,640]{2,1,0:T(8,128)(2,1)}, bf16[256,1536]{1,0:T(8,128)(2,1)}) custom-call(bf16[8,192,640]{2,1,0:T(8,128)(2,1)} %bitcast.149, bf16[256,1536]{1,0:T(8,128)(2,1)} %bitcast.216), custom_call_target="tpu_custom_call" | custom-call | bytes 72000000 | tf_op jit(solution)/shard_map/exchange/pallas_call | solution.py:401
  71.3 2.8 fusion.7
  74.6 29.3 %exchange.6 = bf16[8,192,768]{2,1,0:T(8,128)(2,1)} custom-call(bf16[8,192,768]{2,1,0:T(8,128)(2,1)} %get-tuple-element.178.blocks), custom_call_target="tpu_custom_call" | custom-call | bytes 87000000 | tf_op jit(solution)/shard_map/exchange/pallas_call | solution.py:401
  104.5 3.7 fusion
  110.5 1.9 select_maximum_fusion
  112.4 1.4 fusion.6
  113.9 29.4 %exchange.7 = bf16[8,192,768]{2,1,0:T(8,128)(2,1)} custom-call(bf16[8,192,768]{2,1,0:T(8,128)(2,1)} %get-tuple-element.180.blocks), custom_call_target="tpu_custom_call" | custom-call | bytes 87000000 | tf_op jit(solution)/shard_map/exchange/pallas_call | solution.py:401
  143.3 3.1 fusion.5
  146.4 22.4 %all-gather.15.cloned.1.call-done.w1_hbm = bf16[1536,768]{1,0:T(8,128)(2,1)} async-done(((bf16[384,768]{1,0:T(8,128)(2,1)}), bf16[1536,768]{1,0:T(8,128)(2,1)}) %all-gather.15.cloned.1.call-update) | async-done | bytes 2359312 | tf_op jit(solution)/shard_map/all_gather | solution.py:1106
  169.1 35.6 %attn_in.4 = (bf16[8,256,1536]{2,1,0:T(8,128)(2,1)}, bf16[2,8,256,128]{3,2,1,0:T(8,128)(2,1)}, bf16[8,256,128]{2,1,0:T(8,128)(2,1)}, bf16[8,256,128]{2,1,0:T(8,128)(2,1)}, f32[2,1536]{1,0:T(2,128)}) custom-call(bf16[256,1536]{1,0:T(8,128)(2,1)} %get-tuple-element.181.h, bf16[1536,640]{1,0:T(8,128)(2,1)} %all-gather.13.cloned.1.call-done.w_hbm.wa_hbm, ...), custom_call_target="tpu_custom_call" | custom-call | bytes 102000000 | tf_op jit(solution)/shard_map/attn_in/pallas_call | solution.py:401
  204.7 15.7 %attend.4 = (bf16[2048,192]{1,0:T(8,128)(2,1)}, f32[4,1,1024]{2,1,0:T(1,128)}) custom-call(s32[2,4]{1,0:T(2,128)} %pad_add_fusion.bounds, s32[1]{0:T(128)} %dynamic_slice.3.length, bf16[2,2048,128]{2,1,0:T(8,128)(2,1)} %bitcast.157, bf16[2048,128]{1,0:T(8,128)(2,1)} %bitcast.173, bf16[2048,128]{1,0:T(8,128)(2,1)} %bitcast.175, ...), custom_call_target="tpu_custom_call" | custom-call | bytes 45000000 | tf_op jit(solution)/shard_map/attend/pallas_call | solution.py:946
  221.6 93.9 %mlp.4 = (f32[256,1536]{1,0:T(8,128)}, bf16[8,256,1536]{2,1,0:T(8,128)(2,1)}, bf16[8,256,1024]{2,1,0:T(8,128)(2,1)}, bf16[8,256,512]{2,1,0:T(8,128)(2,1)}, bf16[256,1536]{1,0:T(8,128)(2,1)}) custom-call(bf16[256,1536]{1,0:T(8,128)(2,1)} %get-tuple-element.181.h, bf16[8,256,192]{2,1,0:T(8,128)(2,1)} %bitcast.141, f32[2,1536]{1,0:T(2,128)} %get-tuple-element.192.gain, ...), custom_call_target="tpu_custom_call" | custom-call | bytes 288000000 | tf_op jit(solution)/shard_map/mlp/pallas_call | solution.py:401
  315.7 35.6 %attn_in.5 = (bf16[8,256,1536]{2,1,0:T(8,128)(2,1)}, bf16[2,8,256,128]{3,2,1,0:T(8,128)(2,1)}, bf16[8,256,128]{2,1,0:T(8,128)(2,1)}, bf16[8,256,128]{2,1,0:T(8,128)(2,1)}, f32[2,1536]{1,0:T(2,128)}) custom-call(bf16[256,1536]{1,0:T(8,128)(2,1)} %get-tuple-element.198.h, bf16[1536,640]{1,0:T(8,128)(2,1)} %all-gather.19.cloned.1.call-done.w_hbm.wa_hbm, ...), custom_call_target="tpu_custom_call" | custom-call | bytes 102000000 | tf_op jit(solution)/shard_map/attn_in/pallas_call | solution.py:401
  351.3 15.7 %attend.5 = (bf16[2048,192]{1,0:T(8,128)(2,1)}, f32[4,1,1024]{2,1,0:T(1,128)}) custom-call(s32[2,4]{1,0:T(2,128)} %pad_add_fusion.bounds, s32[1]{0:T(128)} %dynamic_slice.3.length, bf16[2,2048,128]{2,1,0:T(8,128)(2,1)} %bitcast.159, bf16[2048,128]{1,0:T(8,128)(2,1)} %bitcast.177, bf16[2048,128]{1,0:T(8,128)(2,1)} %bitcast.179, ...), custom_call_target="tpu_custom_call" | custom-call | bytes 45000000 | tf_op jit(solution)/shard_map/attend/pallas_call | solution.py:946
  368.3 94.0 %mlp.5 = (f32[256,1536]{1,0:T(8,128)}, bf16[8,256,1536]{2,1,0:T(8,128)(2,1)}, bf16[8,256,1024]{2,1,0:T(8,128)(2,1)}, bf16[8,256,512]{2,1,0:T(8,128)(2,1)}, bf16[256,1536]{1,0:T(8,128)(2,1)}) custom-call(bf16[256,1536]{1,0:T(8,128)(2,1)} %get-tuple-element.198.h, bf16[8,256,192]{2,1,0:T(8,128)(2,1)} %bitcast.143, f32[2,1536]{1,0:T(2,128)} %get-tuple-element.205.gain, ...), custom_call_target="tpu_custom_call" | custom-call | bytes 288000000 | tf_op jit(solution)/shard_map/mlp/pallas_call | solution.py:401
  463.5 35.6 %attn_in.6 = (bf16[8,256,1536]{2,1,0:T(8,128)(2,1)}, bf16[2,8,256,128]{3,2,1,0:T(8,128)(2,1)}, bf16[8,256,128]{2,1,0:T(8,128)(2,1)}, bf16[8,256,128]{2,1,0:T(8,128)(2,1)}, f32[2,1536]{1,0:T(2,128)}) custom-call(bf16[256,1536]{1,0:T(8,128)(2,1)} %get-tuple-element.211.h, bf16[1536,640]{1,0:T(8,128)(2,1)} %all-gather.25.cloned.1.call-done.w_hbm.wa_hbm, ...), custom_call_target="tpu_custom_call" | custom-call | bytes 102000000 | tf_op jit(solution)/shard_map/attn_in/pallas_call | solution.py:401
  499.1 15.7 %attend.6 = (bf16[2048,192]{1,0:T(8,128)(2,1)}, f32[4,1,1024]{2,1,0:T(1,128)}) custom-call(s32[2,4]{1,0:T(2,128)} %pad_add_fusion.bounds, s32[1]{0:T(128)} %dynamic_slice.3.length, bf16[2,2048,128]{2,1,0:T(8,128)(2,1)} %bitcast.161, bf16[2048,128]{1,0:T(8,128)(2,1)} %bitcast.181, bf16[2048,128]{1,0:T(8,128)(2,1)} %bitcast.183, ...), custom_call_target="tpu_custom_call" | custom-call | bytes 45000000 | tf_op jit(solution)/shard_map/attend/pallas_call | solution.py:946
  516.1 93.9 %mlp.6 = (f32[256,1536]{1,0:T(8,128)}, bf16[8,256,1536]{2,1,0:T(8,128)(2,1)}, bf16[8,256,1024]{2,1,0:T(8,128)(2,1)}, bf16[8,256,512]{2,1,0:T(8,128)(2,1)}, bf16[256,1536]{1,0:T(8,128)(2,1)}) custom-call(bf16[256,1536]{1,0:T(8,128)(2,1)} %get-tuple-element.211.h, bf16[8,256,192]{2,1,0:T(8,128)(2,1)} %bitcast.145, f32[2,1536]{1,0:T(2,128)} %get-tuple-element.218.gain, ...), custom_call_target="tpu_custom_call" | custom-call | bytes 288000000 | tf_op jit(solution)/shard_map/mlp/pallas_call | solution.py:401
  611.9 35.6 %attn_in.7 = (bf16[8,256,1536]{2,1,0:T(8,128)(2,1)}, bf16[2,8,256,128]{3,2,1,0:T(8,128)(2,1)}, bf16[8,256,128]{2,1,0:T(8,128)(2,1)}, bf16[8,256,128]{2,1,0:T(8,128)(2,1)}, f32[2,1536]{1,0:T(2,128)}) custom-call(bf16[256,1536]{1,0:T(8,128)(2,1)} %get-tuple-element.224.h.refs_0_, bf16[1536,640]{1,0:T(8,128)(2,1)} %all-gather.31.cloned.1.call-done.w_hbm.refs_3_.wa_hbm, ...), custom_call_target="tpu_custom_call" | custom-call | bytes 102000000 | tf_op jit(solution)/shard_map/attn_in/pallas_call | solution.py:401
  647.5 15.7 %attend.7 = (bf16[2048,192]{1,0:T(8,128)(2,1)}, f32[4,1,1024]{2,1,0:T(1,128)}) custom-call(s32[2,4]{1,0:T(2,128)} %pad_add_fusion.bounds, s32[1]{0:T(128)} %dynamic_slice.3.length, bf16[2,2048,128]{2,1,0:T(8,128)(2,1)} %bitcast.163, bf16[2048,128]{1,0:T(8,128)(2,1)} %bitcast.185, bf16[2048,128]{1,0:T(8,128)(2,1)} %bitcast.187, ...), custom_call_target="tpu_custom_call" | custom-call | bytes 45000000 | tf_op jit(solution)/shard_map/attend/pallas_call | solution.py:946
  663.3 110.9 %mlp.7 = (f32[256,1536]{1,0:T(8,128)}, bf16[8,256,1536]{2,1,0:T(8,128)(2,1)}, bf16[8,256,1024]{2,1,0:T(8,128)(2,1)}, bf16[8,256,512]{2,1,0:T(8,128)(2,1)}, bf16[...) custom-call(bf16[256,1536]{1,0:T(8,128)(2,1)} %get-tuple-element.224.h.refs_0_, bf16[8,256,192]{2,1,0:T(8,128)(2,1)} %bitcast.147, ...), custom_call_target="tpu_custom_call" | custom-call | bytes 288000000 | tf_op jit(solution)/shard_map/mlp/pallas_call | solution.py:401
  774.2 2.1 broadcast_select_fusion.refs_0_
  776.3 76.2 %mlp_back.4 = (f32[256,1536]{1,0:T(8,128)}, f32[1,1536]{1,0:T(1,128)}, bf16[256,1536]{1,0:T(8,128)(2,1)}, bf16[1536,1536]{1,0:T(8,128)(2,1)}, bf16[256,1536]{1,0:T(8,128)(2,1)}) custom-call(bf16[256,1536]{1,0:T(8,128)(2,1)} %broadcast_select_fusion.refs_0_, f32[256,1536]{1,0:T(8,128)} %get-tuple-element.234.refs_1_, ...), custom_call_target="tpu_custom_call" | custom-call | bytes 204000000 | tf_op jit(solution)/shard_map/mlp_back/pallas_call | solution.py:401
  852.6 32.3 %dat_gather.4 = (bf16[8,256,1536]{2,1,0:T(8,128)(2,1)}, bf16[8,256,256]{2,1,0:T(8,128)(2,1)}) custom-call(bf16[256,1536]{1,0:T(8,128)(2,1)} %get-tuple-element.242.dat, bf16[1536,640]{1,0:T(8,128)(2,1)} %all-gather.31.cloned.1.call-done.w_hbm.refs_3_.wa_hbm), custom_call_target="tpu_custom_call" | custom-call | bytes 96000000 | tf_op jit(solution)/shard_map/dat_gather/pallas_call | solution.py:401
  884.9 22.9 %attend_back.4 = (bf16[2048,256]{1,0:T(8,128)(2,1)}, f32[2048,128]{1,0:T(8,128)}, f32[2048,128]{1,0:T(8,128)}) custom-call(s32[2,4]{1,0:T(2,128)} %pad_add_fusion.bounds, s32[1]{0:T(128)} %dynamic_slice.3.length, bf16[2,2048,128]{2,1,0:T(8,128)(2,1)} %bitcast.164, bf16[2048,128]{1,0:T(8,128)(2,1)} %bitcast.186, bf16[2048,128]{1,0:T(8,128)(2,1)} %bitcast.188, ...), custom_call_target="tpu_custom_call" | custom-call | bytes 65000000 | tf_op jit(solution)/shard_map/attend_back/pallas_call | solution.py:1013
  907.8 40.8 %attn_back.4 = (bf16[256,1536]{1,0:T(8,128)(2,1)}, bf16[1536,640]{1,0:T(8,128)(2,1)}) custom-call(bf16[256,1536]{1,0:T(8,128)(2,1)} %get-tuple-element.224.h.refs_0_, f32[256,1536]{1,0:T(8,128)} %get-tuple-element.240.dmid, f32[2,1536]{1,0:T(2,128)} %get-tuple-element.230.refs_2_.gain, f32[1,1536]{1,0:T(1,128)} %get-tuple-element.241.gain2_grad, ...), custom_call_target="tpu_custom_call" | custom-call | bytes 108000000 | tf_op jit(solution)/shard_map/attn_back/pallas_call | solution.py:401
  948.7 66.8 %mlp_back.5 = (f32[256,1536]{1,0:T(8,128)}, f32[1,1536]{1,0:T(1,128)}, bf16[256,1536]{1,0:T(8,128)(2,1)}, bf16[1536,1536]{1,0:T(8,128)(2,1)}) custom-call(bf16[256,1536]{1,0:T(8,128)(2,1)} %get-tuple-element.255.e, f32[256,1536]{1,0:T(8,128)} %get-tuple-element.256.mid, f32[2,1536]{1,0:T(2,128)} %get-tuple-element.218.gain, ...), custom_call_target="tpu_custom_call" | custom-call | bytes 204000000 | tf_op jit(solution)/shard_map/mlp_back/pallas_call | solution.py:401
  1015.6 33.3 %dat_gather.5 = (bf16[8,256,1536]{2,1,0:T(8,128)(2,1)}, bf16[8,256,256]{2,1,0:T(8,128)(2,1)}) custom-call(bf16[256,1536]{1,0:T(8,128)(2,1)} %get-tuple-element.265.dat, bf16[1536,640]{1,0:T(8,128)(2,1)} %all-gather.25.cloned.1.call-done.w_hbm.wa_hbm), custom_call_target="tpu_custom_call" | custom-call | bytes 96000000 | tf_op jit(solution)/shard_map/dat_gather/pallas_call | solution.py:401
  1048.9 23.1 %attend_back.5 = (bf16[2048,256]{1,0:T(8,128)(2,1)}, f32[2048,128]{1,0:T(8,128)}, f32[2048,128]{1,0:T(8,128)}) custom-call(s32[2,4]{1,0:T(2,128)} %pad_add_fusion.bounds, s32[1]{0:T(128)} %dynamic_slice.3.length, bf16[2,2048,128]{2,1,0:T(8,128)(2,1)} %bitcast.162, bf16[2048,128]{1,0:T(8,128)(2,1)} %bitcast.182, bf16[2048,128]{1,0:T(8,128)(2,1)} %bitcast.184, ...), custom_call_target="tpu_custom_call" | custom-call | bytes 65000000 | tf_op jit(solution)/shard_map/attend_back/pallas_call | solution.py:1013
  1072.0 40.0 %attn_back.5 = (bf16[256,1536]{1,0:T(8,128)(2,1)}, bf16[1536,640]{1,0:T(8,128)(2,1)}) custom-call(bf16[256,1536]{1,0:T(8,128)(2,1)} %get-tuple-element.211.h, f32[256,1536]{1,0:T(8,128)} %get-tuple-element.260.dmid, f32[2,1536]{1,0:T(2,128)} %get-tuple-element.218.gain, f32[1,1536]{1,0:T(1,128)} %get-tuple-element.261.gain2_grad, ...), custom_call_target="tpu_custom_call" | custom-call | bytes 108000000 | tf_op jit(solution)/shard_map/attn_back/pallas_call | solution.py:401
  1112.1 67.3 %mlp_back.6 = (f32[256,1536]{1,0:T(8,128)}, f32[1,1536]{1,0:T(1,128)}, bf16[256,1536]{1,0:T(8,128)(2,1)}, bf16[1536,1536]{1,0:T(8,128)(2,1)}) custom-call(bf16[256,1536]{1,0:T(8,128)(2,1)} %get-tuple-element.276.e, f32[256,1536]{1,0:T(8,128)} %get-tuple-element.277.mid, f32[2,1536]{1,0:T(2,128)} %get-tuple-element.205.gain, ...), custom_call_target="tpu_custom_call" | custom-call | bytes 204000000 | tf_op jit(solution)/shard_map/mlp_back/pallas_call | solution.py:401
  1179.6 32.7 %dat_gather.6 = (bf16[8,256,1536]{2,1,0:T(8,128)(2,1)}, bf16[8,256,256]{2,1,0:T(8,128)(2,1)}) custom-call(bf16[256,1536]{1,0:T(8,128)(2,1)} %get-tuple-element.286.dat, bf16[1536,640]{1,0:T(8,128)(2,1)} %all-gather.19.cloned.1.call-done.w_hbm.wa_hbm), custom_call_target="tpu_custom_call" | custom-call | bytes 96000000 | tf_op jit(solution)/shard_map/dat_gather/pallas_call | solution.py:401
  1212.3 22.9 %attend_back.6 = (bf16[2048,256]{1,0:T(8,128)(2,1)}, f32[2048,128]{1,0:T(8,128)}, f32[2048,128]{1,0:T(8,128)}) custom-call(s32[2,4]{1,0:T(2,128)} %pad_add_fusion.bounds, s32[1]{0:T(128)} %dynamic_slice.3.length, bf16[2,2048,128]{2,1,0:T(8,128)(2,1)} %bitcast.160, bf16[2048,128]{1,0:T(8,128)(2,1)} %bitcast.178, bf16[2048,128]{1,0:T(8,128)(2,1)} %bitcast.180, ...), custom_call_target="tpu_custom_call" | custom-call | bytes 65000000 | tf_op jit(solution)/shard_map/attend_back/pallas_call | solution.py:1013
  1235.2 40.6 %attn_back.6 = (bf16[256,1536]{1,0:T(8,128)(2,1)}, bf16[1536,640]{1,0:T(8,128)(2,1)}) custom-call(bf16[256,1536]{1,0:T(8,128)(2,1)} %get-tuple-element.198.h, f32[256,1536]{1,0:T(8,128)} %get-tuple-element.281.dmid, f32[2,1536]{1,0:T(2,128)} %get-tuple-element.205.gain, f32[1,1536]{1,0:T(1,128)} %get-tuple-element.282.gain2_grad, ...), custom_call_target="tpu_custom_call" | custom-call | bytes 108000000 | tf_op jit(solution)/shard_map/attn_back/pallas_call | solution.py:401
  1275.9 66.9 %mlp_back.7 = (f32[256,1536]{1,0:T(8,128)}, f32[1,1536]{1,0:T(1,128)}, bf16[256,1536]{1,0:T(8,128)(2,1)}, bf16[1536,1536]{1,0:T(8,128)(2,1)}) custom-call(bf16[256,1536]{1,0:T(8,128)(2,1)} %get-tuple-element.297.e, f32[256,1536]{1,0:T(8,128)} %get-tuple-element.298.mid, f32[2,1536]{1,0:T(2,128)} %get-tuple-element.192.gain, ...), custom_call_target="tpu_custom_call" | custom-call | bytes 204000000 | tf_op jit(solution)/shard_map/mlp_back/pallas_call | solution.py:401
  1342.9 33.3 %dat_gather.7 = (bf16[8,256,1536]{2,1,0:T(8,128)(2,1)}, bf16[8,256,256]{2,1,0:T(8,128)(2,1)}) custom-call(bf16[256,1536]{1,0:T(8,128)(2,1)} %get-tuple-element.307.dat, bf16[1536,640]{1,0:T(8,128)(2,1)} %all-gather.13.cloned.1.call-done.w_hbm.wa_hbm), custom_call_target="tpu_custom_call" | custom-call | bytes 96000000 | tf_op jit(solution)/shard_map/dat_gather/pallas_call | solution.py:401
  1376.2 22.9 %attend_back.7 = (bf16[2048,256]{1,0:T(8,128)(2,1)}, f32[2048,128]{1,0:T(8,128)}, f32[2048,128]{1,0:T(8,128)}) custom-call(s32[2,4]{1,0:T(2,128)} %pad_add_fusion.bounds, s32[1]{0:T(128)} %dynamic_slice.3.length, bf16[2,2048,128]{2,1,0:T(8,128)(2,1)} %bitcast.158, bf16[2048,128]{1,0:T(8,128)(2,1)} %bitcast.174, bf16[2048,128]{1,0:T(8,128)(2,1)} %bitcast.176, ...), custom_call_target="tpu_custom_call" | custom-call | bytes 65000000 | tf_op jit(solution)/shard_map/attend_back/pallas_call | solution.py:1013
  1399.1 40.0 %attn_back.7 = (bf16[256,1536]{1,0:T(8,128)(2,1)}, bf16[1536,640]{1,0:T(8,128)(2,1)}) custom-call(bf16[256,1536]{1,0:T(8,128)(2,1)} %get-tuple-element.181.h, f32[256,1536]{1,0:T(8,128)} %get-tuple-element.302.dmid, f32[2,1536]{1,0:T(2,128)} %get-tuple-element.192.gain, f32[1,1536]{1,0:T(1,128)} %get-tuple-element.303.gain2_grad, ...), custom_call_target="tpu_custom_call" | custom-call | bytes 108000000 | tf_op jit(solution)/shard_map/attn_back/pallas_call | solution.py:401
  1440.4 3.6 pad_maximum_fusion
  1444.0 54.6 %exchange.8.got = bf16[8,192,1536]{2,1,0:T(8,128)(2,1)} custom-call(bf16[8,192,1536]{2,1,0:T(8,128)(2,1)} %bitcast.140), custom_call_target="tpu_custom_call" | custom-call | bytes 174000000 | tf_op jit(solution)/shard_map/exchange/pallas_call | solution.py:401
  1498.6 2.6 pad_maximum_fusion.1
  1501.2 33.5 %exchange.9 = (bf16[8,192,640]{2,1,0:T(8,128)(2,1)}, bf16[256,1536]{1,0:T(8,128)(2,1)}) custom-call(bf16[8,192,640]{2,1,0:T(8,128)(2,1)} %bitcast.150, bf16[256,1536]{1,0:T(8,128)(2,1)} %get-tuple-element.327.refs_1_), custom_call_target="tpu_custom_call" | custom-call | bytes 72000000 | tf_op jit(solution)/shard_map/exchange/pallas_call | solution.py:401
  1534.7 4.0 finish_attn.1
  1540.0 7.6 finish.1
  (133 shorter events, 26.0 us)
Async XLA Ops:
  7.2 3.3 copy-start.10
  7.2 139.2 %all-gather.13.cloned.1.call-start = ((), (), s32[]{:S(2)}) async-start(), calls=%async_computation.8 | async-start | bytes 2457600 | tf_op jit(solution)/shard_map/all_gather | solution.py:1106
  8.8 2.3 copy-start.6
  11.1 1.3 copy-start.7
  16.0 1.9 copy-start.1
  18.7 1.9 copy-start.2
  21.3 2.7 copy-start.14
  74.1 94.7 %all-gather.15.cloned.1.call-start = ((), (), s32[]{:S(2)}) async-start(), calls=%async_computation.9 | async-start | bytes 2949120 | tf_op jit(solution)/shard_map/all_gather | solution.py:1106
  74.6 29.3 %copy-start.15 = (s32[4]{0:T(128)S(1)}, s32[4]{0:T(128)}, u32[]{:S(2)}) copy-start(s32[4]{0:T(128)} %param.13) | copy-start | bytes 52
  110.5 1.9 copy-start
  113.9 107.7 %all-gather.17.cloned.1.call-start = ((), (), s32[]{:S(2)}) async-start(), calls=%async_computation.10 | async-start | bytes 2949120 | tf_op jit(solution)/shard_map/all_gather | solution.py:1106
  168.8 146.7 %all-gather.19.cloned.1.call-start = ((), (), s32[]{:S(2)}) async-start(), calls=%async_computation.11 | async-start | bytes 2457600 | tf_op jit(solution)/shard_map/all_gather | solution.py:1106
  220.5 95.2 %all-gather.21.cloned.1.call-start = ((), (), s32[]{:S(2)}) async-start(), calls=%async_computation.12 | async-start | bytes 2949120 | tf_op jit(solution)/shard_map/all_gather | solution.py:1106
  221.0 147.3 %all-gather.23.cloned.1.call-start = ((), (), s32[]{:S(2)}) async-start(), calls=%async_computation.13 | async-start | bytes 2949120 | tf_op jit(solution)/shard_map/all_gather | solution.py:1106
  315.7 146.7 %all-gather.25.cloned.1.call-start = ((), (), s32[]{:S(2)}) async-start(), calls=%async_computation.14 | async-start | bytes 2457600 | tf_op jit(solution)/shard_map/all_gather | solution.py:1106
  367.1 96.4 %all-gather.27.cloned.1.call-start = ((), (), s32[]{:S(2)}) async-start(), calls=%async_computation.15 | async-start | bytes 2949120 | tf_op jit(solution)/shard_map/all_gather | solution.py:1106
  367.8 148.2 %all-gather.29.cloned.1.call-start = ((), (), s32[]{:S(2)}) async-start(), calls=%async_computation.16 | async-start | bytes 2949120 | tf_op jit(solution)/shard_map/all_gather | solution.py:1106
  463.5 146.5 %all-gather.31.cloned.1.call-start = ((), (), s32[]{:S(2)}) async-start(), calls=%async_computation.17 | async-start | bytes 2457600 | tf_op jit(solution)/shard_map/all_gather | solution.py:1106
  514.8 96.4 %all-gather.33.cloned.1.call-start = ((), (), s32[]{:S(2)}) async-start(), calls=%async_computation.18 | async-start | bytes 2949120 | tf_op jit(solution)/shard_map/all_gather | solution.py:1106
  515.6 147.7 %all-gather.35.cloned.1.call-start = ((), (), s32[]{:S(2)}) async-start(), calls=%async_computation.19 | async-start | bytes 2949120 | tf_op jit(solution)/shard_map/all_gather | solution.py:1106
  611.2 337.4 %reduce-scatter.9.cloned.1.call-start = ((), (), s32[]{:S(2)}) async-start(), calls=%async_computation.20 | async-start | bytes 5898240 | tf_op jit(solution)/shard_map/reduce_scatter | solution.py:1109
  852.5 163.0 %reduce-scatter.11.cloned.1.call-start = ((), (), s32[]{:S(2)}) async-start(), calls=%async_computation.21 | async-start | bytes 2457600 | tf_op jit(solution)/shard_map/reduce_scatter | solution.py:1109
  948.6 163.4 %reduce-scatter.13.cloned.1.call-start = ((), (), s32[]{:S(2)}) async-start(), calls=%async_computation.22 | async-start | bytes 5898240 | tf_op jit(solution)/shard_map/reduce_scatter | solution.py:1109
  1015.5 163.9 %reduce-scatter.15.cloned.1.call-start = ((), (), s32[]{:S(2)}) async-start(), calls=%async_computation.23 | async-start | bytes 2457600 | tf_op jit(solution)/shard_map/reduce_scatter | solution.py:1109
  1112.1 163.7 %reduce-scatter.17.cloned.1.call-start = ((), (), s32[]{:S(2)}) async-start(), calls=%async_computation.24 | async-start | bytes 5898240 | tf_op jit(solution)/shard_map/reduce_scatter | solution.py:1109
  1179.5 163.3 %reduce-scatter.19.cloned.1.call-start = ((), (), s32[]{:S(2)}) async-start(), calls=%async_computation.25 | async-start | bytes 2457600 | tf_op jit(solution)/shard_map/reduce_scatter | solution.py:1109
  1275.8 163.3 %reduce-scatter.21.cloned.1.call-start = ((), (), s32[]{:S(2)}) async-start(), calls=%async_computation.26 | async-start | bytes 5898240 | tf_op jit(solution)/shard_map/reduce_scatter | solution.py:1109
  1342.8 155.7 %reduce-scatter.23.cloned.1.call-start = ((), (), s32[]{:S(2)}) async-start(), calls=%async_computation.27 | async-start | bytes 2457600 | tf_op jit(solution)/shard_map/reduce_scatter | solution.py:1109
  1399.1 40.1 %copy-start.4 = (bf16[384,1536]{1,0:T(8,128)(2,1)S(1)}, bf16[384,1536]{1,0:T(8,128)(2,1)}, u32[]{:S(2)}) copy-start(bf16[384,1536]{1,0:T(8,128)(2,1)} %reduce-scatter.13.cloned.1.call-done) | copy-start | bytes 3538948
  1399.1 40.1 %copy-start.5 = (bf16[384,1536]{1,0:T(8,128)(2,1)S(1)}, bf16[384,1536]{1,0:T(8,128)(2,1)}, u32[]{:S(2)}) copy-start(bf16[384,1536]{1,0:T(8,128)(2,1)} %reduce-scatter.17.cloned.1.call-done) | copy-start | bytes 3538948
  1439.1 1.3 copy-start.3
  1443.9 54.6 %copy-start.11 = (bf16[384,640]{1,0:T(8,128)(2,1)S(1)}, bf16[384,640]{1,0:T(8,128)(2,1)}, u32[]{:S(2)}) copy-start(bf16[384,640]{1,0:T(8,128)(2,1)} %reduce-scatter.11.cloned.1.call-done) | copy-start | bytes 1474564
  1443.9 54.6 %copy-start.12 = (bf16[384,640]{1,0:T(8,128)(2,1)S(1)}, bf16[384,640]{1,0:T(8,128)(2,1)}, u32[]{:S(2)}) copy-start(bf16[384,640]{1,0:T(8,128)(2,1)} %reduce-scatter.15.cloned.1.call-done) | copy-start | bytes 1474564
  1443.9 54.6 %copy-start.13 = (bf16[384,640]{1,0:T(8,128)(2,1)S(1)}, bf16[384,640]{1,0:T(8,128)(2,1)}, u32[]{:S(2)}) copy-start(bf16[384,640]{1,0:T(8,128)(2,1)} %reduce-scatter.19.cloned.1.call-done) | copy-start | bytes 1474564
  1540.0 7.7 copy-start.8
  1540.0 8.5 copy-start.9
Sparse Core Ops, SparseCore 0:
  74.2 43.0 all-gather.12
  119.4 49.3 all-gather.14
  170.9 49.2 all-gather.16
  221.7 42.5 all-gather.18
  266.3 49.3 all-gather.20
  317.6 49.2 all-gather.22
  368.6 43.3 all-gather.24
  414.1 49.3 all-gather.26
  465.0 49.3 all-gather.28
  515.8 43.8 all-gather.30
  561.8 49.3 all-gather.32
  612.6 49.2 all-gather.34
  852.7 85.0 reduce-scatter.8
  948.7 42.9 reduce-scatter.10
  1015.7 86.9 reduce-scatter.12
  1112.2 44.6 reduce-scatter.14
  1179.6 88.3 reduce-scatter.16
  1276.0 46.1 reduce-scatter.18
  1343.0 90.0 reduce-scatter.20
  1439.3 47.8 reduce-scatter.22

commit v8 on v7

--- a/solution.py
+++ b/solution.py
@@ -170,74 +170,88 @@
             started.wait_send()
 
 
+class Gather:
+    def __init__(self, here, full, sems):
+        self.here, self.full = here, full
+        self.piece = full.shape[1] // 4
+        self.net = Sender(*sems)
+
+    def index(self, role, chunk):
+        return (role[0] * 4 + role[1] * 2 + role[2]) * 4 + chunk
+
+    def slot(self, role, chunk):
+        return self.full.at[rank_of(self.here, *role), pl.ds(chunk * self.piece, self.piece)]
+
+    def send(self, role, chunk, to, as_role):
+        where = self.slot(role, chunk)
+        self.net.send(where, where, self.index(as_role, chunk), to)
+
+    def arrived(self, role, chunk):
+        self.net.arrived(self.slot(role, chunk), self.index(role, chunk))
+
+    def own(self, cx, cy):
+        self.send((0, 0, 0), cx, "x", (1, 0, 0))
+        self.send((0, 0, 0), cy, "y", (0, 0, 1))
+
+    def all_own(self):
+        for cx, cy in ((2, 0), (3, 1), (0, 2), (1, 3)):
+            self.own(cx, cy)
+        return self
+
+    def run(self, on_block, before_last=None):
+        send, arrived = self.send, self.arrived
+        at_x, at_y, at_d, at_c = (1, 0, 0), (0, 0, 1), (1, 0, 1), (0, 1, 0)
+        xc, yc, dc = (1, 1, 0), (0, 1, 1), (1, 1, 1)
+
+        def whole(role):
+            for chunk in range(4):
+                arrived(role, chunk)
+
+        def done(role):
+            on_block(rank_of(self.here, *role))
+
+        def pass_on(cx, cy):
+            arrived(at_x, cx)
+            if cx >= 2:
+                send(at_x, cx, "y", at_d)
+            send(at_x, cx, "c", xc)
+            arrived(at_y, cy)
+            if cy < 2:
+                send(at_y, cy, "x", at_d)
+            send(at_y, cy, "c", yc)
+
+        def pass_last(chunks):
+            for chunk in chunks:
+                arrived(at_d, chunk)
+                send(at_d, chunk, "c", dc)
+
+        for chunk in range(4):
+            send((0, 0, 0), chunk, "c", at_c)
+        done((0, 0, 0))
+        pass_on(2, 0)
+        whole(at_c)
+        done(at_c)
+        pass_on(3, 1)
+        pass_on(0, 2)
+        pass_on(1, 3)
+        done(at_x)
+        done(at_y)
+        pass_last((0, 2))
+        whole(xc)
+        done(xc)
+        whole(yc)
+        done(yc)
+        if before_last is not None:
+            before_last()
+        pass_last((1, 3))
+        done(at_d)
+        whole(dc)
+        done(dc)
+        return self.net
+
+
 def run_gather(here, full, sems, on_block, before_last=None):
-    block = full.shape[1]
-    piece = block // 4
-    net = Sender(*sems)
-
-    def index(role, chunk):
-        return (role[0] * 4 + role[1] * 2 + role[2]) * 4 + chunk
-
-    def slot(role, chunk, count=1):
-        return full.at[rank_of(here, *role), pl.ds(chunk * piece, piece * count)]
-
-    def send(role, chunk, to, as_role, count=1):
-        where = slot(role, chunk, count)
-        net.send(where, where, index(as_role, chunk), to)
-
-    def arrived(role, chunk, count=1):
-        net.arrived(slot(role, chunk, count), index(role, chunk))
-
-    def whole(role):
-        for chunk in range(4):
-            arrived(role, chunk)
-
-    def done(role):
-        on_block(rank_of(here, *role))
-
-    own, at_x, at_y, at_d, at_c = (0, 0, 0), (1, 0, 0), (0, 0, 1), (1, 0, 1), (0, 1, 0)
-    xc, yc, dc = (1, 1, 0), (0, 1, 1), (1, 1, 1)
-    for cx, cy in ((2, 0), (3, 1), (0, 2), (1, 3)):
-        send(own, cx, "x", at_x)
-        send(own, cy, "y", at_y)
-    send(own, 0, "c", at_c, 4)
-
-    def pass_on(cx, cy):
-        arrived(at_x, cx)
-        if cx >= 2:
-            send(at_x, cx, "y", at_d)
-        send(at_x, cx, "c", xc)
-        arrived(at_y, cy)
-        if cy < 2:
-            send(at_y, cy, "x", at_d)
-        send(at_y, cy, "c", yc)
-
-    def pass_last(chunks):
-        for chunk in chunks:
-            arrived(at_d, chunk)
-            send(at_d, chunk, "c", dc)
-
-    done(own)
-    pass_on(2, 0)
-    arrived(at_c, 0, 4)
-    done(at_c)
-    pass_on(3, 1)
-    pass_on(0, 2)
-    pass_on(1, 3)
-    done(at_x)
-    done(at_y)
-    pass_last((0, 2))
-    whole(xc)
-    done(xc)
-    whole(yc)
-    done(yc)
-    if before_last is not None:
-        before_last()
-    pass_last((1, 3))
-    done(at_d)
-    whole(dc)
-    done(dc)
-    return net
+    return Gather(here, full, sems).all_own().run(on_block, before_last)
 
 
 class Scatter:
@@ -247,6 +261,7 @@
         self.here, self.parts, self.total, self.fill = here, parts, total, fill
         self.from_c, self.via_x, self.via_y, self.from_x, self.from_y = bufs
         half = parts.shape[1] // 2
+        self.piece = half // 2
         self.lower, self.upper = pl.ds(0, half), pl.ds(half, half)
         self.net = Sender(*sems)
 
@@ -275,53 +290,65 @@
         if n < 3:
             self.add(n, pl.ds(0, self.parts.shape[1]), self.from_c[n])
 
+    def rows(self, number):
+        return pl.ds(number * self.piece, self.piece)
+
     def to_diagonal(self):
         self.combine(0)
-        self.net.send(self.mine(0, self.upper), self.via_x, 4, "x")
-        self.net.send(self.mine(0, self.lower), self.via_y, 5, "y")
-
-    def to_neighbours(self):
+        for n in range(2):
+            self.net.send(self.mine(0, self.rows(n + 2)), self.via_x.at[self.rows(n)], 4 + n, "x")
+            self.net.send(self.mine(0, self.rows(n)), self.via_y.at[self.rows(n)], 6 + n, "y")
+
+    def to_x(self):
         self.combine(1)
-        self.net.send(self.mine(1, self.upper), self.from_x.at[self.upper], 6, "x")
+        self.net.send(self.mine(1, self.upper), self.from_x.at[self.upper], 8, "x")
+
+    def to_y(self):
         self.combine(2)
-        self.net.send(self.mine(2, self.lower), self.from_y.at[self.lower], 7, "y")
+        self.net.send(self.mine(2, self.lower), self.from_y.at[self.lower], 9, "y")
 
     def early(self):
         for n in (1, 2, 3):
             self.sibling(n)
-        self.to_neighbours()
-
-    def run(self, beside=None, early_done=False):
+        self.to_x()
+        self.to_y()
+
+    def run(self, beside=None, early_done=False, on_rows=None):
         net, total, lower, upper = self.net, self.total, self.lower, self.upper
         self.sibling(0)
-        if early_done:
-            self.to_diagonal()
-        else:
+        self.to_diagonal()
+        if not early_done:
             self.sibling(1)
+            self.to_x()
             self.sibling(2)
-            self.to_diagonal()
-            self.to_neighbours()
+            self.to_y()
             self.sibling(3)
         self.combine(3)
         total[...] = self.parts[self.rank(3, 0)].astype(F32) + self.from_c[3].astype(F32)
         if beside is not None:
             beside(0)
-        net.arrived(self.via_y, 5)
-        self.add(1, lower, self.via_y[...])
-        net.send(self.mine(1, lower), self.from_x.at[lower], 8, "x")
-        net.arrived(self.via_x, 4)
-        self.add(2, upper, self.via_x[...])
-        net.send(self.mine(2, upper), self.from_y.at[upper], 9, "y")
+        for n in range(2):
+            at, above = self.rows(n), self.rows(n + 2)
+            net.arrived(self.via_y.at[at], 6 + n)
+            self.add(1, at, self.via_y[at])
+            net.send(self.mine(1, at), self.from_x.at[at], 10 + n, "x")
+            net.arrived(self.via_x.at[at], 4 + n)
+            self.add(2, above, self.via_x[at])
+            net.send(self.mine(2, above), self.from_y.at[above], 12 + n, "y")
         if beside is not None:
             beside(1)
-        net.arrived(self.from_x.at[upper], 6)
-        net.arrived(self.from_y.at[lower], 7)
+        net.arrived(self.from_x.at[upper], 8)
+        net.arrived(self.from_y.at[lower], 9)
         total[upper] += self.from_x[upper].astype(F32)
         total[lower] += self.from_y[lower].astype(F32)
-        net.arrived(self.from_x.at[lower], 8)
-        net.arrived(self.from_y.at[upper], 9)
-        total[lower] += self.from_x[lower].astype(F32)
-        total[upper] += self.from_y[upper].astype(F32)
+        for n in range(2):
+            at, above = self.rows(n), self.rows(n + 2)
+            net.arrived(self.from_x.at[at], 10 + n)
+            net.arrived(self.from_y.at[above], 12 + n)
+            total[at] += self.from_x[at].astype(F32)
+            total[above] += self.from_y[above].astype(F32)
+            if on_rows is not None:
+                on_rows(n)
         return net
 
 
@@ -337,8 +364,8 @@
         pltpu.VMEM((half, width), BF),
         pltpu.VMEM((block, width), BF),
         pltpu.VMEM((block, width), BF),
-        pltpu.SemaphoreType.DMA((10,)),
-        pltpu.SemaphoreType.DMA((10,)),
+        pltpu.SemaphoreType.DMA((14,)),
+        pltpu.SemaphoreType.DMA((14,)),
     ]
 
 
@@ -492,10 +519,22 @@
         parts[r] = dot_nt(o[r], wa[:, QKV:GAIN_AT]).astype(BF)
 
     bufs = (from_c, via_x, via_y, from_x, from_y)
-    net1 = Scatter(here, parts, total, bufs, (send1, recv1), fill).run()
-    mid = h[...].astype(F32) + total[...]
-    mid_out[...] = mid
-    full[rank_of(here, 0, 0, 0)] = (mid * inverse_of(mid) * gain[1:2, :]).astype(BF)
+    gather = Gather(here, full, (send2, recv2))
+    own = rank_of(here, 0, 0, 0)
+
+    def on_rows(n):
+        for piece in (n + 2, n):
+            rows = pl.ds(piece * gather.piece, gather.piece)
+            mid = h[rows].astype(F32) + total[rows]
+            mid_out[rows] = mid
+            full[own, rows] = (mid * inverse_of(mid) * gain[1:2, :]).astype(BF)
+        if n == 0:
+            gather.own(2, 0)
+        else:
+            for pair in ((3, 1), (0, 2), (1, 3)):
+                gather.own(*pair)
+
+    net1 = Scatter(here, parts, total, bufs, (send1, recv1), fill).run(on_rows=on_rows)
     net1.drain()
     saves = []
 
@@ -517,7 +556,7 @@
 
     bufs3 = (from_c3, via_x3, via_y3, from_x3, from_y3)
     scatter = Scatter(here, parts, total, bufs3, (send3, recv3))
-    net2 = run_gather(here, full, (send2, recv2), on_block, scatter.early)
+    net2 = gather.run(on_block, scatter.early)
     net3 = scatter.run(early_done=True)
     next_out[...] = (mid_out[...] + total[...]).astype(BF)
     net2.drain()

time: 1570 us -> 1550 us (0.987)
  Pallas kernels: 1460 us -> 1380 us
  waiting for transfers between devices: 27.3 us -> 77.4 us
    pallas_call x4, Pallas kernels: 91.8 us -> 58.9 us  [attend_back(): pl.pallas_call(functools.partial(back_kernel, scale, scale2, bq, bk), gri...]
    all_gather x12, waiting for transfers between devices: 25 us -> 52.4 us  [whole(): lax.all_gather(part.reshape(-1, part.shape[-1]), 'z', axis=0, tiled=True)]
    pallas_call x25, Pallas kernels: 1290 us -> 1270 us  [plane_call(): pl.pallas_call(kernel, out_shape=out_shape, in_specs=in_specs, out_specs=...]
    pallas_call x4, Pallas kernels: 62.9 us -> 40.1 us  [attend(): pl.pallas_call(functools.partial(attend_kernel, scale2, bq, bk), grid_spe...]
    reduce_scatter x8, waiting for transfers between devices: 0.17 us -> 22.8 us  [reduce_rows(): mine = lax.psum_scatter(sums, 'z', scatter_dimension=0, tiled=True)]
  transfers between devices with their start and end apart: 20 -> 20, of which waited for: 4 -> 11; matrix products, arithmetic and copies ran while one was open for 1% -> 1% of each run, Pallas kernels for 76% -> 73%
where the time goes in v8:
time: 1550 us; the launch traced here: 1530 us
  Pallas kernels  1380 us (89%)
  waiting for transfers between devices  77.4 us (5%)
  local copies, waits for them, and re-layouts  27.2 us (2%)
  other arithmetic  21.7 us (1%)
  between operations  15.5 us (1%)
    pallas_call x25, Pallas kernels, plane_call(): pl.pallas_call(kernel, out_shape=out_shape, in_specs=in_specs, out_specs=...  1270 us
    pallas_call x4, Pallas kernels, attend_back(): pl.pallas_call(functools.partial(back_kernel, scale, scale2, bq, bk), gri...  58.9 us
    all_gather x12, waiting for transfers between devices, whole(): lax.all_gather(part.reshape(-1, part.shape[-1]), 'z', axis=0, tiled=True)  52.4 us
    pallas_call x4, Pallas kernels, attend(): pl.pallas_call(functools.partial(attend_kernel, scale2, bq, bk), grid_spe...  40.1 us
  transfers between devices with their start and end apart: 20, of which 11 were waited for; matrix products, arithmetic and copies ran while one was open for 1% of the time, Pallas kernels for 73%

profile of v8, /device:TPU:2, one launch (start us, length us, event | category | flops | bytes accessed | tf_op | source)
XLA Modules:
  0.0 1525.2 jit_solution(11021272545458944079)
XLA Ops:
  24.1 4.2 concatenate.14
  28.4 42.9 %exchange.5 = (bf16[8,192,640]{2,1,0:T(8,128)(2,1)}, bf16[256,1536]{1,0:T(8,128)(2,1)}) custom-call(bf16[8,192,640]{2,1,0:T(8,128)(2,1)} %bitcast.149, bf16[256,1536]{1,0:T(8,128)(2,1)} %bitcast.216), custom_call_target="tpu_custom_call" | custom-call | bytes 72000000 | tf_op jit(solution)/shard_map/exchange/pallas_call | solution.py:428
  74.6 29.3 %exchange.6 = bf16[8,192,768]{2,1,0:T(8,128)(2,1)} custom-call(bf16[8,192,768]{2,1,0:T(8,128)(2,1)} %get-tuple-element.178.blocks), custom_call_target="tpu_custom_call" | custom-call | bytes 87000000 | tf_op jit(solution)/shard_map/exchange/pallas_call | solution.py:428
  104.5 3.7 fusion
  113.9 29.4 %exchange.7 = bf16[8,192,768]{2,1,0:T(8,128)(2,1)} custom-call(bf16[8,192,768]{2,1,0:T(8,128)(2,1)} %get-tuple-element.180.blocks), custom_call_target="tpu_custom_call" | custom-call | bytes 87000000 | tf_op jit(solution)/shard_map/exchange/pallas_call | solution.py:428
  146.4 22.4 %all-gather.15.cloned.1.call-done.w1_hbm = bf16[1536,768]{1,0:T(8,128)(2,1)} async-done(((bf16[384,768]{1,0:T(8,128)(2,1)}), bf16[1536,768]{1,0:T(8,128)(2,1)}) %all-gather.15.cloned.1.call-update) | async-done | bytes 2359312 | tf_op jit(solution)/shard_map/all_gather | solution.py:1145
  169.1 35.6 %attn_in.4 = (bf16[8,256,1536]{2,1,0:T(8,128)(2,1)}, bf16[2,8,256,128]{3,2,1,0:T(8,128)(2,1)}, bf16[8,256,128]{2,1,0:T(8,128)(2,1)}, bf16[8,256,128]{2,1,0:T(8,128)(2,1)}, f32[2,1536]{1,0:T(2,128)}) custom-call(bf16[256,1536]{1,0:T(8,128)(2,1)} %get-tuple-element.181.h, bf16[1536,640]{1,0:T(8,128)(2,1)} %all-gather.13.cloned.1.call-done.w_hbm.wa_hbm, ...), custom_call_target="tpu_custom_call" | custom-call | bytes 102000000 | tf_op jit(solution)/shard_map/attn_in/pallas_call | solution.py:428
  204.7 10.0 attend.4
  215.8 4.4 all-gather.17.cloned.1.call-done.w2_hbm
  220.2 91.1 %mlp.4 = (f32[256,1536]{1,0:T(8,128)}, bf16[8,256,1536]{2,1,0:T(8,128)(2,1)}, bf16[8,256,1024]{2,1,0:T(8,128)(2,1)}, bf16[8,256,512]{2,1,0:T(8,128)(2,1)}, bf16[256,1536]{1,0:T(8,128)(2,1)}) custom-call(bf16[256,1536]{1,0:T(8,128)(2,1)} %get-tuple-element.181.h, bf16[8,256,192]{2,1,0:T(8,128)(2,1)} %bitcast.141, f32[2,1536]{1,0:T(2,128)} %get-tuple-element.192.gain, ...), custom_call_target="tpu_custom_call" | custom-call | bytes 288000000 | tf_op jit(solution)/shard_map/mlp/pallas_call | solution.py:428
  311.4 4.0 all-gather.21.cloned.1.call-done.w1_hbm
  315.5 35.6 %attn_in.5 = (bf16[8,256,1536]{2,1,0:T(8,128)(2,1)}, bf16[2,8,256,128]{3,2,1,0:T(8,128)(2,1)}, bf16[8,256,128]{2,1,0:T(8,128)(2,1)}, bf16[8,256,128]{2,1,0:T(8,128)(2,1)}, f32[2,1536]{1,0:T(2,128)}) custom-call(bf16[256,1536]{1,0:T(8,128)(2,1)} %get-tuple-element.198.h, bf16[1536,640]{1,0:T(8,128)(2,1)} %all-gather.19.cloned.1.call-done.w_hbm.wa_hbm, ...), custom_call_target="tpu_custom_call" | custom-call | bytes 102000000 | tf_op jit(solution)/shard_map/attn_in/pallas_call | solution.py:428
  351.1 10.0 attend.5
  362.3 4.4 all-gather.23.cloned.1.call-done.w2_hbm
  366.7 91.1 %mlp.5 = (f32[256,1536]{1,0:T(8,128)}, bf16[8,256,1536]{2,1,0:T(8,128)(2,1)}, bf16[8,256,1024]{2,1,0:T(8,128)(2,1)}, bf16[8,256,512]{2,1,0:T(8,128)(2,1)}, bf16[256,1536]{1,0:T(8,128)(2,1)}) custom-call(bf16[256,1536]{1,0:T(8,128)(2,1)} %get-tuple-element.198.h, bf16[8,256,192]{2,1,0:T(8,128)(2,1)} %bitcast.143, f32[2,1536]{1,0:T(2,128)} %get-tuple-element.205.gain, ...), custom_call_target="tpu_custom_call" | custom-call | bytes 288000000 | tf_op jit(solution)/shard_map/mlp/pallas_call | solution.py:428
  457.9 4.4 all-gather.27.cloned.1.call-done.w1_hbm
  462.3 35.6 %attn_in.6 = (bf16[8,256,1536]{2,1,0:T(8,128)(2,1)}, bf16[2,8,256,128]{3,2,1,0:T(8,128)(2,1)}, bf16[8,256,128]{2,1,0:T(8,128)(2,1)}, bf16[8,256,128]{2,1,0:T(8,128)(2,1)}, f32[2,1536]{1,0:T(2,128)}) custom-call(bf16[256,1536]{1,0:T(8,128)(2,1)} %get-tuple-element.211.h, bf16[1536,640]{1,0:T(8,128)(2,1)} %all-gather.25.cloned.1.call-done.w_hbm.wa_hbm, ...), custom_call_target="tpu_custom_call" | custom-call | bytes 102000000 | tf_op jit(solution)/shard_map/attn_in/pallas_call | solution.py:428
  497.9 10.0 attend.6
  509.1 4.1 all-gather.29.cloned.1.call-done.w2_hbm
  513.2 91.1 %mlp.6 = (f32[256,1536]{1,0:T(8,128)}, bf16[8,256,1536]{2,1,0:T(8,128)(2,1)}, bf16[8,256,1024]{2,1,0:T(8,128)(2,1)}, bf16[8,256,512]{2,1,0:T(8,128)(2,1)}, bf16[256,1536]{1,0:T(8,128)(2,1)}) custom-call(bf16[256,1536]{1,0:T(8,128)(2,1)} %get-tuple-element.211.h, bf16[8,256,192]{2,1,0:T(8,128)(2,1)} %bitcast.145, f32[2,1536]{1,0:T(2,128)} %get-tuple-element.218.gain, ...), custom_call_target="tpu_custom_call" | custom-call | bytes 288000000 | tf_op jit(solution)/shard_map/mlp/pallas_call | solution.py:428
  604.3 4.2 all-gather.33.cloned.1.call-done.refs_4_.refs_6_
  609.2 35.6 %attn_in.7 = (bf16[8,256,1536]{2,1,0:T(8,128)(2,1)}, bf16[2,8,256,128]{3,2,1,0:T(8,128)(2,1)}, bf16[8,256,128]{2,1,0:T(8,128)(2,1)}, bf16[8,256,128]{2,1,0:T(8,128)(2,1)}, f32[2,1536]{1,0:T(2,128)}) custom-call(bf16[256,1536]{1,0:T(8,128)(2,1)} %get-tuple-element.224.h.refs_0_, bf16[1536,640]{1,0:T(8,128)(2,1)} %all-gather.31.cloned.1.call-done.w_hbm.refs_3_.wa_hbm, ...), custom_call_target="tpu_custom_call" | custom-call | bytes 102000000 | tf_op jit(solution)/shard_map/attn_in/pallas_call | solution.py:428
  644.8 10.0 attend.7
  654.9 4.4 all-gather.35.cloned.1.call-done.refs_5_.refs_7_
  659.2 107.8 %mlp.7 = (f32[256,1536]{1,0:T(8,128)}, bf16[8,256,1536]{2,1,0:T(8,128)(2,1)}, bf16[8,256,1024]{2,1,0:T(8,128)(2,1)}, bf16[8,256,512]{2,1,0:T(8,128)(2,1)}, bf16[...) custom-call(bf16[256,1536]{1,0:T(8,128)(2,1)} %get-tuple-element.224.h.refs_0_, bf16[8,256,192]{2,1,0:T(8,128)(2,1)} %bitcast.147, ...), custom_call_target="tpu_custom_call" | custom-call | bytes 288000000 | tf_op jit(solution)/shard_map/mlp/pallas_call | solution.py:428
  769.1 71.7 %mlp_back.4 = (f32[256,1536]{1,0:T(8,128)}, f32[1,1536]{1,0:T(1,128)}, bf16[256,1536]{1,0:T(8,128)(2,1)}, bf16[1536,1536]{1,0:T(8,128)(2,1)}, bf16[256,1536]{1,0:T(8,128)(2,1)}) custom-call(bf16[256,1536]{1,0:T(8,128)(2,1)} %broadcast_select_fusion.refs_0_, f32[256,1536]{1,0:T(8,128)} %get-tuple-element.234.refs_1_, ...), custom_call_target="tpu_custom_call" | custom-call | bytes 204000000 | tf_op jit(solution)/shard_map/mlp_back/pallas_call | solution.py:428
  840.9 34.4 %dat_gather.4 = (bf16[8,256,1536]{2,1,0:T(8,128)(2,1)}, bf16[8,256,256]{2,1,0:T(8,128)(2,1)}) custom-call(bf16[256,1536]{1,0:T(8,128)(2,1)} %get-tuple-element.242.dat, bf16[1536,640]{1,0:T(8,128)(2,1)} %all-gather.31.cloned.1.call-done.w_hbm.refs_3_.wa_hbm), custom_call_target="tpu_custom_call" | custom-call | bytes 96000000 | tf_op jit(solution)/shard_map/dat_gather/pallas_call | solution.py:428
  875.3 14.6 attend_back.4
  890.0 39.3 %attn_back.4 = (bf16[256,1536]{1,0:T(8,128)(2,1)}, bf16[1536,640]{1,0:T(8,128)(2,1)}) custom-call(bf16[256,1536]{1,0:T(8,128)(2,1)} %get-tuple-element.224.h.refs_0_, f32[256,1536]{1,0:T(8,128)} %get-tuple-element.240.dmid, f32[2,1536]{1,0:T(2,128)} %get-tuple-element.230.refs_2_.gain, f32[1,1536]{1,0:T(1,128)} %get-tuple-element.241.gain2_grad, ...), custom_call_target="tpu_custom_call" | custom-call | bytes 108000000 | tf_op jit(solution)/shard_map/attn_back/pallas_call | solution.py:428
  929.4 63.6 %mlp_back.5 = (f32[256,1536]{1,0:T(8,128)}, f32[1,1536]{1,0:T(1,128)}, bf16[256,1536]{1,0:T(8,128)(2,1)}, bf16[1536,1536]{1,0:T(8,128)(2,1)}) custom-call(bf16[256,1536]{1,0:T(8,128)(2,1)} %get-tuple-element.255.e, f32[256,1536]{1,0:T(8,128)} %get-tuple-element.256.mid, f32[2,1536]{1,0:T(2,128)} %get-tuple-element.218.gain, ...), custom_call_target="tpu_custom_call" | custom-call | bytes 204000000 | tf_op jit(solution)/shard_map/mlp_back/pallas_call | solution.py:428
  993.1 33.2 %dat_gather.5 = (bf16[8,256,1536]{2,1,0:T(8,128)(2,1)}, bf16[8,256,256]{2,1,0:T(8,128)(2,1)}) custom-call(bf16[256,1536]{1,0:T(8,128)(2,1)} %get-tuple-element.265.dat, bf16[1536,640]{1,0:T(8,128)(2,1)} %all-gather.25.cloned.1.call-done.w_hbm.wa_hbm), custom_call_target="tpu_custom_call" | custom-call | bytes 96000000 | tf_op jit(solution)/shard_map/dat_gather/pallas_call | solution.py:428
  1026.3 14.9 attend_back.5
  1041.3 39.1 %attn_back.5 = (bf16[256,1536]{1,0:T(8,128)(2,1)}, bf16[1536,640]{1,0:T(8,128)(2,1)}) custom-call(bf16[256,1536]{1,0:T(8,128)(2,1)} %get-tuple-element.211.h, f32[256,1536]{1,0:T(8,128)} %get-tuple-element.260.dmid, f32[2,1536]{1,0:T(2,128)} %get-tuple-element.218.gain, f32[1,1536]{1,0:T(1,128)} %get-tuple-element.261.gain2_grad, ...), custom_call_target="tpu_custom_call" | custom-call | bytes 108000000 | tf_op jit(solution)/shard_map/attn_back/pallas_call | solution.py:428
  1080.4 5.0 reduce-scatter.13.cloned.1.call-done
  1085.5 63.7 %mlp_back.6 = (f32[256,1536]{1,0:T(8,128)}, f32[1,1536]{1,0:T(1,128)}, bf16[256,1536]{1,0:T(8,128)(2,1)}, bf16[1536,1536]{1,0:T(8,128)(2,1)}) custom-call(bf16[256,1536]{1,0:T(8,128)(2,1)} %get-tuple-element.276.e, f32[256,1536]{1,0:T(8,128)} %get-tuple-element.277.mid, f32[2,1536]{1,0:T(2,128)} %get-tuple-element.205.gain, ...), custom_call_target="tpu_custom_call" | custom-call | bytes 204000000 | tf_op jit(solution)/shard_map/mlp_back/pallas_call | solution.py:428
  1149.3 35.0 %dat_gather.6 = (bf16[8,256,1536]{2,1,0:T(8,128)(2,1)}, bf16[8,256,256]{2,1,0:T(8,128)(2,1)}) custom-call(bf16[256,1536]{1,0:T(8,128)(2,1)} %get-tuple-element.286.dat, bf16[1536,640]{1,0:T(8,128)(2,1)} %all-gather.19.cloned.1.call-done.w_hbm.wa_hbm), custom_call_target="tpu_custom_call" | custom-call | bytes 96000000 | tf_op jit(solution)/shard_map/dat_gather/pallas_call | solution.py:428
  1184.3 14.6 attend_back.6
  1198.9 38.7 %attn_back.6 = (bf16[256,1536]{1,0:T(8,128)(2,1)}, bf16[1536,640]{1,0:T(8,128)(2,1)}) custom-call(bf16[256,1536]{1,0:T(8,128)(2,1)} %get-tuple-element.198.h, f32[256,1536]{1,0:T(8,128)} %get-tuple-element.281.dmid, f32[2,1536]{1,0:T(2,128)} %get-tuple-element.205.gain, f32[1,1536]{1,0:T(1,128)} %get-tuple-element.282.gain2_grad, ...), custom_call_target="tpu_custom_call" | custom-call | bytes 108000000 | tf_op jit(solution)/shard_map/attn_back/pallas_call | solution.py:428
  1237.7 9.0 reduce-scatter.17.cloned.1.call-done
  1246.7 63.8 %mlp_back.7 = (f32[256,1536]{1,0:T(8,128)}, f32[1,1536]{1,0:T(1,128)}, bf16[256,1536]{1,0:T(8,128)(2,1)}, bf16[1536,1536]{1,0:T(8,128)(2,1)}) custom-call(bf16[256,1536]{1,0:T(8,128)(2,1)} %get-tuple-element.297.e, f32[256,1536]{1,0:T(8,128)} %get-tuple-element.298.mid, f32[2,1536]{1,0:T(2,128)} %get-tuple-element.192.gain, ...), custom_call_target="tpu_custom_call" | custom-call | bytes 204000000 | tf_op jit(solution)/shard_map/mlp_back/pallas_call | solution.py:428
  1310.6 35.0 %dat_gather.7 = (bf16[8,256,1536]{2,1,0:T(8,128)(2,1)}, bf16[8,256,256]{2,1,0:T(8,128)(2,1)}) custom-call(bf16[256,1536]{1,0:T(8,128)(2,1)} %get-tuple-element.307.dat, bf16[1536,640]{1,0:T(8,128)(2,1)} %all-gather.13.cloned.1.call-done.w_hbm.wa_hbm), custom_call_target="tpu_custom_call" | custom-call | bytes 96000000 | tf_op jit(solution)/shard_map/dat_gather/pallas_call | solution.py:428
  1345.6 14.7 attend_back.7
  1360.3 38.7 %attn_back.7 = (bf16[256,1536]{1,0:T(8,128)(2,1)}, bf16[1536,640]{1,0:T(8,128)(2,1)}) custom-call(bf16[256,1536]{1,0:T(8,128)(2,1)} %get-tuple-element.181.h, f32[256,1536]{1,0:T(8,128)} %get-tuple-element.302.dmid, f32[2,1536]{1,0:T(2,128)} %get-tuple-element.192.gain, f32[1,1536]{1,0:T(1,128)} %get-tuple-element.303.gain2_grad, ...), custom_call_target="tpu_custom_call" | custom-call | bytes 108000000 | tf_op jit(solution)/shard_map/attn_back/pallas_call | solution.py:428
  1399.0 8.8 reduce-scatter.21.cloned.1.call-done
  1411.4 54.6 %exchange.8.got = bf16[8,192,1536]{2,1,0:T(8,128)(2,1)} custom-call(bf16[8,192,1536]{2,1,0:T(8,128)(2,1)} %bitcast.140), custom_call_target="tpu_custom_call" | custom-call | bytes 174000000 | tf_op jit(solution)/shard_map/exchange/pallas_call | solution.py:428
  1468.6 34.5 %exchange.9 = (bf16[8,192,640]{2,1,0:T(8,128)(2,1)}, bf16[256,1536]{1,0:T(8,128)(2,1)}) custom-call(bf16[8,192,640]{2,1,0:T(8,128)(2,1)} %bitcast.150, bf16[256,1536]{1,0:T(8,128)(2,1)} %get-tuple-element.327.refs_1_), custom_call_target="tpu_custom_call" | custom-call | bytes 72000000 | tf_op jit(solution)/shard_map/exchange/pallas_call | solution.py:428
  1503.2 4.0 finish_attn.1
  1508.5 7.6 finish.1
  (133 shorter events, 45.8 us)
Async XLA Ops:
  7.2 3.3 copy-start.10
  7.2 139.2 %all-gather.13.cloned.1.call-start = ((), (), s32[]{:S(2)}) async-start(), calls=%async_computation.8 | async-start | bytes 2457600 | tf_op jit(solution)/shard_map/all_gather | solution.py:1145
  8.8 2.3 copy-start.6
  11.1 1.3 copy-start.7
  16.0 1.9 copy-start.1
  18.7 1.9 copy-start.2
  21.3 2.7 copy-start.14
  74.1 94.7 %all-gather.15.cloned.1.call-start = ((), (), s32[]{:S(2)}) async-start(), calls=%async_computation.9 | async-start | bytes 2949120 | tf_op jit(solution)/shard_map/all_gather | solution.py:1145
  74.6 29.3 %copy-start.15 = (s32[4]{0:T(128)S(1)}, s32[4]{0:T(128)}, u32[]{:S(2)}) copy-start(s32[4]{0:T(128)} %param.13) | copy-start | bytes 52
  110.5 1.9 copy-start
  113.9 106.4 %all-gather.17.cloned.1.call-start = ((), (), s32[]{:S(2)}) async-start(), calls=%async_computation.10 | async-start | bytes 2949120 | tf_op jit(solution)/shard_map/all_gather | solution.py:1145
  168.8 142.6 %all-gather.19.cloned.1.call-start = ((), (), s32[]{:S(2)}) async-start(), calls=%async_computation.11 | async-start | bytes 2457600 | tf_op jit(solution)/shard_map/all_gather | solution.py:1145
  214.7 100.7 %all-gather.21.cloned.1.call-start = ((), (), s32[]{:S(2)}) async-start(), calls=%async_computation.12 | async-start | bytes 2949120 | tf_op jit(solution)/shard_map/all_gather | solution.py:1145
  215.3 151.4 %all-gather.23.cloned.1.call-start = ((), (), s32[]{:S(2)}) async-start(), calls=%async_computation.13 | async-start | bytes 2949120 | tf_op jit(solution)/shard_map/all_gather | solution.py:1145
  315.4 142.4 %all-gather.25.cloned.1.call-start = ((), (), s32[]{:S(2)}) async-start(), calls=%async_computation.14 | async-start | bytes 2457600 | tf_op jit(solution)/shard_map/all_gather | solution.py:1145
  361.1 101.1 %all-gather.27.cloned.1.call-start = ((), (), s32[]{:S(2)}) async-start(), calls=%async_computation.15 | async-start | bytes 2949120 | tf_op jit(solution)/shard_map/all_gather | solution.py:1145
  361.8 151.3 %all-gather.29.cloned.1.call-start = ((), (), s32[]{:S(2)}) async-start(), calls=%async_computation.16 | async-start | bytes 2949120 | tf_op jit(solution)/shard_map/all_gather | solution.py:1145
  462.2 142.0 %all-gather.31.cloned.1.call-start = ((), (), s32[]{:S(2)}) async-start(), calls=%async_computation.17 | async-start | bytes 2457600 | tf_op jit(solution)/shard_map/all_gather | solution.py:1145
  507.9 100.6 %all-gather.33.cloned.1.call-start = ((), (), s32[]{:S(2)}) async-start(), calls=%async_computation.18 | async-start | bytes 2949120 | tf_op jit(solution)/shard_map/all_gather | solution.py:1145
  508.6 150.6 %all-gather.35.cloned.1.call-start = ((), (), s32[]{:S(2)}) async-start(), calls=%async_computation.19 | async-start | bytes 2949120 | tf_op jit(solution)/shard_map/all_gather | solution.py:1145
  608.5 320.8 %reduce-scatter.9.cloned.1.call-start = ((), (), s32[]{:S(2)}) async-start(), calls=%async_computation.20 | async-start | bytes 5898240 | tf_op jit(solution)/shard_map/reduce_scatter | solution.py:1148
  840.8 152.2 %reduce-scatter.11.cloned.1.call-start = ((), (), s32[]{:S(2)}) async-start(), calls=%async_computation.21 | async-start | bytes 2457600 | tf_op jit(solution)/shard_map/reduce_scatter | solution.py:1148
  929.3 156.1 %reduce-scatter.13.cloned.1.call-start = ((), (), s32[]{:S(2)}) async-start(), calls=%async_computation.22 | async-start | bytes 5898240 | tf_op jit(solution)/shard_map/reduce_scatter | solution.py:1148
  993.0 156.2 %reduce-scatter.15.cloned.1.call-start = ((), (), s32[]{:S(2)}) async-start(), calls=%async_computation.23 | async-start | bytes 2457600 | tf_op jit(solution)/shard_map/reduce_scatter | solution.py:1148
  1085.4 161.2 %reduce-scatter.17.cloned.1.call-start = ((), (), s32[]{:S(2)}) async-start(), calls=%async_computation.24 | async-start | bytes 5898240 | tf_op jit(solution)/shard_map/reduce_scatter | solution.py:1148
  1149.3 161.2 %reduce-scatter.19.cloned.1.call-start = ((), (), s32[]{:S(2)}) async-start(), calls=%async_computation.25 | async-start | bytes 2457600 | tf_op jit(solution)/shard_map/reduce_scatter | solution.py:1148
  1246.7 161.1 %reduce-scatter.21.cloned.1.call-start = ((), (), s32[]{:S(2)}) async-start(), calls=%async_computation.26 | async-start | bytes 5898240 | tf_op jit(solution)/shard_map/reduce_scatter | solution.py:1148
  1310.6 155.5 %reduce-scatter.23.cloned.1.call-start = ((), (), s32[]{:S(2)}) async-start(), calls=%async_computation.27 | async-start | bytes 2457600 | tf_op jit(solution)/shard_map/reduce_scatter | solution.py:1148
  1360.3 47.5 %copy-start.4 = (bf16[384,1536]{1,0:T(8,128)(2,1)S(1)}, bf16[384,1536]{1,0:T(8,128)(2,1)}, u32[]{:S(2)}) copy-start(bf16[384,1536]{1,0:T(8,128)(2,1)} %reduce-scatter.13.cloned.1.call-done) | copy-start | bytes 3538948
  1360.3 47.5 %copy-start.5 = (bf16[384,1536]{1,0:T(8,128)(2,1)S(1)}, bf16[384,1536]{1,0:T(8,128)(2,1)}, u32[]{:S(2)}) copy-start(bf16[384,1536]{1,0:T(8,128)(2,1)} %reduce-scatter.17.cloned.1.call-done) | copy-start | bytes 3538948
  1399.0 8.8 copy-start.3
  1411.4 54.6 %copy-start.11 = (bf16[384,640]{1,0:T(8,128)(2,1)S(1)}, bf16[384,640]{1,0:T(8,128)(2,1)}, u32[]{:S(2)}) copy-start(bf16[384,640]{1,0:T(8,128)(2,1)} %reduce-scatter.11.cloned.1.call-done) | copy-start | bytes 1474564
  1411.4 54.6 %copy-start.12 = (bf16[384,640]{1,0:T(8,128)(2,1)S(1)}, bf16[384,640]{1,0:T(8,128)(2,1)}, u32[]{:S(2)}) copy-start(bf16[384,640]{1,0:T(8,128)(2,1)} %reduce-scatter.15.cloned.1.call-done) | copy-start | bytes 1474564
  1411.4 54.7 %copy-start.13 = (bf16[384,640]{1,0:T(8,128)(2,1)S(1)}, bf16[384,640]{1,0:T(8,128)(2,1)}, u32[]{:S(2)}) copy-start(bf16[384,640]{1,0:T(8,128)(2,1)} %reduce-scatter.19.cloned.1.call-done) | copy-start | bytes 1474564
  1508.5 7.7 copy-start.8
  1508.5 8.5 copy-start.9
Sparse Core Ops, SparseCore 0:
  74.2 43.0 all-gather.12
  119.4 49.3 all-gather.14
  170.9 49.2 all-gather.16
  221.7 42.3 all-gather.18
  266.1 49.3 all-gather.20
  317.4 49.2 all-gather.22
  368.3 42.3 all-gather.24
  412.8 49.3 all-gather.26
  463.8 49.3 all-gather.28
  514.6 42.3 all-gather.30
  559.1 49.3 all-gather.32
  609.9 49.2 all-gather.34
  841.0 84.5 reduce-scatter.8
  929.4 48.2 reduce-scatter.10
  993.1 92.2 reduce-scatter.12
  1087.6 51.1 reduce-scatter.14
  1149.4 97.1 reduce-scatter.16
  1248.8 51.0 reduce-scatter.18
  1310.7 97.0 reduce-scatter.20
  1409.9 51.0 reduce-scatter.22

commit v9 on v8

--- a/solution.py
+++ b/solution.py
@@ -750,14 +750,17 @@
 
 
 def attn_back_kernel(
-    step, h, dmid, gain, gain2_grad, dq, dk, dv, cosine, sine, o, a1_hbm, dat_hbm, w_hbm, e_out, sums,
-    parts, a1, dat, w, dqkv, gain_rows, total, from_c, via_x, via_y, from_x, from_y, send, recv, local,
+    step, gain, gain2_grad, dq, dk, dv, cosine, sine, h_hbm, dmid_hbm, o_hbm, a1_hbm, dat_hbm, w_hbm, e_out, sums,
+    parts, h, dmid, o, a1, dat, w, dqkv, gain_rows, total, from_c, via_x, via_y, from_x, from_y, send, recv, local,
 ):
     here = token_place()
     loads = Loads(local)
     w_load = loads.start(w_hbm, w)
     a1_load = loads.start(a1_hbm, a1)
     dat_load = loads.start(dat_hbm, dat)
+    o_load = loads.start(o_hbm, o)
+    h_load = loads.start(h_hbm, h)
+    dmid_load = loads.start(dmid_hbm, dmid)
     greet()
     w_load.wait()
 
@@ -775,6 +778,7 @@
         if turn_number == 0:
             a1_load.wait()
             dat_load.wait()
+            o_load.wait()
         half = (count + 1) // 2
         for number in range(turn_number * half, min((turn_number + 1) * half, count)):
             at = slice(number * step, (number + 1) * step)
@@ -782,6 +786,8 @@
             sums[at, QKV:GAIN_AT] = flat_tn(dat, at, o).astype(BF)
 
     net = Scatter(here, parts, total, (from_c, via_x, via_y, from_x, from_y), (send, recv), fill).run(beside)
+    h_load.wait()
+    dmid_load.wait()
     da1 = total[...]
     x = h[...].astype(F32)
     r1 = inverse_of(x)
@@ -809,9 +815,12 @@
             jax.ShapeDtypeStruct((width, PACK), BF),
         ],
         [IN_VMEM, IN_VMEM],
-        [IN_VMEM] * 10 + [ANYWHERE] * 3,
+        [IN_VMEM] * 7 + [ANYWHERE] * 6,
         [
             pltpu.VMEM((8, block, width), BF),
+            pltpu.VMEM(h.shape, h.dtype),
+            pltpu.VMEM(dmid.shape, dmid.dtype),
+            pltpu.VMEM(o.shape, o.dtype),
             pltpu.VMEM((8, block, width), BF),
             pltpu.VMEM((8, block, width), BF),
             pltpu.VMEM(w.shape, BF),
@@ -820,9 +829,9 @@
             pltpu.VMEM((block, width), F32),
         ]
         + scatter_scratch(block, width)
-        + [pltpu.SemaphoreType.DMA((3,))],
+        + [pltpu.SemaphoreType.DMA((6,))],
         36,
-        h, dmid, gain, gain2_grad, dq, dk, dv, cosine, sine, o, a1, dat, w,
+        gain, gain2_grad, dq, dk, dv, cosine, sine, h, dmid, o, a1, dat, w,
     )
 
 
@@ -1129,10 +1138,6 @@
         ],
         axis=2,
     )
-    mlp_pack = jnp.concatenate(
-        [by_rank(w_gate[0]), by_rank(w_up[0]), by_rank(w_down[0].T)], axis=2
-    )
-
     def by_layer(got):
         return got.reshape(layers, halves, rows, -1)
 
@@ -1152,10 +1157,10 @@
         return mine[:, 0]
 
     cut = 3 * ff_cols // 2
-    mlp_blocks = ready(mlp_pack)
     attn_got, hidden_state = exchange(4, ready(attn_pack), inputs[0])
-    first_blocks, attn_got = together(mlp_blocks[..., :cut], attn_got)
-    (first_got,) = exchange(5, first_blocks)
+    gate, up, down, attn_got = together(w_gate[0], w_up[0], w_down[0].T, attn_got)
+    mlp_blocks = ready(jnp.concatenate([by_rank(gate), by_rank(up), by_rank(down)], axis=2))
+    (first_got,) = exchange(5, mlp_blocks[..., :cut])
 
     token_x, token_c, token_y = token_place()
     rank = (token_x * 2 + token_c) * halves + token_y
@@ -1251,9 +1256,9 @@
     def by_place(grads):
         return jnp.stack(grads).reshape(ranks, rows, -1)
 
-    (mlp_home,) = exchange(7, by_place(mlp_grads))
+    mlp_home, input_grad = exchange(7, by_place(mlp_grads), e, True)
     attn_blocks, mlp_home = together(by_place(attn_grads), mlp_home)
-    attn_home, input_grad = exchange(10, attn_blocks, e, True)
+    (attn_home,) = exchange(10, attn_blocks)
     grad_gate, grad_up, grad_down = finish(mlp_home)
     grad_query, grad_key, grad_value, grad_out, gain_sums = finish_attn(attn_home)
     return (

time: 1550 us -> 1540 us (level); the launches traced: 1530 us -> 1530 us
  Pallas kernels: 1380 us -> 1440 us
  waiting for transfers between devices: 77.4 us -> 30.9 us
    pallas_call x4, Pallas kernels: 58.9 us -> 98.3 us  [attend_back(): pl.pallas_call(functools.partial(back_kernel, scale, scale2, bq, bk), gri...]
    pallas_call x4, Pallas kernels: 40.1 us -> 67.4 us  [attend(): pl.pallas_call(functools.partial(attend_kernel, scale2, bq, bk), grid_spe...]
    all_gather x12, waiting for transfers between devices: 52.4 us -> 28.6 us  [whole(): lax.all_gather(part.reshape(-1, part.shape[-1]), 'z', axis=0, tiled=True)]
    reduce_scatter x8, waiting for transfers between devices: 22.8 us -> 0.17 us  [reduce_rows(): mine = lax.psum_scatter(sums, 'z', scatter_dimension=0, tiled=True)]
  transfers between devices with their start and end apart: 20 -> 20, of which waited for: 11 -> 4; matrix products, arithmetic and copies ran while one was open for 1% -> 1% of each run, Pallas kernels for 73% -> 77%
where the time goes in v9:
time: 1540 us; the launch traced here: 1530 us
  Pallas kernels  1440 us (94%)
  waiting for transfers between devices  30.9 us (2%)
  local copies, waits for them, and re-layouts  27.2 us (2%)
  other arithmetic  19.9 us (1%)
  between operations  15.5 us (1%)
    pallas_call x25, Pallas kernels, plane_call(): pl.pallas_call(kernel, out_shape=out_shape, in_specs=in_specs, out_specs=...  1260 us
    pallas_call x4, Pallas kernels, attend_back(): pl.pallas_call(functools.partial(back_kernel, scale, scale2, bq, bk), gri...  98.3 us
    pallas_call x4, Pallas kernels, attend(): pl.pallas_call(functools.partial(attend_kernel, scale2, bq, bk), grid_spe...  67.4 us
  transfers between devices with their start and end apart: 20, of which 4 were waited for; matrix products, arithmetic and copies ran while one was open for 1% of the time, Pallas kernels for 77%

profile of v9, /device:TPU:2, one launch (start us, length us, event | category | flops | bytes accessed | tf_op | source)
XLA Modules:
  0.0 1531.6 jit_solution(13106097541449399640)
XLA Ops:
  13.4 4.2 concatenate.14
  17.6 42.9 %exchange.5 = (bf16[8,192,640]{2,1,0:T(8,128)(2,1)}, bf16[256,1536]{1,0:T(8,128)(2,1)}) custom-call(bf16[8,192,640]{2,1,0:T(8,128)(2,1)} %bitcast.151, bf16[256,1536]{1,0:T(8,128)(2,1)} %bitcast.219), custom_call_target="tpu_custom_call" | custom-call | bytes 72000000 | tf_op jit(solution)/shard_map/exchange/pallas_call | solution.py:428
  60.5 2.9 fusion.7
  68.7 2.7 fusion.4
  71.4 29.2 %exchange.6 = bf16[8,192,768]{2,1,0:T(8,128)(2,1)} custom-call(bf16[8,192,768]{2,1,0:T(8,128)(2,1)} %get-tuple-element.345.blocks), custom_call_target="tpu_custom_call" | custom-call | bytes 87000000 | tf_op jit(solution)/shard_map/exchange/pallas_call | solution.py:428
  101.2 3.7 fusion
  107.2 1.9 select_maximum_fusion
  110.6 29.4 %exchange.7 = bf16[8,192,768]{2,1,0:T(8,128)(2,1)} custom-call(bf16[8,192,768]{2,1,0:T(8,128)(2,1)} %get-tuple-element.184.blocks), custom_call_target="tpu_custom_call" | custom-call | bytes 87000000 | tf_op jit(solution)/shard_map/exchange/pallas_call | solution.py:428
  140.0 3.0 fusion.5
  143.0 17.8 %all-gather.15.cloned.1.call-done.w1_hbm = bf16[1536,768]{1,0:T(8,128)(2,1)} async-done(((bf16[384,768]{1,0:T(8,128)(2,1)}), bf16[1536,768]{1,0:T(8,128)(2,1)}) %all-gather.15.cloned.1.call-update) | async-done | bytes 2359312 | tf_op jit(solution)/shard_map/all_gather | solution.py:1150
  161.2 35.6 %attn_in.4 = (bf16[8,256,1536]{2,1,0:T(8,128)(2,1)}, bf16[2,8,256,128]{3,2,1,0:T(8,128)(2,1)}, bf16[8,256,128]{2,1,0:T(8,128)(2,1)}, bf16[8,256,128]{2,1,0:T(8,128)(2,1)}, f32[2,1536]{1,0:T(2,128)}) custom-call(bf16[256,1536]{1,0:T(8,128)(2,1)} %get-tuple-element.185.h.h_hbm, bf16[1536,640]{1,0:T(8,128)(2,1)} %all-gather.13.cloned.1.call-done.w_hbm.wa_hbm, ...), custom_call_target="tpu_custom_call" | custom-call | bytes 102000000 | tf_op jit(solution)/shard_map/attn_in/pallas_call | solution.py:428
  196.8 16.8 %attend.4 = (bf16[2048,192]{1,0:T(8,128)(2,1)}, f32[4,1,1024]{2,1,0:T(1,128)}) custom-call(s32[2,4]{1,0:T(2,128)} %pad_add_fusion.bounds, s32[1]{0:T(128)} %dynamic_slice.3.length, bf16[2,2048,128]{2,1,0:T(8,128)(2,1)} %bitcast.157, bf16[2048,128]{1,0:T(8,128)(2,1)} %bitcast.176, bf16[2048,128]{1,0:T(8,128)(2,1)} %bitcast.178, ...), custom_call_target="tpu_custom_call" | custom-call | bytes 45000000 | tf_op jit(solution)/shard_map/attend/pallas_call | solution.py:994
  214.7 89.4 %mlp.4 = (f32[256,1536]{1,0:T(8,128)}, bf16[8,256,1536]{2,1,0:T(8,128)(2,1)}, bf16[8,256,1024]{2,1,0:T(8,128)(2,1)}, bf16[8,256,512]{2,1,0:T(8,128)(2,1)}, bf16[256,1536]{1,0:T(8,128)(2,1)}) custom-call(bf16[256,1536]{1,0:T(8,128)(2,1)} %get-tuple-element.185.h.h_hbm, bf16[8,256,192]{2,1,0:T(8,128)(2,1)} %bitcast.143, f32[2,1536]{1,0:T(2,128)} %get-tuple-element.196.gain, ...), custom_call_target="tpu_custom_call" | custom-call | bytes 288000000 | tf_op jit(solution)/shard_map/mlp/pallas_call | solution.py:428
  304.2 3.5 all-gather.21.cloned.1.call-done.w1_hbm
  307.8 35.5 %attn_in.5 = (bf16[8,256,1536]{2,1,0:T(8,128)(2,1)}, bf16[2,8,256,128]{3,2,1,0:T(8,128)(2,1)}, bf16[8,256,128]{2,1,0:T(8,128)(2,1)}, bf16[8,256,128]{2,1,0:T(8,128)(2,1)}, f32[2,1536]{1,0:T(2,128)}) custom-call(bf16[256,1536]{1,0:T(8,128)(2,1)} %get-tuple-element.202.h.h_hbm, bf16[1536,640]{1,0:T(8,128)(2,1)} %all-gather.19.cloned.1.call-done.w_hbm.wa_hbm, ...), custom_call_target="tpu_custom_call" | custom-call | bytes 102000000 | tf_op jit(solution)/shard_map/attn_in/pallas_call | solution.py:428
  343.3 16.8 %attend.5 = (bf16[2048,192]{1,0:T(8,128)(2,1)}, f32[4,1,1024]{2,1,0:T(1,128)}) custom-call(s32[2,4]{1,0:T(2,128)} %pad_add_fusion.bounds, s32[1]{0:T(128)} %dynamic_slice.3.length, bf16[2,2048,128]{2,1,0:T(8,128)(2,1)} %bitcast.159, bf16[2048,128]{1,0:T(8,128)(2,1)} %bitcast.180, bf16[2048,128]{1,0:T(8,128)(2,1)} %bitcast.182, ...), custom_call_target="tpu_custom_call" | custom-call | bytes 45000000 | tf_op jit(solution)/shard_map/attend/pallas_call | solution.py:994
  361.4 89.4 %mlp.5 = (f32[256,1536]{1,0:T(8,128)}, bf16[8,256,1536]{2,1,0:T(8,128)(2,1)}, bf16[8,256,1024]{2,1,0:T(8,128)(2,1)}, bf16[8,256,512]{2,1,0:T(8,128)(2,1)}, bf16[256,1536]{1,0:T(8,128)(2,1)}) custom-call(bf16[256,1536]{1,0:T(8,128)(2,1)} %get-tuple-element.202.h.h_hbm, bf16[8,256,192]{2,1,0:T(8,128)(2,1)} %bitcast.145, f32[2,1536]{1,0:T(2,128)} %get-tuple-element.209.gain, ...), custom_call_target="tpu_custom_call" | custom-call | bytes 288000000 | tf_op jit(solution)/shard_map/mlp/pallas_call | solution.py:428
  450.9 3.6 all-gather.27.cloned.1.call-done.w1_hbm
  454.6 35.6 %attn_in.6 = (bf16[8,256,1536]{2,1,0:T(8,128)(2,1)}, bf16[2,8,256,128]{3,2,1,0:T(8,128)(2,1)}, bf16[8,256,128]{2,1,0:T(8,128)(2,1)}, bf16[8,256,128]{2,1,0:T(8,128)(2,1)}, f32[2,1536]{1,0:T(2,128)}) custom-call(bf16[256,1536]{1,0:T(8,128)(2,1)} %get-tuple-element.215.h.h_hbm, bf16[1536,640]{1,0:T(8,128)(2,1)} %all-gather.25.cloned.1.call-done.w_hbm.wa_hbm, ...), custom_call_target="tpu_custom_call" | custom-call | bytes 102000000 | tf_op jit(solution)/shard_map/attn_in/pallas_call | solution.py:428
  490.2 16.8 %attend.6 = (bf16[2048,192]{1,0:T(8,128)(2,1)}, f32[4,1,1024]{2,1,0:T(1,128)}) custom-call(s32[2,4]{1,0:T(2,128)} %pad_add_fusion.bounds, s32[1]{0:T(128)} %dynamic_slice.3.length, bf16[2,2048,128]{2,1,0:T(8,128)(2,1)} %bitcast.161, bf16[2048,128]{1,0:T(8,128)(2,1)} %bitcast.184, bf16[2048,128]{1,0:T(8,128)(2,1)} %bitcast.186, ...), custom_call_target="tpu_custom_call" | custom-call | bytes 45000000 | tf_op jit(solution)/shard_map/attend/pallas_call | solution.py:994
  508.3 89.5 %mlp.6 = (f32[256,1536]{1,0:T(8,128)}, bf16[8,256,1536]{2,1,0:T(8,128)(2,1)}, bf16[8,256,1024]{2,1,0:T(8,128)(2,1)}, bf16[8,256,512]{2,1,0:T(8,128)(2,1)}, bf16[256,1536]{1,0:T(8,128)(2,1)}) custom-call(bf16[256,1536]{1,0:T(8,128)(2,1)} %get-tuple-element.215.h.h_hbm, bf16[8,256,192]{2,1,0:T(8,128)(2,1)} %bitcast.147, f32[2,1536]{1,0:T(2,128)} %get-tuple-element.222.gain, ...), custom_call_target="tpu_custom_call" | custom-call | bytes 288000000 | tf_op jit(solution)/shard_map/mlp/pallas_call | solution.py:428
  597.8 3.5 all-gather.33.cloned.1.call-done.refs_4_.refs_6_
  602.0 35.6 %attn_in.7 = (bf16[8,256,1536]{2,1,0:T(8,128)(2,1)}, bf16[2,8,256,128]{3,2,1,0:T(8,128)(2,1)}, bf16[8,256,128]{2,1,0:T(8,128)(2,1)}, bf16[8,256,128]{2,1,0:T(8,128)(2,1)}, f32[2,1536]{1,0:T(2,128)}) custom-call(bf16[256,1536]{1,0:T(8,128)(2,1)} %get-tuple-element.228.h.refs_0_.h_hbm, bf16[1536,640]{1,0:T(8,128)(2,1)} %all-gather.31.cloned.1.call-done.w_hbm.refs_3_.wa_hbm, ...), custom_call_target="tpu_custom_call" | custom-call | bytes 102000000 | tf_op jit(solution)/shard_map/attn_in/pallas_call | solution.py:428
  637.7 16.8 %attend.7 = (bf16[2048,192]{1,0:T(8,128)(2,1)}, f32[4,1,1024]{2,1,0:T(1,128)}) custom-call(s32[2,4]{1,0:T(2,128)} %pad_add_fusion.bounds, s32[1]{0:T(128)} %dynamic_slice.3.length, bf16[2,2048,128]{2,1,0:T(8,128)(2,1)} %bitcast.163, bf16[2048,128]{1,0:T(8,128)(2,1)} %bitcast.188, bf16[2048,128]{1,0:T(8,128)(2,1)} %bitcast.190, ...), custom_call_target="tpu_custom_call" | custom-call | bytes 45000000 | tf_op jit(solution)/shard_map/attend/pallas_call | solution.py:994
  654.5 107.4 %mlp.7 = (f32[256,1536]{1,0:T(8,128)}, bf16[8,256,1536]{2,1,0:T(8,128)(2,1)}, bf16[8,256,1024]{2,1,0:T(8,128)(2,1)}, bf16[8,256,512]{2,1,0:T(8,128)(2,1)}, bf16[...) custom-call(bf16[256,1536]{1,0:T(8,128)(2,1)} %get-tuple-element.228.h.refs_0_.h_hbm, bf16[8,256,192]{2,1,0:T(8,128)(2,1)} %bitcast.149, ...), custom_call_target="tpu_custom_call" | custom-call | bytes 288000000 | tf_op jit(solution)/shard_map/mlp/pallas_call | solution.py:428
  761.9 2.1 broadcast_select_fusion.refs_0_
  764.0 71.6 %mlp_back.4 = (f32[256,1536]{1,0:T(8,128)}, f32[1,1536]{1,0:T(1,128)}, bf16[256,1536]{1,0:T(8,128)(2,1)}, bf16[1536,1536]{1,0:T(8,128)(2,1)}, bf16[256,1536]{1,0:T(8,128)(2,1)}) custom-call(bf16[256,1536]{1,0:T(8,128)(2,1)} %broadcast_select_fusion.refs_0_, f32[256,1536]{1,0:T(8,128)} %get-tuple-element.238.refs_1_, ...), custom_call_target="tpu_custom_call" | custom-call | bytes 204000000 | tf_op jit(solution)/shard_map/mlp_back/pallas_call | solution.py:428
  835.7 34.5 %dat_gather.4 = (bf16[8,256,1536]{2,1,0:T(8,128)(2,1)}, bf16[8,256,256]{2,1,0:T(8,128)(2,1)}) custom-call(bf16[256,1536]{1,0:T(8,128)(2,1)} %get-tuple-element.245.dat, bf16[1536,640]{1,0:T(8,128)(2,1)} %all-gather.31.cloned.1.call-done.w_hbm.refs_3_.wa_hbm), custom_call_target="tpu_custom_call" | custom-call | bytes 96000000 | tf_op jit(solution)/shard_map/dat_gather/pallas_call | solution.py:428
  870.2 24.5 %attend_back.4 = (bf16[2048,256]{1,0:T(8,128)(2,1)}, f32[2048,128]{1,0:T(8,128)}, f32[2048,128]{1,0:T(8,128)}) custom-call(s32[2,4]{1,0:T(2,128)} %pad_add_fusion.bounds, s32[1]{0:T(128)} %dynamic_slice.3.length, bf16[2,2048,128]{2,1,0:T(8,128)(2,1)} %bitcast.164, bf16[2048,128]{1,0:T(8,128)(2,1)} %bitcast.189, bf16[2048,128]{1,0:T(8,128)(2,1)} %bitcast.191, ...), custom_call_target="tpu_custom_call" | custom-call | bytes 65000000 | tf_op jit(solution)/shard_map/attend_back/pallas_call | solution.py:1061
  894.7 38.2 %attn_back.4 = (bf16[256,1536]{1,0:T(8,128)(2,1)}, bf16[1536,640]{1,0:T(8,128)(2,1)}) custom-call(f32[2,1536]{1,0:T(2,128)} %get-tuple-element.234.refs_2_.gain, f32[1,1536]{1,0:T(1,128)} %get-tuple-element.244.gain2_grad, bf16[8,256,256]{2,1,0:T(8,128)(2,1)} %bitcast.213, f32[8,256,128]{2,1,0:T(8,128)} %bitcast.214, f32[8,256,128]{2,1,0:T(8,128)} %bitcast.215, ...), custom_call_target="tpu_custom_call" | custom-call | bytes 108000000 | tf_op jit(solution)/shard_map/attn_back/pallas_call | solution.py:428
  933.0 63.9 %mlp_back.5 = (f32[256,1536]{1,0:T(8,128)}, f32[1,1536]{1,0:T(1,128)}, bf16[256,1536]{1,0:T(8,128)(2,1)}, bf16[1536,1536]{1,0:T(8,128)(2,1)}) custom-call(bf16[256,1536]{1,0:T(8,128)(2,1)} %get-tuple-element.259.e, f32[256,1536]{1,0:T(8,128)} %get-tuple-element.260.mid, f32[2,1536]{1,0:T(2,128)} %get-tuple-element.222.gain, ...), custom_call_target="tpu_custom_call" | custom-call | bytes 204000000 | tf_op jit(solution)/shard_map/mlp_back/pallas_call | solution.py:428
  997.0 33.4 %dat_gather.5 = (bf16[8,256,1536]{2,1,0:T(8,128)(2,1)}, bf16[8,256,256]{2,1,0:T(8,128)(2,1)}) custom-call(bf16[256,1536]{1,0:T(8,128)(2,1)} %get-tuple-element.268.dat, bf16[1536,640]{1,0:T(8,128)(2,1)} %all-gather.25.cloned.1.call-done.w_hbm.wa_hbm), custom_call_target="tpu_custom_call" | custom-call | bytes 96000000 | tf_op jit(solution)/shard_map/dat_gather/pallas_call | solution.py:428
  1030.4 24.7 %attend_back.5 = (bf16[2048,256]{1,0:T(8,128)(2,1)}, f32[2048,128]{1,0:T(8,128)}, f32[2048,128]{1,0:T(8,128)}) custom-call(s32[2,4]{1,0:T(2,128)} %pad_add_fusion.bounds, s32[1]{0:T(128)} %dynamic_slice.3.length, bf16[2,2048,128]{2,1,0:T(8,128)(2,1)} %bitcast.162, bf16[2048,128]{1,0:T(8,128)(2,1)} %bitcast.185, bf16[2048,128]{1,0:T(8,128)(2,1)} %bitcast.187, ...), custom_call_target="tpu_custom_call" | custom-call | bytes 65000000 | tf_op jit(solution)/shard_map/attend_back/pallas_call | solution.py:1061
  1055.2 38.2 %attn_back.5 = (bf16[256,1536]{1,0:T(8,128)(2,1)}, bf16[1536,640]{1,0:T(8,128)(2,1)}) custom-call(f32[2,1536]{1,0:T(2,128)} %get-tuple-element.222.gain, f32[1,1536]{1,0:T(1,128)} %get-tuple-element.264.gain2_grad, bf16[8,256,256]{2,1,0:T(8,128)(2,1)} %bitcast.207, f32[8,256,128]{2,1,0:T(8,128)} %bitcast.208, f32[8,256,128]{2,1,0:T(8,128)} %bitcast.209, ...), custom_call_target="tpu_custom_call" | custom-call | bytes 108000000 | tf_op jit(solution)/shard_map/attn_back/pallas_call | solution.py:428
  1093.4 63.9 %mlp_back.6 = (f32[256,1536]{1,0:T(8,128)}, f32[1,1536]{1,0:T(1,128)}, bf16[256,1536]{1,0:T(8,128)(2,1)}, bf16[1536,1536]{1,0:T(8,128)(2,1)}) custom-call(bf16[256,1536]{1,0:T(8,128)(2,1)} %get-tuple-element.280.e, f32[256,1536]{1,0:T(8,128)} %get-tuple-element.281.mid, f32[2,1536]{1,0:T(2,128)} %get-tuple-element.209.gain, ...), custom_call_target="tpu_custom_call" | custom-call | bytes 204000000 | tf_op jit(solution)/shard_map/mlp_back/pallas_call | solution.py:428
  1157.5 33.2 %dat_gather.6 = (bf16[8,256,1536]{2,1,0:T(8,128)(2,1)}, bf16[8,256,256]{2,1,0:T(8,128)(2,1)}) custom-call(bf16[256,1536]{1,0:T(8,128)(2,1)} %get-tuple-element.289.dat, bf16[1536,640]{1,0:T(8,128)(2,1)} %all-gather.19.cloned.1.call-done.w_hbm.wa_hbm), custom_call_target="tpu_custom_call" | custom-call | bytes 96000000 | tf_op jit(solution)/shard_map/dat_gather/pallas_call | solution.py:428
  1190.7 24.5 %attend_back.6 = (bf16[2048,256]{1,0:T(8,128)(2,1)}, f32[2048,128]{1,0:T(8,128)}, f32[2048,128]{1,0:T(8,128)}) custom-call(s32[2,4]{1,0:T(2,128)} %pad_add_fusion.bounds, s32[1]{0:T(128)} %dynamic_slice.3.length, bf16[2,2048,128]{2,1,0:T(8,128)(2,1)} %bitcast.160, bf16[2048,128]{1,0:T(8,128)(2,1)} %bitcast.181, bf16[2048,128]{1,0:T(8,128)(2,1)} %bitcast.183, ...), custom_call_target="tpu_custom_call" | custom-call | bytes 65000000 | tf_op jit(solution)/shard_map/attend_back/pallas_call | solution.py:1061
  1215.3 38.3 %attn_back.6 = (bf16[256,1536]{1,0:T(8,128)(2,1)}, bf16[1536,640]{1,0:T(8,128)(2,1)}) custom-call(f32[2,1536]{1,0:T(2,128)} %get-tuple-element.209.gain, f32[1,1536]{1,0:T(1,128)} %get-tuple-element.285.gain2_grad, bf16[8,256,256]{2,1,0:T(8,128)(2,1)} %bitcast.210, f32[8,256,128]{2,1,0:T(8,128)} %bitcast.211, f32[8,256,128]{2,1,0:T(8,128)} %bitcast.212, ...), custom_call_target="tpu_custom_call" | custom-call | bytes 108000000 | tf_op jit(solution)/shard_map/attn_back/pallas_call | solution.py:428
  1253.7 64.0 %mlp_back.7 = (f32[256,1536]{1,0:T(8,128)}, f32[1,1536]{1,0:T(1,128)}, bf16[256,1536]{1,0:T(8,128)(2,1)}, bf16[1536,1536]{1,0:T(8,128)(2,1)}) custom-call(bf16[256,1536]{1,0:T(8,128)(2,1)} %get-tuple-element.301.e, f32[256,1536]{1,0:T(8,128)} %get-tuple-element.302.mid, f32[2,1536]{1,0:T(2,128)} %get-tuple-element.196.gain, ...), custom_call_target="tpu_custom_call" | custom-call | bytes 204000000 | tf_op jit(solution)/shard_map/mlp_back/pallas_call | solution.py:428
  1317.8 33.3 %dat_gather.7 = (bf16[8,256,1536]{2,1,0:T(8,128)(2,1)}, bf16[8,256,256]{2,1,0:T(8,128)(2,1)}) custom-call(bf16[256,1536]{1,0:T(8,128)(2,1)} %get-tuple-element.310.dat, bf16[1536,640]{1,0:T(8,128)(2,1)} %all-gather.13.cloned.1.call-done.w_hbm.wa_hbm), custom_call_target="tpu_custom_call" | custom-call | bytes 96000000 | tf_op jit(solution)/shard_map/dat_gather/pallas_call | solution.py:428
  1351.0 24.5 %attend_back.7 = (bf16[2048,256]{1,0:T(8,128)(2,1)}, f32[2048,128]{1,0:T(8,128)}, f32[2048,128]{1,0:T(8,128)}) custom-call(s32[2,4]{1,0:T(2,128)} %pad_add_fusion.bounds, s32[1]{0:T(128)} %dynamic_slice.3.length, bf16[2,2048,128]{2,1,0:T(8,128)(2,1)} %bitcast.158, bf16[2048,128]{1,0:T(8,128)(2,1)} %bitcast.177, bf16[2048,128]{1,0:T(8,128)(2,1)} %bitcast.179, ...), custom_call_target="tpu_custom_call" | custom-call | bytes 65000000 | tf_op jit(solution)/shard_map/attend_back/pallas_call | solution.py:1061
  1375.6 38.4 %attn_back.7 = (bf16[256,1536]{1,0:T(8,128)(2,1)}, bf16[1536,640]{1,0:T(8,128)(2,1)}) custom-call(f32[2,1536]{1,0:T(2,128)} %get-tuple-element.196.gain, f32[1,1536]{1,0:T(1,128)} %get-tuple-element.306.gain2_grad, bf16[8,256,256]{2,1,0:T(8,128)(2,1)} %bitcast.204, f32[8,256,128]{2,1,0:T(8,128)} %bitcast.205, f32[8,256,128]{2,1,0:T(8,128)} %bitcast.206, ...), custom_call_target="tpu_custom_call" | custom-call | bytes 108000000 | tf_op jit(solution)/shard_map/attn_back/pallas_call | solution.py:428
  1415.2 3.6 pad_maximum_fusion
  1418.9 63.0 %exchange.8 = (bf16[8,192,1536]{2,1,0:T(8,128)(2,1)}, bf16[256,1536]{1,0:T(8,128)(2,1)}) custom-call(bf16[8,192,1536]{2,1,0:T(8,128)(2,1)} %bitcast.142, bf16[256,1536]{1,0:T(8,128)(2,1)} %get-tuple-element.326.refs_1_), custom_call_target="tpu_custom_call" | custom-call | bytes 174000000 | tf_op jit(solution)/shard_map/exchange/pallas_call | solution.py:428
  1481.9 2.6 pad_maximum_fusion.1
  1484.5 25.0 %exchange.9.got = bf16[8,192,640]{2,1,0:T(8,128)(2,1)} custom-call(bf16[8,192,640]{2,1,0:T(8,128)(2,1)} %bitcast.152), custom_call_target="tpu_custom_call" | custom-call | bytes 72000000 | tf_op jit(solution)/shard_map/exchange/pallas_call | solution.py:428
  1509.5 4.0 finish_attn.1
  1514.9 7.6 finish.1
  (132 shorter events, 24.9 us)
Async XLA Ops:
  7.2 3.3 copy-start.11
  7.2 135.9 %all-gather.13.cloned.1.call-start = ((), (), s32[]{:S(2)}) async-start(), calls=%async_computation.8 | async-start | bytes 2457600 | tf_op jit(solution)/shard_map/all_gather | solution.py:1150
  8.8 2.3 copy-start.7
  11.1 1.3 copy-start.8
  12.4 0.8 copy-start.15
  60.5 3.3 copy-start.1
  63.5 97.4 %all-gather.15.cloned.1.call-start = ((), (), s32[]{:S(2)}) async-start(), calls=%async_computation.9 | async-start | bytes 2949120 | tf_op jit(solution)/shard_map/all_gather | solution.py:1150
  64.0 1.9 copy-start.2
  65.9 1.9 copy-start.3
  71.4 29.2 %copy-start.16 = (s32[4]{0:T(128)S(1)}, s32[4]{0:T(128)}, u32[]{:S(2)}) copy-start(s32[4]{0:T(128)} %param.13) | copy-start | bytes 52
  107.2 1.9 copy-start
  110.5 104.2 %all-gather.17.cloned.1.call-start = ((), (), s32[]{:S(2)}) async-start(), calls=%async_computation.10 | async-start | bytes 2949120 | tf_op jit(solution)/shard_map/all_gather | solution.py:1150
  160.9 143.3 %all-gather.19.cloned.1.call-start = ((), (), s32[]{:S(2)}) async-start(), calls=%async_computation.11 | async-start | bytes 2457600 | tf_op jit(solution)/shard_map/all_gather | solution.py:1150
  213.6 94.1 %all-gather.21.cloned.1.call-start = ((), (), s32[]{:S(2)}) async-start(), calls=%async_computation.12 | async-start | bytes 2949120 | tf_op jit(solution)/shard_map/all_gather | solution.py:1150
  214.2 147.2 %all-gather.23.cloned.1.call-start = ((), (), s32[]{:S(2)}) async-start(), calls=%async_computation.13 | async-start | bytes 2949120 | tf_op jit(solution)/shard_map/all_gather | solution.py:1150
  307.7 143.1 %all-gather.25.cloned.1.call-start = ((), (), s32[]{:S(2)}) async-start(), calls=%async_computation.14 | async-start | bytes 2457600 | tf_op jit(solution)/shard_map/all_gather | solution.py:1150
  360.2 94.3 %all-gather.27.cloned.1.call-start = ((), (), s32[]{:S(2)}) async-start(), calls=%async_computation.15 | async-start | bytes 2949120 | tf_op jit(solution)/shard_map/all_gather | solution.py:1150
  360.9 147.3 %all-gather.29.cloned.1.call-start = ((), (), s32[]{:S(2)}) async-start(), calls=%async_computation.16 | async-start | bytes 2949120 | tf_op jit(solution)/shard_map/all_gather | solution.py:1150
  454.5 143.2 %all-gather.31.cloned.1.call-start = ((), (), s32[]{:S(2)}) async-start(), calls=%async_computation.17 | async-start | bytes 2457600 | tf_op jit(solution)/shard_map/all_gather | solution.py:1150
  507.0 94.2 %all-gather.33.cloned.1.call-start = ((), (), s32[]{:S(2)}) async-start(), calls=%async_computation.18 | async-start | bytes 2949120 | tf_op jit(solution)/shard_map/all_gather | solution.py:1150
  507.8 146.7 %all-gather.35.cloned.1.call-start = ((), (), s32[]{:S(2)}) async-start(), calls=%async_computation.19 | async-start | bytes 2949120 | tf_op jit(solution)/shard_map/all_gather | solution.py:1150
  601.3 331.7 %reduce-scatter.9.cloned.1.call-start = ((), (), s32[]{:S(2)}) async-start(), calls=%async_computation.20 | async-start | bytes 5898240 | tf_op jit(solution)/shard_map/reduce_scatter | solution.py:1153
  835.6 161.3 %reduce-scatter.11.cloned.1.call-start = ((), (), s32[]{:S(2)}) async-start(), calls=%async_computation.21 | async-start | bytes 2457600 | tf_op jit(solution)/shard_map/reduce_scatter | solution.py:1153
  933.0 160.4 %reduce-scatter.13.cloned.1.call-start = ((), (), s32[]{:S(2)}) async-start(), calls=%async_computation.22 | async-start | bytes 5898240 | tf_op jit(solution)/shard_map/reduce_scatter | solution.py:1153
  997.0 160.4 %reduce-scatter.15.cloned.1.call-start = ((), (), s32[]{:S(2)}) async-start(), calls=%async_computation.23 | async-start | bytes 2457600 | tf_op jit(solution)/shard_map/reduce_scatter | solution.py:1153
  1093.4 160.2 %reduce-scatter.17.cloned.1.call-start = ((), (), s32[]{:S(2)}) async-start(), calls=%async_computation.24 | async-start | bytes 5898240 | tf_op jit(solution)/shard_map/reduce_scatter | solution.py:1153
  1157.4 160.2 %reduce-scatter.19.cloned.1.call-start = ((), (), s32[]{:S(2)}) async-start(), calls=%async_computation.25 | async-start | bytes 2457600 | tf_op jit(solution)/shard_map/reduce_scatter | solution.py:1153
  1253.7 160.3 %reduce-scatter.21.cloned.1.call-start = ((), (), s32[]{:S(2)}) async-start(), calls=%async_computation.26 | async-start | bytes 5898240 | tf_op jit(solution)/shard_map/reduce_scatter | solution.py:1153
  1317.7 164.2 %reduce-scatter.23.cloned.1.call-start = ((), (), s32[]{:S(2)}) async-start(), calls=%async_computation.27 | async-start | bytes 2457600 | tf_op jit(solution)/shard_map/reduce_scatter | solution.py:1153
  1375.6 38.5 %copy-start.5 = (bf16[384,1536]{1,0:T(8,128)(2,1)S(1)}, bf16[384,1536]{1,0:T(8,128)(2,1)}, u32[]{:S(2)}) copy-start(bf16[384,1536]{1,0:T(8,128)(2,1)} %reduce-scatter.13.cloned.1.call-done) | copy-start | bytes 3538948
  1375.6 38.5 %copy-start.6 = (bf16[384,1536]{1,0:T(8,128)(2,1)S(1)}, bf16[384,1536]{1,0:T(8,128)(2,1)}, u32[]{:S(2)}) copy-start(bf16[384,1536]{1,0:T(8,128)(2,1)} %reduce-scatter.17.cloned.1.call-done) | copy-start | bytes 3538948
  1414.0 1.3 copy-start.4
  1418.8 63.0 %copy-start.12 = (bf16[384,640]{1,0:T(8,128)(2,1)S(1)}, bf16[384,640]{1,0:T(8,128)(2,1)}, u32[]{:S(2)}) copy-start(bf16[384,640]{1,0:T(8,128)(2,1)} %reduce-scatter.11.cloned.1.call-done) | copy-start | bytes 1474564
  1418.8 63.1 %copy-start.13 = (bf16[384,640]{1,0:T(8,128)(2,1)S(1)}, bf16[384,640]{1,0:T(8,128)(2,1)}, u32[]{:S(2)}) copy-start(bf16[384,640]{1,0:T(8,128)(2,1)} %reduce-scatter.15.cloned.1.call-done) | copy-start | bytes 1474564
  1418.9 63.1 %copy-start.14 = (bf16[384,640]{1,0:T(8,128)(2,1)S(1)}, bf16[384,640]{1,0:T(8,128)(2,1)}, u32[]{:S(2)}) copy-start(bf16[384,640]{1,0:T(8,128)(2,1)} %reduce-scatter.19.cloned.1.call-done) | copy-start | bytes 1474564
  1514.9 7.7 copy-start.9
  1514.9 8.5 copy-start.10
Sparse Core Ops, SparseCore 0:
  63.6 43.0 all-gather.12
  110.7 50.1 all-gather.14
  163.0 49.2 all-gather.16
  213.8 42.5 all-gather.18
  258.3 49.3 all-gather.20
  309.7 49.2 all-gather.22
  360.6 42.3 all-gather.24
  405.1 49.3 all-gather.26
  456.1 49.3 all-gather.28
  507.2 42.5 all-gather.30
  551.9 49.3 all-gather.32
  602.7 49.2 all-gather.34
  835.8 84.1 reduce-scatter.8
  933.1 39.4 reduce-scatter.10
  997.1 82.9 reduce-scatter.12
  1093.5 39.0 reduce-scatter.14
  1157.6 82.8 reduce-scatter.16
  1253.8 39.0 reduce-scatter.18
  1317.8 82.8 reduce-scatter.20
  1414.1 53.1 reduce-scatter.22

commit v10 on v9

--- a/solution.py
+++ b/solution.py
@@ -1157,7 +1157,7 @@
         return mine[:, 0]
 
     cut = 3 * ff_cols // 2
-    attn_got, hidden_state = exchange(4, ready(attn_pack), inputs[0])
+    (attn_got,) = exchange(4, ready(attn_pack))
     gate, up, down, attn_got = together(w_gate[0], w_up[0], w_down[0].T, attn_got)
     mlp_blocks = ready(jnp.concatenate([by_rank(gate), by_rank(up), by_rank(down)], axis=2))
     (first_got,) = exchange(5, mlp_blocks[..., :cut])
@@ -1198,7 +1198,7 @@
     second_blocks, first_got, cosine, sine, cosine3, sine3, bounds, query_rows = together(
         mlp_blocks[..., cut:], first_got, cosine, sine, cosine3, sine3, bounds, query_rows
     )
-    (second_got,) = exchange(6, second_blocks)
+    second_got, hidden_state = exchange(6, second_blocks, inputs[0])
     attn_parts, first_parts, second_parts = by_layer(attn_got), by_layer(first_got), by_layer(second_got)
 
     def flat(array):

time: 1540 us -> 1540 us (level)
  transfers between devices with their start and end apart: 20 -> 20, of which waited for: 4 -> 4; matrix products, arithmetic and copies ran while one was open for 1% -> 1% of each run, Pallas kernels for 77% -> 79%
where the time goes in v10:
time: 1540 us; the launch traced here: 1530 us
  Pallas kernels  1450 us (94%)
  local copies, waits for them, and re-layouts  27.2 us (2%)
  waiting for transfers between devices  21.6 us (1%)
  other arithmetic  19.8 us (1%)
  between operations  15.5 us (1%)
    pallas_call x25, Pallas kernels, plane_call(): pl.pallas_call(kernel, out_shape=out_shape, in_specs=in_specs, out_specs=...  1270 us
    pallas_call x4, Pallas kernels, attend_back(): pl.pallas_call(functools.partial(back_kernel, scale, scale2, bq, bk), gri...  98.3 us
    pallas_call x4, Pallas kernels, attend(): pl.pallas_call(functools.partial(attend_kernel, scale2, bq, bk), grid_spe...  67.4 us
  transfers between devices with their start and end apart: 20, of which 4 were waited for; matrix products, arithmetic and copies ran while one was open for 1% of the time, Pallas kernels for 79%

profile of v10, /device:TPU:2, one launch (start us, length us, event | category | flops | bytes accessed | tf_op | source)
XLA Modules:
  0.0 1532.2 jit_solution(2725723839237425320)
XLA Ops:
  13.4 4.2 concatenate.14
  17.6 25.1 %exchange.5 = bf16[8,192,640]{2,1,0:T(8,128)(2,1)} custom-call(bf16[8,192,640]{2,1,0:T(8,128)(2,1)} %bitcast.151), custom_call_target="tpu_custom_call" | custom-call | bytes 72000000 | tf_op jit(solution)/shard_map/exchange/pallas_call | solution.py:428
  42.7 2.9 fusion.7
  50.8 2.7 fusion.4
  53.5 29.2 %exchange.6 = bf16[8,192,768]{2,1,0:T(8,128)(2,1)} custom-call(bf16[8,192,768]{2,1,0:T(8,128)(2,1)} %get-tuple-element.345.blocks), custom_call_target="tpu_custom_call" | custom-call | bytes 87000000 | tf_op jit(solution)/shard_map/exchange/pallas_call | solution.py:428
  83.4 3.7 fusion
  89.3 1.9 select_maximum_fusion
  92.7 47.4 %exchange.7 = (bf16[8,192,768]{2,1,0:T(8,128)(2,1)}, bf16[256,1536]{1,0:T(8,128)(2,1)}) custom-call(bf16[8,192,768]{2,1,0:T(8,128)(2,1)} %get-tuple-element.180.refs_0_, bf16[256,1536]{1,0:T(8,128)(2,1)} %bitcast.219), custom_call_target="tpu_custom_call" | custom-call | bytes 87000000 | tf_op jit(solution)/shard_map/exchange/pallas_call | solution.py:428
  140.2 3.0 fusion.5
  143.2 7.9 all-gather.15.cloned.1.call-done.w1_hbm
  151.3 46.0 %attn_in.4 = (bf16[8,256,1536]{2,1,0:T(8,128)(2,1)}, bf16[2,8,256,128]{3,2,1,0:T(8,128)(2,1)}, bf16[8,256,128]{2,1,0:T(8,128)(2,1)}, bf16[8,256,128]{2,1,0:T(8,128)(2,1)}, f32[2,1536]{1,0:T(2,128)}) custom-call(bf16[256,1536]{1,0:T(8,128)(2,1)} %get-tuple-element.185.h.h_hbm, bf16[1536,640]{1,0:T(8,128)(2,1)} %all-gather.13.cloned.1.call-done.w_hbm.wa_hbm, ...), custom_call_target="tpu_custom_call" | custom-call | bytes 102000000 | tf_op jit(solution)/shard_map/attn_in/pallas_call | solution.py:428
  197.3 16.9 %attend.4 = (bf16[2048,192]{1,0:T(8,128)(2,1)}, f32[4,1,1024]{2,1,0:T(1,128)}) custom-call(s32[2,4]{1,0:T(2,128)} %pad_add_fusion.bounds, s32[1]{0:T(128)} %dynamic_slice.3.length, bf16[2,2048,128]{2,1,0:T(8,128)(2,1)} %bitcast.157, bf16[2048,128]{1,0:T(8,128)(2,1)} %bitcast.176, bf16[2048,128]{1,0:T(8,128)(2,1)} %bitcast.178, ...), custom_call_target="tpu_custom_call" | custom-call | bytes 45000000 | tf_op jit(solution)/shard_map/attend/pallas_call | solution.py:994
  215.3 89.4 %mlp.4 = (f32[256,1536]{1,0:T(8,128)}, bf16[8,256,1536]{2,1,0:T(8,128)(2,1)}, bf16[8,256,1024]{2,1,0:T(8,128)(2,1)}, bf16[8,256,512]{2,1,0:T(8,128)(2,1)}, bf16[256,1536]{1,0:T(8,128)(2,1)}) custom-call(bf16[256,1536]{1,0:T(8,128)(2,1)} %get-tuple-element.185.h.h_hbm, bf16[8,256,192]{2,1,0:T(8,128)(2,1)} %bitcast.143, f32[2,1536]{1,0:T(2,128)} %get-tuple-element.196.gain, ...), custom_call_target="tpu_custom_call" | custom-call | bytes 288000000 | tf_op jit(solution)/shard_map/mlp/pallas_call | solution.py:428
  304.7 4.2 all-gather.21.cloned.1.call-done.w1_hbm
  309.0 35.5 %attn_in.5 = (bf16[8,256,1536]{2,1,0:T(8,128)(2,1)}, bf16[2,8,256,128]{3,2,1,0:T(8,128)(2,1)}, bf16[8,256,128]{2,1,0:T(8,128)(2,1)}, bf16[8,256,128]{2,1,0:T(8,128)(2,1)}, f32[2,1536]{1,0:T(2,128)}) custom-call(bf16[256,1536]{1,0:T(8,128)(2,1)} %get-tuple-element.202.h.h_hbm, bf16[1536,640]{1,0:T(8,128)(2,1)} %all-gather.19.cloned.1.call-done.w_hbm.wa_hbm, ...), custom_call_target="tpu_custom_call" | custom-call | bytes 102000000 | tf_op jit(solution)/shard_map/attn_in/pallas_call | solution.py:428
  344.5 16.8 %attend.5 = (bf16[2048,192]{1,0:T(8,128)(2,1)}, f32[4,1,1024]{2,1,0:T(1,128)}) custom-call(s32[2,4]{1,0:T(2,128)} %pad_add_fusion.bounds, s32[1]{0:T(128)} %dynamic_slice.3.length, bf16[2,2048,128]{2,1,0:T(8,128)(2,1)} %bitcast.159, bf16[2048,128]{1,0:T(8,128)(2,1)} %bitcast.180, bf16[2048,128]{1,0:T(8,128)(2,1)} %bitcast.182, ...), custom_call_target="tpu_custom_call" | custom-call | bytes 45000000 | tf_op jit(solution)/shard_map/attend/pallas_call | solution.py:994
  362.6 89.4 %mlp.5 = (f32[256,1536]{1,0:T(8,128)}, bf16[8,256,1536]{2,1,0:T(8,128)(2,1)}, bf16[8,256,1024]{2,1,0:T(8,128)(2,1)}, bf16[8,256,512]{2,1,0:T(8,128)(2,1)}, bf16[256,1536]{1,0:T(8,128)(2,1)}) custom-call(bf16[256,1536]{1,0:T(8,128)(2,1)} %get-tuple-element.202.h.h_hbm, bf16[8,256,192]{2,1,0:T(8,128)(2,1)} %bitcast.145, f32[2,1536]{1,0:T(2,128)} %get-tuple-element.209.gain, ...), custom_call_target="tpu_custom_call" | custom-call | bytes 288000000 | tf_op jit(solution)/shard_map/mlp/pallas_call | solution.py:428
  452.1 3.6 all-gather.27.cloned.1.call-done.w1_hbm
  455.8 35.6 %attn_in.6 = (bf16[8,256,1536]{2,1,0:T(8,128)(2,1)}, bf16[2,8,256,128]{3,2,1,0:T(8,128)(2,1)}, bf16[8,256,128]{2,1,0:T(8,128)(2,1)}, bf16[8,256,128]{2,1,0:T(8,128)(2,1)}, f32[2,1536]{1,0:T(2,128)}) custom-call(bf16[256,1536]{1,0:T(8,128)(2,1)} %get-tuple-element.215.h.h_hbm, bf16[1536,640]{1,0:T(8,128)(2,1)} %all-gather.25.cloned.1.call-done.w_hbm.wa_hbm, ...), custom_call_target="tpu_custom_call" | custom-call | bytes 102000000 | tf_op jit(solution)/shard_map/attn_in/pallas_call | solution.py:428
  491.4 16.8 %attend.6 = (bf16[2048,192]{1,0:T(8,128)(2,1)}, f32[4,1,1024]{2,1,0:T(1,128)}) custom-call(s32[2,4]{1,0:T(2,128)} %pad_add_fusion.bounds, s32[1]{0:T(128)} %dynamic_slice.3.length, bf16[2,2048,128]{2,1,0:T(8,128)(2,1)} %bitcast.161, bf16[2048,128]{1,0:T(8,128)(2,1)} %bitcast.184, bf16[2048,128]{1,0:T(8,128)(2,1)} %bitcast.186, ...), custom_call_target="tpu_custom_call" | custom-call | bytes 45000000 | tf_op jit(solution)/shard_map/attend/pallas_call | solution.py:994
  509.5 89.5 %mlp.6 = (f32[256,1536]{1,0:T(8,128)}, bf16[8,256,1536]{2,1,0:T(8,128)(2,1)}, bf16[8,256,1024]{2,1,0:T(8,128)(2,1)}, bf16[8,256,512]{2,1,0:T(8,128)(2,1)}, bf16[256,1536]{1,0:T(8,128)(2,1)}) custom-call(bf16[256,1536]{1,0:T(8,128)(2,1)} %get-tuple-element.215.h.h_hbm, bf16[8,256,192]{2,1,0:T(8,128)(2,1)} %bitcast.147, f32[2,1536]{1,0:T(2,128)} %get-tuple-element.222.gain, ...), custom_call_target="tpu_custom_call" | custom-call | bytes 288000000 | tf_op jit(solution)/shard_map/mlp/pallas_call | solution.py:428
  599.0 3.5 all-gather.33.cloned.1.call-done.refs_4_.refs_6_
  603.2 35.6 %attn_in.7 = (bf16[8,256,1536]{2,1,0:T(8,128)(2,1)}, bf16[2,8,256,128]{3,2,1,0:T(8,128)(2,1)}, bf16[8,256,128]{2,1,0:T(8,128)(2,1)}, bf16[8,256,128]{2,1,0:T(8,128)(2,1)}, f32[2,1536]{1,0:T(2,128)}) custom-call(bf16[256,1536]{1,0:T(8,128)(2,1)} %get-tuple-element.228.h.refs_0_.h_hbm, bf16[1536,640]{1,0:T(8,128)(2,1)} %all-gather.31.cloned.1.call-done.w_hbm.refs_3_.wa_hbm, ...), custom_call_target="tpu_custom_call" | custom-call | bytes 102000000 | tf_op jit(solution)/shard_map/attn_in/pallas_call | solution.py:428
  638.8 16.8 %attend.7 = (bf16[2048,192]{1,0:T(8,128)(2,1)}, f32[4,1,1024]{2,1,0:T(1,128)}) custom-call(s32[2,4]{1,0:T(2,128)} %pad_add_fusion.bounds, s32[1]{0:T(128)} %dynamic_slice.3.length, bf16[2,2048,128]{2,1,0:T(8,128)(2,1)} %bitcast.163, bf16[2048,128]{1,0:T(8,128)(2,1)} %bitcast.188, bf16[2048,128]{1,0:T(8,128)(2,1)} %bitcast.190, ...), custom_call_target="tpu_custom_call" | custom-call | bytes 45000000 | tf_op jit(solution)/shard_map/attend/pallas_call | solution.py:994
  655.6 107.4 %mlp.7 = (f32[256,1536]{1,0:T(8,128)}, bf16[8,256,1536]{2,1,0:T(8,128)(2,1)}, bf16[8,256,1024]{2,1,0:T(8,128)(2,1)}, bf16[8,256,512]{2,1,0:T(8,128)(2,1)}, bf16[...) custom-call(bf16[256,1536]{1,0:T(8,128)(2,1)} %get-tuple-element.228.h.refs_0_.h_hbm, bf16[8,256,192]{2,1,0:T(8,128)(2,1)} %bitcast.149, ...), custom_call_target="tpu_custom_call" | custom-call | bytes 288000000 | tf_op jit(solution)/shard_map/mlp/pallas_call | solution.py:428
  763.0 2.1 broadcast_select_fusion.refs_0_
  765.1 71.6 %mlp_back.4 = (f32[256,1536]{1,0:T(8,128)}, f32[1,1536]{1,0:T(1,128)}, bf16[256,1536]{1,0:T(8,128)(2,1)}, bf16[1536,1536]{1,0:T(8,128)(2,1)}, bf16[256,1536]{1,0:T(8,128)(2,1)}) custom-call(bf16[256,1536]{1,0:T(8,128)(2,1)} %broadcast_select_fusion.refs_0_, f32[256,1536]{1,0:T(8,128)} %get-tuple-element.238.refs_1_, ...), custom_call_target="tpu_custom_call" | custom-call | bytes 204000000 | tf_op jit(solution)/shard_map/mlp_back/pallas_call | solution.py:428
  836.8 34.5 %dat_gather.4 = (bf16[8,256,1536]{2,1,0:T(8,128)(2,1)}, bf16[8,256,256]{2,1,0:T(8,128)(2,1)}) custom-call(bf16[256,1536]{1,0:T(8,128)(2,1)} %get-tuple-element.245.dat, bf16[1536,640]{1,0:T(8,128)(2,1)} %all-gather.31.cloned.1.call-done.w_hbm.refs_3_.wa_hbm), custom_call_target="tpu_custom_call" | custom-call | bytes 96000000 | tf_op jit(solution)/shard_map/dat_gather/pallas_call | solution.py:428
  871.4 24.5 %attend_back.4 = (bf16[2048,256]{1,0:T(8,128)(2,1)}, f32[2048,128]{1,0:T(8,128)}, f32[2048,128]{1,0:T(8,128)}) custom-call(s32[2,4]{1,0:T(2,128)} %pad_add_fusion.bounds, s32[1]{0:T(128)} %dynamic_slice.3.length, bf16[2,2048,128]{2,1,0:T(8,128)(2,1)} %bitcast.164, bf16[2048,128]{1,0:T(8,128)(2,1)} %bitcast.189, bf16[2048,128]{1,0:T(8,128)(2,1)} %bitcast.191, ...), custom_call_target="tpu_custom_call" | custom-call | bytes 65000000 | tf_op jit(solution)/shard_map/attend_back/pallas_call | solution.py:1061
  895.9 38.2 %attn_back.4 = (bf16[256,1536]{1,0:T(8,128)(2,1)}, bf16[1536,640]{1,0:T(8,128)(2,1)}) custom-call(f32[2,1536]{1,0:T(2,128)} %get-tuple-element.234.refs_2_.gain, f32[1,1536]{1,0:T(1,128)} %get-tuple-element.244.gain2_grad, bf16[8,256,256]{2,1,0:T(8,128)(2,1)} %bitcast.213, f32[8,256,128]{2,1,0:T(8,128)} %bitcast.214, f32[8,256,128]{2,1,0:T(8,128)} %bitcast.215, ...), custom_call_target="tpu_custom_call" | custom-call | bytes 108000000 | tf_op jit(solution)/shard_map/attn_back/pallas_call | solution.py:428
  934.2 63.9 %mlp_back.5 = (f32[256,1536]{1,0:T(8,128)}, f32[1,1536]{1,0:T(1,128)}, bf16[256,1536]{1,0:T(8,128)(2,1)}, bf16[1536,1536]{1,0:T(8,128)(2,1)}) custom-call(bf16[256,1536]{1,0:T(8,128)(2,1)} %get-tuple-element.259.e, f32[256,1536]{1,0:T(8,128)} %get-tuple-element.260.mid, f32[2,1536]{1,0:T(2,128)} %get-tuple-element.222.gain, ...), custom_call_target="tpu_custom_call" | custom-call | bytes 204000000 | tf_op jit(solution)/shard_map/mlp_back/pallas_call | solution.py:428
  998.2 33.4 %dat_gather.5 = (bf16[8,256,1536]{2,1,0:T(8,128)(2,1)}, bf16[8,256,256]{2,1,0:T(8,128)(2,1)}) custom-call(bf16[256,1536]{1,0:T(8,128)(2,1)} %get-tuple-element.268.dat, bf16[1536,640]{1,0:T(8,128)(2,1)} %all-gather.25.cloned.1.call-done.w_hbm.wa_hbm), custom_call_target="tpu_custom_call" | custom-call | bytes 96000000 | tf_op jit(solution)/shard_map/dat_gather/pallas_call | solution.py:428
  1031.6 24.7 %attend_back.5 = (bf16[2048,256]{1,0:T(8,128)(2,1)}, f32[2048,128]{1,0:T(8,128)}, f32[2048,128]{1,0:T(8,128)}) custom-call(s32[2,4]{1,0:T(2,128)} %pad_add_fusion.bounds, s32[1]{0:T(128)} %dynamic_slice.3.length, bf16[2,2048,128]{2,1,0:T(8,128)(2,1)} %bitcast.162, bf16[2048,128]{1,0:T(8,128)(2,1)} %bitcast.185, bf16[2048,128]{1,0:T(8,128)(2,1)} %bitcast.187, ...), custom_call_target="tpu_custom_call" | custom-call | bytes 65000000 | tf_op jit(solution)/shard_map/attend_back/pallas_call | solution.py:1061
  1056.3 38.2 %attn_back.5 = (bf16[256,1536]{1,0:T(8,128)(2,1)}, bf16[1536,640]{1,0:T(8,128)(2,1)}) custom-call(f32[2,1536]{1,0:T(2,128)} %get-tuple-element.222.gain, f32[1,1536]{1,0:T(1,128)} %get-tuple-element.264.gain2_grad, bf16[8,256,256]{2,1,0:T(8,128)(2,1)} %bitcast.207, f32[8,256,128]{2,1,0:T(8,128)} %bitcast.208, f32[8,256,128]{2,1,0:T(8,128)} %bitcast.209, ...), custom_call_target="tpu_custom_call" | custom-call | bytes 108000000 | tf_op jit(solution)/shard_map/attn_back/pallas_call | solution.py:428
  1094.6 63.9 %mlp_back.6 = (f32[256,1536]{1,0:T(8,128)}, f32[1,1536]{1,0:T(1,128)}, bf16[256,1536]{1,0:T(8,128)(2,1)}, bf16[1536,1536]{1,0:T(8,128)(2,1)}) custom-call(bf16[256,1536]{1,0:T(8,128)(2,1)} %get-tuple-element.280.e, f32[256,1536]{1,0:T(8,128)} %get-tuple-element.281.mid, f32[2,1536]{1,0:T(2,128)} %get-tuple-element.209.gain, ...), custom_call_target="tpu_custom_call" | custom-call | bytes 204000000 | tf_op jit(solution)/shard_map/mlp_back/pallas_call | solution.py:428
  1158.6 33.2 %dat_gather.6 = (bf16[8,256,1536]{2,1,0:T(8,128)(2,1)}, bf16[8,256,256]{2,1,0:T(8,128)(2,1)}) custom-call(bf16[256,1536]{1,0:T(8,128)(2,1)} %get-tuple-element.289.dat, bf16[1536,640]{1,0:T(8,128)(2,1)} %all-gather.19.cloned.1.call-done.w_hbm.wa_hbm), custom_call_target="tpu_custom_call" | custom-call | bytes 96000000 | tf_op jit(solution)/shard_map/dat_gather/pallas_call | solution.py:428
  1191.9 24.5 %attend_back.6 = (bf16[2048,256]{1,0:T(8,128)(2,1)}, f32[2048,128]{1,0:T(8,128)}, f32[2048,128]{1,0:T(8,128)}) custom-call(s32[2,4]{1,0:T(2,128)} %pad_add_fusion.bounds, s32[1]{0:T(128)} %dynamic_slice.3.length, bf16[2,2048,128]{2,1,0:T(8,128)(2,1)} %bitcast.160, bf16[2048,128]{1,0:T(8,128)(2,1)} %bitcast.181, bf16[2048,128]{1,0:T(8,128)(2,1)} %bitcast.183, ...), custom_call_target="tpu_custom_call" | custom-call | bytes 65000000 | tf_op jit(solution)/shard_map/attend_back/pallas_call | solution.py:1061
  1216.4 38.3 %attn_back.6 = (bf16[256,1536]{1,0:T(8,128)(2,1)}, bf16[1536,640]{1,0:T(8,128)(2,1)}) custom-call(f32[2,1536]{1,0:T(2,128)} %get-tuple-element.209.gain, f32[1,1536]{1,0:T(1,128)} %get-tuple-element.285.gain2_grad, bf16[8,256,256]{2,1,0:T(8,128)(2,1)} %bitcast.210, f32[8,256,128]{2,1,0:T(8,128)} %bitcast.211, f32[8,256,128]{2,1,0:T(8,128)} %bitcast.212, ...), custom_call_target="tpu_custom_call" | custom-call | bytes 108000000 | tf_op jit(solution)/shard_map/attn_back/pallas_call | solution.py:428
  1254.8 63.6 %mlp_back.7 = (f32[256,1536]{1,0:T(8,128)}, f32[1,1536]{1,0:T(1,128)}, bf16[256,1536]{1,0:T(8,128)(2,1)}, bf16[1536,1536]{1,0:T(8,128)(2,1)}) custom-call(bf16[256,1536]{1,0:T(8,128)(2,1)} %get-tuple-element.301.e, f32[256,1536]{1,0:T(8,128)} %get-tuple-element.302.mid, f32[2,1536]{1,0:T(2,128)} %get-tuple-element.196.gain, ...), custom_call_target="tpu_custom_call" | custom-call | bytes 204000000 | tf_op jit(solution)/shard_map/mlp_back/pallas_call | solution.py:428
  1318.5 33.4 %dat_gather.7 = (bf16[8,256,1536]{2,1,0:T(8,128)(2,1)}, bf16[8,256,256]{2,1,0:T(8,128)(2,1)}) custom-call(bf16[256,1536]{1,0:T(8,128)(2,1)} %get-tuple-element.310.dat, bf16[1536,640]{1,0:T(8,128)(2,1)} %all-gather.13.cloned.1.call-done.w_hbm.wa_hbm), custom_call_target="tpu_custom_call" | custom-call | bytes 96000000 | tf_op jit(solution)/shard_map/dat_gather/pallas_call | solution.py:428
  1351.9 24.5 %attend_back.7 = (bf16[2048,256]{1,0:T(8,128)(2,1)}, f32[2048,128]{1,0:T(8,128)}, f32[2048,128]{1,0:T(8,128)}) custom-call(s32[2,4]{1,0:T(2,128)} %pad_add_fusion.bounds, s32[1]{0:T(128)} %dynamic_slice.3.length, bf16[2,2048,128]{2,1,0:T(8,128)(2,1)} %bitcast.158, bf16[2048,128]{1,0:T(8,128)(2,1)} %bitcast.177, bf16[2048,128]{1,0:T(8,128)(2,1)} %bitcast.179, ...), custom_call_target="tpu_custom_call" | custom-call | bytes 65000000 | tf_op jit(solution)/shard_map/attend_back/pallas_call | solution.py:1061
  1376.4 38.2 %attn_back.7 = (bf16[256,1536]{1,0:T(8,128)(2,1)}, bf16[1536,640]{1,0:T(8,128)(2,1)}) custom-call(f32[2,1536]{1,0:T(2,128)} %get-tuple-element.196.gain, f32[1,1536]{1,0:T(1,128)} %get-tuple-element.306.gain2_grad, bf16[8,256,256]{2,1,0:T(8,128)(2,1)} %bitcast.204, f32[8,256,128]{2,1,0:T(8,128)} %bitcast.205, f32[8,256,128]{2,1,0:T(8,128)} %bitcast.206, ...), custom_call_target="tpu_custom_call" | custom-call | bytes 108000000 | tf_op jit(solution)/shard_map/attn_back/pallas_call | solution.py:428
  1415.9 3.6 pad_maximum_fusion
  1419.5 63.0 %exchange.8 = (bf16[8,192,1536]{2,1,0:T(8,128)(2,1)}, bf16[256,1536]{1,0:T(8,128)(2,1)}) custom-call(bf16[8,192,1536]{2,1,0:T(8,128)(2,1)} %bitcast.142, bf16[256,1536]{1,0:T(8,128)(2,1)} %get-tuple-element.326.refs_1_), custom_call_target="tpu_custom_call" | custom-call | bytes 174000000 | tf_op jit(solution)/shard_map/exchange/pallas_call | solution.py:428
  1482.6 2.6 pad_maximum_fusion.1
  1485.1 25.0 %exchange.9.got = bf16[8,192,640]{2,1,0:T(8,128)(2,1)} custom-call(bf16[8,192,640]{2,1,0:T(8,128)(2,1)} %bitcast.152), custom_call_target="tpu_custom_call" | custom-call | bytes 72000000 | tf_op jit(solution)/shard_map/exchange/pallas_call | solution.py:428
  1510.2 4.0 finish_attn.1
  1515.5 7.6 finish.1
  (132 shorter events, 24.9 us)
Async XLA Ops:
  7.2 3.3 copy-start.11
  7.2 136.0 %all-gather.13.cloned.1.call-start = ((), (), s32[]{:S(2)}) async-start(), calls=%async_computation.8 | async-start | bytes 2457600 | tf_op jit(solution)/shard_map/all_gather | solution.py:1150
  8.8 2.3 copy-start.7
  11.1 1.3 copy-start.8
  12.4 0.8 copy-start.15
  42.7 3.3 copy-start.1
  45.7 105.4 %all-gather.15.cloned.1.call-start = ((), (), s32[]{:S(2)}) async-start(), calls=%async_computation.9 | async-start | bytes 2949120 | tf_op jit(solution)/shard_map/all_gather | solution.py:1150
  46.2 1.9 copy-start.2
  48.1 1.9 copy-start.3
  53.5 29.2 %copy-start.16 = (s32[4]{0:T(128)S(1)}, s32[4]{0:T(128)}, u32[]{:S(2)}) copy-start(s32[4]{0:T(128)} %param.13) | copy-start | bytes 52
  89.3 1.9 copy-start
  92.7 122.6 %all-gather.17.cloned.1.call-start = ((), (), s32[]{:S(2)}) async-start(), calls=%async_computation.10 | async-start | bytes 2949120 | tf_op jit(solution)/shard_map/all_gather | solution.py:1150
  151.1 153.6 %all-gather.19.cloned.1.call-start = ((), (), s32[]{:S(2)}) async-start(), calls=%async_computation.11 | async-start | bytes 2457600 | tf_op jit(solution)/shard_map/all_gather | solution.py:1150
  214.2 94.7 %all-gather.21.cloned.1.call-start = ((), (), s32[]{:S(2)}) async-start(), calls=%async_computation.12 | async-start | bytes 2949120 | tf_op jit(solution)/shard_map/all_gather | solution.py:1150
  214.8 147.8 %all-gather.23.cloned.1.call-start = ((), (), s32[]{:S(2)}) async-start(), calls=%async_computation.13 | async-start | bytes 2949120 | tf_op jit(solution)/shard_map/all_gather | solution.py:1150
  308.9 143.2 %all-gather.25.cloned.1.call-start = ((), (), s32[]{:S(2)}) async-start(), calls=%async_computation.14 | async-start | bytes 2457600 | tf_op jit(solution)/shard_map/all_gather | solution.py:1150
  361.4 94.3 %all-gather.27.cloned.1.call-start = ((), (), s32[]{:S(2)}) async-start(), calls=%async_computation.15 | async-start | bytes 2949120 | tf_op jit(solution)/shard_map/all_gather | solution.py:1150
  362.2 147.3 %all-gather.29.cloned.1.call-start = ((), (), s32[]{:S(2)}) async-start(), calls=%async_computation.16 | async-start | bytes 2949120 | tf_op jit(solution)/shard_map/all_gather | solution.py:1150
  455.7 143.2 %all-gather.31.cloned.1.call-start = ((), (), s32[]{:S(2)}) async-start(), calls=%async_computation.17 | async-start | bytes 2457600 | tf_op jit(solution)/shard_map/all_gather | solution.py:1150
  508.2 94.2 %all-gather.33.cloned.1.call-start = ((), (), s32[]{:S(2)}) async-start(), calls=%async_computation.18 | async-start | bytes 2949120 | tf_op jit(solution)/shard_map/all_gather | solution.py:1150
  509.0 146.7 %all-gather.35.cloned.1.call-start = ((), (), s32[]{:S(2)}) async-start(), calls=%async_computation.19 | async-start | bytes 2949120 | tf_op jit(solution)/shard_map/all_gather | solution.py:1150
  602.5 331.6 %reduce-scatter.9.cloned.1.call-start = ((), (), s32[]{:S(2)}) async-start(), calls=%async_computation.20 | async-start | bytes 5898240 | tf_op jit(solution)/shard_map/reduce_scatter | solution.py:1153
  836.8 161.3 %reduce-scatter.11.cloned.1.call-start = ((), (), s32[]{:S(2)}) async-start(), calls=%async_computation.21 | async-start | bytes 2457600 | tf_op jit(solution)/shard_map/reduce_scatter | solution.py:1153
  934.1 160.4 %reduce-scatter.13.cloned.1.call-start = ((), (), s32[]{:S(2)}) async-start(), calls=%async_computation.22 | async-start | bytes 5898240 | tf_op jit(solution)/shard_map/reduce_scatter | solution.py:1153
  998.1 160.4 %reduce-scatter.15.cloned.1.call-start = ((), (), s32[]{:S(2)}) async-start(), calls=%async_computation.23 | async-start | bytes 2457600 | tf_op jit(solution)/shard_map/reduce_scatter | solution.py:1153
  1094.5 160.2 %reduce-scatter.17.cloned.1.call-start = ((), (), s32[]{:S(2)}) async-start(), calls=%async_computation.24 | async-start | bytes 5898240 | tf_op jit(solution)/shard_map/reduce_scatter | solution.py:1153
  1158.6 159.8 %reduce-scatter.19.cloned.1.call-start = ((), (), s32[]{:S(2)}) async-start(), calls=%async_computation.25 | async-start | bytes 2457600 | tf_op jit(solution)/shard_map/reduce_scatter | solution.py:1153
  1254.7 159.9 %reduce-scatter.21.cloned.1.call-start = ((), (), s32[]{:S(2)}) async-start(), calls=%async_computation.26 | async-start | bytes 5898240 | tf_op jit(solution)/shard_map/reduce_scatter | solution.py:1153
  1318.4 164.1 %reduce-scatter.23.cloned.1.call-start = ((), (), s32[]{:S(2)}) async-start(), calls=%async_computation.27 | async-start | bytes 2457600 | tf_op jit(solution)/shard_map/reduce_scatter | solution.py:1153
  1376.4 38.3 %copy-start.5 = (bf16[384,1536]{1,0:T(8,128)(2,1)S(1)}, bf16[384,1536]{1,0:T(8,128)(2,1)}, u32[]{:S(2)}) copy-start(bf16[384,1536]{1,0:T(8,128)(2,1)} %reduce-scatter.13.cloned.1.call-done) | copy-start | bytes 3538948
  1376.4 38.3 %copy-start.6 = (bf16[384,1536]{1,0:T(8,128)(2,1)S(1)}, bf16[384,1536]{1,0:T(8,128)(2,1)}, u32[]{:S(2)}) copy-start(bf16[384,1536]{1,0:T(8,128)(2,1)} %reduce-scatter.17.cloned.1.call-done) | copy-start | bytes 3538948
  1414.6 1.3 copy-start.4
  1419.5 63.0 %copy-start.12 = (bf16[384,640]{1,0:T(8,128)(2,1)S(1)}, bf16[384,640]{1,0:T(8,128)(2,1)}, u32[]{:S(2)}) copy-start(bf16[384,640]{1,0:T(8,128)(2,1)} %reduce-scatter.11.cloned.1.call-done) | copy-start | bytes 1474564
  1419.5 63.1 %copy-start.13 = (bf16[384,640]{1,0:T(8,128)(2,1)S(1)}, bf16[384,640]{1,0:T(8,128)(2,1)}, u32[]{:S(2)}) copy-start(bf16[384,640]{1,0:T(8,128)(2,1)} %reduce-scatter.15.cloned.1.call-done) | copy-start | bytes 1474564
  1419.5 63.1 %copy-start.14 = (bf16[384,640]{1,0:T(8,128)(2,1)S(1)}, bf16[384,640]{1,0:T(8,128)(2,1)}, u32[]{:S(2)}) copy-start(bf16[384,640]{1,0:T(8,128)(2,1)} %reduce-scatter.19.cloned.1.call-done) | copy-start | bytes 1474564
  1515.5 7.7 copy-start.9
  1515.5 8.5 copy-start.10
Sparse Core Ops, SparseCore 0:
  45.8 44.7 all-gather.12
  92.8 58.2 all-gather.14
  153.2 60.2 all-gather.16
  214.9 42.6 all-gather.18
  259.6 49.3 all-gather.20
  310.9 49.2 all-gather.22
  361.8 42.3 all-gather.24
  406.3 49.3 all-gather.26
  457.3 49.3 all-gather.28
  508.4 42.5 all-gather.30
  553.1 49.3 all-gather.32
  603.9 49.2 all-gather.34
  836.9 84.1 reduce-scatter.8
  934.2 39.3 reduce-scatter.10
  998.3 82.9 reduce-scatter.12
  1094.7 39.4 reduce-scatter.14
  1158.7 83.8 reduce-scatter.16
  1254.9 40.7 reduce-scatter.18
  1318.6 85.1 reduce-scatter.20
  1414.8 56.2 reduce-scatter.22
